TPU v7x, 32 devices: a whole 2x2x4 slice. The times are simulated.
32 devices in a mesh: grp: 4 (over y, x), frm: 8 (over z, core).
Axes of the slice: x: 2, y: 2, z: 4, core: 2. Of those that a mesh axis runs over, the one named last changes fastest.
Arguments:
- query_in: bfloat16 [8, 128, 2048], P(None, ('grp', 'frm')), may hold values from -32 to 32
- key_in: bfloat16 [8, 128, 2048], P(None, ('grp', 'frm')), may hold values from -32 to 32
- value_in: bfloat16 [8, 128, 2048], P(None, ('grp', 'frm')), may hold values from -6 to 6
- cotangent: bfloat16 [8, 128, 2048], P('frm', 'grp'), may hold values from -6 to 6
- w_in: bfloat16 [4, 2048, 4096], P('grp', None, 'frm'), may hold values from -0.1875 to 0.1875
- w_out: bfloat16 [4, 4096, 2048], P('grp', 'frm'), may hold values from -0.125 to 0.125
- gate_probs: float32 [2, 32], replicated, may hold values from 0.5 to 1
- chosen: int32 [2, 32], replicated, may hold values from 0 to 1023, as said below
Outputs:
- grad_query: bfloat16 [8, 128, 2048], P(None, ('grp', 'frm'))
- grad_key: bfloat16 [8, 128, 2048], P(None, ('grp', 'frm'))
- grad_value: bfloat16 [8, 128, 2048], P(None, ('grp', 'frm'))
Inputs may be any that keep to these rules, and one draw needn't show every extreme that they name: `chosen`: row e lists 32 distinct tokens, token t = frame * 128 + patch. Call the tokens of 4 consecutive patches starting at a multiple of 4, over all frames, a block: an expert takes at most 2 tokens of a block, and exactly 2 of some block in every row.
All inputs are finite; a program needn't handle non-finite values.
Results may differ from a plain program's by a relative error of at most 0.025.
Values may be sent and summed in bfloat16 or wider, within the bound.
No kernel may reach another device: no remote copies, remote signals or barrier semaphores. Data moves between devices by JAX's collectives and lax.ppermute only.
A program may use at most 64 MiB of HBM per device.

v0:
```python
import jax
import jax.numpy as jnp
from jax import lax
from jax.sharding import PartitionSpec as P

HEADS = 16
MOST = 2


root_half = 0.7071067811865476
inv_root_tau = 0.3989422804014327


def gelu_slope(pre_act):
    normal_cdf = 0.5 * (1.0 + jax.scipy.special.erf(pre_act * root_half))
    density = jnp.exp(-0.5 * pre_act * pre_act) * inv_root_tau
    return normal_cdf + pre_act * density


def body(query_in, key_in, value_in, cotangent, w_in, w_out, gate_probs, chosen):
    frames, blocks, features = query_in.shape
    head_dim = features // HEADS
    scaling = head_dim ** (-0.5)
    groups = lax.axis_size("grp")
    columns = lax.axis_size("frm")
    experts = gate_probs.shape[0]
    local_rows = frames * blocks
    cot_patch = lax.all_to_all(cotangent, "frm", split_axis=1, concat_axis=0, tiled=True)
    cot_flat = cot_patch.reshape(local_rows, features)
    query_heads = query_in.reshape(frames, blocks, HEADS, head_dim)
    key_heads = key_in.reshape(frames, blocks, HEADS, head_dim)
    value_heads = value_in.reshape(frames, blocks, HEADS, head_dim)
    scores = (
        jnp.einsum("fphd,gphd->phfg", query_heads, key_heads, preferred_element_type=jnp.float32)
        * scaling
    )
    highest = jnp.max(scores, axis=-1, keepdims=True)
    raised = jnp.exp(scores - highest)
    attn_probs = raised / jnp.sum(raised, axis=-1, keepdims=True)
    weights = attn_probs.astype(jnp.bfloat16)
    attn_out = jnp.einsum(
        "phfg,gphd->fphd", weights, value_heads, preferred_element_type=jnp.float32
    )
    attn_out = attn_out.astype(jnp.bfloat16).reshape(local_rows, features)
    patches_all = blocks * groups * columns
    frame_of = chosen // patches_all
    patch_of = chosen % patches_all
    holder = patch_of // blocks
    position = frame_of * blocks + patch_of % blocks
    myself = lax.axis_index("grp") * columns + lax.axis_index("frm")
    owned_here = (holder == myself).astype(jnp.int32)
    ranking = jnp.cumsum(owned_here, axis=1) - 1
    slot_ids = jnp.arange(MOST, dtype=jnp.int32)
    selected = owned_here[:, None, :] * (ranking[:, None, :] == slot_ids[None, :, None]).astype(
        jnp.int32
    )
    position_at = jnp.sum(selected * position[:, None, :], axis=2)
    filled = jnp.sum(selected, axis=2)
    weight_at = jnp.sum(selected.astype(jnp.float32) * gate_probs[:, None, :], axis=2)
    row_ids = jnp.arange(local_rows, dtype=jnp.int32)
    onehot = (
        (position_at[:, :, None] == row_ids[None, None, :]) & (filled[:, :, None] > 0)
    ).astype(jnp.bfloat16)
    picked_in = jnp.einsum(
        "eml,ld->emd", onehot, attn_out, preferred_element_type=jnp.float32
    ).astype(jnp.bfloat16)
    picked_cot = jnp.einsum(
        "eml,ld->emd",
        onehot,
        cot_patch.reshape(local_rows, features),
        preferred_element_type=jnp.float32,
    )
    scaled = (weight_at[:, :, None] * picked_cot).astype(jnp.bfloat16)
    stacked = jnp.stack([picked_in, scaled], axis=2)
    own_in = w_in[0]
    own_out = w_out[0]
    slot_depth = MOST
    outgoing = jnp.broadcast_to(stacked[:, None], (experts, 2, MOST, 2, features)).reshape(
        groups, MOST, 2, features
    )
    routed = jnp.broadcast_to(onehot[:, None, :, None, :], (experts, 2, MOST, 1, local_rows))
    pieces = 1
    slice_width = own_in.shape[1] // pieces
    arrived = lax.all_to_all(outgoing, "grp", split_axis=0, concat_axis=0, tiled=True)
    shard_rows = lax.all_gather(
        arrived.reshape(groups * slot_depth, 2, features), "frm", axis=0, tiled=True
    )
    row_count = shard_rows.shape[0]
    pre_act = jnp.dot(shard_rows[:, 0, :], own_in, preferred_element_type=jnp.float32)
    back_act = lax.dot_general(
        shard_rows[:, 1, :], own_out, (((1,), (1,)), ((), ())), preferred_element_type=jnp.float32
    )
    slope = (back_act * gelu_slope(pre_act)).astype(jnp.bfloat16)
    product = jnp.einsum(
        "rks,dks->rkd",
        slope.reshape(row_count, pieces, slice_width),
        own_in.reshape(features, pieces, slice_width),
        preferred_element_type=jnp.float32,
    )
    partial_value = product.reshape(row_count, pieces * features)
    summed = lax.psum_scatter(
        partial_value.astype(jnp.bfloat16), "frm", scatter_dimension=0, tiled=True
    )
    returned = lax.all_to_all(
        summed.reshape(groups, slot_depth, pieces, features),
        "grp",
        split_axis=0,
        concat_axis=0,
        tiled=True,
    )
    flat_back = returned.reshape(groups * slot_depth * pieces, features)
    flat_route = routed.reshape(groups * slot_depth * pieces, local_rows)
    added = jnp.einsum("nl,nd->ld", flat_route, flat_back, preferred_element_type=jnp.float32)
    grad_stream = (cot_flat.astype(jnp.float32) + added).astype(jnp.bfloat16)
    grad_heads = grad_stream.reshape(frames, blocks, HEADS, head_dim)
    grad_value = jnp.einsum(
        "phfg,fphd->gphd", weights, grad_heads, preferred_element_type=jnp.float32
    ).astype(jnp.bfloat16)
    grad_prob = jnp.einsum(
        "fphd,gphd->phfg", grad_heads, value_heads, preferred_element_type=jnp.float32
    )
    centre = jnp.sum(attn_probs * grad_prob, axis=-1, keepdims=True)
    grad_score = (attn_probs * (grad_prob - centre)).astype(jnp.bfloat16)
    grad_query = (
        jnp.einsum("phfg,gphd->fphd", grad_score, key_heads, preferred_element_type=jnp.float32)
        * scaling
    ).astype(jnp.bfloat16)
    grad_key = (
        jnp.einsum("phfg,fphd->gphd", grad_score, query_heads, preferred_element_type=jnp.float32)
        * scaling
    ).astype(jnp.bfloat16)
    return (
        grad_query.reshape(frames, blocks, features),
        grad_key.reshape(frames, blocks, features),
        grad_value.reshape(frames, blocks, features),
    )


def solution(mesh):
    return jax.shard_map(
        body,
        mesh=mesh,
        in_specs=(
            P(None, ("grp", "frm"), None),
            P(None, ("grp", "frm"), None),
            P(None, ("grp", "frm"), None),
            P("frm", "grp", None),
            P("grp", None, "frm"),
            P("grp", "frm", None),
            P(),
            P(),
        ),
        out_specs=(
            P(None, ("grp", "frm"), None),
            P(None, ("grp", "frm"), None),
            P(None, ("grp", "frm"), None),
        ),
        check_vma=False,
    )
```

profile of v0, /device:TPU:0, one launch (start us, length us, event | category | flops | bytes accessed | tf_op | source)
XLA Modules:
  0.0 103.0 jit_solution(2572997079568323676)
XLA Ops:
  7.2 0.0 copy-start
  7.2 1.3 %copy.133 = bf16[1,32,2048]{2,0,1:T(2,128)(2,1)S(1)} copy(bf16[1,32,2048]{2,1,0:T(8,128)(2,1)} %param.11) | data formatting | bytes 262144 | tf_op args[3]
  8.4 0.5 broadcast.123
  9.0 0.0 copy-start.4
  9.0 0.0 copy-start.5
  9.0 1.4 %reduce = bf16[32,2048]{1,0:T(8,128)(2,1)S(1)} reduce(bf16[32,1,2048]{2,1,0:T(2,128)(2,1)S(1)} %bitcast.66, bf16[]{:T(256)} %broadcast.123), dimensions={1}, to_apply=%bitcast.65.reduce_sub_computation | reduce | bytes 262146
  10.4 0.8 reshape.103
  11.1 6.3 %all-to-all-start = ((bf16[8,2,4096]{2,1,0:T(2,128)(2,1)}), bf16[8,2,4096]{2,1,0:T(2,128)(2,1)S(1)}, u32[]{:S(2)}, u32[]{:S(2)}) async-start(bf16[8,2,4096]{2,1,0:T(2,128)(2,1)} %reshape.103), calls=%async_computation | async-start | bytes 262144 | tf_op jit(solution)/shard_map/all_to_all | solution.py:28
  17.5 0.0 reduce-scatter.2.cloned.1.call-start
  17.5 1.0 reshape.86
  18.5 1.0 reshape.87
  19.5 1.0 reshape.89
  20.5 0.0 copy-start.1
  20.5 0.3 fusion.72
  20.8 0.0 copy-start.2
  20.8 0.3 copy-done.1
  21.2 0.3 copy-done.2
  21.4 0.3 fusion.20
  21.8 0.1 reshape.99
  21.8 0.0 copy-done.4
  21.9 0.2 reduce_window_sum.11
  22.1 0.2 multiply_reduce_fusion.2
  22.3 0.0 copy-done.5
  22.3 0.1 multiply_reduce_fusion.1
  22.4 0.2 fusion.3
  22.6 1.7 %all-to-all-done = bf16[8,2,4096]{2,1,0:T(2,128)(2,1)S(1)} async-done(((bf16[8,2,4096]{2,1,0:T(2,128)(2,1)}), bf16[8,2,4096]{2,1,0:T(2,128)(2,1)S(1)}, u32[]{:S(2)}, u32[]{:S(2)}) %all-to-all-start) | async-done | bytes 131104 | tf_op jit(solution)/shard_map/all_to_all | solution.py:28
  24.2 0.1 reshape.104
  24.4 0.2 fusion.4
  24.7 8.4 %all_to_all.19 = bf16[4,2,2,2048]{3,1,2,0:T(2,128)(2,1)S(1)} all-to-all(bf16[4,2,2,2048]{3,1,2,0:T(2,128)(2,1)S(1)} %bitcast.69), channel_id=1, replica_groups=mesh['grp'=4,'frm'=8] {'grp'}, dimensions={0} | all-to-all | bytes 131072 | tf_op jit(solution)/shard_map/all_to_all | solution.py:84
  33.2 14.8 %all_gather.3 = bf16[64,2,2048]{2,0,1:T(8,128)(2,1)S(1)} all-gather(bf16[8,2,2048]{2,0,1:T(8,128)(2,1)S(1)} %reshape.92), channel_id=1, replica_groups=mesh['grp'=4,'frm'=8] {'frm'}, dimensions={0}, use_global_device_ids=true | all-gather | bytes 589824 | tf_op jit(solution)/shard_map/all_gather | solution.py:85
  48.0 0.0 copy-done
  48.0 0.5 fusion.6
  48.5 3.7 %convolution_convert_fusion = bf16[64,2048]{1,0:T(8,128)(2,1)} fusion(bf16[1,2048,512]{2,1,0:T(8,128)(2,1)S(1)} %copy-done, bf16[1,512,2048]{2,1,0:T(8,128)(2,1)} %param.13, bf16[64,2,2048]{2,0,1:T(8,128)(2,1)S(1)} %all_gather.3, f32[64,512]{1,0:T(8,128)S(1)} %fusion.6), kind=kOutput, calls=%fused_computation.1 | convolution fusion | flops 268894208 | bytes 4849664 | tf_op jit(solution)/shard_map/rks,dks->rkd/dot_general | solution.py:94
  52.2 0.0 copy-start.3
  52.2 0.0 reduce-scatter.2.cloned.1.call-update
  52.2 28.8 %reduce-scatter.2.cloned.1.call-done = bf16[8,2048]{1,0:T(8,128)(2,1)} async-done(((bf16[64,2048]{1,0:T(8,128)(2,1)}), bf16[8,2048]{1,0:T(8,128)(2,1)}) %reduce-scatter.2.cloned.1.call-update) | async-done | bytes 32784 | tf_op jit(solution)/shard_map/reduce_scatter | solution.py:101
  81.0 1.4 %reshape.93 = bf16[4,2,1,2048]{3,1,0,2:T(2,128)(2,1)} reshape(bf16[8,2048]{1,0:T(8,128)(2,1)} %reduce-scatter.2.cloned.1.call-done) | data formatting | bytes 65536 | tf_op jit(solution)/shard_map/reshape | solution.py:105
  82.4 3.7 %all-to-all-start.2 = ((bf16[4,2,1,2048]{3,1,2,0:T(2,128)(2,1)}), bf16[4,2,1,2048]{3,1,2,0:T(2,128)(2,1)S(1)}, u32[]{:S(2)}, u32[]{:S(2)}) async-start(bf16[4,2,1,2048]{3,1,2,0:T(2,128)(2,1)} %bitcast.9), calls=%async_computation.3 | async-start | bytes 65536 | tf_op jit(solution)/shard_map/all_to_all | solution.py:104
  86.1 0.1 fusion.71
  86.2 4.7 %all-to-all-done.2 = bf16[4,2,1,2048]{3,1,2,0:T(2,128)(2,1)S(1)} async-done(((bf16[4,2,1,2048]{3,1,2,0:T(2,128)(2,1)}), bf16[4,2,1,2048]{3,1,2,0:T(2,128)(2,1)S(1)}, u32[]{:S(2)}, u32[]{:S(2)}) %all-to-all-start.2) | async-done | bytes 32800 | tf_op jit(solution)/shard_map/all_to_all | solution.py:104
  90.9 0.2 fusion.21
  91.1 1.0 fusion.16
  92.1 1.2 %multiply_reduce_fusion = (f32[4,16,8]{2,1,0:T(8,128)S(1)}, f32[4,16,8,8]{2,3,1,0:T(8,128)S(1)}) fusion(f32[4,16,8,8]{2,3,1,0:T(8,128)S(1)} %get-tuple-element.18, f32[4,16,8]{2,1,0:T(8,128)} %copy-done.2, bf16[8,4,16,128]{3,2,1,0:T(8,128)(2,1)} %copy-done.1, bf16[8,4,16,128]{3,2,1,0:T(8,128)(2,1)S(1)} %bitcast.71), kind=kOutput, calls=%fused_computation.33 | convolution fusion | flops 1060352 | bytes 299008 | tf_op jit(solution)/shard_map/fphd,gphd->phfg/dot_general | solution.py:119
  93.3 0.0 copy-done.3
  93.3 0.1 multiply_convert_fusion
  93.4 0.2 fusion.15
  93.6 0.3 fusion.13
  93.9 0.8 copy.89
  94.6 0.8 copy.88
  95.4 0.8 copy.87
  (13 shorter events, 0.3 us)
Async XLA Ops:
  7.2 40.9 %copy-start = (bf16[1,2048,512]{2,1,0:T(8,128)(2,1)S(1)}, bf16[1,2048,512]{2,1,0:T(8,128)(2,1)}, u32[]{:S(2)}) copy-start(bf16[1,2048,512]{2,1,0:T(8,128)(2,1)} %param.12) | copy-start | bytes 6291460
  9.0 12.9 %copy-start.4 = (s32[2,32]{1,0:T(2,128)S(1)}, s32[2,32]{1,0:T(2,128)}, u32[]{:S(2)}) copy-start(s32[2,32]{1,0:T(2,128)} %param.15) | copy-start | bytes 772
  9.0 13.3 %copy-start.5 = (f32[2,32]{1,0:T(2,128)S(1)}, f32[2,32]{1,0:T(2,128)}, u32[]{:S(2)}) copy-start(f32[2,32]{1,0:T(2,128)} %param.14) | copy-start | bytes 772
  11.1 13.1 %all-to-all-start = ((bf16[8,2,4096]{2,1,0:T(2,128)(2,1)}), bf16[8,2,4096]{2,1,0:T(2,128)(2,1)S(1)}, u32[]{:S(2)}, u32[]{:S(2)}) async-start(bf16[8,2,4096]{2,1,0:T(2,128)(2,1)} %reshape.103), calls=%async_computation | async-start | bytes 262144 | tf_op jit(solution)/shard_map/all_to_all | solution.py:28
  17.5 63.6 %reduce-scatter.2.cloned.1.call-start = ((), (), s32[]{:S(2)}) async-start(), calls=%async_computation.4 | async-start | bytes 294912 | tf_op jit(solution)/shard_map/reduce_scatter | solution.py:101
  20.5 0.7 copy-start.1
  20.8 0.6 copy-start.2
  52.2 41.1 %copy-start.3 = (f32[4,16,8]{2,1,0:T(8,128)S(1)}, f32[4,16,8]{2,1,0:T(8,128)}, u32[]{:S(2)}) copy-start(f32[4,16,8]{2,1,0:T(8,128)} %copy-done.2) | copy-start | bytes 6148
  82.4 8.4 %all-to-all-start.2 = ((bf16[4,2,1,2048]{3,1,2,0:T(2,128)(2,1)}), bf16[4,2,1,2048]{3,1,2,0:T(2,128)(2,1)S(1)}, u32[]{:S(2)}, u32[]{:S(2)}) async-start(bf16[4,2,1,2048]{3,1,2,0:T(2,128)(2,1)} %bitcast.9), calls=%async_computation.3 | async-start | bytes 65536 | tf_op jit(solution)/shard_map/all_to_all | solution.py:104
Sparse Core Ops, SparseCore 0:
  52.4 28.6 reduce-scatter.1
where the time goes:
time: 104 us; the launch traced here: 103 us
  waiting for transfers between devices  35.1 us (34%)
  blocking collectives  23.2 us (22%)
  between operations  14.3 us (14%)
  local copies, waits for them, and re-layouts  10.2 us (10%)
  starting transfers between devices  10 us (10%)
  matrix products  8.08 us (8%)
  other arithmetic  2.09 us (2%)
    reduce_scatter x1, waiting for transfers between devices, body(): lax.psum_scatter(partial_value.astype(jnp.bfloat16), 'frm', scatter_dimen...  28.8 us
    all_gather x1, blocking collectives, body(): lax.all_gather(arrived.reshape(groups * slot_depth, 2, features), 'frm',...  14.8 us
    all_to_all x1, blocking collectives, body(): lax.all_to_all(outgoing, 'grp', split_axis=0, concat_axis=0, tiled=True)  8.36 us
    all_to_all x1, starting transfers between devices, body(): lax.all_to_all(cotangent, 'frm', split_axis=1, concat_axis=0, tiled=True)  6.33 us
    unnamed x20, local copies, waits for them, and re-layouts  5.6 us
    all_to_all x1, waiting for transfers between devices, body(): lax.all_to_all(summed.reshape(groups, slot_depth, pieces, features), 'grp...  4.68 us
    dot_general x1, matrix products, body(): jnp.einsum('rks,dks->rkd', slope.reshape(row_count, pieces, slice_width),...  3.73 us
    all_to_all x1, starting transfers between devices, body(): lax.all_to_all(summed.reshape(groups, slot_depth, pieces, features), 'grp...  3.65 us
  transfers between devices with their start and end apart: 3, of which 3 were waited for; matrix products, arithmetic and copies ran while one was open for 4% of the time, Pallas kernels for 0%

commit v1 on v0

--- a/solution.py
+++ b/solution.py
@@ -74,43 +74,38 @@
     stacked = jnp.stack([picked_in, scaled], axis=2)
     own_in = w_in[0]
     own_out = w_out[0]
-    slot_depth = MOST
-    outgoing = jnp.broadcast_to(stacked[:, None], (experts, 2, MOST, 2, features)).reshape(
-        groups, MOST, 2, features
-    )
-    routed = jnp.broadcast_to(onehot[:, None, :, None, :], (experts, 2, MOST, 1, local_rows))
-    pieces = 1
-    slice_width = own_in.shape[1] // pieces
-    arrived = lax.all_to_all(outgoing, "grp", split_axis=0, concat_axis=0, tiled=True)
-    shard_rows = lax.all_gather(
-        arrived.reshape(groups * slot_depth, 2, features), "frm", axis=0, tiled=True
-    )
-    row_count = shard_rows.shape[0]
+    devices = groups * columns
+    share = devices // experts
+    outgoing = jnp.broadcast_to(
+        stacked.reshape(experts, 1, MOST * 2, features), (experts, share, MOST * 2, features)
+    ).reshape(devices, MOST * 2, features)
+    arrived = lax.all_to_all(outgoing, ("grp", "frm"), split_axis=0, concat_axis=0, tiled=True)
+    shard_rows = arrived.reshape(devices * MOST, 2, features)
     pre_act = jnp.dot(shard_rows[:, 0, :], own_in, preferred_element_type=jnp.float32)
     back_act = lax.dot_general(
         shard_rows[:, 1, :], own_out, (((1,), (1,)), ((), ())), preferred_element_type=jnp.float32
     )
     slope = (back_act * gelu_slope(pre_act)).astype(jnp.bfloat16)
-    product = jnp.einsum(
-        "rks,dks->rkd",
-        slope.reshape(row_count, pieces, slice_width),
-        own_in.reshape(features, pieces, slice_width),
-        preferred_element_type=jnp.float32,
-    )
-    partial_value = product.reshape(row_count, pieces * features)
-    summed = lax.psum_scatter(
-        partial_value.astype(jnp.bfloat16), "frm", scatter_dimension=0, tiled=True
-    )
+    product = lax.dot_general(
+        slope, own_in, (((1,), (1,)), ((), ())), preferred_element_type=jnp.float32
+    ).astype(jnp.bfloat16)
     returned = lax.all_to_all(
-        summed.reshape(groups, slot_depth, pieces, features),
-        "grp",
+        product.reshape(devices, MOST, features),
+        ("grp", "frm"),
         split_axis=0,
         concat_axis=0,
         tiled=True,
     )
-    flat_back = returned.reshape(groups * slot_depth * pieces, features)
-    flat_route = routed.reshape(groups * slot_depth * pieces, local_rows)
-    added = jnp.einsum("nl,nd->ld", flat_route, flat_back, preferred_element_type=jnp.float32)
+    summed = jnp.sum(
+        returned.reshape(experts, share, MOST, features).astype(jnp.float32), axis=1
+    )
+    added = jnp.einsum(
+        "eml,emd->ld",
+        onehot.astype(jnp.float32),
+        summed,
+        preferred_element_type=jnp.float32,
+        precision=lax.Precision.HIGHEST,
+    )
     grad_stream = (cot_flat.astype(jnp.float32) + added).astype(jnp.bfloat16)
     grad_heads = grad_stream.reshape(frames, blocks, HEADS, head_dim)
     grad_value = jnp.einsum(

time: 104 us -> 65.9 us (0.63)
  waiting for transfers between devices: 35.1 us -> 0.01 us
  between operations: 14.3 us -> 0.89 us
  blocking collectives: 23.2 us -> 34.6 us
  starting transfers between devices: 10 us -> 6.33 us
  other arithmetic: 2.09 us -> 4.54 us
  matrix products: 8.08 us -> 9.47 us
    reduce_scatter x1 -> x0, waiting for transfers between devices: 28.8 us -> none  [body(): lax.psum_scatter(partial_value.astype(jnp.bfloat16), 'frm', scatter_dimen...]
    all_to_all x1 -> x2, blocking collectives: 8.36 us -> 34.6 us  [the longest x1 22.2 us: body(): lax.all_to_all(outgoing, ('grp', 'frm'), split_axis=0, concat_axis=0, til...]
    all_gather x1 -> x0, blocking collectives: 14.8 us -> none  [body(): lax.all_gather(arrived.reshape(groups * slot_depth, 2, features), 'frm',...]
    all_to_all x1 -> x0, waiting for transfers between devices: 4.68 us -> none  [body(): lax.all_to_all(summed.reshape(groups, slot_depth, pieces, features), 'grp...]
    all_to_all x1 -> x0, starting transfers between devices: 3.65 us -> none  [body(): lax.all_to_all(summed.reshape(groups, slot_depth, pieces, features), 'grp...]
    all_to_all x1, waiting for transfers between devices: 1.66 us -> 0.01 us  [body(): lax.all_to_all(cotangent, 'frm', split_axis=1, concat_axis=0, tiled=True)]
    unnamed x20 -> x24, local copies, waits for them, and re-layouts: 5.6 us -> 5.01 us
  transfers between devices with their start and end apart: 3 -> 1, of which waited for: 3 -> 0; matrix products, arithmetic and copies ran while one was open for 4% -> 11% of each run, Pallas kernels for 0% -> 0%
where the time goes in v1:
time: 65.9 us; the launch traced here: 65.4 us
  blocking collectives  34.6 us (53%)
  local copies, waits for them, and re-layouts  9.56 us (15%)
  matrix products  9.47 us (14%)
  starting transfers between devices  6.33 us (10%)
  other arithmetic  4.54 us (7%)
  between operations  0.89 us (1%)
    all_to_all x1, blocking collectives, body(): lax.all_to_all(outgoing, ('grp', 'frm'), split_axis=0, concat_axis=0, til...  22.2 us
    all_to_all x1, blocking collectives, body(): lax.all_to_all(product.reshape(devices, MOST, features), ('grp', 'frm'),...  12.4 us
    all_to_all x1, starting transfers between devices, body(): lax.all_to_all(cotangent, 'frm', split_axis=1, concat_axis=0, tiled=True)  6.33 us
    unnamed x24, local copies, waits for them, and re-layouts  5.01 us
    dot_general x1, matrix products, body(): lax.dot_general(slope, own_in, (((1,), (1,)), ((), ())), preferred_elemen...  3.04 us
    unnamed x1, other arithmetic  1.39 us
  transfers between devices with their start and end apart: 1, of which 0 were waited for; matrix products, arithmetic and copies ran while one was open for 11% of the time, Pallas kernels for 0%

profile of v1, /device:TPU:0, one launch (start us, length us, event | category | flops | bytes accessed | tf_op | source)
XLA Modules:
  0.0 65.4 jit_solution(11837140832427806764)
XLA Ops:
  0.6 0.0 copy-start
  0.6 1.3 %copy.158 = bf16[1,32,2048]{2,0,1:T(2,128)(2,1)S(1)} copy(bf16[1,32,2048]{2,1,0:T(8,128)(2,1)} %param.11) | data formatting | bytes 262144 | tf_op args[3]
  1.9 0.5 broadcast.111
  2.4 0.0 copy-start.7
  2.4 1.4 %reduce = bf16[32,2048]{1,0:T(8,128)(2,1)S(1)} reduce(bf16[32,1,2048]{2,1,0:T(2,128)(2,1)S(1)} %bitcast.72, bf16[]{:T(256)} %broadcast.111), dimensions={1}, to_apply=%bitcast.70.reduce_sub_computation | reduce | bytes 262146
  3.8 0.8 %reshape.89 = bf16[8,2,4096]{2,1,0:T(2,128)(2,1)} reshape(bf16[32,2048]{1,0:T(8,128)(2,1)S(1)} %reduce) | data formatting | bytes 262144
  4.6 6.3 %all-to-all-start = ((bf16[8,2,4096]{2,1,0:T(2,128)(2,1)}), bf16[8,2,4096]{2,1,0:T(2,128)(2,1)S(1)}, u32[]{:S(2)}, u32[]{:S(2)}) async-start(bf16[8,2,4096]{2,1,0:T(2,128)(2,1)} %reshape.89), calls=%async_computation | async-start | bytes 262144 | tf_op jit(solution)/shard_map/all_to_all | solution.py:28
  10.9 0.7 %fusion.62 = s32[2,32]{1,0:T(2,128)S(1)} fusion(s32[2,32]{1,0:T(2,128)} %param.15), kind=kLoop, calls=%fused_computation.83 | loop fusion | flops 2048 | bytes 512 | tf_op jit(solution)/shard_map/add | solution.py:49
  11.6 0.7 %compare_convert_fusion = s32[2,32]{1,0:T(2,128)S(1)} fusion(s32[]{:T(128)S(6)} %add.36, s32[2,32]{1,0:T(2,128)} %param.15), kind=kLoop, calls=%fused_computation.74 | loop fusion | flops 1792 | bytes 516 | tf_op jit(solution)/shard_map/convert_element_type | solution.py:51
  12.3 0.2 reduce_window_sum.11
  12.5 0.2 multiply_reduce_fusion.2
  12.7 1.0 %reshape.71 = bf16[8,4,16,128]{3,2,1,0:T(8,128)(2,1)S(1)} reshape(bf16[8,4,2048]{2,1,0:T(4,128)(2,1)} %param.8) | data formatting | bytes 262144 | tf_op jit(solution)/shard_map/reshape | solution.py:30
  13.7 0.0 copy-start.1
  13.7 1.0 %reshape.72 = bf16[8,4,16,128]{3,2,1,0:T(8,128)(2,1)S(1)} reshape(bf16[8,4,2048]{2,1,0:T(4,128)(2,1)} %param.9) | data formatting | bytes 262144 | tf_op jit(solution)/shard_map/reshape | solution.py:31
  14.7 1.0 %reshape.74 = bf16[8,4,16,128]{3,2,1,0:T(8,128)(2,1)S(1)} reshape(bf16[8,4,2048]{2,1,0:T(4,128)(2,1)} %param.10) | data formatting | bytes 262144 | tf_op jit(solution)/shard_map/reshape | solution.py:32
  15.7 0.0 copy-start.3
  15.7 1.0 %fusion.79 = (f32[4,16,8]{2,1,0:T(8,128)S(1)}, f32[4,16,8,8]{2,3,1,0:T(8,128)}) fusion(bf16[8,4,16,128]{3,2,1,0:T(8,128)(2,1)S(1)} %reshape.72, bf16[8,4,16,128]{3,2,1,0:T(8,128)(2,1)S(1)} %reshape.71), kind=kOutput, calls=%fused_computation.98 | convolution fusion | flops 1060871 | bytes 280576 | tf_op jit(solution)/shard_map/sub | solution.py:38
  16.8 0.0 copy-start.5
  16.8 0.0 copy-done.3
  16.8 1.2 %fusion.21 = bf16[8,4,16,128]{3,0,2,1:T(8,128)(2,1)S(1)} fusion(bf16[8,4,16,128]{3,2,1,0:T(8,128)(2,1)S(1)} %reshape.74, f32[4,16,8,8]{2,3,1,0:T(8,128)} %get-tuple-element.23, f32[4,16,8]{2,1,0:T(8,128)S(1)} %get-tuple-element.22), kind=kOutput, calls=%fused_computation.28 | convolution fusion | flops 1122304 | bytes 280576 | tf_op jit(solution)/shard_map/phfg,gphd->fphd/dot_general | solution.py:41
  18.0 0.1 reshape.84
  18.1 0.0 copy-done.7
  18.1 0.1 multiply_reduce_fusion.1
  18.2 0.2 fusion.4
  18.4 0.0 all-to-all-done
  18.4 0.1 reshape.90
  18.6 0.2 fusion.5
  18.9 0.2 broadcast_in_dim.5
  19.1 0.0 copy-done.1
  19.1 0.0 copy-done.5
  19.1 22.2 %all_to_all.19 = bf16[32,4,2048]{2,1,0:T(4,128)(2,1)S(1)} all-to-all(bf16[32,4,2048]{2,1,0:T(4,128)(2,1)S(1)} %bitcast.71), channel_id=1, replica_groups=mesh['grp'=4,'frm'=8] {'grp','frm'}, dimensions={0} | all-to-all | bytes 1048576 | tf_op jit(solution)/shard_map/all_to_all | solution.py:82
  41.4 0.3 reshape.77
  41.6 0.7 %fusion.78 = (bf16[64,1,2048]{2,1,0:T(2,128)(2,1)S(1)}, bf16[64,1,2048]{2,1,0:T(2,128)(2,1)S(1)}) fusion(bf16[64,2,2048]{2,1,0:T(2,128)(2,1)S(1)} %reshape.77), kind=kLoop, calls=%fused_computation.97 | loop fusion | bytes 1048576 | tf_op jit(solution)/shard_map/slice | solution.py:84
  42.4 0.0 copy-done
  42.4 0.5 fusion.7
  42.8 3.0 %convolution_convert_fusion = bf16[64,2048]{1,0:T(8,128)(2,1)S(1)} fusion(bf16[1,2048,512]{2,1,0:T(8,128)(2,1)S(1)} %copy-done, bf16[1,512,2048]{2,1,0:T(8,128)(2,1)} %param.13, bf16[64,1,2048]{2,1,0:T(2,128)(2,1)S(1)} %get-tuple-element.21, f32[64,512]{1,0:T(8,128)S(1)} %fusion.7), kind=kOutput, calls=%fused_computation.1 | convolution fusion | flops 268894208 | bytes 4849664 | tf_op jit(solution)/shard_map/dot_general | solution.py:89
  45.9 0.0 copy-start.4
  45.9 0.0 copy-start.6
  45.9 0.2 reshape.78
  46.1 12.4 %all_to_all.20 = bf16[32,2,2048]{2,1,0:T(2,128)(2,1)S(1)} all-to-all(bf16[32,2,2048]{2,1,0:T(2,128)(2,1)S(1)} %reshape.78), channel_id=1, replica_groups=mesh['grp'=4,'frm'=8] {'grp','frm'}, dimensions={0} | all-to-all | bytes 524288 | tf_op jit(solution)/shard_map/all_to_all | solution.py:92
  58.5 0.0 copy-start.2
  58.5 0.2 convert_reduce_fusion
  58.7 0.4 fusion.22
  59.2 1.2 %fusion.17 = bf16[8,4,2048]{2,0,1:T(8,128)(2,1)S(1)} fusion(bf16[8,4,16,128]{3,2,1,0:T(8,128)(2,1)S(1)} %bitcast.75, f32[4,16,8,8]{2,3,1,0:T(8,128)} %get-tuple-element.23, f32[4,16,8]{2,1,0:T(8,128)} %copy-done.5), kind=kOutput, calls=%fused_computation.25 | convolution fusion | flops 1122304 | bytes 280576 | tf_op jit(solution)/shard_map/phfg,fphd->gphd/dot_general | solution.py:111
  60.4 0.0 copy-done.4
  60.4 0.0 copy-done.6
  60.4 1.2 %multiply_reduce_fusion = (f32[4,16,8]{2,1,0:T(8,128)S(1)}, f32[4,16,8,8]{2,3,1,0:T(8,128)S(1)}) fusion(f32[4,16,8,8]{2,3,1,0:T(8,128)} %get-tuple-element.23, f32[4,16,8]{2,1,0:T(8,128)S(1)} %copy-done.6, bf16[8,4,16,128]{3,2,1,0:T(8,128)(2,1)S(1)} %copy-done.4, bf16[8,4,16,128]{3,2,1,0:T(8,128)(2,1)S(1)} %bitcast.76), kind=kOutput, calls=%fused_computation.37 | convolution fusion | flops 1060352 | bytes 299008 | tf_op jit(solution)/shard_map/fphd,gphd->phfg/dot_general | solution.py:114
  61.6 1.0 %multiply_convert_fusion = bf16[4,16,8,8]{2,3,1,0:T(8,128)(2,1)S(1)} fusion(f32[4,16,8,8]{2,3,1,0:T(8,128)S(1)} %get-tuple-element.25, f32[4,16,8]{2,1,0:T(8,128)S(1)} %get-tuple-element.24, f32[4,16,8,8]{2,3,1,0:T(8,128)} %get-tuple-element.23, f32[4,16,8]{2,1,0:T(8,128)S(1)} %copy-done.6), kind=kLoop, calls=%fused_computation.36 | loop fusion | flops 16384 | bytes 45056 | tf_op jit(solution)/shard_map/convert_element_type | solution.py:118
  62.6 0.0 copy-done.2
  62.7 0.2 fusion.16
  62.9 0.3 fusion.14
  63.1 0.8 %copy.103 = bf16[8,4,2048]{2,1,0:T(4,128)(2,1)} copy(bf16[8,4,2048]{2,0,1:T(8,128)(2,1)S(1)} %fusion.17) | data formatting | bytes 262144
  63.9 0.8 %copy.101 = bf16[8,4,2048]{2,1,0:T(4,128)(2,1)} copy(bf16[8,4,2048]{2,0,1:T(8,128)(2,1)S(1)} %fusion.14) | data formatting | bytes 262144
  64.7 0.8 %copy.102 = bf16[8,4,2048]{2,1,0:T(4,128)(2,1)} copy(bf16[8,4,2048]{2,0,1:T(8,128)(2,1)S(1)} %fusion.16) | data formatting | bytes 262144
  (7 shorter events, 0.2 us)
Async XLA Ops:
  0.6 41.7 %copy-start = (bf16[1,2048,512]{2,1,0:T(8,128)(2,1)S(1)}, bf16[1,2048,512]{2,1,0:T(8,128)(2,1)}, u32[]{:S(2)}) copy-start(bf16[1,2048,512]{2,1,0:T(8,128)(2,1)} %param.12) | copy-start | bytes 6291460
  2.4 15.7 %copy-start.7 = (f32[2,32]{1,0:T(2,128)S(1)}, f32[2,32]{1,0:T(2,128)}, u32[]{:S(2)}) copy-start(f32[2,32]{1,0:T(2,128)} %param.14) | copy-start | bytes 772
  4.6 13.8 %all-to-all-start = ((bf16[8,2,4096]{2,1,0:T(2,128)(2,1)}), bf16[8,2,4096]{2,1,0:T(2,128)(2,1)S(1)}, u32[]{:S(2)}, u32[]{:S(2)}) async-start(bf16[8,2,4096]{2,1,0:T(2,128)(2,1)} %reshape.89), calls=%async_computation | async-start | bytes 262144 | tf_op jit(solution)/shard_map/all_to_all | solution.py:28
  13.7 5.4 %copy-start.1 = (bf16[8,4,16,128]{3,2,1,0:T(8,128)(2,1)}, bf16[8,4,16,128]{3,2,1,0:T(8,128)(2,1)S(1)}, u32[]{:S(2)}) copy-start(bf16[8,4,16,128]{3,2,1,0:T(8,128)(2,1)S(1)} %reshape.71) | copy-start | bytes 393220
  15.7 1.0 %copy-start.3 = (bf16[8,4,16,128]{3,2,1,0:T(8,128)(2,1)}, bf16[8,4,16,128]{3,2,1,0:T(8,128)(2,1)S(1)}, u32[]{:S(2)}) copy-start(bf16[8,4,16,128]{3,2,1,0:T(8,128)(2,1)S(1)} %reshape.74) | copy-start | bytes 393220
  16.8 2.4 %copy-start.5 = (f32[4,16,8]{2,1,0:T(8,128)}, f32[4,16,8]{2,1,0:T(8,128)S(1)}, u32[]{:S(2)}) copy-start(f32[4,16,8]{2,1,0:T(8,128)S(1)} %get-tuple-element.22) | copy-start | bytes 6148
  45.9 14.5 %copy-start.4 = (bf16[8,4,16,128]{3,2,1,0:T(8,128)(2,1)S(1)}, bf16[8,4,16,128]{3,2,1,0:T(8,128)(2,1)}, u32[]{:S(2)}) copy-start(bf16[8,4,16,128]{3,2,1,0:T(8,128)(2,1)} %copy-done.3) | copy-start | bytes 393220
  45.9 14.5 %copy-start.6 = (f32[4,16,8]{2,1,0:T(8,128)S(1)}, f32[4,16,8]{2,1,0:T(8,128)}, u32[]{:S(2)}) copy-start(f32[4,16,8]{2,1,0:T(8,128)} %copy-done.5) | copy-start | bytes 6148
  58.5 4.1 %copy-start.2 = (bf16[8,4,16,128]{3,2,1,0:T(8,128)(2,1)S(1)}, bf16[8,4,16,128]{3,2,1,0:T(8,128)(2,1)}, u32[]{:S(2)}) copy-start(bf16[8,4,16,128]{3,2,1,0:T(8,128)(2,1)} %copy-done.1) | copy-start | bytes 393220

commit v2 on v1

--- a/solution.py
+++ b/solution.py
@@ -5,6 +5,7 @@
 
 HEADS = 16
 MOST = 2
+CORES = 2
 
 
 root_half = 0.7071067811865476
@@ -61,43 +62,61 @@
     onehot = (
         (position_at[:, :, None] == row_ids[None, None, :]) & (filled[:, :, None] > 0)
     ).astype(jnp.bfloat16)
+    per_expert = groups // experts
+    levels = columns // CORES
+    expert_here = lax.axis_index("grp") // per_expert
+    order = expert_here ^ jnp.arange(experts, dtype=jnp.int32)
+    onehot = onehot[order]
+    weight_at = weight_at[order]
     picked_in = jnp.einsum(
         "eml,ld->emd", onehot, attn_out, preferred_element_type=jnp.float32
     ).astype(jnp.bfloat16)
     picked_cot = jnp.einsum(
-        "eml,ld->emd",
-        onehot,
-        cot_patch.reshape(local_rows, features),
-        preferred_element_type=jnp.float32,
+        "eml,ld->emd", onehot, cot_flat, preferred_element_type=jnp.float32
     )
     scaled = (weight_at[:, :, None] * picked_cot).astype(jnp.bfloat16)
-    stacked = jnp.stack([picked_in, scaled], axis=2)
+    stacked = jnp.concatenate([picked_in, scaled], axis=1)
     own_in = w_in[0]
     own_out = w_out[0]
-    devices = groups * columns
-    share = devices // experts
-    outgoing = jnp.broadcast_to(
-        stacked.reshape(experts, 1, MOST * 2, features), (experts, share, MOST * 2, features)
-    ).reshape(devices, MOST * 2, features)
-    arrived = lax.all_to_all(outgoing, ("grp", "frm"), split_axis=0, concat_axis=0, tiled=True)
-    shard_rows = arrived.reshape(devices * MOST, 2, features)
-    pre_act = jnp.dot(shard_rows[:, 0, :], own_in, preferred_element_type=jnp.float32)
-    back_act = lax.dot_general(
-        shard_rows[:, 1, :], own_out, (((1,), (1,)), ((), ())), preferred_element_type=jnp.float32
+
+    def swap(values, axis, step):
+        size = lax.axis_size(axis)
+        return lax.ppermute(values, axis, [(i, i ^ step) for i in range(size)])
+
+    row = jnp.stack(
+        [stacked[0]] + [swap(stacked[k // per_expert], "grp", k) for k in range(1, groups)]
     )
-    slope = (back_act * gelu_slope(pre_act)).astype(jnp.bfloat16)
-    product = lax.dot_general(
-        slope, own_in, (((1,), (1,)), ((), ())), preferred_element_type=jnp.float32
-    ).astype(jnp.bfloat16)
-    returned = lax.all_to_all(
-        product.reshape(devices, MOST, features),
-        ("grp", "frm"),
-        split_axis=0,
-        concat_axis=0,
-        tiled=True,
+    plane = jnp.stack([row] + [swap(row, "frm", CORES * k) for k in range(1, levels)])
+    other = swap(plane, "frm", 1)
+
+    def expert(rows):
+        rows = rows.reshape(levels * groups, 2, MOST, features)
+        pre_act = jnp.dot(
+            rows[:, 0].reshape(-1, features), own_in, preferred_element_type=jnp.float32
+        )
+        back_act = lax.dot_general(
+            rows[:, 1].reshape(-1, features),
+            own_out,
+            (((1,), (1,)), ((), ())),
+            preferred_element_type=jnp.float32,
+        )
+        slope = (back_act * gelu_slope(pre_act)).astype(jnp.bfloat16)
+        return lax.dot_general(
+            slope, own_in, (((1,), (1,)), ((), ())), preferred_element_type=jnp.float32
+        )
+
+    back = swap(expert(other).astype(jnp.bfloat16), "frm", 1)
+    mine = (expert(plane) + back.astype(jnp.float32)).astype(jnp.bfloat16)
+    mine = mine.reshape(levels, groups, MOST, features)
+    over_z = mine[0].astype(jnp.float32)
+    for k in range(1, levels):
+        over_z = over_z + swap(mine[k], "frm", CORES * k).astype(jnp.float32)
+    over_z = over_z.astype(jnp.bfloat16)
+    summed = jnp.stack(
+        [over_z[0]] + [swap(over_z[k], "grp", k) for k in range(1, groups)]
     )
     summed = jnp.sum(
-        returned.reshape(experts, share, MOST, features).astype(jnp.float32), axis=1
+        summed.reshape(experts, per_expert, MOST, features).astype(jnp.float32), axis=1
     )
     added = jnp.einsum(
         "eml,emd->ld",

time: 65.9 us -> 64.9 us (0.985)
  blocking collectives: 34.6 us -> 0 us
  waiting for transfers between devices: 0.01 us -> 16.8 us
  starting transfers between devices: 6.33 us -> 21.8 us
  local copies, waits for them, and re-layouts: 9.56 us -> 11.2 us
    all_to_all x2 -> x0, blocking collectives: 34.6 us -> none  [the longest x1 22.2 us: body(): lax.all_to_all(outgoing, ('grp', 'frm'), split_axis=0, concat_axis=0, til...]
    ppermute x0 -> x14, waiting for transfers between devices: none -> 16.8 us  [swap(): return lax.ppermute(values, axis, [(i, i ^ step) for i in range(size)])]
    ppermute x0 -> x14, starting transfers between devices: none -> 15.4 us  [swap(): return lax.ppermute(values, axis, [(i, i ^ step) for i in range(size)])]
    dot_general x3 -> x5, matrix products: 3.7 us -> 7.04 us  [the longest x2 5.96 us: expert(): lax.dot_general(slope, own_in, (((1,), (1,)), ((), ())), preferred_elemen...]
    gather x0 -> x2, local copies, waits for them, and re-layouts: none -> 1.13 us  [the longest x1 0.57 us: body(): onehot = onehot[order]]
    dot_general x1, matrix products: 1.23 us -> 0.27 us  [body(): jnp.einsum('fphd,gphd->phfg', grad_heads, value_heads, preferred_element_...]
    dot_general x1, matrix products: 1.24 us -> 0.29 us  [body(): jnp.einsum('phfg,gphd->fphd', weights, value_heads, preferred_element_typ...]
    dot_general x1, matrix products: 1.18 us -> 0.23 us  [body(): jnp.einsum('phfg,fphd->gphd', weights, grad_heads, preferred_element_type...]
  transfers between devices with their start and end apart: 1 -> 15, of which waited for: 0 -> 13; matrix products, arithmetic and copies ran while one was open for 11% -> 13% of each run, Pallas kernels for 0% -> 0%
where the time goes in v2:
time: 64.9 us; the launch traced here: 64.4 us
  starting transfers between devices  21.8 us (34%)
  waiting for transfers between devices  16.8 us (26%)
  local copies, waits for them, and re-layouts  11.2 us (17%)
  matrix products  9.13 us (14%)
  other arithmetic  4.57 us (7%)
  between operations  0.98 us (2%)
    ppermute x14, waiting for transfers between devices, swap(): return lax.ppermute(values, axis, [(i, i ^ step) for i in range(size)])  16.8 us
    ppermute x14, starting transfers between devices, swap(): return lax.ppermute(values, axis, [(i, i ^ step) for i in range(size)])  15.4 us
    all_to_all x1, starting transfers between devices, body(): lax.all_to_all(cotangent, 'frm', split_axis=1, concat_axis=0, tiled=True)  6.33 us
    dot_general x2, matrix products, expert(): lax.dot_general(slope, own_in, (((1,), (1,)), ((), ())), preferred_elemen...  5.96 us
    unnamed x22, local copies, waits for them, and re-layouts  5.01 us
    unnamed x1, other arithmetic  1.38 us
  transfers between devices with their start and end apart: 15, of which 13 were waited for; matrix products, arithmetic and copies ran while one was open for 13% of the time, Pallas kernels for 0%

profile of v2, /device:TPU:0, one launch (start us, length us, event | category | flops | bytes accessed | tf_op | source)
XLA Modules:
  0.0 64.4 jit_solution(13094005280881693007)
XLA Ops:
  0.6 1.3 %copy.123 = bf16[1,32,2048]{2,0,1:T(2,128)(2,1)S(1)} copy(bf16[1,32,2048]{2,1,0:T(8,128)(2,1)} %param.11) | data formatting | bytes 262144 | tf_op args[3]
  1.9 0.5 broadcast.219
  2.4 1.4 %reduce = bf16[32,2048]{1,0:T(8,128)(2,1)S(1)} reduce(bf16[32,1,2048]{2,1,0:T(2,128)(2,1)S(1)} %bitcast.103, bf16[]{:T(256)} %broadcast.219), dimensions={1}, to_apply=%bitcast.102.reduce_sub_computation | reduce | bytes 262146
  3.8 0.8 %reshape.126 = bf16[8,2,4096]{2,1,0:T(2,128)(2,1)} reshape(bf16[32,2048]{1,0:T(8,128)(2,1)S(1)} %reduce) | data formatting | bytes 262144
  4.6 6.3 %all-to-all-start = ((bf16[8,2,4096]{2,1,0:T(2,128)(2,1)}), bf16[8,2,4096]{2,1,0:T(2,128)(2,1)S(1)}, u32[]{:S(2)}, u32[]{:S(2)}) async-start(bf16[8,2,4096]{2,1,0:T(2,128)(2,1)} %reshape.126), calls=%async_computation | async-start | bytes 262144 | tf_op jit(solution)/shard_map/all_to_all | solution.py:29
  10.9 0.7 %compare_convert_fusion = s32[2,32]{1,0:T(2,128)S(1)} fusion(s32[]{:T(128)S(6)} %add.63, s32[2,32]{1,0:T(2,128)} %param.15), kind=kLoop, calls=%fused_computation.107 | loop fusion | flops 1792 | bytes 516 | tf_op jit(solution)/shard_map/convert_element_type | solution.py:52
  11.6 0.2 reduce_window_sum.11
  11.8 0.7 %fusion.84 = (s32[2,32]{1,0:T(2,128)S(1)}, s32[2,32]{1,0:T(2,128)S(1)}) fusion(s32[2,32]{1,0:T(2,128)} %param.15, s32[2,32]{1,0:T(2,128)S(1)} %reduce_window_sum.11), kind=kLoop, calls=%fused_computation.116 | loop fusion | flops 2112 | bytes 1024 | tf_op jit(solution)/shard_map/add | solution.py:50
  12.5 0.8 %multiply_reduce_fusion.1 = f32[2,2]{1,0:T(2,128)S(1)} fusion(f32[2,32]{1,0:T(2,128)} %param.14, s32[2,32]{1,0:T(2,128)S(1)} %compare_convert_fusion, s32[2,32]{1,0:T(2,128)S(1)} %get-tuple-element.36), kind=kLoop, calls=%fused_computation.102 | loop fusion | flops 636 | bytes 784 | tf_op jit(solution)/shard_map/reduce_sum | solution.py:60
  13.3 0.1 multiply_reduce_fusion.2
  13.4 1.0 %reshape.92 = bf16[8,4,16,128]{3,2,1,0:T(8,128)(2,1)S(1)} reshape(bf16[8,4,2048]{2,1,0:T(4,128)(2,1)} %param.8) | data formatting | bytes 262144 | tf_op jit(solution)/shard_map/reshape | solution.py:31
  14.4 1.0 %reshape.93 = bf16[8,4,16,128]{3,2,1,0:T(8,128)(2,1)S(1)} reshape(bf16[8,4,2048]{2,1,0:T(4,128)(2,1)} %param.9) | data formatting | bytes 262144 | tf_op jit(solution)/shard_map/reshape | solution.py:32
  15.4 1.0 %reshape.95 = bf16[8,4,16,128]{3,2,1,0:T(8,128)(2,1)S(1)} reshape(bf16[8,4,2048]{2,1,0:T(4,128)(2,1)} %param.10) | data formatting | bytes 262144 | tf_op jit(solution)/shard_map/reshape | solution.py:33
  16.4 0.1 compare_and_fusion
  16.5 0.3 fusion.110
  16.9 0.3 fusion.22
  17.2 0.6 gather_fusion
  17.7 0.6 gather_fusion.1
  18.4 0.1 convolution_convert_fusion.1
  18.6 0.1 reshape.127
  18.7 0.2 fusion.3
  18.9 1.6 %collective-permute-start = (bf16[4,2048]{1,0:T(4,128)(2,1)S(1)}, bf16[4,2048]{1,0:T(4,128)(2,1)S(1)}, u32[]{:S(2)}, u32[]{:S(2)}) collective-permute-start(bf16[4,2048]{1,0:T(4,128)(2,1)S(1)} %bitcast.106), channel_id=1, source_target_pairs={{0,8},{8,0},{16,24},{24,16},{1,9},{9,1},{17,25},{25,17},{2,10},{10... | collective-permute-start | bytes 49160 | tf_op jit(solution)/shard_map/ppermute | solution.py:84
  20.5 1.5 %collective-permute-start.2 = (bf16[4,2048]{1,0:T(4,128)(2,1)S(1)}, bf16[4,2048]{1,0:T(4,128)(2,1)S(1)}, u32[]{:S(2)}, u32[]{:S(2)}) collective-permute-start(bf16[4,2048]{1,0:T(4,128)(2,1)S(1)} %get-tuple-element.30), channel_id=1, source_target_pairs={{0,24},{8,16},{16,8},{24,0},{1,25},{9,17},{17,9},{25,1},{2,26},{10... | collective-permute-start | bytes 49160 | tf_op jit(solution)/shard_map/ppermute | solution.py:84
  22.0 0.5 collective-permute-start.1
  22.5 0.2 collective-permute-done
  22.7 2.4 %collective-permute-done.2 = bf16[4,2048]{1,0:T(4,128)(2,1)S(1)} collective-permute-done((bf16[4,2048]{1,0:T(4,128)(2,1)S(1)}, bf16[4,2048]{1,0:T(4,128)(2,1)S(1)}, u32[]{:S(2)}, u32[]{:S(2)}) %collective-permute-start.2) | collective-permute-done | bytes 16416 | tf_op jit(solution)/shard_map/ppermute | solution.py:84
  25.1 0.6 collective-permute-done.1
  25.8 3.0 %collective-permute-start.4 = (bf16[4,4,2048]{2,1,0:T(4,128)(2,1)S(1)}, bf16[4,4,2048]{2,1,0:T(4,128)(2,1)S(1)}, u32[]{:S(2)}, u32[]{:S(2)}) collective-permute-start(bf16[4,4,2048]{2,1,0:T(4,128)(2,1)S(1)} %pad_maximum_fusion.1), channel_id=1, source_target_pairs={{0,4},{1,5},{2,6},{3,7},{4,0},{5,1},{6,2},{7,3},{8,12},{9,13},{10,... | collective-permute-start | bytes 196616 | tf_op jit(solution)/shard_map/ppermute | solution.py:84
  28.7 1.5 %collective-permute-start.3 = (bf16[4,4,2048]{2,1,0:T(4,128)(2,1)S(1)}, bf16[4,4,2048]{2,1,0:T(4,128)(2,1)S(1)}, u32[]{:S(2)}, u32[]{:S(2)}) collective-permute-start(bf16[4,4,2048]{2,1,0:T(4,128)(2,1)S(1)} %pad_maximum_fusion.1), channel_id=1, source_target_pairs={{0,2},{1,3},{2,0},{3,1},{4,6},{5,7},{6,4},{7,5},{8,10},{9,11},{10,... | collective-permute-start | bytes 196616 | tf_op jit(solution)/shard_map/ppermute | solution.py:84
  30.2 0.1 collective-permute-start.5
  30.3 1.1 %collective-permute-done.4 = bf16[4,4,2048]{2,1,0:T(4,128)(2,1)S(1)} collective-permute-done((bf16[4,4,2048]{2,1,0:T(4,128)(2,1)S(1)}, bf16[4,4,2048]{2,1,0:T(4,128)(2,1)S(1)}, u32[]{:S(2)}, u32[]{:S(2)}) %collective-permute-start.4) | collective-permute-done | bytes 65568 | tf_op jit(solution)/shard_map/ppermute | solution.py:84
  31.4 2.2 %collective-permute-done.3 = bf16[4,4,2048]{2,1,0:T(4,128)(2,1)S(1)} collective-permute-done((bf16[4,4,2048]{2,1,0:T(4,128)(2,1)S(1)}, bf16[4,4,2048]{2,1,0:T(4,128)(2,1)S(1)}, u32[]{:S(2)}, u32[]{:S(2)}) %collective-permute-start.3) | collective-permute-done | bytes 65568 | tf_op jit(solution)/shard_map/ppermute | solution.py:84
  33.6 2.7 %collective-permute-done.5 = bf16[4,4,2048]{2,1,0:T(4,128)(2,1)S(1)} collective-permute-done((bf16[4,4,2048]{2,1,0:T(4,128)(2,1)S(1)}, bf16[4,4,2048]{2,1,0:T(4,128)(2,1)S(1)}, u32[]{:S(2)}, u32[]{:S(2)}) %collective-permute-start.5) | collective-permute-done | bytes 65568 | tf_op jit(solution)/shard_map/ppermute | solution.py:84
  36.3 0.2 pad_maximum_fusion
  36.5 0.1 reshape.97
  36.7 0.2 fusion.107
  37.0 1.4 %collective-permute-done.6 = bf16[4,4,4,2048]{3,2,1,0:T(4,128)(2,1)} collective-permute-done((bf16[4,4,4,2048]{3,2,1,0:T(4,128)(2,1)S(1)}, bf16[4,4,4,2048]{3,2,1,0:T(4,128)(2,1)}, u32[]{:S(2)}, u32[]{:S(2)}) %collective-permute-start.6) | collective-permute-done | bytes 262176 | tf_op jit(solution)/shard_map/ppermute | solution.py:84
  38.4 1.1 %reshape.98 = bf16[16,2,2,2048]{3,2,1,0:T(2,128)(2,1)S(1)} reshape(bf16[4,4,4,2048]{3,2,1,0:T(4,128)(2,1)} %collective-permute-done.6) | data formatting | bytes 524288 | tf_op jit(solution)/shard_map/reshape | solution.py:93
  39.5 0.2 fusion.106
  39.8 0.5 fusion.5
  40.3 3.0 %convolution_convert_fusion = bf16[32,2048]{1,0:T(8,128)(2,1)S(1)} fusion(bf16[1,2048,512]{2,1,0:T(8,128)(2,1)S(1)} %copy-done, bf16[32,2048]{1,0:T(8,128)(2,1)S(1)} %reshape_squeeze.14, bf16[1,512,2048]{2,1,0:T(8,128)(2,1)} %param.13, f32[32,512]{1,0:T(8,128)S(1)} %fusion.5), kind=kOutput, calls=%fused_computation.6 | convolution fusion | flops 134447104 | bytes 4521984 | tf_op jit(solution)/shard_map/dot_general | solution.py:104
  43.2 0.2 collective-permute-start.7
  43.4 0.4 fusion.9
  44.0 0.8 %collective-permute-done.7 = bf16[32,2048]{1,0:T(8,128)(2,1)} collective-permute-done((bf16[32,2048]{1,0:T(8,128)(2,1)S(1)}, bf16[32,2048]{1,0:T(8,128)(2,1)}, u32[]{:S(2)}, u32[]{:S(2)}) %collective-permute-start.7) | collective-permute-done | bytes 131104 | tf_op jit(solution)/shard_map/ppermute | solution.py:84
  44.8 3.0 %add_convert_fusion = bf16[32,2048]{1,0:T(8,128)(2,1)S(1)} fusion(bf16[32,2048]{1,0:T(8,128)(2,1)} %collective-permute-done.7, bf16[1,2048,512]{2,1,0:T(8,128)(2,1)S(1)} %copy-done, bf16[32,2048]{1,0:T(8,128)(2,1)S(1)} %reshape_squeeze.12, bf16[1,512,2048]{2,1,0:T(8,128)(2,1)} %param.13, f32[32,512]{1,0:T(8,128)S(1)} %fusion.9), kind=kOutput, calls=%fused_computation.42 | convolution fusion | flops 134578176 | bytes 4653056 | tf_op jit(solution)/shard_map/dot_general | solution.py:104
  47.9 0.1 collective-permute-start.9
  48.0 1.1 %collective-permute-start.10 = (bf16[4,2,2048]{2,1,0:T(2,128)(2,1)S(1)}, bf16[4,2,2048]{2,1,0:T(2,128)(2,1)S(1)}, u32[]{:S(2)}, u32[]{:S(2)}) collective-permute-start(bf16[4,2,2048]{2,1,0:T(2,128)(2,1)S(1)} %squeeze.38), channel_id=1, source_target_pairs={{0,6},{1,7},{2,4},{3,5},{4,2},{5,3},{6,0},{7,1},{8,14},{9,15},{10,... | collective-permute-start | bytes 98312 | tf_op jit(solution)/shard_map/ppermute | solution.py:84
  49.1 2.3 %collective-permute-start.8 = (bf16[4,2,2048]{2,1,0:T(2,128)(2,1)S(1)}, bf16[4,2,2048]{2,1,0:T(2,128)(2,1)S(1)}, u32[]{:S(2)}, u32[]{:S(2)}) collective-permute-start(bf16[4,2,2048]{2,1,0:T(2,128)(2,1)S(1)} %squeeze.36), channel_id=1, source_target_pairs={{0,2},{1,3},{2,0},{3,1},{4,6},{5,7},{6,4},{7,5},{8,10},{9,11},{10,... | collective-permute-start | bytes 98312 | tf_op jit(solution)/shard_map/ppermute | solution.py:84
  51.5 1.6 %collective-permute-done.9 = bf16[4,2,2048]{2,1,0:T(2,128)(2,1)S(1)} collective-permute-done((bf16[4,2,2048]{2,1,0:T(2,128)(2,1)S(1)}, bf16[4,2,2048]{2,1,0:T(2,128)(2,1)S(1)}, u32[]{:S(2)}, u32[]{:S(2)}) %collective-permute-start.9) | collective-permute-done | bytes 32800 | tf_op jit(solution)/shard_map/ppermute | solution.py:84
  53.1 0.7 %collective-permute-done.10 = bf16[4,2,2048]{2,1,0:T(2,128)(2,1)S(1)} collective-permute-done((bf16[4,2,2048]{2,1,0:T(2,128)(2,1)S(1)}, bf16[4,2,2048]{2,1,0:T(2,128)(2,1)S(1)}, u32[]{:S(2)}, u32[]{:S(2)}) %collective-permute-start.10) | collective-permute-done | bytes 32800 | tf_op jit(solution)/shard_map/ppermute | solution.py:84
  53.9 1.5 %collective-permute-start.13 = (bf16[2,2048]{1,0:T(2,128)(2,1)S(1)}, bf16[2,2048]{1,0:T(2,128)(2,1)S(1)}, u32[]{:S(2)}, u32[]{:S(2)}) collective-permute-start(bf16[2,2048]{1,0:T(2,128)(2,1)S(1)} %get-tuple-element.26), channel_id=1, source_target_pairs={{0,24},{8,16},{16,8},{24,0},{1,25},{9,17},{17,9},{25,1},{2,26},{10... | collective-permute-start | bytes 24584 | tf_op jit(solution)/shard_map/ppermute | solution.py:84
  55.4 1.5 %collective-permute-start.12 = (bf16[2,2048]{1,0:T(2,128)(2,1)S(1)}, bf16[2,2048]{1,0:T(2,128)(2,1)S(1)}, u32[]{:S(2)}, u32[]{:S(2)}) collective-permute-start(bf16[2,2048]{1,0:T(2,128)(2,1)S(1)} %get-tuple-element.27), channel_id=1, source_target_pairs={{0,16},{8,24},{16,0},{24,8},{1,17},{9,25},{17,1},{25,9},{2,18},{10... | collective-permute-start | bytes 24584 | tf_op jit(solution)/shard_map/ppermute | solution.py:84
  57.0 0.5 collective-permute-start.11
  57.5 1.1 %collective-permute-done.13 = bf16[2,2048]{1,0:T(2,128)(2,1)S(1)} collective-permute-done((bf16[2,2048]{1,0:T(2,128)(2,1)S(1)}, bf16[2,2048]{1,0:T(2,128)(2,1)S(1)}, u32[]{:S(2)}, u32[]{:S(2)}) %collective-permute-start.13) | collective-permute-done | bytes 8224 | tf_op jit(solution)/shard_map/ppermute | solution.py:84
  58.5 0.5 collective-permute-done.12
  59.1 1.5 %collective-permute-done.11 = bf16[2,2048]{1,0:T(2,128)(2,1)S(1)} collective-permute-done((bf16[2,2048]{1,0:T(2,128)(2,1)S(1)}, bf16[2,2048]{1,0:T(2,128)(2,1)S(1)}, u32[]{:S(2)}, u32[]{:S(2)}) %collective-permute-start.11) | collective-permute-done | bytes 8224 | tf_op jit(solution)/shard_map/ppermute | solution.py:84
  60.6 0.4 fusion.23
  61.1 0.2 fusion.21
  61.3 0.3 multiply_reduce_fusion
  61.7 0.2 fusion.20
  61.9 0.3 fusion.18
  62.2 0.8 %copy.79 = bf16[8,4,2048]{2,1,0:T(4,128)(2,1)} copy(bf16[8,4,2048]{2,0,1:T(8,128)(2,1)S(1)} %fusion.21) | data formatting | bytes 262144
  62.9 0.8 %copy.77 = bf16[8,4,2048]{2,1,0:T(4,128)(2,1)} copy(bf16[8,4,2048]{2,0,1:T(8,128)(2,1)S(1)} %fusion.18) | data formatting | bytes 262144
  63.7 0.8 %copy.78 = bf16[8,4,2048]{2,1,0:T(4,128)(2,1)} copy(bf16[8,4,2048]{2,0,1:T(8,128)(2,1)S(1)} %fusion.20) | data formatting | bytes 262144
  (39 shorter events, 1.0 us)
Async XLA Ops:
  0.6 39.2 %copy-start = (bf16[1,2048,512]{2,1,0:T(8,128)(2,1)S(1)}, bf16[1,2048,512]{2,1,0:T(8,128)(2,1)}, u32[]{:S(2)}) copy-start(bf16[1,2048,512]{2,1,0:T(8,128)(2,1)} %param.12) | copy-start | bytes 6291460
  4.6 14.0 %all-to-all-start = ((bf16[8,2,4096]{2,1,0:T(2,128)(2,1)}), bf16[8,2,4096]{2,1,0:T(2,128)(2,1)S(1)}, u32[]{:S(2)}, u32[]{:S(2)}) async-start(bf16[8,2,4096]{2,1,0:T(2,128)(2,1)} %reshape.126), calls=%async_computation | async-start | bytes 262144 | tf_op jit(solution)/shard_map/all_to_all | solution.py:29
  16.4 19.9 %copy-start.3 = (bf16[8,4,16,128]{3,2,1,0:T(8,128)(2,1)}, bf16[8,4,16,128]{3,2,1,0:T(8,128)(2,1)S(1)}, u32[]{:S(2)}) copy-start(bf16[8,4,16,128]{3,2,1,0:T(8,128)(2,1)S(1)} %reshape.95) | copy-start | bytes 393220
  16.8 0.9 %copy-start.1 = (f32[4,16,8,8]{2,3,1,0:T(8,128)}, f32[4,16,8,8]{2,3,1,0:T(8,128)S(1)}, u32[]{:S(2)}) copy-start(f32[4,16,8,8]{2,3,1,0:T(8,128)S(1)} %get-tuple-element.32) | copy-start | bytes 49156
  16.8 1.7 %copy-start.5 = (f32[4,16,8]{2,1,0:T(8,128)}, f32[4,16,8]{2,1,0:T(8,128)S(1)}, u32[]{:S(2)}) copy-start(f32[4,16,8]{2,1,0:T(8,128)S(1)} %get-tuple-element.31) | copy-start | bytes 6148
  18.9 3.8 %collective-permute-start = (bf16[4,2048]{1,0:T(4,128)(2,1)S(1)}, bf16[4,2048]{1,0:T(4,128)(2,1)S(1)}, u32[]{:S(2)}, u32[]{:S(2)}) collective-permute-start(bf16[4,2048]{1,0:T(4,128)(2,1)S(1)} %bitcast.106), channel_id=1, source_target_pairs={{0,8},{8,0},{16,24},{24,16},{1,9},{9,1},{17,25},{25,17},{2,10},{10... | collective-permute-start | bytes 49160 | tf_op jit(solution)/shard_map/ppermute | solution.py:84
  20.5 4.6 %collective-permute-start.2 = (bf16[4,2048]{1,0:T(4,128)(2,1)S(1)}, bf16[4,2048]{1,0:T(4,128)(2,1)S(1)}, u32[]{:S(2)}, u32[]{:S(2)}) collective-permute-start(bf16[4,2048]{1,0:T(4,128)(2,1)S(1)} %get-tuple-element.30), channel_id=1, source_target_pairs={{0,24},{8,16},{16,8},{24,0},{1,25},{9,17},{17,9},{25,1},{2,26},{10... | collective-permute-start | bytes 49160 | tf_op jit(solution)/shard_map/ppermute | solution.py:84
  22.0 3.7 %collective-permute-start.1 = (bf16[4,2048]{1,0:T(4,128)(2,1)S(1)}, bf16[4,2048]{1,0:T(4,128)(2,1)S(1)}, u32[]{:S(2)}, u32[]{:S(2)}) collective-permute-start(bf16[4,2048]{1,0:T(4,128)(2,1)S(1)} %get-tuple-element.30), channel_id=1, source_target_pairs={{0,16},{8,24},{16,0},{24,8},{1,17},{9,25},{17,1},{25,9},{2,18},{10... | collective-permute-start | bytes 49160 | tf_op jit(solution)/shard_map/ppermute | solution.py:84
  25.8 5.6 %collective-permute-start.4 = (bf16[4,4,2048]{2,1,0:T(4,128)(2,1)S(1)}, bf16[4,4,2048]{2,1,0:T(4,128)(2,1)S(1)}, u32[]{:S(2)}, u32[]{:S(2)}) collective-permute-start(bf16[4,4,2048]{2,1,0:T(4,128)(2,1)S(1)} %pad_maximum_fusion.1), channel_id=1, source_target_pairs={{0,4},{1,5},{2,6},{3,7},{4,0},{5,1},{6,2},{7,3},{8,12},{9,13},{10,... | collective-permute-start | bytes 196616 | tf_op jit(solution)/shard_map/ppermute | solution.py:84
  28.7 4.8 %collective-permute-start.3 = (bf16[4,4,2048]{2,1,0:T(4,128)(2,1)S(1)}, bf16[4,4,2048]{2,1,0:T(4,128)(2,1)S(1)}, u32[]{:S(2)}, u32[]{:S(2)}) collective-permute-start(bf16[4,4,2048]{2,1,0:T(4,128)(2,1)S(1)} %pad_maximum_fusion.1), channel_id=1, source_target_pairs={{0,2},{1,3},{2,0},{3,1},{4,6},{5,7},{6,4},{7,5},{8,10},{9,11},{10,... | collective-permute-start | bytes 196616 | tf_op jit(solution)/shard_map/ppermute | solution.py:84
  30.2 6.1 %collective-permute-start.5 = (bf16[4,4,2048]{2,1,0:T(4,128)(2,1)S(1)}, bf16[4,4,2048]{2,1,0:T(4,128)(2,1)S(1)}, u32[]{:S(2)}, u32[]{:S(2)}) collective-permute-start(bf16[4,4,2048]{2,1,0:T(4,128)(2,1)S(1)} %pad_maximum_fusion.1), channel_id=1, source_target_pairs={{0,6},{1,7},{2,4},{3,5},{4,2},{5,3},{6,0},{7,1},{8,14},{9,15},{10,... | collective-permute-start | bytes 196616 | tf_op jit(solution)/shard_map/ppermute | solution.py:84
  36.7 1.7 %collective-permute-start.6 = (bf16[4,4,4,2048]{3,2,1,0:T(4,128)(2,1)S(1)}, bf16[4,4,4,2048]{3,2,1,0:T(4,128)(2,1)}, u32[]{:S(2)}, u32[]{:S(2)}) collective-permute-start(bf16[4,4,4,2048]{3,2,1,0:T(4,128)(2,1)S(1)} %pad_maximum_fusion), channel_id=1, source_target_pairs={{0,1},{1,0},{2,3},{3,2},{4,5},{5,4},{6,7},{7,6},{8,9},{9,8},{10,11... | collective-permute-start | bytes 786440 | tf_op jit(solution)/shard_map/ppermute | solution.py:84
  43.2 1.5 %collective-permute-start.7 = (bf16[32,2048]{1,0:T(8,128)(2,1)S(1)}, bf16[32,2048]{1,0:T(8,128)(2,1)}, u32[]{:S(2)}, u32[]{:S(2)}) collective-permute-start(bf16[32,2048]{1,0:T(8,128)(2,1)S(1)} %convolution_convert_fusion), channel_id=1, source_target_pairs={{0,1},{1,0},{2,3},{3,2},{4,5},{5,4},{6,7},{7,6},{8,9},{9,8},{10,11... | collective-permute-start | bytes 393224 | tf_op jit(solution)/shard_map/ppermute | solution.py:84
  43.9 17.1 %copy-start.2 = (f32[4,16,8,8]{2,3,1,0:T(8,128)S(1)}, f32[4,16,8,8]{2,3,1,0:T(8,128)}, u32[]{:S(2)}) copy-start(f32[4,16,8,8]{2,3,1,0:T(8,128)} %copy-done.1) | copy-start | bytes 49156
  44.8 16.3 %copy-start.6 = (f32[4,16,8]{2,1,0:T(8,128)S(1)}, f32[4,16,8]{2,1,0:T(8,128)}, u32[]{:S(2)}) copy-start(f32[4,16,8]{2,1,0:T(8,128)} %copy-done.5) | copy-start | bytes 6148
  47.8 13.5 %copy-start.4 = (bf16[8,4,16,128]{3,2,1,0:T(8,128)(2,1)S(1)}, bf16[8,4,16,128]{3,2,1,0:T(8,128)(2,1)}, u32[]{:S(2)}) copy-start(bf16[8,4,16,128]{3,2,1,0:T(8,128)(2,1)} %copy-done.3) | copy-start | bytes 393220
  47.9 5.2 %collective-permute-start.9 = (bf16[4,2,2048]{2,1,0:T(2,128)(2,1)S(1)}, bf16[4,2,2048]{2,1,0:T(2,128)(2,1)S(1)}, u32[]{:S(2)}, u32[]{:S(2)}) collective-permute-start(bf16[4,2,2048]{2,1,0:T(2,128)(2,1)S(1)} %squeeze.37), channel_id=1, source_target_pairs={{0,4},{1,5},{2,6},{3,7},{4,0},{5,1},{6,2},{7,3},{8,12},{9,13},{10,... | collective-permute-start | bytes 98312 | tf_op jit(solution)/shard_map/ppermute | solution.py:84
  48.0 5.8 %collective-permute-start.10 = (bf16[4,2,2048]{2,1,0:T(2,128)(2,1)S(1)}, bf16[4,2,2048]{2,1,0:T(2,128)(2,1)S(1)}, u32[]{:S(2)}, u32[]{:S(2)}) collective-permute-start(bf16[4,2,2048]{2,1,0:T(2,128)(2,1)S(1)} %squeeze.38), channel_id=1, source_target_pairs={{0,6},{1,7},{2,4},{3,5},{4,2},{5,3},{6,0},{7,1},{8,14},{9,15},{10,... | collective-permute-start | bytes 98312 | tf_op jit(solution)/shard_map/ppermute | solution.py:84
  49.1 4.7 %collective-permute-start.8 = (bf16[4,2,2048]{2,1,0:T(2,128)(2,1)S(1)}, bf16[4,2,2048]{2,1,0:T(2,128)(2,1)S(1)}, u32[]{:S(2)}, u32[]{:S(2)}) collective-permute-start(bf16[4,2,2048]{2,1,0:T(2,128)(2,1)S(1)} %squeeze.36), channel_id=1, source_target_pairs={{0,2},{1,3},{2,0},{3,1},{4,6},{5,7},{6,4},{7,5},{8,10},{9,11},{10,... | collective-permute-start | bytes 98312 | tf_op jit(solution)/shard_map/ppermute | solution.py:84
  53.9 4.6 %collective-permute-start.13 = (bf16[2,2048]{1,0:T(2,128)(2,1)S(1)}, bf16[2,2048]{1,0:T(2,128)(2,1)S(1)}, u32[]{:S(2)}, u32[]{:S(2)}) collective-permute-start(bf16[2,2048]{1,0:T(2,128)(2,1)S(1)} %get-tuple-element.26), channel_id=1, source_target_pairs={{0,24},{8,16},{16,8},{24,0},{1,25},{9,17},{17,9},{25,1},{2,26},{10... | collective-permute-start | bytes 24584 | tf_op jit(solution)/shard_map/ppermute | solution.py:84
  55.4 3.7 %collective-permute-start.12 = (bf16[2,2048]{1,0:T(2,128)(2,1)S(1)}, bf16[2,2048]{1,0:T(2,128)(2,1)S(1)}, u32[]{:S(2)}, u32[]{:S(2)}) collective-permute-start(bf16[2,2048]{1,0:T(2,128)(2,1)S(1)} %get-tuple-element.27), channel_id=1, source_target_pairs={{0,16},{8,24},{16,0},{24,8},{1,17},{9,25},{17,1},{25,9},{2,18},{10... | collective-permute-start | bytes 24584 | tf_op jit(solution)/shard_map/ppermute | solution.py:84
  57.0 3.7 %collective-permute-start.11 = (bf16[2,2048]{1,0:T(2,128)(2,1)S(1)}, bf16[2,2048]{1,0:T(2,128)(2,1)S(1)}, u32[]{:S(2)}, u32[]{:S(2)}) collective-permute-start(bf16[2,2048]{1,0:T(2,128)(2,1)S(1)} %get-tuple-element.28), channel_id=1, source_target_pairs={{0,8},{8,0},{16,24},{24,16},{1,9},{9,1},{17,25},{25,17},{2,10},{10... | collective-permute-start | bytes 24584 | tf_op jit(solution)/shard_map/ppermute | solution.py:84

commit v3 on v1

v3 whole, which is shorter than its diff:
```python
import functools

import jax
import jax.numpy as jnp
from jax import lax
from jax.experimental import pallas as pl
from jax.experimental.pallas import tpu as pltpu
from jax.sharding import PartitionSpec as P

HEADS = 16
MOST = 2
CORES = 2
SUBLANES = 8

root_half = 0.7071067811865476
inv_root_tau = 0.3989422804014327

LANES_BOTH = (((1,), (1,)), ((), ()))


def gelu_slope(pre_act):
    normal_cdf = 0.5 * (1.0 + lax.erf(pre_act * root_half))
    density = jnp.exp(-0.5 * pre_act * pre_act) * inv_root_tau
    return normal_cdf + pre_act * density


def dot(a, b):
    return jnp.dot(a, b, preferred_element_type=jnp.float32)


def dot_lanes(a, b):
    return lax.dot_general(a, b, LANES_BOTH, preferred_element_type=jnp.float32)


def over_frames(values, op, blocks):
    rows = values.shape[0]
    total = values[:SUBLANES]
    for start in range(SUBLANES, rows, SUBLANES):
        total = op(total, values[start : start + SUBLANES])
    step = blocks
    while step < SUBLANES:
        total = op(total, pltpu.roll(total, step, 0))
        step *= 2
    return jnp.concatenate([total] * (rows // SUBLANES), axis=0)


def heads_of(values):
    width = values.shape[1] // HEADS
    return [values[:, h * width : (h + 1) * width] for h in range(HEADS)]


def turn_kernel(blocks, pieces, place_ref, cot_ref, *out_refs):
    rows = cot_ref.shape[1]
    want = lax.broadcasted_iota(jnp.int32, (rows, rows), 0)
    have = lax.broadcasted_iota(jnp.int32, (rows, rows), 1)
    source = ((want // blocks) ^ place_ref[0]) * blocks + want % blocks
    turned = dot((source == have).astype(jnp.bfloat16), cot_ref[0]).astype(jnp.bfloat16)
    size = rows // pieces
    for i, out_ref in enumerate(out_refs):
        out_ref[...] = turned[i * size : (i + 1) * size]


def forward_kernel(
    experts, patches_all, place_ref, query_ref, key_ref, value_ref, chosen_ref, gate_ref,
    probs_ref, picked_ref, here_ref, weight_ref,
):
    frames, blocks, features = query_ref.shape
    rows = frames * blocks
    scaling = (features // HEADS) ** (-0.5)
    query = query_ref[...].reshape(rows, features)
    key = key_ref[...].reshape(rows, features)
    value = value_ref[...].reshape(rows, features)
    scores = jnp.concatenate(
        [dot_lanes(k, q) for k, q in zip(heads_of(key), heads_of(query))], axis=1
    )
    scores = scores * scaling
    raised = jnp.exp(scores - over_frames(scores, jnp.maximum, blocks))
    probs = raised / over_frames(raised, jnp.add, blocks)
    patch_in = lax.broadcasted_iota(jnp.int32, probs.shape, 0) % blocks
    patch_out = lax.broadcasted_iota(jnp.int32, probs.shape, 1) % blocks
    probs = jnp.where(patch_in == patch_out, probs, 0.0)
    probs_ref[...] = probs
    weights = probs.T.astype(jnp.bfloat16)
    mixed = jnp.concatenate(
        [dot(weights[h * rows : (h + 1) * rows], v) for h, v in enumerate(heads_of(value))],
        axis=1,
    ).astype(jnp.bfloat16)

    myself = place_ref[1]
    expert_here = place_ref[2]
    cap = chosen_ref.shape[1]
    before = (
        lax.broadcasted_iota(jnp.int32, (cap, cap), 0)
        < lax.broadcasted_iota(jnp.int32, (cap, cap), 1)
    ).astype(jnp.bfloat16)
    slot = lax.broadcasted_iota(jnp.int32, (SUBLANES, cap), 0)
    row_at = lax.broadcasted_iota(jnp.int32, (rows, cap), 0)
    found = []
    for k in range(experts):
        tokens = chosen_ref[pl.ds(expert_here ^ k, 1), :]
        gates = gate_ref[pl.ds(expert_here ^ k, 1), :]
        patch = tokens % patches_all
        owned = jnp.broadcast_to((patch // blocks == myself).astype(jnp.float32), slot.shape)
        rank = dot(owned.astype(jnp.bfloat16), before)
        taken = jnp.where((rank == slot.astype(jnp.float32)) & (owned > 0.0), 1.0, 0.0)
        position = (tokens // patches_all) * blocks + patch % blocks
        at_row = (row_at == position).astype(jnp.bfloat16)
        here = dot_lanes(taken.astype(jnp.bfloat16), at_row)
        weight = jnp.sum(taken * gates, axis=1, keepdims=True)
        here_ref[k * MOST : (k + 1) * MOST, :] = here[:MOST]
        weight_ref[k * MOST : (k + 1) * MOST, :] = jnp.broadcast_to(
            weight[:MOST], (MOST, weight_ref.shape[1])
        )
        found.append(here[:MOST])
    here = jnp.concatenate(found, axis=0).astype(jnp.bfloat16)
    picked_ref[...] = dot(here, mixed).astype(jnp.bfloat16)


def gather_kernel(blocks, place_ref, *refs):
    *part_refs, other_ref, cot_ref = refs
    rows = cot_ref.shape[0]
    mine = jnp.concatenate([part_ref[:blocks] for part_ref in part_refs], axis=0)
    half = rows // CORES
    want = lax.broadcasted_iota(jnp.int32, (rows, half), 0)
    have = lax.broadcasted_iota(jnp.int32, (rows, half), 1)
    step = (want // blocks) ^ place_ref[0]
    level = (step // CORES) * blocks + want % blocks
    near = ((level == have) & (step % CORES == 0)).astype(jnp.bfloat16)
    far = ((level == have) & (step % CORES == 1)).astype(jnp.bfloat16)
    cot_ref[...] = (dot(near, mine) + dot(far, other_ref[...])).astype(jnp.bfloat16)


def pick_kernel(experts, here_ref, weight_ref, picked_ref, cot_ref, *out_refs):
    rows = dot(here_ref[...].astype(jnp.bfloat16), cot_ref[...])
    rows = (rows * weight_ref[:, :1]).astype(jnp.bfloat16)
    for k, out_ref in enumerate(out_refs):
        out_ref[0] = picked_ref[k * MOST : (k + 1) * MOST]
        out_ref[1] = rows[k * MOST : (k + 1) * MOST]


def expert_kernel(mine_ref, other_ref, w_in_ref, w_out_ref, kept_ref, sent_ref):
    half = mine_ref.shape[1]
    w_in = w_in_ref[0]
    rows_in = jnp.concatenate([mine_ref[0], other_ref[0]], axis=0)
    rows_cot = jnp.concatenate([mine_ref[1], other_ref[1]], axis=0)
    pre_act = dot(rows_in, w_in)
    back_act = dot_lanes(rows_cot, w_out_ref[0])
    slope = (back_act * gelu_slope(pre_act)).astype(jnp.bfloat16)
    product = dot_lanes(slope, w_in)
    kept_ref[...] = product[:half]
    sent_ref[...] = product[half:].astype(jnp.bfloat16)


def backward_kernel(
    here_ref, cot_ref, probs_ref, query_ref, key_ref, value_ref, *refs
):
    *sum_refs, grad_query_ref, grad_key_ref, grad_value_ref = refs
    frames, blocks, features = query_ref.shape
    rows = frames * blocks
    scaling = (features // HEADS) ** (-0.5)
    query = query_ref[...].reshape(rows, features)
    key = key_ref[...].reshape(rows, features)
    value = value_ref[...].reshape(rows, features)
    sums = jnp.concatenate([sum_ref[...] for sum_ref in sum_refs], axis=0)
    added = lax.dot_general(
        here_ref[...].astype(jnp.bfloat16),
        sums,
        (((0,), (0,)), ((), ())),
        preferred_element_type=jnp.float32,
    )
    stream = (cot_ref[...].astype(jnp.float32) + added).astype(jnp.bfloat16)
    probs = probs_ref[...]
    grad_prob = jnp.concatenate(
        [dot_lanes(v, g) for v, g in zip(heads_of(value), heads_of(stream))], axis=1
    )
    centre = over_frames(probs * grad_prob, jnp.add, blocks)
    grad_score = probs * (grad_prob - centre)
    turned = grad_score.T.astype(jnp.bfloat16)
    grad_score = grad_score.astype(jnp.bfloat16)
    weights = probs.astype(jnp.bfloat16)

    def joined(parts):
        return jnp.concatenate(parts, axis=1).astype(jnp.bfloat16).reshape(frames, blocks, features)

    grad_value_ref[...] = joined(
        [dot(w, g) for w, g in zip(heads_of(weights), heads_of(stream))]
    )
    grad_key_ref[...] = joined(
        [dot(s, q) * scaling for s, q in zip(heads_of(grad_score), heads_of(query))]
    )
    grad_query_ref[...] = joined(
        [dot(turned[h * rows : (h + 1) * rows], k) * scaling for h, k in enumerate(heads_of(key))]
    )


def call(kernel, outs, scalars=0, flops=0, moved=0):
    smem = pl.BlockSpec(memory_space=pltpu.SMEM)
    vmem = pl.BlockSpec(memory_space=pltpu.VMEM)

    def run(*operands):
        return pl.pallas_call(
            kernel,
            out_shape=[jax.ShapeDtypeStruct(shape, dtype) for shape, dtype in outs],
            in_specs=[smem] * scalars + [vmem] * (len(operands) - scalars),
            out_specs=[vmem] * len(outs),
            cost_estimate=pl.CostEstimate(
                flops=flops, bytes_accessed=moved, transcendentals=0
            ),
            compiler_params=pltpu.CompilerParams(vmem_limit_bytes=40 * 1024 * 1024),
        )(*operands)

    return run


def swap(values, axis, step):
    size = lax.axis_size(axis)
    return lax.ppermute(values, axis, [(i, i ^ step) for i in range(size)])


def body(query_in, key_in, value_in, cotangent, w_in, w_out, gate_probs, chosen):
    bf16, f32 = jnp.bfloat16, jnp.float32
    frames, blocks, features = query_in.shape
    groups = lax.axis_size("grp")
    columns = lax.axis_size("frm")
    experts = gate_probs.shape[0]
    rows = frames * blocks
    patches_all = blocks * groups * columns
    per_expert = groups // experts
    levels = columns // CORES
    group, column = lax.axis_index("grp"), lax.axis_index("frm")
    place = jnp.stack([column, group * columns + column, group // per_expert])
    place = place.astype(jnp.int32)
    slots = experts * MOST

    span = cotangent.shape[1] // levels
    parts = call(
        functools.partial(turn_kernel, blocks, levels),
        [((span, features), bf16)] * levels,
        scalars=1,
    )(place, cotangent)
    arrived = [parts[0]] + [swap(parts[k], "frm", CORES * k) for k in range(1, levels)]
    probs, picked, here, weight = call(
        functools.partial(forward_kernel, experts, patches_all),
        [
            ((rows, HEADS * rows), f32),
            ((slots, features), bf16),
            ((slots, rows), f32),
            ((slots, 128), f32),
        ],
        scalars=1,
    )(place, query_in, key_in, value_in, chosen, gate_probs)
    away = swap(jnp.concatenate([part[blocks:] for part in arrived], axis=0), "frm", 1)
    (cot,) = call(
        functools.partial(gather_kernel, blocks), [((rows, features), bf16)], scalars=1
    )(place, *arrived, away)
    outgoing = call(
        functools.partial(pick_kernel, experts), [((2, MOST, features), bf16)] * experts
    )(here, weight, picked, cot)

    held = [outgoing[0]]
    held += [swap(outgoing[k], "grp", k * per_expert) for k in range(1, experts)]
    held = jnp.concatenate(held, axis=1)
    held = jnp.concatenate(
        [held] + [swap(held, "frm", CORES * k) for k in range(1, levels)], axis=1
    )
    held = jnp.concatenate(
        [held] + [swap(held, "grp", k) for k in range(1, per_expert)], axis=1
    )
    other = swap(held, "frm", 1)
    count = held.shape[1]
    kept, sent = call(
        expert_kernel, [((count, features), f32), ((count, features), bf16)]
    )(held, other, w_in, w_out)

    total = kept + swap(sent, "frm", 1).astype(f32)
    total = total.reshape(per_expert, count // per_expert, features)
    over_x = total[0]
    for k in range(1, per_expert):
        over_x = over_x + swap(total[k].astype(bf16), "grp", k).astype(f32)
    over_x = over_x.reshape(levels, slots, features)
    over_z = over_x[0]
    for k in range(1, levels):
        over_z = over_z + swap(over_x[k].astype(bf16), "frm", CORES * k).astype(f32)
    over_z = over_z.astype(bf16).reshape(experts, MOST, features)
    sums = [over_z[0]] + [swap(over_z[k], "grp", k * per_expert) for k in range(1, experts)]
    return call(backward_kernel, [((frames, blocks, features), bf16)] * 3)(
        here, cot, probs, query_in, key_in, value_in, *sums
    )


def solution(mesh):
    return jax.shard_map(
        body,
        mesh=mesh,
        in_specs=(
            P(None, ("grp", "frm"), None),
            P(None, ("grp", "frm"), None),
            P(None, ("grp", "frm"), None),
            P("frm", "grp", None),
            P("grp", None, "frm"),
            P("grp", "frm", None),
            P(),
            P(),
        ),
        out_specs=(
            P(None, ("grp", "frm"), None),
            P(None, ("grp", "frm"), None),
            P(None, ("grp", "frm"), None),
        ),
        check_vma=False,
    )
```

time: 65.9 us -> 59.7 us (0.906)
  blocking collectives: 34.6 us -> 0 us
  waiting for transfers between devices: 0.01 us -> 24.9 us
  starting transfers between devices: 6.33 us -> 20.4 us
  matrix products: 9.47 us -> 0 us
  Pallas kernels: 0 us -> 6.08 us
  other arithmetic: 4.54 us -> 0.22 us
  local copies, waits for them, and re-layouts: 9.56 us -> 7.04 us
    all_to_all x2 -> x0, blocking collectives: 34.6 us -> none  [the longest x1 22.2 us: body(): lax.all_to_all(outgoing, ('grp', 'frm'), split_axis=0, concat_axis=0, til...]
    ppermute x0 -> x16, waiting for transfers between devices: none -> 24.9 us  [swap(): return lax.ppermute(values, axis, [(i, i ^ step) for i in range(size)])]
    ppermute x0 -> x16, starting transfers between devices: none -> 20.4 us  [swap(): return lax.ppermute(values, axis, [(i, i ^ step) for i in range(size)])]
    dot_general x10 -> x0, matrix products: 8.46 us -> none  [the longest x1 3.04 us: body(): lax.dot_general(slope, own_in, (((1,), (1,)), ((), ())), preferred_elemen...]
    all_to_all x1 -> x0, starting transfers between devices: 6.33 us -> none  [body(): lax.all_to_all(cotangent, 'frm', split_axis=1, concat_axis=0, tiled=True)]
    pallas_call x0 -> x6, Pallas kernels: none -> 6.08 us  [run(): pl.pallas_call(kernel, out_shape=[jax.ShapeDtypeStruct(shape, dtype) for...]
    reshape x6 -> x0, local copies, waits for them, and re-layouts: 3.53 us -> none  [the longest x1 1.04 us: body(): key_heads = key_in.reshape(frames, blocks, HEADS, head_dim)]
    convert_element_type x2 -> x1, other arithmetic: 1.72 us -> 0.02 us  [body(): over_z = over_z.astype(bf16).reshape(experts, MOST, features)]
  transfers between devices with their start and end apart: 1 -> 16, of which waited for: 0 -> 12; matrix products, arithmetic and copies ran while one was open for 11% -> 0% of each run, Pallas kernels for 0% -> 2%
where the time goes in v3:
time: 59.7 us; the launch traced here: 59.4 us
  waiting for transfers between devices  24.9 us (42%)
  starting transfers between devices  20.4 us (34%)
  local copies, waits for them, and re-layouts  7.04 us (12%)
  Pallas kernels  6.08 us (10%)
  between operations  0.82 us (1%)
    ppermute x16, waiting for transfers between devices, swap(): return lax.ppermute(values, axis, [(i, i ^ step) for i in range(size)])  24.9 us
    ppermute x16, starting transfers between devices, swap(): return lax.ppermute(values, axis, [(i, i ^ step) for i in range(size)])  20.4 us
    unnamed x22, local copies, waits for them, and re-layouts  6.71 us
    pallas_call x6, Pallas kernels, run(): pl.pallas_call(kernel, out_shape=[jax.ShapeDtypeStruct(shape, dtype) for...  6.08 us
  transfers between devices with their start and end apart: 16, of which 12 were waited for; matrix products, arithmetic and copies ran while one was open for 0% of the time, Pallas kernels for 2%

profile of v3, /device:TPU:0, one launch (start us, length us, event | category | flops | bytes accessed | tf_op | source)
XLA Modules:
  0.0 59.4 jit_solution(17866658612434806245)
XLA Ops:
  0.6 0.0 copy-start
  0.7 0.1 pad_add_fusion.place_ref
  0.7 0.0 copy-start.8
  0.7 1.0 %copy-done.8 = bf16[1,32,2048]{2,1,0:T(8,128)(2,1)S(1)} copy-done((bf16[1,32,2048]{2,1,0:T(8,128)(2,1)S(1)}, bf16[1,32,2048]{2,1,0:T(8,128)(2,1)}, u32[]{:S(2)}) %copy-start.8) | copy-done | bytes 131096
  1.8 0.7 %shard_map.104 = (bf16[8,2048]{1,0:T(8,128)(2,1)S(1)}, bf16[8,2048]{1,0:T(8,128)(2,1)S(1)}, bf16[8,2048]{1,0:T(8,128)(2,1)S(1)}, bf16[8,2048]{1,0:T(8,128)(2,1)S(1)}) custom-call(s32[3]{0:T(128)S(1)} %pad_add_fusion.place_ref, bf16[1,32,2048]{2,1,0:T(8,128)(2,1)S(1)} %copy-done.8), custom_call_target="tpu_custom_call" | custom-call | tf_op jit(solution)/shard_map/pallas_call | solution.py:201
  2.5 3.1 %collective-permute-start = (bf16[8,2048]{1,0:T(8,128)(2,1)S(1)}, bf16[8,2048]{1,0:T(8,128)(2,1)S(1)}, u32[]{:S(2)}, u32[]{:S(2)}) collective-permute-start(bf16[8,2048]{1,0:T(8,128)(2,1)S(1)} %get-tuple-element.17), channel_id=1, source_target_pairs={{0,2},{1,3},{2,0},{3,1},{4,6},{5,7},{6,4},{7,5},{8,10},{9,11},{10,... | collective-permute-start | bytes 98312 | tf_op jit(solution)/shard_map/ppermute | solution.py:217
  5.6 2.6 %collective-permute-start.1 = (bf16[8,2048]{1,0:T(8,128)(2,1)S(1)}, bf16[8,2048]{1,0:T(8,128)(2,1)S(1)}, u32[]{:S(2)}, u32[]{:S(2)}) collective-permute-start(bf16[8,2048]{1,0:T(8,128)(2,1)S(1)} %get-tuple-element.18), channel_id=1, source_target_pairs={{0,4},{1,5},{2,6},{3,7},{4,0},{5,1},{6,2},{7,3},{8,12},{9,13},{10,... | collective-permute-start | bytes 98312 | tf_op jit(solution)/shard_map/ppermute | solution.py:217
  8.2 0.0 collective-permute-start.2
  8.2 0.0 collective-permute-done.refs_1_
  8.2 2.8 %collective-permute-done.1.refs_2_ = bf16[8,2048]{1,0:T(8,128)(2,1)S(1)} collective-permute-done((bf16[8,2048]{1,0:T(8,128)(2,1)S(1)}, bf16[8,2048]{1,0:T(8,128)(2,1)S(1)}, u32[]{:S(2)}, u32[]{:S(2)}) %collective-permute-start.1) | collective-permute-done | bytes 32800 | tf_op jit(solution)/shard_map/ppermute | solution.py:217
  11.0 2.9 %collective-permute-done.2.refs_3_ = bf16[8,2048]{1,0:T(8,128)(2,1)S(1)} collective-permute-done((bf16[8,2048]{1,0:T(8,128)(2,1)S(1)}, bf16[8,2048]{1,0:T(8,128)(2,1)S(1)}, u32[]{:S(2)}, u32[]{:S(2)}) %collective-permute-start.2) | collective-permute-done | bytes 32800 | tf_op jit(solution)/shard_map/ppermute | solution.py:217
  13.9 0.1 collective-permute-start.3
  14.0 0.0 copy-start.2
  14.0 0.9 %copy-done.2 = bf16[8,4,2048]{2,1,0:T(4,128)(2,1)S(1)} copy-done((bf16[8,4,2048]{2,1,0:T(4,128)(2,1)S(1)}, bf16[8,4,2048]{2,1,0:T(4,128)(2,1)}, u32[]{:S(2)}) %copy-start.2) | copy-done | bytes 131096
  14.9 0.0 copy-start.4
  14.9 0.9 %copy-done.4 = bf16[8,4,2048]{2,1,0:T(4,128)(2,1)S(1)} copy-done((bf16[8,4,2048]{2,1,0:T(4,128)(2,1)S(1)}, bf16[8,4,2048]{2,1,0:T(4,128)(2,1)}, u32[]{:S(2)}) %copy-start.4) | copy-done | bytes 131096
  15.8 0.0 copy-start.6
  15.8 0.9 %copy-done.6 = bf16[8,4,2048]{2,1,0:T(4,128)(2,1)S(1)} copy-done((bf16[8,4,2048]{2,1,0:T(4,128)(2,1)S(1)}, bf16[8,4,2048]{2,1,0:T(4,128)(2,1)}, u32[]{:S(2)}) %copy-start.6) | copy-done | bytes 131096
  16.7 0.0 copy-start.9
  16.7 0.7 %copy-done.9 = s32[2,32]{1,0:T(2,128)S(1)} copy-done((s32[2,32]{1,0:T(2,128)S(1)}, s32[2,32]{1,0:T(2,128)}, u32[]{:S(2)}) %copy-start.9) | copy-done | bytes 280
  17.4 0.0 copy-start.10
  17.4 0.7 %copy-done.10 = f32[2,32]{1,0:T(2,128)S(1)} copy-done((f32[2,32]{1,0:T(2,128)S(1)}, f32[2,32]{1,0:T(2,128)}, u32[]{:S(2)}) %copy-start.10) | copy-done | bytes 280
  18.1 1.3 %shard_map.103 = (f32[32,512]{1,0:T(8,128)S(1)}, bf16[4,2048]{1,0:T(4,128)(2,1)S(1)}, f32[4,32]{1,0:T(4,128)S(1)}, f32[4,128]{1,0:T(4,128)S(1)}) custom-call(s32[3]{0:T(128)S(1)} %pad_add_fusion.place_ref, bf16[8,4,2048]{2,1,0:T(4,128)(2,1)S(1)} %copy-done.2, bf16[8,4,2048]{2,1,0:T(4,128)(2,1)S(1)} %copy-done.4, bf16[8,4,2048]{2,1,0:T(4,128)(2,1)S(1)} %copy-done.6, ...), custom_call_target="tpu_custom_call" | custom-call | tf_op jit(solution)/shard_map/pallas_call | solution.py:201
  19.4 0.0 collective-permute-done.3.refs_4_
  19.4 0.8 %shard_map.105.cot_ref = bf16[32,2048]{1,0:T(8,128)(2,1)S(1)} custom-call(s32[3]{0:T(128)S(1)} %pad_add_fusion.place_ref, bf16[8,2048]{1,0:T(8,128)(2,1)S(1)} %get-tuple-element.16.refs_0_, bf16[8,2048]{1,0:T(8,128)(2,1)S(1)} %collective-permute-done.refs_1_, bf16[8,2048]{1,0:T(8,128)(2,1)S(1)} %collective-permute-done.1.refs_2_, ...), custom_call_target="tpu_custom_call" | custom-call | tf_op jit(solution)/shard_map/pallas_call | solution.py:201
  20.2 0.1 shard_map.106
  20.3 1.6 %collective-permute-start.4 = (bf16[2,2,2048]{2,1,0:T(2,128)(2,1)S(1)}, bf16[2,2,2048]{2,1,0:T(2,128)(2,1)S(1)}, u32[]{:S(2)}, u32[]{:S(2)}) collective-permute-start(bf16[2,2,2048]{2,1,0:T(2,128)(2,1)S(1)} %get-tuple-element.24), channel_id=1, source_target_pairs={{0,16},{8,24},{16,0},{24,8},{1,17},{9,25},{17,1},{25,9},{2,18},{10... | collective-permute-start | bytes 49160 | tf_op jit(solution)/shard_map/ppermute | solution.py:217
  21.9 2.2 %collective-permute-done.4 = bf16[2,2,2048]{2,1,0:T(2,128)(2,1)S(1)} collective-permute-done((bf16[2,2,2048]{2,1,0:T(2,128)(2,1)S(1)}, bf16[2,2,2048]{2,1,0:T(2,128)(2,1)S(1)}, u32[]{:S(2)}, u32[]{:S(2)}) %collective-permute-start.4) | collective-permute-done | bytes 16416 | tf_op jit(solution)/shard_map/ppermute | solution.py:217
  24.2 0.4 collective-permute-start.7
  24.6 0.1 collective-permute-start.6
  24.7 3.9 %collective-permute-start.5 = (bf16[2,4,2048]{2,1,0:T(4,128)(2,1)S(1)}, bf16[2,4,2048]{2,1,0:T(4,128)(2,1)S(1)}, u32[]{:S(2)}, u32[]{:S(2)}) collective-permute-start(bf16[2,4,2048]{2,1,0:T(4,128)(2,1)S(1)} %pad_maximum_fusion.1), channel_id=1, source_target_pairs={{0,2},{1,3},{2,0},{3,1},{4,6},{5,7},{6,4},{7,5},{8,10},{9,11},{10,... | collective-permute-start | bytes 98312 | tf_op jit(solution)/shard_map/ppermute | solution.py:217
  28.6 1.3 %collective-permute-done.7 = bf16[2,4,2048]{2,1,0:T(4,128)(2,1)S(1)} collective-permute-done((bf16[2,4,2048]{2,1,0:T(4,128)(2,1)S(1)}, bf16[2,4,2048]{2,1,0:T(4,128)(2,1)S(1)}, u32[]{:S(2)}, u32[]{:S(2)}) %collective-permute-start.7) | collective-permute-done | bytes 32800 | tf_op jit(solution)/shard_map/ppermute | solution.py:217
  30.0 0.0 collective-permute-done.6
  30.0 0.6 collective-permute-done.5
  30.5 0.1 concatenate.16
  30.6 1.6 %collective-permute-start.8 = (bf16[2,16,2048]{2,1,0:T(8,128)(2,1)S(1)}, bf16[2,16,2048]{2,1,0:T(8,128)(2,1)S(1)}, u32[]{:S(2)}, u32[]{:S(2)}) collective-permute-start(bf16[2,16,2048]{2,1,0:T(8,128)(2,1)S(1)} %concatenate.16), channel_id=1, source_target_pairs={{0,8},{8,0},{16,24},{24,16},{1,9},{9,1},{17,25},{25,17},{2,10},{10... | collective-permute-start | bytes 393224 | tf_op jit(solution)/shard_map/ppermute | solution.py:217
  32.2 3.5 %collective-permute-done.8 = bf16[2,16,2048]{2,1,0:T(8,128)(2,1)S(1)} collective-permute-done((bf16[2,16,2048]{2,1,0:T(8,128)(2,1)S(1)}, bf16[2,16,2048]{2,1,0:T(8,128)(2,1)S(1)}, u32[]{:S(2)}, u32[]{:S(2)}) %collective-permute-start.8) | collective-permute-done | bytes 131104 | tf_op jit(solution)/shard_map/ppermute | solution.py:217
  35.7 0.1 concatenate.17.mine_ref
  35.8 0.1 collective-permute-start.9
  35.9 1.5 %collective-permute-done.9.other_ref = bf16[2,32,2048]{2,1,0:T(8,128)(2,1)S(1)} collective-permute-done((bf16[2,32,2048]{2,1,0:T(8,128)(2,1)S(1)}, bf16[2,32,2048]{2,1,0:T(8,128)(2,1)S(1)}, u32[]{:S(2)}, u32[]{:S(2)}) %collective-permute-start.9) | collective-permute-done | bytes 262176 | tf_op jit(solution)/shard_map/ppermute | solution.py:217
  37.4 0.0 copy-done
  37.4 0.0 copy-start.1
  37.4 1.6 %copy-done.1 = bf16[1,512,2048]{2,1,0:T(8,128)(2,1)S(1)} copy-done((bf16[1,512,2048]{2,1,0:T(8,128)(2,1)S(1)}, bf16[1,512,2048]{2,1,0:T(8,128)(2,1)}, u32[]{:S(2)}) %copy-start.1) | copy-done | bytes 2097176
  39.0 0.0 copy-start.3
  39.0 0.0 copy-start.5
  39.0 0.0 copy-start.7
  39.0 1.8 %shard_map.107 = (f32[32,2048]{1,0:T(8,128)S(1)}, bf16[32,2048]{1,0:T(8,128)(2,1)S(1)}) custom-call(bf16[2,32,2048]{2,1,0:T(8,128)(2,1)S(1)} %concatenate.17.mine_ref, bf16[2,32,2048]{2,1,0:T(8,128)(2,1)S(1)} %collective-permute-done.9.other_ref, bf16[1,2048,512]{2,1,0:T(8,128)(2,1)S(1)} %copy-done, bf16[1,512,2048]{2,1,0:T(8,128)(2,1)S(1)} %copy-done.1), custom_call_target="tpu_custom_call" | custom-call | tf_op jit(solution)/shard_map/pallas_call | solution.py:201
  40.8 0.2 collective-permute-start.10
  41.0 1.2 %collective-permute-done.10 = bf16[32,2048]{1,0:T(8,128)(2,1)S(1)} collective-permute-done((bf16[32,2048]{1,0:T(8,128)(2,1)S(1)}, bf16[32,2048]{1,0:T(8,128)(2,1)S(1)}, u32[]{:S(2)}, u32[]{:S(2)}) %collective-permute-start.10) | collective-permute-done | bytes 131104 | tf_op jit(solution)/shard_map/ppermute | solution.py:217
  42.3 1.6 %collective-permute-start.11 = (bf16[16,2048]{1,0:T(8,128)(2,1)S(1)}, bf16[16,2048]{1,0:T(8,128)(2,1)S(1)}, u32[]{:S(2)}, u32[]{:S(2)}) collective-permute-start(bf16[16,2048]{1,0:T(8,128)(2,1)S(1)} %slice.80), channel_id=1, source_target_pairs={{0,8},{8,0},{16,24},{24,16},{1,9},{9,1},{17,25},{25,17},{2,10},{10... | collective-permute-start | bytes 196616 | tf_op jit(solution)/shard_map/ppermute | solution.py:217
  43.8 2.8 %collective-permute-done.11 = bf16[16,2048]{1,0:T(8,128)(2,1)S(1)} collective-permute-done((bf16[16,2048]{1,0:T(8,128)(2,1)S(1)}, bf16[16,2048]{1,0:T(8,128)(2,1)S(1)}, u32[]{:S(2)}, u32[]{:S(2)}) %collective-permute-start.11) | collective-permute-done | bytes 65568 | tf_op jit(solution)/shard_map/ppermute | solution.py:217
  46.6 2.1 %collective-permute-start.12 = (bf16[4,2048]{1,0:T(4,128)(2,1)S(1)}, bf16[4,2048]{1,0:T(4,128)(2,1)S(1)}, u32[]{:S(2)}, u32[]{:S(2)}) collective-permute-start(bf16[4,2048]{1,0:T(4,128)(2,1)S(1)} %get-tuple-element.29), channel_id=1, source_target_pairs={{0,2},{1,3},{2,0},{3,1},{4,6},{5,7},{6,4},{7,5},{8,10},{9,11},{10,... | collective-permute-start | bytes 49160 | tf_op jit(solution)/shard_map/ppermute | solution.py:217
  48.7 0.4 collective-permute-start.14
  49.1 1.1 %collective-permute-start.13 = (bf16[4,2048]{1,0:T(4,128)(2,1)S(1)}, bf16[4,2048]{1,0:T(4,128)(2,1)S(1)}, u32[]{:S(2)}, u32[]{:S(2)}) collective-permute-start(bf16[4,2048]{1,0:T(4,128)(2,1)S(1)} %get-tuple-element.31), channel_id=1, source_target_pairs={{0,4},{1,5},{2,6},{3,7},{4,0},{5,1},{6,2},{7,3},{8,12},{9,13},{10,... | collective-permute-start | bytes 49160 | tf_op jit(solution)/shard_map/ppermute | solution.py:217
  50.3 0.2 collective-permute-done.12
  50.4 3.8 %collective-permute-done.14 = bf16[4,2048]{1,0:T(4,128)(2,1)S(1)} collective-permute-done((bf16[4,2048]{1,0:T(4,128)(2,1)S(1)}, bf16[4,2048]{1,0:T(4,128)(2,1)S(1)}, u32[]{:S(2)}, u32[]{:S(2)}) %collective-permute-start.14) | collective-permute-done | bytes 16416 | tf_op jit(solution)/shard_map/ppermute | solution.py:217
  54.3 0.0 collective-permute-done.13
  54.3 1.6 %collective-permute-start.15 = (bf16[2,2048]{1,0:T(2,128)(2,1)S(1)}, bf16[2,2048]{1,0:T(2,128)(2,1)S(1)}, u32[]{:S(2)}, u32[]{:S(2)}) collective-permute-start(bf16[2,2048]{1,0:T(2,128)(2,1)S(1)} %get-tuple-element.32), channel_id=1, source_target_pairs={{0,16},{8,24},{16,0},{24,8},{1,17},{9,25},{17,1},{25,9},{2,18},{10... | collective-permute-start | bytes 24584 | tf_op jit(solution)/shard_map/ppermute | solution.py:217
  55.9 2.1 %collective-permute-done.15.refs_1_ = bf16[2,2048]{1,0:T(2,128)(2,1)S(1)} collective-permute-done((bf16[2,2048]{1,0:T(2,128)(2,1)S(1)}, bf16[2,2048]{1,0:T(2,128)(2,1)S(1)}, u32[]{:S(2)}, u32[]{:S(2)}) %collective-permute-start.15) | collective-permute-done | bytes 8224 | tf_op jit(solution)/shard_map/ppermute | solution.py:217
  58.0 0.0 copy-done.3
  58.0 0.0 copy-done.5
  58.0 0.0 copy-done.7
  58.0 1.4 %shard_map.108 = (bf16[8,4,2048]{2,1,0:T(4,128)(2,1)}, bf16[8,4,2048]{2,1,0:T(4,128)(2,1)}, bf16[8,4,2048]{2,1,0:T(4,128)(2,1)}) custom-call(f32[4,32]{1,0:T(4,128)S(1)} %get-tuple-element.15.here_ref, bf16[32,2048]{1,0:T(8,128)(2,1)S(1)} %shard_map.105.cot_ref, f32[32,512]{1,0:T(8,128)S(1)} %get-tuple-element.20.probs_ref, ...), custom_call_target="tpu_custom_call" | custom-call | tf_op jit(solution)/shard_map/pallas_call | solution.py:201
  (12 shorter events, 0.2 us)
Async XLA Ops:
  0.6 36.8 %copy-start = (bf16[1,2048,512]{2,1,0:T(8,128)(2,1)S(1)}, bf16[1,2048,512]{2,1,0:T(8,128)(2,1)}, u32[]{:S(2)}) copy-start(bf16[1,2048,512]{2,1,0:T(8,128)(2,1)} %w_in_ref.1) | copy-start | bytes 6291460
  0.7 1.0 %copy-start.8 = (bf16[1,32,2048]{2,1,0:T(8,128)(2,1)S(1)}, bf16[1,32,2048]{2,1,0:T(8,128)(2,1)}, u32[]{:S(2)}) copy-start(bf16[1,32,2048]{2,1,0:T(8,128)(2,1)} %cot_ref.1) | copy-start | bytes 393220
  2.5 5.7 %collective-permute-start = (bf16[8,2048]{1,0:T(8,128)(2,1)S(1)}, bf16[8,2048]{1,0:T(8,128)(2,1)S(1)}, u32[]{:S(2)}, u32[]{:S(2)}) collective-permute-start(bf16[8,2048]{1,0:T(8,128)(2,1)S(1)} %get-tuple-element.17), channel_id=1, source_target_pairs={{0,2},{1,3},{2,0},{3,1},{4,6},{5,7},{6,4},{7,5},{8,10},{9,11},{10,... | collective-permute-start | bytes 98312 | tf_op jit(solution)/shard_map/ppermute | solution.py:217
  5.6 5.4 %collective-permute-start.1 = (bf16[8,2048]{1,0:T(8,128)(2,1)S(1)}, bf16[8,2048]{1,0:T(8,128)(2,1)S(1)}, u32[]{:S(2)}, u32[]{:S(2)}) collective-permute-start(bf16[8,2048]{1,0:T(8,128)(2,1)S(1)} %get-tuple-element.18), channel_id=1, source_target_pairs={{0,4},{1,5},{2,6},{3,7},{4,0},{5,1},{6,2},{7,3},{8,12},{9,13},{10,... | collective-permute-start | bytes 98312 | tf_op jit(solution)/shard_map/ppermute | solution.py:217
  8.2 5.7 %collective-permute-start.2 = (bf16[8,2048]{1,0:T(8,128)(2,1)S(1)}, bf16[8,2048]{1,0:T(8,128)(2,1)S(1)}, u32[]{:S(2)}, u32[]{:S(2)}) collective-permute-start(bf16[8,2048]{1,0:T(8,128)(2,1)S(1)} %get-tuple-element.19), channel_id=1, source_target_pairs={{0,6},{1,7},{2,4},{3,5},{4,2},{5,3},{6,0},{7,1},{8,14},{9,15},{10,... | collective-permute-start | bytes 98312 | tf_op jit(solution)/shard_map/ppermute | solution.py:217
  13.9 5.5 %collective-permute-start.3 = (bf16[16,2048]{1,0:T(8,128)(2,1)S(1)}, bf16[16,2048]{1,0:T(8,128)(2,1)S(1)}, u32[]{:S(2)}, u32[]{:S(2)}) collective-permute-start(bf16[16,2048]{1,0:T(8,128)(2,1)S(1)} %pad_maximum_fusion), channel_id=1, source_target_pairs={{0,1},{1,0},{2,3},{3,2},{4,5},{5,4},{6,7},{7,6},{8,9},{9,8},{10,11... | collective-permute-start | bytes 196616 | tf_op jit(solution)/shard_map/ppermute | solution.py:217
  14.0 0.9 %copy-start.2 = (bf16[8,4,2048]{2,1,0:T(4,128)(2,1)S(1)}, bf16[8,4,2048]{2,1,0:T(4,128)(2,1)}, u32[]{:S(2)}) copy-start(bf16[8,4,2048]{2,1,0:T(4,128)(2,1)} %query_ref.3) | copy-start | bytes 393220
  14.9 0.9 %copy-start.4 = (bf16[8,4,2048]{2,1,0:T(4,128)(2,1)S(1)}, bf16[8,4,2048]{2,1,0:T(4,128)(2,1)}, u32[]{:S(2)}) copy-start(bf16[8,4,2048]{2,1,0:T(4,128)(2,1)} %key_ref.3) | copy-start | bytes 393220
  15.8 0.9 %copy-start.6 = (bf16[8,4,2048]{2,1,0:T(4,128)(2,1)S(1)}, bf16[8,4,2048]{2,1,0:T(4,128)(2,1)}, u32[]{:S(2)}) copy-start(bf16[8,4,2048]{2,1,0:T(4,128)(2,1)} %value_ref.3) | copy-start | bytes 393220
  16.7 0.7 %copy-start.9 = (s32[2,32]{1,0:T(2,128)S(1)}, s32[2,32]{1,0:T(2,128)}, u32[]{:S(2)}) copy-start(s32[2,32]{1,0:T(2,128)} %chosen_ref.1) | copy-start | bytes 772
  17.4 0.7 %copy-start.10 = (f32[2,32]{1,0:T(2,128)S(1)}, f32[2,32]{1,0:T(2,128)}, u32[]{:S(2)}) copy-start(f32[2,32]{1,0:T(2,128)} %gate_ref.1) | copy-start | bytes 772
  20.3 3.8 %collective-permute-start.4 = (bf16[2,2,2048]{2,1,0:T(2,128)(2,1)S(1)}, bf16[2,2,2048]{2,1,0:T(2,128)(2,1)S(1)}, u32[]{:S(2)}, u32[]{:S(2)}) collective-permute-start(bf16[2,2,2048]{2,1,0:T(2,128)(2,1)S(1)} %get-tuple-element.24), channel_id=1, source_target_pairs={{0,16},{8,24},{16,0},{24,8},{1,17},{9,25},{17,1},{25,9},{2,18},{10... | collective-permute-start | bytes 49160 | tf_op jit(solution)/shard_map/ppermute | solution.py:217
  24.2 5.8 %collective-permute-start.7 = (bf16[2,4,2048]{2,1,0:T(4,128)(2,1)S(1)}, bf16[2,4,2048]{2,1,0:T(4,128)(2,1)S(1)}, u32[]{:S(2)}, u32[]{:S(2)}) collective-permute-start(bf16[2,4,2048]{2,1,0:T(4,128)(2,1)S(1)} %pad_maximum_fusion.1), channel_id=1, source_target_pairs={{0,6},{1,7},{2,4},{3,5},{4,2},{5,3},{6,0},{7,1},{8,14},{9,15},{10,... | collective-permute-start | bytes 98312 | tf_op jit(solution)/shard_map/ppermute | solution.py:217
  24.6 5.4 %collective-permute-start.6 = (bf16[2,4,2048]{2,1,0:T(4,128)(2,1)S(1)}, bf16[2,4,2048]{2,1,0:T(4,128)(2,1)S(1)}, u32[]{:S(2)}, u32[]{:S(2)}) collective-permute-start(bf16[2,4,2048]{2,1,0:T(4,128)(2,1)S(1)} %pad_maximum_fusion.1), channel_id=1, source_target_pairs={{0,4},{1,5},{2,6},{3,7},{4,0},{5,1},{6,2},{7,3},{8,12},{9,13},{10,... | collective-permute-start | bytes 98312 | tf_op jit(solution)/shard_map/ppermute | solution.py:217
  24.7 5.8 %collective-permute-start.5 = (bf16[2,4,2048]{2,1,0:T(4,128)(2,1)S(1)}, bf16[2,4,2048]{2,1,0:T(4,128)(2,1)S(1)}, u32[]{:S(2)}, u32[]{:S(2)}) collective-permute-start(bf16[2,4,2048]{2,1,0:T(4,128)(2,1)S(1)} %pad_maximum_fusion.1), channel_id=1, source_target_pairs={{0,2},{1,3},{2,0},{3,1},{4,6},{5,7},{6,4},{7,5},{8,10},{9,11},{10,... | collective-permute-start | bytes 98312 | tf_op jit(solution)/shard_map/ppermute | solution.py:217
  30.6 5.0 %collective-permute-start.8 = (bf16[2,16,2048]{2,1,0:T(8,128)(2,1)S(1)}, bf16[2,16,2048]{2,1,0:T(8,128)(2,1)S(1)}, u32[]{:S(2)}, u32[]{:S(2)}) collective-permute-start(bf16[2,16,2048]{2,1,0:T(8,128)(2,1)S(1)} %concatenate.16), channel_id=1, source_target_pairs={{0,8},{8,0},{16,24},{24,16},{1,9},{9,1},{17,25},{25,17},{2,10},{10... | collective-permute-start | bytes 393224 | tf_op jit(solution)/shard_map/ppermute | solution.py:217
  35.8 1.6 %collective-permute-start.9 = (bf16[2,32,2048]{2,1,0:T(8,128)(2,1)S(1)}, bf16[2,32,2048]{2,1,0:T(8,128)(2,1)S(1)}, u32[]{:S(2)}, u32[]{:S(2)}) collective-permute-start(bf16[2,32,2048]{2,1,0:T(8,128)(2,1)S(1)} %concatenate.17.mine_ref), channel_id=1, source_target_pairs={{0,1},{1,0},{2,3},{3,2},{4,5},{5,4},{6,7},{7,6},{8,9},{9,8},{10,11... | collective-permute-start | bytes 786440 | tf_op jit(solution)/shard_map/ppermute | solution.py:217
  37.4 1.6 %copy-start.1 = (bf16[1,512,2048]{2,1,0:T(8,128)(2,1)S(1)}, bf16[1,512,2048]{2,1,0:T(8,128)(2,1)}, u32[]{:S(2)}) copy-start(bf16[1,512,2048]{2,1,0:T(8,128)(2,1)} %w_out_ref.1) | copy-start | bytes 6291460
  39.0 19.0 %copy-start.3 = (bf16[8,4,2048]{2,1,0:T(4,128)(2,1)S(1)}, bf16[8,4,2048]{2,1,0:T(4,128)(2,1)}, u32[]{:S(2)}) copy-start(bf16[8,4,2048]{2,1,0:T(4,128)(2,1)} %query_ref.3) | copy-start | bytes 393220
  39.0 19.0 %copy-start.5 = (bf16[8,4,2048]{2,1,0:T(4,128)(2,1)S(1)}, bf16[8,4,2048]{2,1,0:T(4,128)(2,1)}, u32[]{:S(2)}) copy-start(bf16[8,4,2048]{2,1,0:T(4,128)(2,1)} %key_ref.3) | copy-start | bytes 393220
  39.0 19.0 %copy-start.7 = (bf16[8,4,2048]{2,1,0:T(4,128)(2,1)S(1)}, bf16[8,4,2048]{2,1,0:T(4,128)(2,1)}, u32[]{:S(2)}) copy-start(bf16[8,4,2048]{2,1,0:T(4,128)(2,1)} %value_ref.3) | copy-start | bytes 393220
  40.8 1.4 %collective-permute-start.10 = (bf16[32,2048]{1,0:T(8,128)(2,1)S(1)}, bf16[32,2048]{1,0:T(8,128)(2,1)S(1)}, u32[]{:S(2)}, u32[]{:S(2)}) collective-permute-start(bf16[32,2048]{1,0:T(8,128)(2,1)S(1)} %get-tuple-element.26), channel_id=1, source_target_pairs={{0,1},{1,0},{2,3},{3,2},{4,5},{5,4},{6,7},{7,6},{8,9},{9,8},{10,11... | collective-permute-start | bytes 393224 | tf_op jit(solution)/shard_map/ppermute | solution.py:217
  42.3 4.3 %collective-permute-start.11 = (bf16[16,2048]{1,0:T(8,128)(2,1)S(1)}, bf16[16,2048]{1,0:T(8,128)(2,1)S(1)}, u32[]{:S(2)}, u32[]{:S(2)}) collective-permute-start(bf16[16,2048]{1,0:T(8,128)(2,1)S(1)} %slice.80), channel_id=1, source_target_pairs={{0,8},{8,0},{16,24},{24,16},{1,9},{9,1},{17,25},{25,17},{2,10},{10... | collective-permute-start | bytes 196616 | tf_op jit(solution)/shard_map/ppermute | solution.py:217
  46.6 3.8 %collective-permute-start.12 = (bf16[4,2048]{1,0:T(4,128)(2,1)S(1)}, bf16[4,2048]{1,0:T(4,128)(2,1)S(1)}, u32[]{:S(2)}, u32[]{:S(2)}) collective-permute-start(bf16[4,2048]{1,0:T(4,128)(2,1)S(1)} %get-tuple-element.29), channel_id=1, source_target_pairs={{0,2},{1,3},{2,0},{3,1},{4,6},{5,7},{6,4},{7,5},{8,10},{9,11},{10,... | collective-permute-start | bytes 49160 | tf_op jit(solution)/shard_map/ppermute | solution.py:217
  48.7 5.5 %collective-permute-start.14 = (bf16[4,2048]{1,0:T(4,128)(2,1)S(1)}, bf16[4,2048]{1,0:T(4,128)(2,1)S(1)}, u32[]{:S(2)}, u32[]{:S(2)}) collective-permute-start(bf16[4,2048]{1,0:T(4,128)(2,1)S(1)} %get-tuple-element.30), channel_id=1, source_target_pairs={{0,6},{1,7},{2,4},{3,5},{4,2},{5,3},{6,0},{7,1},{8,14},{9,15},{10,... | collective-permute-start | bytes 49160 | tf_op jit(solution)/shard_map/ppermute | solution.py:217
  49.1 5.1 %collective-permute-start.13 = (bf16[4,2048]{1,0:T(4,128)(2,1)S(1)}, bf16[4,2048]{1,0:T(4,128)(2,1)S(1)}, u32[]{:S(2)}, u32[]{:S(2)}) collective-permute-start(bf16[4,2048]{1,0:T(4,128)(2,1)S(1)} %get-tuple-element.31), channel_id=1, source_target_pairs={{0,4},{1,5},{2,6},{3,7},{4,0},{5,1},{6,2},{7,3},{8,12},{9,13},{10,... | collective-permute-start | bytes 49160 | tf_op jit(solution)/shard_map/ppermute | solution.py:217
  54.3 3.7 %collective-permute-start.15 = (bf16[2,2048]{1,0:T(2,128)(2,1)S(1)}, bf16[2,2048]{1,0:T(2,128)(2,1)S(1)}, u32[]{:S(2)}, u32[]{:S(2)}) collective-permute-start(bf16[2,2048]{1,0:T(2,128)(2,1)S(1)} %get-tuple-element.32), channel_id=1, source_target_pairs={{0,16},{8,24},{16,0},{24,8},{1,17},{9,25},{17,1},{25,9},{2,18},{10... | collective-permute-start | bytes 24584 | tf_op jit(solution)/shard_map/ppermute | solution.py:217

commit v4 on v3

v4 whole, which is shorter than its diff:
```python
import functools

import jax
import jax.numpy as jnp
from jax import lax
from jax.experimental import pallas as pl
from jax.experimental.pallas import tpu as pltpu
from jax.sharding import PartitionSpec as P

HEADS = 16
MOST = 2
CORES = 2
SUBLANES = 8

root_half = 0.7071067811865476
inv_root_tau = 0.3989422804014327

LANES_BOTH = (((1,), (1,)), ((), ()))
FIRST_BOTH = (((0,), (0,)), ((), ()))


def gelu_slope(pre_act):
    normal_cdf = 0.5 * (1.0 + lax.erf(pre_act * root_half))
    density = jnp.exp(-0.5 * pre_act * pre_act) * inv_root_tau
    return normal_cdf + pre_act * density


def dot(a, b):
    return jnp.dot(a, b, preferred_element_type=jnp.float32)


def dot_lanes(a, b):
    return lax.dot_general(a, b, LANES_BOTH, preferred_element_type=jnp.float32)


def over_frames(values, op, blocks):
    rows = values.shape[0]
    total = values[:SUBLANES]
    for start in range(SUBLANES, rows, SUBLANES):
        total = op(total, values[start : start + SUBLANES])
    step = blocks
    while step < SUBLANES:
        total = op(total, pltpu.roll(total, step, 0))
        step *= 2
    return jnp.concatenate([total] * (rows // SUBLANES), axis=0)


def heads_of(values):
    width = values.shape[1] // HEADS
    return [values[:, h * width : (h + 1) * width] for h in range(HEADS)]


def turn_kernel(cot_ref, out_ref):
    out_ref[...] = cot_ref[...].reshape(out_ref.shape)


def forward_kernel(
    patches_all, share, place_ref, query_hbm, key_hbm, value_hbm, chosen_ref, gate_ref,
    probs_ref, picked_ref, here_ref, weight_ref, spread_ref,
    query_ref, key_ref, value_ref, sems,
):
    copies = [
        pltpu.make_async_copy(source, target, sems.at[i])
        for i, (source, target) in enumerate(
            [(query_hbm, query_ref), (key_hbm, key_ref), (value_hbm, value_ref)]
        )
    ]
    for copy in copies:
        copy.start()
    frames, blocks, features = query_ref.shape
    rows = frames * blocks
    scaling = (features // HEADS) ** (-0.5)

    experts, cap = chosen_ref.shape
    myself = place_ref[0]
    before = (
        lax.broadcasted_iota(jnp.int32, (cap, cap), 0)
        < lax.broadcasted_iota(jnp.int32, (cap, cap), 1)
    ).astype(jnp.bfloat16)
    slot = lax.broadcasted_iota(jnp.int32, (SUBLANES, cap), 0)
    row_at = lax.broadcasted_iota(jnp.int32, (rows, cap), 0)
    found = []
    for e in range(experts):
        tokens = chosen_ref[e : e + 1, :]
        gates = gate_ref[e : e + 1, :]
        patch = tokens % patches_all
        owned = jnp.broadcast_to((patch // blocks == myself).astype(jnp.float32), slot.shape)
        rank = dot(owned.astype(jnp.bfloat16), before)
        taken = jnp.where((rank == slot.astype(jnp.float32)) & (owned > 0.0), 1.0, 0.0)
        position = (tokens // patches_all) * blocks + patch % blocks
        at_row = (row_at == position).astype(jnp.bfloat16)
        here = dot_lanes(taken.astype(jnp.bfloat16), at_row)
        weight = jnp.sum(taken * gates, axis=1, keepdims=True)
        here_ref[e * MOST : (e + 1) * MOST, :] = here[:MOST]
        weight_ref[e * MOST : (e + 1) * MOST, :] = jnp.broadcast_to(
            weight[:MOST], (MOST, weight_ref.shape[1])
        )
        found.append(here[:MOST])
    here = jnp.concatenate(found, axis=0).astype(jnp.bfloat16)
    cores, _, returns = spread_ref.shape
    slot_at = lax.broadcasted_iota(jnp.int32, (experts * MOST, returns), 0)
    back_at = lax.broadcasted_iota(jnp.int32, (experts * MOST, returns), 1)
    sender = back_at // MOST
    same = (sender // share == slot_at // MOST) & (back_at % MOST == slot_at % MOST)
    for c in range(cores):
        spread_ref[c] = lax.dot_general(
            here,
            (same & (sender % cores == c)).astype(jnp.bfloat16),
            FIRST_BOTH,
            preferred_element_type=jnp.float32,
        ).astype(jnp.bfloat16)

    for copy in copies:
        copy.wait()
    query = query_ref[...].reshape(rows, features)
    key = key_ref[...].reshape(rows, features)
    value = value_ref[...].reshape(rows, features)
    scores = jnp.concatenate(
        [dot_lanes(k, q) for k, q in zip(heads_of(key), heads_of(query))], axis=1
    )
    scores = scores * scaling
    raised = jnp.exp(scores - over_frames(scores, jnp.maximum, blocks))
    probs = raised / over_frames(raised, jnp.add, blocks)
    patch_in = lax.broadcasted_iota(jnp.int32, probs.shape, 0) % blocks
    patch_out = lax.broadcasted_iota(jnp.int32, probs.shape, 1) % blocks
    probs = jnp.where(patch_in == patch_out, probs, 0.0)
    probs_ref[...] = probs
    weights = probs.T.astype(jnp.bfloat16)
    mixed = jnp.concatenate(
        [dot(weights[h * rows : (h + 1) * rows], v) for h, v in enumerate(heads_of(value))],
        axis=1,
    ).astype(jnp.bfloat16)
    picked_ref[...] = dot(here, mixed).astype(jnp.bfloat16)


def pick_kernel(share, here_ref, weight_ref, picked_ref, cot_ref, out_ref):
    frames, blocks, features = cot_ref.shape
    rows = dot(here_ref[...].astype(jnp.bfloat16), cot_ref[...].reshape(frames * blocks, features))
    rows = (rows * weight_ref[:, :1]).astype(jnp.bfloat16)
    part = features // CORES
    for e in range(out_ref.shape[0] // share):
        slots = slice(e * MOST, (e + 1) * MOST)
        both = jnp.concatenate([picked_ref[slots], rows[slots]], axis=0)
        for i in range(share):
            c = i % CORES
            out_ref[e * share + i] = both[:, c * part : (c + 1) * part]


def half_expert(part, rows_ref, w_in_ref, w_out_hbm, held_ref, sem):
    width = rows_ref.shape[2]
    start = pl.multiple_of(part * width, width)
    copy = pltpu.make_async_copy(w_out_hbm.at[0, :, pl.ds(start, width)], held_ref, sem)
    copy.start()
    rows = rows_ref[...].reshape(-1, width)
    pre_act = dot(rows, w_in_ref[0, pl.ds(start, width), :])
    copy.wait()
    return pre_act, dot_lanes(rows, held_ref[...])


def first_kernel(place_ref, rows_ref, w_in_ref, w_out_hbm, pre_ref, back_ref, held_ref, sem):
    pre_ref[...], back_ref[...] = half_expert(
        place_ref[1], rows_ref, w_in_ref, w_out_hbm, held_ref, sem
    )


def second_kernel(
    place_ref, rows_ref, pre_ref, back_ref, w_in_ref, w_out_hbm, kept_ref, sent_ref, held_ref, sem
):
    mine = place_ref[1]
    pre_act, back_act = half_expert(
        1 - mine, rows_ref, w_in_ref, w_out_hbm, held_ref, sem
    )
    pre_act = pre_act + pre_ref[...]
    back_act = back_act + back_ref[...]
    count = pre_act.shape[0]
    back_act = pltpu.roll(back_act, count - MOST, 0)
    slope = (back_act * gelu_slope(pre_act)).astype(jnp.bfloat16)
    want = lax.broadcasted_iota(jnp.int32, (count // 2, count), 0)
    have = lax.broadcasted_iota(jnp.int32, (count // 2, count), 1)
    chosen = (have == (want // MOST) * (2 * MOST) + want % MOST).astype(jnp.bfloat16)
    slope = dot(chosen, slope).astype(jnp.bfloat16)
    width = rows_ref.shape[2]
    here = pl.multiple_of(mine * width, width)
    there = pl.multiple_of((1 - mine) * width, width)
    sent = dot_lanes(slope, w_in_ref[0, pl.ds(there, width), :])
    sent_ref[...] = sent.astype(jnp.bfloat16).reshape(sent_ref.shape)
    kept = dot_lanes(slope, w_in_ref[0, pl.ds(here, width), :])
    kept_ref[...] = kept.reshape(kept_ref.shape)


def backward_kernel(
    spread_ref, back_ref, cot_ref, probs_ref, query_ref, key_ref, value_ref,
    grad_query_ref, grad_key_ref, grad_value_ref,
):
    frames, blocks, features = query_ref.shape
    rows = frames * blocks
    scaling = (features // HEADS) ** (-0.5)
    query = query_ref[...].reshape(rows, features)
    key = key_ref[...].reshape(rows, features)
    value = value_ref[...].reshape(rows, features)
    back = back_ref[...].reshape(-1, back_ref.shape[2])
    added = jnp.concatenate([dot(spread_ref[c], back) for c in range(CORES)], axis=1)
    cot = cot_ref[...].reshape(rows, features)
    stream = (cot.astype(jnp.float32) + added).astype(jnp.bfloat16)
    probs = probs_ref[...]
    grad_prob = jnp.concatenate(
        [dot_lanes(v, g) for v, g in zip(heads_of(value), heads_of(stream))], axis=1
    )
    centre = over_frames(probs * grad_prob, jnp.add, blocks)
    grad_score = probs * (grad_prob - centre)
    turned = grad_score.T.astype(jnp.bfloat16)
    grad_score = grad_score.astype(jnp.bfloat16)
    weights = probs.astype(jnp.bfloat16)

    def joined(parts):
        return jnp.concatenate(parts, axis=1).astype(jnp.bfloat16).reshape(frames, blocks, features)

    grad_value_ref[...] = joined(
        [dot(w, g) for w, g in zip(heads_of(weights), heads_of(stream))]
    )
    grad_key_ref[...] = joined(
        [dot(s, q) * scaling for s, q in zip(heads_of(grad_score), heads_of(query))]
    )
    grad_query_ref[...] = joined(
        [dot(turned[h * rows : (h + 1) * rows], k) * scaling for h, k in enumerate(heads_of(key))]
    )


def call(kernel, outs, operands, places, scratch=()):
    smem, vmem, hbm = (
        pl.BlockSpec(memory_space=space) for space in (pltpu.SMEM, pltpu.VMEM, pltpu.HBM)
    )
    spaces = {"s": smem, "v": vmem, "h": hbm}
    return pl.pallas_call(
        kernel,
        out_shape=[jax.ShapeDtypeStruct(shape, dtype) for shape, dtype in outs],
        in_specs=[spaces[place] for place in places],
        out_specs=[vmem] * len(outs),
        scratch_shapes=list(scratch),
        compiler_params=pltpu.CompilerParams(vmem_limit_bytes=40 * 1024 * 1024),
    )(*operands)


def body(query_in, key_in, value_in, cotangent, w_in, w_out, gate_probs, chosen):
    bf16, f32 = jnp.bfloat16, jnp.float32
    frames, blocks, features = query_in.shape
    groups = lax.axis_size("grp")
    columns = lax.axis_size("frm")
    experts = gate_probs.shape[0]
    devices = groups * columns
    share = devices // experts
    rows = frames * blocks
    slots = experts * MOST
    part = features // CORES
    hidden = w_in.shape[2]
    column = lax.axis_index("frm")
    place = jnp.stack([lax.axis_index("grp") * columns + column, column % CORES])
    place = place.astype(jnp.int32)
    everyone = ("grp", "frm")

    def swap(values):
        return lax.ppermute(values, "frm", [(i, i ^ 1) for i in range(columns)])

    (turned,) = call(
        turn_kernel, [((columns, blocks, features), bf16)], [cotangent], "v"
    )
    cot = lax.all_to_all(turned, "frm", split_axis=0, concat_axis=0, tiled=True)
    probs, picked, here, weight, spread = call(
        functools.partial(forward_kernel, blocks * devices, share),
        [
            ((rows, HEADS * rows), f32),
            ((slots, features), bf16),
            ((slots, rows), f32),
            ((slots, 128), f32),
            ((CORES, rows, devices * MOST), bf16),
        ],
        [place, query_in, key_in, value_in, chosen, gate_probs],
        "shhhvv",
        [pltpu.VMEM(query_in.shape, bf16)] * 3 + [pltpu.SemaphoreType.DMA((3,))],
    )
    (outgoing,) = call(
        functools.partial(pick_kernel, share),
        [((devices, 2 * MOST, part), bf16)],
        [here, weight, picked, cot],
        "vvvv",
    )
    held = lax.all_to_all(outgoing, everyone, split_axis=0, concat_axis=0, tiled=True)
    other = swap(held)
    acts = ((devices * 2 * MOST, hidden), f32)
    scratch = [pltpu.VMEM((hidden, part), bf16), pltpu.SemaphoreType.DMA]
    pre_act, back_act = call(
        first_kernel, [acts, acts], [place, held, w_in, w_out], "svvh", scratch
    )
    piece = (devices, MOST, part)
    kept, sent = call(
        second_kernel,
        [(piece, f32), (piece, bf16)],
        [place, other, pre_act, back_act, w_in, w_out],
        "svvvvh",
        scratch,
    )
    total = (kept + swap(sent).astype(f32)).astype(bf16)
    back = lax.all_to_all(total, everyone, split_axis=0, concat_axis=0, tiled=True)
    return call(
        backward_kernel,
        [((frames, blocks, features), bf16)] * 3,
        [spread, back, cot, probs, query_in, key_in, value_in],
        "vvvvvvv",
    )


def solution(mesh):
    return jax.shard_map(
        body,
        mesh=mesh,
        in_specs=(
            P(None, ("grp", "frm"), None),
            P(None, ("grp", "frm"), None),
            P(None, ("grp", "frm"), None),
            P("frm", "grp", None),
            P("grp", None, "frm"),
            P("grp", "frm", None),
            P(),
            P(),
        ),
        out_specs=(
            P(None, ("grp", "frm"), None),
            P(None, ("grp", "frm"), None),
            P(None, ("grp", "frm"), None),
        ),
        check_vma=False,
    )
```

time: 59.7 us -> 53 us (0.89)
  blocking collectives: 0 us -> 26.1 us
  waiting for transfers between devices: 24.9 us -> 1.69 us
  starting transfers between devices: 20.4 us -> 6.91 us
  Pallas kernels: 6.08 us -> 8.11 us
  local copies, waits for them, and re-layouts: 7.04 us -> 8.87 us
    all_to_all x0 -> x2, blocking collectives: none -> 26.1 us  [the longest x1 15.8 us: body(): lax.all_to_all(outgoing, everyone, split_axis=0, concat_axis=0, tiled=True)]
    ppermute x16 -> x2, waiting for transfers between devices: 24.9 us -> 1.22 us  [swap(): return lax.ppermute(values, 'frm', [(i, i ^ 1) for i in range(columns)])]
    ppermute x16 -> x2, starting transfers between devices: 20.4 us -> 0.58 us  [swap(): return lax.ppermute(values, 'frm', [(i, i ^ 1) for i in range(columns)])]
    all_to_all x0 -> x1, starting transfers between devices: none -> 6.33 us  [body(): cot = lax.all_to_all(turned, 'frm', split_axis=0, concat_axis=0, tiled=True)]
    unnamed x22 -> x26, local copies, waits for them, and re-layouts: 6.71 us -> 8.87 us
    pallas_call x6, Pallas kernels: 6.08 us -> 8.11 us  [call(): pl.pallas_call(kernel, out_shape=[jax.ShapeDtypeStruct(shape, dtype) for...]
  transfers between devices with their start and end apart: 16 -> 3, of which waited for: 12 -> 2; matrix products, arithmetic and copies ran while one was open for 0% -> 0% of each run, Pallas kernels for 2% -> 7%
where the time goes in v4:
time: 53 us; the launch traced here: 52.6 us
  blocking collectives  26.1 us (49%)
  local copies, waits for them, and re-layouts  8.87 us (17%)
  Pallas kernels  8.11 us (15%)
  starting transfers between devices  6.91 us (13%)
  waiting for transfers between devices  1.69 us (3%)
  between operations  0.7 us (1%)
    all_to_all x1, blocking collectives, body(): lax.all_to_all(outgoing, everyone, split_axis=0, concat_axis=0, tiled=True)  15.8 us
    all_to_all x1, blocking collectives, body(): lax.all_to_all(total, everyone, split_axis=0, concat_axis=0, tiled=True)  10.3 us
    unnamed x26, local copies, waits for them, and re-layouts  8.87 us
    pallas_call x6, Pallas kernels, call(): pl.pallas_call(kernel, out_shape=[jax.ShapeDtypeStruct(shape, dtype) for...  8.11 us
    all_to_all x1, starting transfers between devices, body(): cot = lax.all_to_all(turned, 'frm', split_axis=0, concat_axis=0, tiled=True)  6.33 us
    ppermute x2, waiting for transfers between devices, swap(): return lax.ppermute(values, 'frm', [(i, i ^ 1) for i in range(columns)])  1.22 us
  transfers between devices with their start and end apart: 3, of which 2 were waited for; matrix products, arithmetic and copies ran while one was open for 0% of the time, Pallas kernels for 7%

profile of v4, /device:TPU:0, one launch (start us, length us, event | category | flops | bytes accessed | tf_op | source)
XLA Modules:
  0.0 52.6 jit_solution(9971067342057405057)
XLA Ops:
  0.6 0.0 copy-start.10
  0.6 0.9 %copy-done.10 = bf16[1,32,2048]{2,1,0:T(8,128)(2,1)S(1)} copy-done((bf16[1,32,2048]{2,1,0:T(8,128)(2,1)S(1)}, bf16[1,32,2048]{2,1,0:T(8,128)(2,1)}, u32[]{:S(2)}) %copy-start.10) | copy-done | bytes 131096
  1.5 0.7 %shard_map.104 = bf16[8,4,2048]{2,1,0:T(4,128)(2,1)} custom-call(bf16[1,32,2048]{2,1,0:T(8,128)(2,1)S(1)} %copy-done.10), custom_call_target="tpu_custom_call" | custom-call | tf_op jit(solution)/shard_map/pallas_call | solution.py:234
  2.2 6.3 %all-to-all-start = ((bf16[8,4,2048]{2,1,0:T(4,128)(2,1)}), bf16[8,4,2048]{2,1,0:T(4,128)(2,1)S(1)}, u32[]{:S(2)}, u32[]{:S(2)}) async-start(bf16[8,4,2048]{2,1,0:T(4,128)(2,1)} %shard_map.104), calls=%async_computation | async-start | bytes 262144 | tf_op jit(solution)/shard_map/all_to_all | solution.py:267
  8.5 0.1 pad_add_fusion.place_ref
  8.6 0.0 copy-start.4
  8.6 0.9 %copy-done.4 = bf16[8,4,2048]{2,1,0:T(4,128)(2,1)S(1)} copy-done((bf16[8,4,2048]{2,1,0:T(4,128)(2,1)S(1)}, bf16[8,4,2048]{2,1,0:T(4,128)(2,1)}, u32[]{:S(2)}) %copy-start.4) | copy-done | bytes 131096
  9.5 0.0 copy-start.6
  9.5 0.9 %copy-done.6 = bf16[8,4,2048]{2,1,0:T(4,128)(2,1)S(1)} copy-done((bf16[8,4,2048]{2,1,0:T(4,128)(2,1)S(1)}, bf16[8,4,2048]{2,1,0:T(4,128)(2,1)}, u32[]{:S(2)}) %copy-start.6) | copy-done | bytes 131096
  10.4 0.0 copy-start.8
  10.4 0.9 %copy-done.8 = bf16[8,4,2048]{2,1,0:T(4,128)(2,1)S(1)} copy-done((bf16[8,4,2048]{2,1,0:T(4,128)(2,1)S(1)}, bf16[8,4,2048]{2,1,0:T(4,128)(2,1)}, u32[]{:S(2)}) %copy-start.8) | copy-done | bytes 131096
  11.3 0.0 copy-start.11
  11.3 0.7 %copy-done.11 = s32[2,32]{1,0:T(2,128)S(1)} copy-done((s32[2,32]{1,0:T(2,128)S(1)}, s32[2,32]{1,0:T(2,128)}, u32[]{:S(2)}) %copy-start.11) | copy-done | bytes 280
  12.0 0.0 copy-start.12
  12.0 0.7 %copy-done.12 = f32[2,32]{1,0:T(2,128)S(1)} copy-done((f32[2,32]{1,0:T(2,128)S(1)}, f32[2,32]{1,0:T(2,128)}, u32[]{:S(2)}) %copy-start.12) | copy-done | bytes 280
  12.7 2.2 %shard_map.103 = (f32[32,512]{1,0:T(8,128)S(1)}, bf16[4,2048]{1,0:T(4,128)(2,1)S(1)}, f32[4,32]{1,0:T(4,128)S(1)}, f32[4,128]{1,0:T(4,128)S(1)}, bf16[2,32,64]{2,1,0:T(8,128)(2,1)S(1)}) custom-call(s32[2]{0:T(128)S(1)} %pad_add_fusion.place_ref, bf16[8,4,2048]{2,1,0:T(4,128)(2,1)S(1)} %copy-done.4, bf16[8,4,2048]{2,1,0:T(4,128)(2,1)S(1)} %copy-done.6, ...), custom_call_target="tpu_custom_call" | custom-call | tf_op jit(solution)/shard_map/pallas_call | solution.py:234
  14.8 0.5 all-to-all-done.cot_ref
  15.3 0.2 shard_map.105
  15.5 15.8 %all_to_all.15.rows_ref = bf16[32,4,1024]{2,1,0:T(4,128)(2,1)S(1)} all-to-all(bf16[32,4,1024]{2,1,0:T(4,128)(2,1)S(1)} %shard_map.105), channel_id=1, replica_groups=mesh['grp'=4,'frm'=8] {'grp','frm'}, dimensions={0} | all-to-all | bytes 524288 | tf_op jit(solution)/shard_map/all_to_all | solution.py:287
  31.3 0.4 collective-permute-start
  31.7 0.0 copy-start
  31.7 1.6 %copy-done = bf16[1,2048,512]{2,1,0:T(8,128)(2,1)S(1)} copy-done((bf16[1,2048,512]{2,1,0:T(8,128)(2,1)S(1)}, bf16[1,2048,512]{2,1,0:T(8,128)(2,1)}, u32[]{:S(2)}) %copy-start) | copy-done | bytes 2097176
  33.3 0.0 copy-start.2
  33.3 1.6 %copy-done.2 = bf16[1,512,2048]{2,1,0:T(8,128)(2,1)S(1)} copy-done((bf16[1,512,2048]{2,1,0:T(8,128)(2,1)S(1)}, bf16[1,512,2048]{2,1,0:T(8,128)(2,1)}, u32[]{:S(2)}) %copy-start.2) | copy-done | bytes 2097176
  34.8 0.0 copy-start.1
  34.8 0.0 copy-start.3
  34.9 1.5 %shard_map.106 = (f32[128,512]{1,0:T(8,128)S(1)}, f32[128,512]{1,0:T(8,128)S(1)}) custom-call(s32[2]{0:T(128)S(1)} %pad_add_fusion.place_ref, bf16[32,4,1024]{2,1,0:T(4,128)(2,1)S(1)} %all_to_all.15.rows_ref, bf16[1,2048,512]{2,1,0:T(8,128)(2,1)S(1)} %copy-done, bf16[1,512,2048]{2,1,0:T(8,128)(2,1)S(1)} %copy-done.2), custom_call_target="tpu_custom_call" | custom-call | tf_op jit(solution)/shard_map/pallas_call | solution.py:234
  36.4 0.0 collective-permute-done.rows_ref
  36.4 0.1 copy-done.1
  36.4 0.6 %copy-done.3 = bf16[1,512,2048]{2,1,0:T(8,128)(2,1)S(1)} copy-done((bf16[1,512,2048]{2,1,0:T(8,128)(2,1)S(1)}, bf16[1,512,2048]{2,1,0:T(8,128)(2,1)}, u32[]{:S(2)}) %copy-start.3) | copy-done | bytes 2097176
  37.1 0.0 copy-start.5
  37.1 0.0 copy-start.7
  37.1 0.0 copy-start.9
  37.1 2.3 %shard_map.107 = (f32[32,2,1024]{2,1,0:T(2,128)S(1)}, bf16[32,2,1024]{2,1,0:T(2,128)(2,1)S(1)}) custom-call(s32[2]{0:T(128)S(1)} %pad_add_fusion.place_ref, bf16[32,4,1024]{2,1,0:T(4,128)(2,1)S(1)} %collective-permute-done.rows_ref, f32[128,512]{1,0:T(8,128)S(1)} %get-tuple-element.16.pre_ref, f32[128,512]{1,0:T(8,128)S(1)} %get-tuple-element.17.back_ref, ...), custom_call_target="tpu_custom_call" | custom-call | tf_op jit(solution)/shard_map/pallas_call | solution.py:234
  39.4 0.2 collective-permute-start.1
  39.6 1.2 %collective-permute-done.1 = bf16[32,2,1024]{2,1,0:T(2,128)(2,1)S(1)} collective-permute-done((bf16[32,2,1024]{2,1,0:T(2,128)(2,1)S(1)}, bf16[32,2,1024]{2,1,0:T(2,128)(2,1)S(1)}, u32[]{:S(2)}, u32[]{:S(2)}) %collective-permute-start.1) | collective-permute-done | bytes 131104 | tf_op jit(solution)/shard_map/ppermute | solution.py:262
  40.8 0.1 add_convert_fusion
  40.9 10.3 %all_to_all.16.back_ref = bf16[32,2,1024]{2,1,0:T(2,128)(2,1)S(1)} all-to-all(bf16[32,2,1024]{2,1,0:T(2,128)(2,1)S(1)} %add_convert_fusion), channel_id=1, replica_groups=mesh['grp'=4,'frm'=8] {'grp','frm'}, dimensions={0} | all-to-all | bytes 262144 | tf_op jit(solution)/shard_map/all_to_all | solution.py:303
  51.2 0.0 copy-done.5
  51.2 0.0 copy-done.7
  51.2 0.0 copy-done.9
  51.2 1.4 %shard_map.108 = (bf16[8,4,2048]{2,1,0:T(4,128)(2,1)}, bf16[8,4,2048]{2,1,0:T(4,128)(2,1)}, bf16[8,4,2048]{2,1,0:T(4,128)(2,1)}) custom-call(bf16[2,32,64]{2,1,0:T(8,128)(2,1)S(1)} %get-tuple-element.12.spread_ref, bf16[32,2,1024]{2,1,0:T(2,128)(2,1)S(1)} %all_to_all.16.back_ref, bf16[8,4,2048]{2,1,0:T(4,128)(2,1)S(1)} %all-to-all-done.cot_ref, ...), custom_call_target="tpu_custom_call" | custom-call | tf_op jit(solution)/shard_map/pallas_call | solution.py:234
Async XLA Ops:
  0.6 0.9 %copy-start.10 = (bf16[1,32,2048]{2,1,0:T(8,128)(2,1)S(1)}, bf16[1,32,2048]{2,1,0:T(8,128)(2,1)}, u32[]{:S(2)}) copy-start(bf16[1,32,2048]{2,1,0:T(8,128)(2,1)} %cot_ref.1) | copy-start | bytes 393220
  2.2 13.1 %all-to-all-start = ((bf16[8,4,2048]{2,1,0:T(4,128)(2,1)}), bf16[8,4,2048]{2,1,0:T(4,128)(2,1)S(1)}, u32[]{:S(2)}, u32[]{:S(2)}) async-start(bf16[8,4,2048]{2,1,0:T(4,128)(2,1)} %shard_map.104), calls=%async_computation | async-start | bytes 262144 | tf_op jit(solution)/shard_map/all_to_all | solution.py:267
  8.6 0.9 %copy-start.4 = (bf16[8,4,2048]{2,1,0:T(4,128)(2,1)S(1)}, bf16[8,4,2048]{2,1,0:T(4,128)(2,1)}, u32[]{:S(2)}) copy-start(bf16[8,4,2048]{2,1,0:T(4,128)(2,1)} %query_ref.1) | copy-start | bytes 393220
  9.5 0.9 %copy-start.6 = (bf16[8,4,2048]{2,1,0:T(4,128)(2,1)S(1)}, bf16[8,4,2048]{2,1,0:T(4,128)(2,1)}, u32[]{:S(2)}) copy-start(bf16[8,4,2048]{2,1,0:T(4,128)(2,1)} %key_ref.1) | copy-start | bytes 393220
  10.4 0.9 %copy-start.8 = (bf16[8,4,2048]{2,1,0:T(4,128)(2,1)S(1)}, bf16[8,4,2048]{2,1,0:T(4,128)(2,1)}, u32[]{:S(2)}) copy-start(bf16[8,4,2048]{2,1,0:T(4,128)(2,1)} %value_ref.1) | copy-start | bytes 393220
  11.3 0.7 %copy-start.11 = (s32[2,32]{1,0:T(2,128)S(1)}, s32[2,32]{1,0:T(2,128)}, u32[]{:S(2)}) copy-start(s32[2,32]{1,0:T(2,128)} %chosen_ref.1) | copy-start | bytes 772
  12.0 0.7 %copy-start.12 = (f32[2,32]{1,0:T(2,128)S(1)}, f32[2,32]{1,0:T(2,128)}, u32[]{:S(2)}) copy-start(f32[2,32]{1,0:T(2,128)} %gate_ref.1) | copy-start | bytes 772
  31.3 5.1 %collective-permute-start = (bf16[32,4,1024]{2,1,0:T(4,128)(2,1)S(1)}, bf16[32,4,1024]{2,1,0:T(4,128)(2,1)S(1)}, u32[]{:S(2)}, u32[]{:S(2)}) collective-permute-start(bf16[32,4,1024]{2,1,0:T(4,128)(2,1)S(1)} %all_to_all.15.rows_ref), channel_id=1, source_target_pairs={{0,1},{1,0},{2,3},{3,2},{4,5},{5,4},{6,7},{7,6},{8,9},{9,8},{10,11... | collective-permute-start | bytes 786440 | tf_op jit(solution)/shard_map/ppermute | solution.py:262
  31.7 1.6 %copy-start = (bf16[1,2048,512]{2,1,0:T(8,128)(2,1)S(1)}, bf16[1,2048,512]{2,1,0:T(8,128)(2,1)}, u32[]{:S(2)}) copy-start(bf16[1,2048,512]{2,1,0:T(8,128)(2,1)} %w_in_ref.3) | copy-start | bytes 6291460
  33.3 1.6 %copy-start.2 = (bf16[1,512,2048]{2,1,0:T(8,128)(2,1)S(1)}, bf16[1,512,2048]{2,1,0:T(8,128)(2,1)}, u32[]{:S(2)}) copy-start(bf16[1,512,2048]{2,1,0:T(8,128)(2,1)} %w_out_hbm.3) | copy-start | bytes 6291460
  34.8 1.6 %copy-start.1 = (bf16[1,2048,512]{2,1,0:T(8,128)(2,1)S(1)}, bf16[1,2048,512]{2,1,0:T(8,128)(2,1)}, u32[]{:S(2)}) copy-start(bf16[1,2048,512]{2,1,0:T(8,128)(2,1)} %w_in_ref.3) | copy-start | bytes 6291460
  34.8 2.2 %copy-start.3 = (bf16[1,512,2048]{2,1,0:T(8,128)(2,1)S(1)}, bf16[1,512,2048]{2,1,0:T(8,128)(2,1)}, u32[]{:S(2)}) copy-start(bf16[1,512,2048]{2,1,0:T(8,128)(2,1)} %w_out_hbm.3) | copy-start | bytes 6291460
  37.1 14.1 %copy-start.5 = (bf16[8,4,2048]{2,1,0:T(4,128)(2,1)S(1)}, bf16[8,4,2048]{2,1,0:T(4,128)(2,1)}, u32[]{:S(2)}) copy-start(bf16[8,4,2048]{2,1,0:T(4,128)(2,1)} %query_ref.1) | copy-start | bytes 393220
  37.1 14.1 %copy-start.7 = (bf16[8,4,2048]{2,1,0:T(4,128)(2,1)S(1)}, bf16[8,4,2048]{2,1,0:T(4,128)(2,1)}, u32[]{:S(2)}) copy-start(bf16[8,4,2048]{2,1,0:T(4,128)(2,1)} %key_ref.1) | copy-start | bytes 393220
  37.1 14.1 %copy-start.9 = (bf16[8,4,2048]{2,1,0:T(4,128)(2,1)S(1)}, bf16[8,4,2048]{2,1,0:T(4,128)(2,1)}, u32[]{:S(2)}) copy-start(bf16[8,4,2048]{2,1,0:T(4,128)(2,1)} %value_ref.1) | copy-start | bytes 393220
  39.4 1.4 %collective-permute-start.1 = (bf16[32,2,1024]{2,1,0:T(2,128)(2,1)S(1)}, bf16[32,2,1024]{2,1,0:T(2,128)(2,1)S(1)}, u32[]{:S(2)}, u32[]{:S(2)}) collective-permute-start(bf16[32,2,1024]{2,1,0:T(2,128)(2,1)S(1)} %get-tuple-element.19), channel_id=1, source_target_pairs={{0,1},{1,0},{2,3},{3,2},{4,5},{5,4},{6,7},{7,6},{8,9},{9,8},{10,11... | collective-permute-start | bytes 393224 | tf_op jit(solution)/shard_map/ppermute | solution.py:262

commit v5 on v4

--- a/solution.py
+++ b/solution.py
@@ -11,6 +11,7 @@
 MOST = 2
 CORES = 2
 SUBLANES = 8
+LANES = 128
 
 root_half = 0.7071067811865476
 inv_root_tau = 0.3989422804014327
@@ -50,20 +51,25 @@
     return [values[:, h * width : (h + 1) * width] for h in range(HEADS)]
 
 
-def turn_kernel(cot_ref, out_ref):
+def turn_kernel(cot_hbm, out_ref, cot_ref, sem):
+    copy = pltpu.make_async_copy(cot_hbm, cot_ref, sem)
+    copy.start()
+    copy.wait()
     out_ref[...] = cot_ref[...].reshape(out_ref.shape)
 
 
 def forward_kernel(
-    patches_all, share, place_ref, query_hbm, key_hbm, value_hbm, chosen_ref, gate_ref,
+    patches_all, share, place_ref,
+    chosen_hbm, gate_hbm, query_hbm, key_hbm, value_hbm, w_in_hbm, w_out_hbm,
+    query_ref, key_ref, value_ref, w_in_ref, w_out_ref,
     probs_ref, picked_ref, here_ref, weight_ref, spread_ref,
-    query_ref, key_ref, value_ref, sems,
+    chosen_ref, gate_ref, sems,
 ):
+    sources = [chosen_hbm, gate_hbm, query_hbm, key_hbm, value_hbm, w_in_hbm, w_out_hbm]
+    targets = [chosen_ref, gate_ref, query_ref, key_ref, value_ref, w_in_ref, w_out_ref]
     copies = [
         pltpu.make_async_copy(source, target, sems.at[i])
-        for i, (source, target) in enumerate(
-            [(query_hbm, query_ref), (key_hbm, key_ref), (value_hbm, value_ref)]
-        )
+        for i, (source, target) in enumerate(zip(sources, targets))
     ]
     for copy in copies:
         copy.start()
@@ -71,6 +77,8 @@
     rows = frames * blocks
     scaling = (features // HEADS) ** (-0.5)
 
+    for copy in copies[:2]:
+        copy.wait()
     experts, cap = chosen_ref.shape
     myself = place_ref[0]
     before = (
@@ -110,7 +118,7 @@
             preferred_element_type=jnp.float32,
         ).astype(jnp.bfloat16)
 
-    for copy in copies:
+    for copy in copies[2:5]:
         copy.wait()
     query = query_ref[...].reshape(rows, features)
     key = key_ref[...].reshape(rows, features)
@@ -131,6 +139,8 @@
         axis=1,
     ).astype(jnp.bfloat16)
     picked_ref[...] = dot(here, mixed).astype(jnp.bfloat16)
+    for copy in copies[5:]:
+        copy.wait()
 
 
 def pick_kernel(share, here_ref, weight_ref, picked_ref, cot_ref, out_ref):
@@ -146,40 +156,47 @@
             out_ref[e * share + i] = both[:, c * part : (c + 1) * part]
 
 
-def half_expert(part, rows_ref, w_in_ref, w_out_hbm, held_ref, sem):
+def half_expert(part, rows_ref, w_in_ref, w_out_ref, pre_ref, back_ref):
     width = rows_ref.shape[2]
     start = pl.multiple_of(part * width, width)
-    copy = pltpu.make_async_copy(w_out_hbm.at[0, :, pl.ds(start, width)], held_ref, sem)
-    copy.start()
     rows = rows_ref[...].reshape(-1, width)
     pre_act = dot(rows, w_in_ref[0, pl.ds(start, width), :])
-    copy.wait()
-    return pre_act, dot_lanes(rows, held_ref[...])
-
-
-def first_kernel(place_ref, rows_ref, w_in_ref, w_out_hbm, pre_ref, back_ref, held_ref, sem):
-    pre_ref[...], back_ref[...] = half_expert(
-        place_ref[1], rows_ref, w_in_ref, w_out_hbm, held_ref, sem
-    )
+    back_act = dot_lanes(rows, w_out_ref[0, :, pl.ds(start, width)])
+    for i in range(pre_ref.shape[0]):
+        pre_ref[i] = pre_act[:, i * LANES : (i + 1) * LANES]
+        back_ref[i] = back_act[:, i * LANES : (i + 1) * LANES]
+
+
+def first_kernel(place_ref, rows_ref, w_in_ref, w_out_ref, pre_ref, back_ref):
+    half_expert(place_ref[1], rows_ref, w_in_ref, w_out_ref, pre_ref, back_ref)
 
 
 def second_kernel(
-    place_ref, rows_ref, pre_ref, back_ref, w_in_ref, w_out_hbm, kept_ref, sent_ref, held_ref, sem
+    place_ref, rows_ref, pre_ref, back_ref, w_in_ref, w_out_ref,
+    kept_ref, sent_ref, more_pre_ref, more_back_ref,
 ):
     mine = place_ref[1]
-    pre_act, back_act = half_expert(
-        1 - mine, rows_ref, w_in_ref, w_out_hbm, held_ref, sem
-    )
-    pre_act = pre_act + pre_ref[...]
-    back_act = back_act + back_ref[...]
-    count = pre_act.shape[0]
-    back_act = pltpu.roll(back_act, count - MOST, 0)
-    slope = (back_act * gelu_slope(pre_act)).astype(jnp.bfloat16)
-    want = lax.broadcasted_iota(jnp.int32, (count // 2, count), 0)
-    have = lax.broadcasted_iota(jnp.int32, (count // 2, count), 1)
-    chosen = (have == (want // MOST) * (2 * MOST) + want % MOST).astype(jnp.bfloat16)
-    slope = dot(chosen, slope).astype(jnp.bfloat16)
-    width = rows_ref.shape[2]
+    half_expert(1 - mine, rows_ref, w_in_ref, w_out_ref, more_pre_ref, more_back_ref)
+    devices, stride, width = rows_ref.shape
+
+    def every(start, *refs):
+        parts = [
+            sum(ref[i, pl.ds(start, devices, stride=stride), :] for ref in refs)
+            for i in range(refs[0].shape[0])
+        ]
+        return jnp.concatenate(parts, axis=1)
+
+    slope = jnp.concatenate(
+        [
+            every(MOST + m, back_ref, more_back_ref) * gelu_slope(every(m, pre_ref, more_pre_ref))
+            for m in range(MOST)
+        ],
+        axis=0,
+    ).astype(jnp.bfloat16)
+    want = lax.broadcasted_iota(jnp.int32, (devices * MOST, devices * MOST), 0)
+    have = lax.broadcasted_iota(jnp.int32, (devices * MOST, devices * MOST), 1)
+    order = (have == (want % MOST) * devices + want // MOST).astype(jnp.bfloat16)
+    slope = dot(order, slope).astype(jnp.bfloat16)
     here = pl.multiple_of(mine * width, width)
     there = pl.multiple_of((1 - mine) * width, width)
     sent = dot_lanes(slope, w_in_ref[0, pl.ds(there, width), :])
@@ -237,8 +254,11 @@
         in_specs=[spaces[place] for place in places],
         out_specs=[vmem] * len(outs),
         scratch_shapes=list(scratch),
-        compiler_params=pltpu.CompilerParams(vmem_limit_bytes=40 * 1024 * 1024),
-    )(*operands)
+        compiler_params=pltpu.CompilerParams(vmem_limit_bytes=32 * 1024 * 1024),
+    )(*[
+        pltpu.with_memory_space_constraint(operand, pltpu.HBM) if place == "h" else operand
+        for operand, place in zip(operands, places)
+    ])
 
 
 def body(query_in, key_in, value_in, cotangent, w_in, w_out, gate_probs, chosen):
@@ -262,21 +282,27 @@
         return lax.ppermute(values, "frm", [(i, i ^ 1) for i in range(columns)])
 
     (turned,) = call(
-        turn_kernel, [((columns, blocks, features), bf16)], [cotangent], "v"
+        turn_kernel, [((columns, blocks, features), bf16)], [cotangent], "h",
+        [pltpu.VMEM(cotangent.shape, bf16), pltpu.SemaphoreType.DMA],
     )
     cot = lax.all_to_all(turned, "frm", split_axis=0, concat_axis=0, tiled=True)
-    probs, picked, here, weight, spread = call(
+    query, key, value, w_in_near, w_out_near, probs, picked, here, weight, spread = call(
         functools.partial(forward_kernel, blocks * devices, share),
         [
+            *[(array.shape, bf16) for array in (query_in, key_in, value_in, w_in, w_out)],
             ((rows, HEADS * rows), f32),
             ((slots, features), bf16),
             ((slots, rows), f32),
-            ((slots, 128), f32),
+            ((slots, LANES), f32),
             ((CORES, rows, devices * MOST), bf16),
         ],
-        [place, query_in, key_in, value_in, chosen, gate_probs],
-        "shhhvv",
-        [pltpu.VMEM(query_in.shape, bf16)] * 3 + [pltpu.SemaphoreType.DMA((3,))],
+        [place, chosen, gate_probs, query_in, key_in, value_in, w_in, w_out],
+        "shhhhhhh",
+        [
+            pltpu.VMEM(chosen.shape, jnp.int32),
+            pltpu.VMEM(gate_probs.shape, f32),
+            pltpu.SemaphoreType.DMA((7,)),
+        ],
     )
     (outgoing,) = call(
         functools.partial(pick_kernel, share),
@@ -286,25 +312,24 @@
     )
     held = lax.all_to_all(outgoing, everyone, split_axis=0, concat_axis=0, tiled=True)
     other = swap(held)
-    acts = ((devices * 2 * MOST, hidden), f32)
-    scratch = [pltpu.VMEM((hidden, part), bf16), pltpu.SemaphoreType.DMA]
+    acts = (hidden // LANES, devices * 2 * MOST, LANES)
     pre_act, back_act = call(
-        first_kernel, [acts, acts], [place, held, w_in, w_out], "svvh", scratch
+        first_kernel, [(acts, f32), (acts, f32)], [place, held, w_in_near, w_out_near], "svvv"
     )
     piece = (devices, MOST, part)
     kept, sent = call(
         second_kernel,
         [(piece, f32), (piece, bf16)],
-        [place, other, pre_act, back_act, w_in, w_out],
-        "svvvvh",
-        scratch,
+        [place, other, pre_act, back_act, w_in_near, w_out_near],
+        "svvvvv",
+        [pltpu.VMEM(acts, f32), pltpu.VMEM(acts, f32)],
     )
     total = (kept + swap(sent).astype(f32)).astype(bf16)
     back = lax.all_to_all(total, everyone, split_axis=0, concat_axis=0, tiled=True)
     return call(
         backward_kernel,
         [((frames, blocks, features), bf16)] * 3,
-        [spread, back, cot, probs, query_in, key_in, value_in],
+        [spread, back, cot, probs, query, key, value],
         "vvvvvvv",
     )
 

time: 53 us -> 48.2 us (0.909)
  local copies, waits for them, and re-layouts: 8.87 us -> 2.93 us
  waiting for transfers between devices: 1.69 us -> 3.5 us
  blocking collectives: 26.1 us -> 24.3 us
  Pallas kernels: 8.11 us -> 9.37 us
    unnamed x26 -> x4, local copies, waits for them, and re-layouts: 8.87 us -> 2.93 us
    all_to_all x1, blocking collectives: 15.8 us -> 14 us  [body(): lax.all_to_all(outgoing, everyone, split_axis=0, concat_axis=0, tiled=True)]
    all_to_all x1, waiting for transfers between devices: 0.47 us -> 2.28 us  [body(): cot = lax.all_to_all(turned, 'frm', split_axis=0, concat_axis=0, tiled=True)]
    pallas_call x6, Pallas kernels: 8.11 us -> 9.37 us  [call(): pl.pallas_call(kernel, out_shape=[jax.ShapeDtypeStruct(shape, dtype) for...]
  transfers between devices with their start and end apart: 3 -> 3, of which waited for: 2 -> 2; matrix products, arithmetic and copies ran while one was open for 0% -> 0% of each run, Pallas kernels for 7% -> 9%
where the time goes in v5:
time: 48.2 us; the launch traced here: 47.9 us
  blocking collectives  24.3 us (50%)
  Pallas kernels  9.37 us (19%)
  starting transfers between devices  6.92 us (14%)
  waiting for transfers between devices  3.5 us (7%)
  local copies, waits for them, and re-layouts  2.93 us (6%)
  between operations  0.69 us (1%)
    all_to_all x1, blocking collectives, body(): lax.all_to_all(outgoing, everyone, split_axis=0, concat_axis=0, tiled=True)  14 us
    all_to_all x1, blocking collectives, body(): lax.all_to_all(total, everyone, split_axis=0, concat_axis=0, tiled=True)  10.3 us
    pallas_call x6, Pallas kernels, call(): pl.pallas_call(kernel, out_shape=[jax.ShapeDtypeStruct(shape, dtype) for...  9.37 us
    all_to_all x1, starting transfers between devices, body(): cot = lax.all_to_all(turned, 'frm', split_axis=0, concat_axis=0, tiled=True)  6.34 us
    unnamed x4, local copies, waits for them, and re-layouts  2.93 us
    all_to_all x1, waiting for transfers between devices, body(): cot = lax.all_to_all(turned, 'frm', split_axis=0, concat_axis=0, tiled=True)  2.28 us
    ppermute x2, waiting for transfers between devices, swap(): return lax.ppermute(values, 'frm', [(i, i ^ 1) for i in range(columns)])  1.22 us
  transfers between devices with their start and end apart: 3, of which 2 were waited for; matrix products, arithmetic and copies ran while one was open for 0% of the time, Pallas kernels for 9%

profile of v5, /device:TPU:0, one launch (start us, length us, event | category | flops | bytes accessed | tf_op | source)
XLA Modules:
  0.0 47.9 jit_solution(2065078676134860388)
XLA Ops:
  0.6 1.6 %shard_map.104 = bf16[8,4,2048]{2,1,0:T(4,128)(2,1)} custom-call(bf16[1,32,2048]{2,1,0:T(8,128)(2,1)} %cot_hbm.1), custom_call_target="tpu_custom_call" | custom-call | tf_op jit(solution)/shard_map/pallas_call | solution.py:251
  2.2 6.3 %all-to-all-start = ((bf16[8,4,2048]{2,1,0:T(4,128)(2,1)}), bf16[8,4,2048]{2,1,0:T(4,128)(2,1)S(1)}, u32[]{:S(2)}, u32[]{:S(2)}) async-start(bf16[8,4,2048]{2,1,0:T(4,128)(2,1)} %shard_map.104), calls=%async_computation | async-start | bytes 262144 | tf_op jit(solution)/shard_map/all_to_all | solution.py:288
  8.6 0.1 pad_add_fusion.place_ref
  8.6 3.1 %shard_map.103 = (bf16[8,4,2048]{2,1,0:T(4,128)(2,1)S(1)}, bf16[8,4,2048]{2,1,0:T(4,128)(2,1)S(1)}, bf16[8,4,2048]{2,1,0:T(4,128)(2,1)S(1)}, bf16[1,2048,512]{2,...) custom-call(s32[2]{0:T(128)S(1)} %pad_add_fusion.place_ref, ...), custom_call_target="tpu_custom_call" | custom-call | tf_op jit(solution)/shard_map/pallas_call | solution.py:251
  11.7 0.0 copy-start
  11.7 1.3 %copy-done = bf16[1,512,2048]{2,1,0:T(8,128)(2,1)} copy-done((bf16[1,512,2048]{2,1,0:T(8,128)(2,1)}, bf16[1,512,2048]{2,1,0:T(8,128)(2,1)S(1)}, u32[]{:S(2)}) %copy-start) | copy-done | bytes 2097176
  13.1 2.3 %all-to-all-done.cot_ref = bf16[8,4,2048]{2,1,0:T(4,128)(2,1)S(1)} async-done(((bf16[8,4,2048]{2,1,0:T(4,128)(2,1)}), bf16[8,4,2048]{2,1,0:T(4,128)(2,1)S(1)}, u32[]{:S(2)}, u32[]{:S(2)}) %all-to-all-start) | async-done | bytes 131104 | tf_op jit(solution)/shard_map/all_to_all | solution.py:288
  15.3 0.2 shard_map.105
  15.5 14.0 %all_to_all.15.rows_ref = bf16[32,4,1024]{2,1,0:T(4,128)(2,1)S(1)} all-to-all(bf16[32,4,1024]{2,1,0:T(4,128)(2,1)S(1)} %shard_map.105), channel_id=1, replica_groups=mesh['grp'=4,'frm'=8] {'grp','frm'}, dimensions={0} | all-to-all | bytes 524288 | tf_op jit(solution)/shard_map/all_to_all | solution.py:313
  29.5 0.4 collective-permute-start
  29.9 0.0 copy-start.1
  29.9 1.6 %copy-done.1 = bf16[1,512,2048]{2,1,0:T(8,128)(2,1)S(1)} copy-done((bf16[1,512,2048]{2,1,0:T(8,128)(2,1)S(1)}, bf16[1,512,2048]{2,1,0:T(8,128)(2,1)}, u32[]{:S(2)}) %copy-start.1) | copy-done | bytes 2097176
  31.5 1.2 %shard_map.106 = (f32[4,128,128]{2,1,0:T(8,128)S(1)}, f32[4,128,128]{2,1,0:T(8,128)S(1)}) custom-call(s32[2]{0:T(128)S(1)} %pad_add_fusion.place_ref, bf16[32,4,1024]{2,1,0:T(4,128)(2,1)S(1)} %all_to_all.15.rows_ref, bf16[1,2048,512]{2,1,0:T(8,128)(2,1)S(1)} %get-tuple-element.21.w_in_ref, bf16[1,512,2048]{2,1,0:T(8,128)(2,1)S(1)} %copy-done.1), custom_call_target="tpu_custom_call" | custom-call | tf_op jit(solution)/shard_map/pallas_call | solution.py:251
  32.6 0.0 collective-permute-done.rows_ref
  32.7 2.0 %shard_map.107 = (f32[32,2,1024]{2,1,0:T(2,128)S(1)}, bf16[32,2,1024]{2,1,0:T(2,128)(2,1)S(1)}) custom-call(s32[2]{0:T(128)S(1)} %pad_add_fusion.place_ref, bf16[32,4,1024]{2,1,0:T(4,128)(2,1)S(1)} %collective-permute-done.rows_ref, f32[4,128,128]{2,1,0:T(8,128)S(1)} %get-tuple-element.23.pre_ref, f32[4,128,128]{2,1,0:T(8,128)S(1)} %get-tuple-element.24.back_ref, ...), custom_call_target="tpu_custom_call" | custom-call | tf_op jit(solution)/shard_map/pallas_call | solution.py:251
  34.7 0.2 collective-permute-start.1
  34.9 1.2 %collective-permute-done.1 = bf16[32,2,1024]{2,1,0:T(2,128)(2,1)S(1)} collective-permute-done((bf16[32,2,1024]{2,1,0:T(2,128)(2,1)S(1)}, bf16[32,2,1024]{2,1,0:T(2,128)(2,1)S(1)}, u32[]{:S(2)}, u32[]{:S(2)}) %collective-permute-start.1) | collective-permute-done | bytes 131104 | tf_op jit(solution)/shard_map/ppermute | solution.py:282
  36.1 0.1 add_convert_fusion
  36.2 10.3 %all_to_all.16.back_ref = bf16[32,2,1024]{2,1,0:T(2,128)(2,1)S(1)} all-to-all(bf16[32,2,1024]{2,1,0:T(2,128)(2,1)S(1)} %add_convert_fusion), channel_id=1, replica_groups=mesh['grp'=4,'frm'=8] {'grp','frm'}, dimensions={0} | all-to-all | bytes 262144 | tf_op jit(solution)/shard_map/all_to_all | solution.py:328
  46.5 1.4 %shard_map.108 = (bf16[8,4,2048]{2,1,0:T(4,128)(2,1)}, bf16[8,4,2048]{2,1,0:T(4,128)(2,1)}, bf16[8,4,2048]{2,1,0:T(4,128)(2,1)}) custom-call(bf16[2,32,64]{2,1,0:T(8,128)(2,1)S(1)} %get-tuple-element.17.spread_ref, bf16[32,2,1024]{2,1,0:T(2,128)(2,1)S(1)} %all_to_all.16.back_ref, bf16[8,4,2048]{2,1,0:T(4,128)(2,1)S(1)} %all-to-all-done.cot_ref, ...), custom_call_target="tpu_custom_call" | custom-call | tf_op jit(solution)/shard_map/pallas_call | solution.py:251
Async XLA Ops:
  2.2 13.1 %all-to-all-start = ((bf16[8,4,2048]{2,1,0:T(4,128)(2,1)}), bf16[8,4,2048]{2,1,0:T(4,128)(2,1)S(1)}, u32[]{:S(2)}, u32[]{:S(2)}) async-start(bf16[8,4,2048]{2,1,0:T(4,128)(2,1)} %shard_map.104), calls=%async_computation | async-start | bytes 262144 | tf_op jit(solution)/shard_map/all_to_all | solution.py:288
  11.7 1.3 %copy-start = (bf16[1,512,2048]{2,1,0:T(8,128)(2,1)}, bf16[1,512,2048]{2,1,0:T(8,128)(2,1)S(1)}, u32[]{:S(2)}) copy-start(bf16[1,512,2048]{2,1,0:T(8,128)(2,1)S(1)} %get-tuple-element.22.w_out_ref) | copy-start | bytes 6291460
  29.5 3.2 %collective-permute-start = (bf16[32,4,1024]{2,1,0:T(4,128)(2,1)S(1)}, bf16[32,4,1024]{2,1,0:T(4,128)(2,1)S(1)}, u32[]{:S(2)}, u32[]{:S(2)}) collective-permute-start(bf16[32,4,1024]{2,1,0:T(4,128)(2,1)S(1)} %all_to_all.15.rows_ref), channel_id=1, source_target_pairs={{0,1},{1,0},{2,3},{3,2},{4,5},{5,4},{6,7},{7,6},{8,9},{9,8},{10,11... | collective-permute-start | bytes 786440 | tf_op jit(solution)/shard_map/ppermute | solution.py:282
  29.9 1.6 %copy-start.1 = (bf16[1,512,2048]{2,1,0:T(8,128)(2,1)S(1)}, bf16[1,512,2048]{2,1,0:T(8,128)(2,1)}, u32[]{:S(2)}) copy-start(bf16[1,512,2048]{2,1,0:T(8,128)(2,1)} %copy-done) | copy-start | bytes 6291460
  34.7 1.4 %collective-permute-start.1 = (bf16[32,2,1024]{2,1,0:T(2,128)(2,1)S(1)}, bf16[32,2,1024]{2,1,0:T(2,128)(2,1)S(1)}, u32[]{:S(2)}, u32[]{:S(2)}) collective-permute-start(bf16[32,2,1024]{2,1,0:T(2,128)(2,1)S(1)} %get-tuple-element.26), channel_id=1, source_target_pairs={{0,1},{1,0},{2,3},{3,2},{4,5},{5,4},{6,7},{7,6},{8,9},{9,8},{10,11... | collective-permute-start | bytes 393224 | tf_op jit(solution)/shard_map/ppermute | solution.py:282

commit v6 on v5

--- a/solution.py
+++ b/solution.py
@@ -12,6 +12,7 @@
 CORES = 2
 SUBLANES = 8
 LANES = 128
+TILE = 16
 
 root_half = 0.7071067811865476
 inv_root_tau = 0.3989422804014327
@@ -51,22 +52,42 @@
     return [values[:, h * width : (h + 1) * width] for h in range(HEADS)]
 
 
-def turn_kernel(cot_hbm, out_ref, cot_ref, sem):
-    copy = pltpu.make_async_copy(cot_hbm, cot_ref, sem)
-    copy.start()
-    copy.wait()
-    out_ref[...] = cot_ref[...].reshape(out_ref.shape)
+def turn_kernel(cot_hbm, out_hbm, cot_ref, turned_ref, sems):
+    _, rows, _ = cot_ref.shape
+    columns, blocks, features = turned_ref.shape
+    pieces = rows // TILE
+    span = columns // pieces
+    arrivals = [
+        pltpu.make_async_copy(
+            cot_hbm.at[:, pl.ds(i * TILE, TILE)], cot_ref.at[:, pl.ds(i * TILE, TILE)], sems.at[0, i]
+        )
+        for i in range(pieces)
+    ]
+    for copy in arrivals:
+        copy.start()
+    leaving = []
+    for i, copy in enumerate(arrivals):
+        copy.wait()
+        part = slice(i * span, (i + 1) * span)
+        turned_ref[part] = cot_ref[0, i * TILE : (i + 1) * TILE, :].reshape(span, blocks, features)
+        copy = pltpu.make_async_copy(
+            turned_ref.at[pl.ds(i * span, span)], out_hbm.at[pl.ds(i * span, span)], sems.at[1, i]
+        )
+        copy.start()
+        leaving.append(copy)
+    for copy in leaving:
+        copy.wait()
 
 
 def forward_kernel(
     patches_all, share, place_ref,
-    chosen_hbm, gate_hbm, query_hbm, key_hbm, value_hbm, w_in_hbm, w_out_hbm,
-    query_ref, key_ref, value_ref, w_in_ref, w_out_ref,
+    chosen_hbm, gate_hbm, query_hbm, key_hbm, value_hbm, w_in_hbm,
+    query_ref, key_ref, value_ref, w_in_ref,
     probs_ref, picked_ref, here_ref, weight_ref, spread_ref,
     chosen_ref, gate_ref, sems,
 ):
-    sources = [chosen_hbm, gate_hbm, query_hbm, key_hbm, value_hbm, w_in_hbm, w_out_hbm]
-    targets = [chosen_ref, gate_ref, query_ref, key_ref, value_ref, w_in_ref, w_out_ref]
+    sources = [chosen_hbm, gate_hbm, query_hbm, key_hbm, value_hbm, w_in_hbm]
+    targets = [chosen_ref, gate_ref, query_ref, key_ref, value_ref, w_in_ref]
     copies = [
         pltpu.make_async_copy(source, target, sems.at[i])
         for i, (source, target) in enumerate(zip(sources, targets))
@@ -156,58 +177,74 @@
             out_ref[e * share + i] = both[:, c * part : (c + 1) * part]
 
 
-def half_expert(part, rows_ref, w_in_ref, w_out_ref, pre_ref, back_ref):
+def put_tiles(ref, values):
+    for i in range(ref.shape[0]):
+        ref[i] = values[:, i * LANES : (i + 1) * LANES]
+
+
+def take_tiles(ref):
+    return jnp.concatenate([ref[i] for i in range(ref.shape[0])], axis=1)
+
+
+def part_of(part, width):
+    return pl.ds(pl.multiple_of(part * width, width), width)
+
+
+def first_kernel(
+    place_ref, rows_ref, w_in_ref, w_out_hbm, pre_ref, back_ref, far_ref, near_ref, sems
+):
     width = rows_ref.shape[2]
-    start = pl.multiple_of(part * width, width)
+    mine = place_ref[1]
+    copies = [
+        pltpu.make_async_copy(
+            w_out_hbm.at[0, :, part_of(part, width)], target, sems.at[i]
+        )
+        for i, (part, target) in enumerate([(mine, near_ref), (1 - mine, far_ref)])
+    ]
+    for copy in copies:
+        copy.start()
     rows = rows_ref[...].reshape(-1, width)
-    pre_act = dot(rows, w_in_ref[0, pl.ds(start, width), :])
-    back_act = dot_lanes(rows, w_out_ref[0, :, pl.ds(start, width)])
+    put_tiles(pre_ref, dot(rows, w_in_ref[0, part_of(mine, width), :]))
+    copies[0].wait()
+    put_tiles(back_ref, dot_lanes(rows, near_ref[...]))
+    copies[1].wait()
+
+
+def second_kernel(
+    place_ref, rows_ref, pre_ref, back_ref, w_in_ref, far_ref,
+    slope_ref, sent_ref, more_pre_ref, more_back_ref, mixed_ref,
+):
+    devices, stride, width = rows_ref.shape
+    other = part_of(1 - place_ref[1], width)
+    rows = rows_ref[...].reshape(-1, width)
+    put_tiles(more_pre_ref, dot(rows, w_in_ref[0, other, :]))
+    put_tiles(more_back_ref, dot_lanes(rows, far_ref[...]))
     for i in range(pre_ref.shape[0]):
-        pre_ref[i] = pre_act[:, i * LANES : (i + 1) * LANES]
-        back_ref[i] = back_act[:, i * LANES : (i + 1) * LANES]
-
-
-def first_kernel(place_ref, rows_ref, w_in_ref, w_out_ref, pre_ref, back_ref):
-    half_expert(place_ref[1], rows_ref, w_in_ref, w_out_ref, pre_ref, back_ref)
-
-
-def second_kernel(
-    place_ref, rows_ref, pre_ref, back_ref, w_in_ref, w_out_ref,
-    kept_ref, sent_ref, more_pre_ref, more_back_ref,
-):
-    mine = place_ref[1]
-    half_expert(1 - mine, rows_ref, w_in_ref, w_out_ref, more_pre_ref, more_back_ref)
-    devices, stride, width = rows_ref.shape
-
-    def every(start, *refs):
-        parts = [
-            sum(ref[i, pl.ds(start, devices, stride=stride), :] for ref in refs)
-            for i in range(refs[0].shape[0])
-        ]
-        return jnp.concatenate(parts, axis=1)
-
-    slope = jnp.concatenate(
-        [
-            every(MOST + m, back_ref, more_back_ref) * gelu_slope(every(m, pre_ref, more_pre_ref))
-            for m in range(MOST)
-        ],
-        axis=0,
-    ).astype(jnp.bfloat16)
-    want = lax.broadcasted_iota(jnp.int32, (devices * MOST, devices * MOST), 0)
-    have = lax.broadcasted_iota(jnp.int32, (devices * MOST, devices * MOST), 1)
-    order = (have == (want % MOST) * devices + want // MOST).astype(jnp.bfloat16)
-    slope = dot(order, slope).astype(jnp.bfloat16)
-    here = pl.multiple_of(mine * width, width)
-    there = pl.multiple_of((1 - mine) * width, width)
-    sent = dot_lanes(slope, w_in_ref[0, pl.ds(there, width), :])
-    sent_ref[...] = sent.astype(jnp.bfloat16).reshape(sent_ref.shape)
-    kept = dot_lanes(slope, w_in_ref[0, pl.ds(here, width), :])
-    kept_ref[...] = kept.reshape(kept_ref.shape)
+        for m in range(MOST):
+            at_in = pl.ds(m, devices, stride=stride)
+            at_cot = pl.ds(MOST + m, devices, stride=stride)
+            pre_act = pre_ref[i, at_in, :] + more_pre_ref[i, at_in, :]
+            back_act = back_ref[i, at_cot, :] + more_back_ref[i, at_cot, :]
+            mixed_ref[i, pl.ds(m, devices, stride=MOST), :] = back_act * gelu_slope(pre_act)
+    slope = take_tiles(mixed_ref).astype(jnp.bfloat16)
+    slope_ref[...] = slope
+    sent_ref[...] = dot_lanes(slope, w_in_ref[0, other, :]).astype(jnp.bfloat16)
+
+
+def third_kernel(place_ref, slope_ref, w_in_ref, kept_ref):
+    width = kept_ref.shape[1]
+    kept_ref[...] = dot_lanes(slope_ref[...], w_in_ref[0, part_of(place_ref[1], width), :])
+
+
+def sum_kernel(kept_ref, came_ref, out_ref):
+    total = kept_ref[...] + came_ref[...].astype(jnp.float32)
+    out_ref[...] = total.astype(jnp.bfloat16).reshape(out_ref.shape)
 
 
 def backward_kernel(
     spread_ref, back_ref, cot_ref, probs_ref, query_ref, key_ref, value_ref,
-    grad_query_ref, grad_key_ref, grad_value_ref,
+    grad_query_hbm, grad_key_hbm, grad_value_hbm,
+    grad_query_ref, grad_key_ref, grad_value_ref, sems,
 ):
     frames, blocks, features = query_ref.shape
     rows = frames * blocks
@@ -220,6 +257,21 @@
     cot = cot_ref[...].reshape(rows, features)
     stream = (cot.astype(jnp.float32) + added).astype(jnp.bfloat16)
     probs = probs_ref[...]
+    weights = probs.astype(jnp.bfloat16)
+    copies = []
+
+    def put(ref, hbm, parts):
+        joined = jnp.concatenate(parts, axis=1).astype(jnp.bfloat16)
+        ref[...] = joined.reshape(frames, blocks, features)
+        copy = pltpu.make_async_copy(ref, hbm, sems.at[len(copies)])
+        copy.start()
+        copies.append(copy)
+
+    put(
+        grad_value_ref,
+        grad_value_hbm,
+        [dot(w, g) for w, g in zip(heads_of(weights), heads_of(stream))],
+    )
     grad_prob = jnp.concatenate(
         [dot_lanes(v, g) for v, g in zip(heads_of(value), heads_of(stream))], axis=1
     )
@@ -227,32 +279,30 @@
     grad_score = probs * (grad_prob - centre)
     turned = grad_score.T.astype(jnp.bfloat16)
     grad_score = grad_score.astype(jnp.bfloat16)
-    weights = probs.astype(jnp.bfloat16)
-
-    def joined(parts):
-        return jnp.concatenate(parts, axis=1).astype(jnp.bfloat16).reshape(frames, blocks, features)
-
-    grad_value_ref[...] = joined(
-        [dot(w, g) for w, g in zip(heads_of(weights), heads_of(stream))]
-    )
-    grad_key_ref[...] = joined(
-        [dot(s, q) * scaling for s, q in zip(heads_of(grad_score), heads_of(query))]
-    )
-    grad_query_ref[...] = joined(
-        [dot(turned[h * rows : (h + 1) * rows], k) * scaling for h, k in enumerate(heads_of(key))]
-    )
-
-
-def call(kernel, outs, operands, places, scratch=()):
+    put(
+        grad_key_ref,
+        grad_key_hbm,
+        [dot(s, q) * scaling for s, q in zip(heads_of(grad_score), heads_of(query))],
+    )
+    put(
+        grad_query_ref,
+        grad_query_hbm,
+        [dot(turned[h * rows : (h + 1) * rows], k) * scaling for h, k in enumerate(heads_of(key))],
+    )
+    for copy in copies:
+        copy.wait()
+
+
+def call(kernel, outs, operands, places, scratch=(), results="v"):
     smem, vmem, hbm = (
-        pl.BlockSpec(memory_space=space) for space in (pltpu.SMEM, pltpu.VMEM, pltpu.HBM)
+        pl.BlockSpec(memory_space=space) for space in (pltpu.SMEM, pltpu.VMEM, pl.ANY)
     )
     spaces = {"s": smem, "v": vmem, "h": hbm}
     return pl.pallas_call(
         kernel,
         out_shape=[jax.ShapeDtypeStruct(shape, dtype) for shape, dtype in outs],
         in_specs=[spaces[place] for place in places],
-        out_specs=[vmem] * len(outs),
+        out_specs=[spaces[results]] * len(outs),
         scratch_shapes=list(scratch),
         compiler_params=pltpu.CompilerParams(vmem_limit_bytes=32 * 1024 * 1024),
     )(*[
@@ -283,25 +333,30 @@
 
     (turned,) = call(
         turn_kernel, [((columns, blocks, features), bf16)], [cotangent], "h",
-        [pltpu.VMEM(cotangent.shape, bf16), pltpu.SemaphoreType.DMA],
+        [
+            pltpu.VMEM(cotangent.shape, bf16),
+            pltpu.VMEM((columns, blocks, features), bf16),
+            pltpu.SemaphoreType.DMA((2, cotangent.shape[1] // TILE)),
+        ],
+        "h",
     )
     cot = lax.all_to_all(turned, "frm", split_axis=0, concat_axis=0, tiled=True)
-    query, key, value, w_in_near, w_out_near, probs, picked, here, weight, spread = call(
+    query, key, value, w_in_near, probs, picked, here, weight, spread = call(
         functools.partial(forward_kernel, blocks * devices, share),
         [
-            *[(array.shape, bf16) for array in (query_in, key_in, value_in, w_in, w_out)],
+            *[(array.shape, bf16) for array in (query_in, key_in, value_in, w_in)],
             ((rows, HEADS * rows), f32),
             ((slots, features), bf16),
             ((slots, rows), f32),
             ((slots, LANES), f32),
             ((CORES, rows, devices * MOST), bf16),
         ],
-        [place, chosen, gate_probs, query_in, key_in, value_in, w_in, w_out],
-        "shhhhhhh",
+        [place, chosen, gate_probs, query_in, key_in, value_in, w_in],
+        "shhhhhh",
         [
             pltpu.VMEM(chosen.shape, jnp.int32),
             pltpu.VMEM(gate_probs.shape, f32),
-            pltpu.SemaphoreType.DMA((7,)),
+            pltpu.SemaphoreType.DMA((6,)),
         ],
     )
     (outgoing,) = call(
@@ -313,24 +368,38 @@
     held = lax.all_to_all(outgoing, everyone, split_axis=0, concat_axis=0, tiled=True)
     other = swap(held)
     acts = (hidden // LANES, devices * 2 * MOST, LANES)
-    pre_act, back_act = call(
-        first_kernel, [(acts, f32), (acts, f32)], [place, held, w_in_near, w_out_near], "svvv"
-    )
-    piece = (devices, MOST, part)
-    kept, sent = call(
+    half = (hidden, part)
+    pre_act, back_act, w_out_far = call(
+        first_kernel,
+        [(acts, f32), (acts, f32), (half, bf16)],
+        [place, held, w_in_near, w_out],
+        "svvh",
+        [pltpu.VMEM(half, bf16), pltpu.SemaphoreType.DMA((2,))],
+    )
+    slope, sent = call(
         second_kernel,
-        [(piece, f32), (piece, bf16)],
-        [place, other, pre_act, back_act, w_in_near, w_out_near],
+        [((devices * MOST, hidden), bf16), ((devices * MOST, part), bf16)],
+        [place, other, pre_act, back_act, w_in_near, w_out_far],
         "svvvvv",
-        [pltpu.VMEM(acts, f32), pltpu.VMEM(acts, f32)],
-    )
-    total = (kept + swap(sent).astype(f32)).astype(bf16)
+        [
+            pltpu.VMEM(acts, f32),
+            pltpu.VMEM(acts, f32),
+            pltpu.VMEM((hidden // LANES, devices * MOST, LANES), f32),
+        ],
+    )
+    came = swap(sent)
+    (kept,) = call(
+        third_kernel, [((devices * MOST, part), f32)], [place, slope, w_in_near], "svv"
+    )
+    (total,) = call(sum_kernel, [((devices, MOST, part), bf16)], [kept, came], "vv")
     back = lax.all_to_all(total, everyone, split_axis=0, concat_axis=0, tiled=True)
     return call(
         backward_kernel,
         [((frames, blocks, features), bf16)] * 3,
         [spread, back, cot, probs, query, key, value],
         "vvvvvvv",
+        [pltpu.VMEM((frames, blocks, features), bf16)] * 3 + [pltpu.SemaphoreType.DMA((3,))],
+        "h",
     )
 
 

time: 48.2 us -> 47.1 us (0.977)
  local copies, waits for them, and re-layouts: 2.93 us -> 0 us
  Pallas kernels: 9.37 us -> 10.4 us
  waiting for transfers between devices: 3.5 us -> 4.52 us
    unnamed x4 -> x0, local copies, waits for them, and re-layouts: 2.93 us -> none
    all_to_all x1, waiting for transfers between devices: 2.28 us -> 4.27 us  [body(): cot = lax.all_to_all(turned, 'frm', split_axis=0, concat_axis=0, tiled=True)]
    pallas_call x6 -> x8, Pallas kernels: 9.37 us -> 10.4 us  [call(): pl.pallas_call(kernel, out_shape=[jax.ShapeDtypeStruct(shape, dtype) for...]
    ppermute x2, waiting for transfers between devices: 1.22 us -> 0.25 us  [swap(): return lax.ppermute(values, 'frm', [(i, i ^ 1) for i in range(columns)])]
  transfers between devices with their start and end apart: 3 -> 3, of which waited for: 2 -> 2; matrix products, arithmetic and copies ran while one was open for 0% -> 0% of each run, Pallas kernels for 9% -> 12%
where the time goes in v6:
time: 47.1 us; the launch traced here: 46.7 us
  blocking collectives  24.1 us (51%)
  Pallas kernels  10.4 us (22%)
  starting transfers between devices  6.91 us (15%)
  waiting for transfers between devices  4.52 us (10%)
  between operations  0.68 us (1%)
    all_to_all x1, blocking collectives, body(): lax.all_to_all(outgoing, everyone, split_axis=0, concat_axis=0, tiled=True)  13.9 us
    pallas_call x8, Pallas kernels, call(): pl.pallas_call(kernel, out_shape=[jax.ShapeDtypeStruct(shape, dtype) for...  10.4 us
    all_to_all x1, blocking collectives, body(): lax.all_to_all(total, everyone, split_axis=0, concat_axis=0, tiled=True)  10.3 us
    all_to_all x1, starting transfers between devices, body(): cot = lax.all_to_all(turned, 'frm', split_axis=0, concat_axis=0, tiled=True)  6.34 us
    all_to_all x1, waiting for transfers between devices, body(): cot = lax.all_to_all(turned, 'frm', split_axis=0, concat_axis=0, tiled=True)  4.27 us
  transfers between devices with their start and end apart: 3, of which 2 were waited for; matrix products, arithmetic and copies ran while one was open for 0% of the time, Pallas kernels for 12%

profile of v6, /device:TPU:0, one launch (start us, length us, event | category | flops | bytes accessed | tf_op | source)
XLA Modules:
  0.0 46.7 jit_solution(623535008713660420)
XLA Ops:
  0.6 1.5 %shard_map.104 = bf16[8,4,2048]{2,1,0:T(4,128)(2,1)} custom-call(bf16[1,32,2048]{2,1,0:T(8,128)(2,1)} %cot_hbm.1), custom_call_target="tpu_custom_call" | custom-call | tf_op jit(solution)/shard_map/pallas_call | solution.py:301
  2.2 6.3 %all-to-all-start = ((bf16[8,4,2048]{2,1,0:T(4,128)(2,1)}), bf16[8,4,2048]{2,1,0:T(4,128)(2,1)S(1)}, u32[]{:S(2)}, u32[]{:S(2)}) async-start(bf16[8,4,2048]{2,1,0:T(4,128)(2,1)} %shard_map.104), calls=%async_computation | async-start | bytes 262144 | tf_op jit(solution)/shard_map/all_to_all | solution.py:343
  8.5 0.1 pad_add_fusion.place_ref
  8.6 2.4 %shard_map.103 = (bf16[8,4,2048]{2,1,0:T(4,128)(2,1)S(1)}, bf16[8,4,2048]{2,1,0:T(4,128)(2,1)S(1)}, bf16[8,4,2048]{2,1,0:T(4,128)(2,1)S(1)}, bf16[1,2048,512]{2,...) custom-call(s32[2]{0:T(128)S(1)} %pad_add_fusion.place_ref, ...), custom_call_target="tpu_custom_call" | custom-call | tf_op jit(solution)/shard_map/pallas_call | solution.py:301
  11.0 4.3 %all-to-all-done.cot_ref = bf16[8,4,2048]{2,1,0:T(4,128)(2,1)S(1)} async-done(((bf16[8,4,2048]{2,1,0:T(4,128)(2,1)}), bf16[8,4,2048]{2,1,0:T(4,128)(2,1)S(1)}, u32[]{:S(2)}, u32[]{:S(2)}) %all-to-all-start) | async-done | bytes 131104 | tf_op jit(solution)/shard_map/all_to_all | solution.py:343
  15.3 0.2 shard_map.105
  15.5 13.9 %all_to_all.15.rows_ref = bf16[32,4,1024]{2,1,0:T(4,128)(2,1)S(1)} all-to-all(bf16[32,4,1024]{2,1,0:T(4,128)(2,1)S(1)} %shard_map.105), channel_id=1, replica_groups=mesh['grp'=4,'frm'=8] {'grp','frm'}, dimensions={0} | all-to-all | bytes 524288 | tf_op jit(solution)/shard_map/all_to_all | solution.py:368
  29.3 0.4 collective-permute-start
  29.7 2.3 %shard_map.106 = (f32[4,128,128]{2,1,0:T(8,128)S(1)}, f32[4,128,128]{2,1,0:T(8,128)S(1)}, bf16[512,1024]{1,0:T(8,128)(2,1)S(1)}) custom-call(s32[2]{0:T(128)S(1)} %pad_add_fusion.place_ref, bf16[32,4,1024]{2,1,0:T(4,128)(2,1)S(1)} %all_to_all.15.rows_ref, bf16[1,2048,512]{2,1,0:T(8,128)(2,1)S(1)} %get-tuple-element.21.w_in_ref, bf16[1,512,2048]{2,1,0:T(8,128)(2,1)} %w_out_hbm.1), custom_call_target="tpu_custom_call" | custom-call | tf_op jit(solution)/shard_map/pallas_call | solution.py:301
  32.0 0.0 collective-permute-done.rows_ref
  32.0 1.6 %shard_map.107 = (bf16[64,512]{1,0:T(8,128)(2,1)S(1)}, bf16[64,1024]{1,0:T(8,128)(2,1)S(1)}) custom-call(s32[2]{0:T(128)S(1)} %pad_add_fusion.place_ref, bf16[32,4,1024]{2,1,0:T(4,128)(2,1)S(1)} %collective-permute-done.rows_ref, f32[4,128,128]{2,1,0:T(8,128)S(1)} %get-tuple-element.22.pre_ref, f32[4,128,128]{2,1,0:T(8,128)S(1)} %get-tuple-element.23.back_ref, ...), custom_call_target="tpu_custom_call" | custom-call | tf_op jit(solution)/shard_map/pallas_call | solution.py:301
  33.6 0.2 collective-permute-start.1
  33.8 1.0 %shard_map.108.kept_ref = f32[64,1024]{1,0:T(8,128)S(1)} custom-call(s32[2]{0:T(128)S(1)} %pad_add_fusion.place_ref, bf16[64,512]{1,0:T(8,128)(2,1)S(1)} %get-tuple-element.25.slope_ref, bf16[1,2048,512]{2,1,0:T(8,128)(2,1)S(1)} %get-tuple-element.21.w_in_ref), custom_call_target="tpu_custom_call" | custom-call | tf_op jit(solution)/shard_map/pallas_call | solution.py:301
  34.7 0.2 collective-permute-done.1.came_ref
  35.0 10.3 %all_to_all.16.back_ref = bf16[32,2,1024]{2,1,0:T(2,128)(2,1)S(1)} all-to-all(bf16[32,2,1024]{2,1,0:T(2,128)(2,1)S(1)} %shard_map.109), channel_id=1, replica_groups=mesh['grp'=4,'frm'=8] {'grp','frm'}, dimensions={0} | all-to-all | bytes 262144 | tf_op jit(solution)/shard_map/all_to_all | solution.py:395
  45.3 1.4 %shard_map.110 = (bf16[8,4,2048]{2,1,0:T(4,128)(2,1)}, bf16[8,4,2048]{2,1,0:T(4,128)(2,1)}, bf16[8,4,2048]{2,1,0:T(4,128)(2,1)}) custom-call(bf16[2,32,64]{2,1,0:T(8,128)(2,1)S(1)} %get-tuple-element.17.spread_ref, bf16[32,2,1024]{2,1,0:T(2,128)(2,1)S(1)} %all_to_all.16.back_ref, bf16[8,4,2048]{2,1,0:T(4,128)(2,1)S(1)} %all-to-all-done.cot_ref, ...), custom_call_target="tpu_custom_call" | custom-call | tf_op jit(solution)/shard_map/pallas_call | solution.py:301
  (1 shorter events, 0.0 us)
Async XLA Ops:
  2.2 13.1 %all-to-all-start = ((bf16[8,4,2048]{2,1,0:T(4,128)(2,1)}), bf16[8,4,2048]{2,1,0:T(4,128)(2,1)S(1)}, u32[]{:S(2)}, u32[]{:S(2)}) async-start(bf16[8,4,2048]{2,1,0:T(4,128)(2,1)} %shard_map.104), calls=%async_computation | async-start | bytes 262144 | tf_op jit(solution)/shard_map/all_to_all | solution.py:343
  29.3 2.7 %collective-permute-start = (bf16[32,4,1024]{2,1,0:T(4,128)(2,1)S(1)}, bf16[32,4,1024]{2,1,0:T(4,128)(2,1)S(1)}, u32[]{:S(2)}, u32[]{:S(2)}) collective-permute-start(bf16[32,4,1024]{2,1,0:T(4,128)(2,1)S(1)} %all_to_all.15.rows_ref), channel_id=1, source_target_pairs={{0,1},{1,0},{2,3},{3,2},{4,5},{5,4},{6,7},{7,6},{8,9},{9,8},{10,11... | collective-permute-start | bytes 786440 | tf_op jit(solution)/shard_map/ppermute | solution.py:332
  33.6 1.4 %collective-permute-start.1 = (bf16[64,1024]{1,0:T(8,128)(2,1)S(1)}, bf16[64,1024]{1,0:T(8,128)(2,1)S(1)}, u32[]{:S(2)}, u32[]{:S(2)}) collective-permute-start(bf16[64,1024]{1,0:T(8,128)(2,1)S(1)} %get-tuple-element.26), channel_id=1, source_target_pairs={{0,1},{1,0},{2,3},{3,2},{4,5},{5,4},{6,7},{7,6},{8,9},{9,8},{10,11... | collective-permute-start | bytes 393224 | tf_op jit(solution)/shard_map/ppermute | solution.py:332

commit v7 on v6

--- a/solution.py
+++ b/solution.py
@@ -169,71 +169,56 @@
     rows = dot(here_ref[...].astype(jnp.bfloat16), cot_ref[...].reshape(frames * blocks, features))
     rows = (rows * weight_ref[:, :1]).astype(jnp.bfloat16)
     part = features // CORES
+    picked = picked_ref[...]
+    both = [
+        jnp.concatenate(
+            [half[:, c * part : (c + 1) * part] for half in (picked, rows)], axis=1
+        )
+        for c in range(CORES)
+    ]
     for e in range(out_ref.shape[0] // share):
-        slots = slice(e * MOST, (e + 1) * MOST)
-        both = jnp.concatenate([picked_ref[slots], rows[slots]], axis=0)
         for i in range(share):
-            c = i % CORES
-            out_ref[e * share + i] = both[:, c * part : (c + 1) * part]
-
-
-def put_tiles(ref, values):
-    for i in range(ref.shape[0]):
-        ref[i] = values[:, i * LANES : (i + 1) * LANES]
-
-
-def take_tiles(ref):
-    return jnp.concatenate([ref[i] for i in range(ref.shape[0])], axis=1)
-
-
-def part_of(part, width):
-    return pl.ds(pl.multiple_of(part * width, width), width)
-
-
-def first_kernel(
-    place_ref, rows_ref, w_in_ref, w_out_hbm, pre_ref, back_ref, far_ref, near_ref, sems
+            out_ref[e * share + i] = both[i % CORES][e * MOST : (e + 1) * MOST]
+
+
+def in_order(mine, near, far):
+    return jnp.where(mine == 0, near, far), jnp.where(mine == 0, far, near)
+
+
+def first_kernel(place_ref, rows_ref, w_in_ref, w_out_hbm, pre_ref, w_out_ref, sem):
+    copy = pltpu.make_async_copy(w_out_hbm.at[0], w_out_ref, sem)
+    copy.start()
+    rows = rows_ref[...].reshape(pre_ref.shape[0], -1)
+    width = rows.shape[1] // 2
+    for c in range(CORES):
+
+        @pl.when(place_ref[1] == c)
+        def _():
+            pre_ref[...] = dot(rows[:, :width], w_in_ref[0, c * width : (c + 1) * width, :])
+
+    copy.wait()
+
+
+def second_kernel(
+    place_ref, near_ref, far_ref, pre_ref, w_in_ref, w_out_ref, kept_ref, sent_ref, sum_ref
 ):
-    width = rows_ref.shape[2]
+    near = near_ref[...].reshape(pre_ref.shape[0], -1)
+    far = far_ref[...].reshape(pre_ref.shape[0], -1)
+    width = near.shape[1] // 2
     mine = place_ref[1]
-    copies = [
-        pltpu.make_async_copy(
-            w_out_hbm.at[0, :, part_of(part, width)], target, sems.at[i]
-        )
-        for i, (part, target) in enumerate([(mine, near_ref), (1 - mine, far_ref)])
-    ]
-    for copy in copies:
-        copy.start()
-    rows = rows_ref[...].reshape(-1, width)
-    put_tiles(pre_ref, dot(rows, w_in_ref[0, part_of(mine, width), :]))
-    copies[0].wait()
-    put_tiles(back_ref, dot_lanes(rows, near_ref[...]))
-    copies[1].wait()
-
-
-def second_kernel(
-    place_ref, rows_ref, pre_ref, back_ref, w_in_ref, far_ref,
-    slope_ref, sent_ref, more_pre_ref, more_back_ref, mixed_ref,
-):
-    devices, stride, width = rows_ref.shape
-    other = part_of(1 - place_ref[1], width)
-    rows = rows_ref[...].reshape(-1, width)
-    put_tiles(more_pre_ref, dot(rows, w_in_ref[0, other, :]))
-    put_tiles(more_back_ref, dot_lanes(rows, far_ref[...]))
-    for i in range(pre_ref.shape[0]):
-        for m in range(MOST):
-            at_in = pl.ds(m, devices, stride=stride)
-            at_cot = pl.ds(MOST + m, devices, stride=stride)
-            pre_act = pre_ref[i, at_in, :] + more_pre_ref[i, at_in, :]
-            back_act = back_ref[i, at_cot, :] + more_back_ref[i, at_cot, :]
-            mixed_ref[i, pl.ds(m, devices, stride=MOST), :] = back_act * gelu_slope(pre_act)
-    slope = take_tiles(mixed_ref).astype(jnp.bfloat16)
-    slope_ref[...] = slope
-    sent_ref[...] = dot_lanes(slope, w_in_ref[0, other, :]).astype(jnp.bfloat16)
-
-
-def third_kernel(place_ref, slope_ref, w_in_ref, kept_ref):
-    width = kept_ref.shape[1]
-    kept_ref[...] = dot_lanes(slope_ref[...], w_in_ref[0, part_of(place_ref[1], width), :])
+    for c in range(CORES):
+
+        @pl.when(mine == 1 - c)
+        def _():
+            sum_ref[...] = dot(far[:, :width], w_in_ref[0, c * width : (c + 1) * width, :])
+
+    cots = jnp.concatenate(in_order(mine, near[:, width:], far[:, width:]), axis=1)
+    back_act = dot_lanes(cots, w_out_ref[...])
+    slope = back_act * gelu_slope(pre_ref[...] + sum_ref[...])
+    product = dot_lanes(slope.astype(jnp.bfloat16), w_in_ref[0])
+    kept, sent = in_order(mine, product[:, :width], product[:, width:])
+    kept_ref[...] = kept
+    sent_ref[...] = sent.astype(jnp.bfloat16)
 
 
 def sum_kernel(kept_ref, came_ref, out_ref):
@@ -361,36 +346,28 @@
     )
     (outgoing,) = call(
         functools.partial(pick_kernel, share),
-        [((devices, 2 * MOST, part), bf16)],
+        [((devices, MOST, 2 * part), bf16)],
         [here, weight, picked, cot],
         "vvvv",
     )
     held = lax.all_to_all(outgoing, everyone, split_axis=0, concat_axis=0, tiled=True)
     other = swap(held)
-    acts = (hidden // LANES, devices * 2 * MOST, LANES)
-    half = (hidden, part)
-    pre_act, back_act, w_out_far = call(
+    acts = (devices * MOST, hidden)
+    pre_act, w_out_near = call(
         first_kernel,
-        [(acts, f32), (acts, f32), (half, bf16)],
+        [(acts, f32), (w_out.shape[1:], bf16)],
         [place, held, w_in_near, w_out],
         "svvh",
-        [pltpu.VMEM(half, bf16), pltpu.SemaphoreType.DMA((2,))],
-    )
-    slope, sent = call(
+        [pltpu.SemaphoreType.DMA],
+    )
+    kept, sent = call(
         second_kernel,
-        [((devices * MOST, hidden), bf16), ((devices * MOST, part), bf16)],
-        [place, other, pre_act, back_act, w_in_near, w_out_far],
+        [((devices * MOST, part), f32), ((devices * MOST, part), bf16)],
+        [place, held, other, pre_act, w_in_near, w_out_near],
         "svvvvv",
-        [
-            pltpu.VMEM(acts, f32),
-            pltpu.VMEM(acts, f32),
-            pltpu.VMEM((hidden // LANES, devices * MOST, LANES), f32),
-        ],
+        [pltpu.VMEM(acts, f32)],
     )
     came = swap(sent)
-    (kept,) = call(
-        third_kernel, [((devices * MOST, part), f32)], [place, slope, w_in_near], "svv"
-    )
     (total,) = call(sum_kernel, [((devices, MOST, part), bf16)], [kept, came], "vv")
     back = lax.all_to_all(total, everyone, split_axis=0, concat_axis=0, tiled=True)
     return call(

time: 47.1 us -> 47.7 us (1.013)
  waiting for transfers between devices: 4.52 us -> 5.5 us
    ppermute x2, waiting for transfers between devices: 0.25 us -> 1.22 us  [swap(): return lax.ppermute(values, 'frm', [(i, i ^ 1) for i in range(columns)])]
    pallas_call x8 -> x7, Pallas kernels: 10.4 us -> 10 us  [call(): pl.pallas_call(kernel, out_shape=[jax.ShapeDtypeStruct(shape, dtype) for...]
  transfers between devices with their start and end apart: 3 -> 3, of which waited for: 2 -> 2; matrix products, arithmetic and copies ran while one was open for 0% -> 0% of each run, Pallas kernels for 12% -> 10%
where the time goes in v7:
time: 47.7 us; the launch traced here: 47.3 us
  blocking collectives  24.1 us (51%)
  Pallas kernels  10 us (21%)
  starting transfers between devices  6.91 us (14%)
  waiting for transfers between devices  5.5 us (12%)
  between operations  0.67 us (1%)
    all_to_all x1, blocking collectives, body(): lax.all_to_all(outgoing, everyone, split_axis=0, concat_axis=0, tiled=True)  13.9 us
    all_to_all x1, blocking collectives, body(): lax.all_to_all(total, everyone, split_axis=0, concat_axis=0, tiled=True)  10.3 us
    pallas_call x7, Pallas kernels, call(): pl.pallas_call(kernel, out_shape=[jax.ShapeDtypeStruct(shape, dtype) for...  10 us
    all_to_all x1, starting transfers between devices, body(): cot = lax.all_to_all(turned, 'frm', split_axis=0, concat_axis=0, tiled=True)  6.34 us
    all_to_all x1, waiting for transfers between devices, body(): cot = lax.all_to_all(turned, 'frm', split_axis=0, concat_axis=0, tiled=True)  4.27 us
    ppermute x2, waiting for transfers between devices, swap(): return lax.ppermute(values, 'frm', [(i, i ^ 1) for i in range(columns)])  1.22 us
  transfers between devices with their start and end apart: 3, of which 2 were waited for; matrix products, arithmetic and copies ran while one was open for 0% of the time, Pallas kernels for 10%

profile of v7, /device:TPU:0, one launch (start us, length us, event | category | flops | bytes accessed | tf_op | source)
XLA Modules:
  0.0 47.3 jit_solution(1055580878600176360)
XLA Ops:
  0.6 1.5 %shard_map.104 = bf16[8,4,2048]{2,1,0:T(4,128)(2,1)} custom-call(bf16[1,32,2048]{2,1,0:T(8,128)(2,1)} %cot_hbm.1), custom_call_target="tpu_custom_call" | custom-call | tf_op jit(solution)/shard_map/pallas_call | solution.py:286
  2.2 6.3 %all-to-all-start = ((bf16[8,4,2048]{2,1,0:T(4,128)(2,1)}), bf16[8,4,2048]{2,1,0:T(4,128)(2,1)S(1)}, u32[]{:S(2)}, u32[]{:S(2)}) async-start(bf16[8,4,2048]{2,1,0:T(4,128)(2,1)} %shard_map.104), calls=%async_computation | async-start | bytes 262144 | tf_op jit(solution)/shard_map/all_to_all | solution.py:328
  8.5 0.1 pad_add_fusion.place_ref
  8.6 2.4 %shard_map.103 = (bf16[8,4,2048]{2,1,0:T(4,128)(2,1)S(1)}, bf16[8,4,2048]{2,1,0:T(4,128)(2,1)S(1)}, bf16[8,4,2048]{2,1,0:T(4,128)(2,1)S(1)}, bf16[1,2048,512]{2,...) custom-call(s32[2]{0:T(128)S(1)} %pad_add_fusion.place_ref, ...), custom_call_target="tpu_custom_call" | custom-call | tf_op jit(solution)/shard_map/pallas_call | solution.py:286
  11.0 4.3 %all-to-all-done.cot_ref = bf16[8,4,2048]{2,1,0:T(4,128)(2,1)S(1)} async-done(((bf16[8,4,2048]{2,1,0:T(4,128)(2,1)}), bf16[8,4,2048]{2,1,0:T(4,128)(2,1)S(1)}, u32[]{:S(2)}, u32[]{:S(2)}) %all-to-all-start) | async-done | bytes 131104 | tf_op jit(solution)/shard_map/all_to_all | solution.py:328
  15.3 0.2 shard_map.105
  15.5 13.9 %all_to_all.15.rows_ref.near_ref = bf16[32,2,2048]{2,1,0:T(2,128)(2,1)S(1)} all-to-all(bf16[32,2,2048]{2,1,0:T(2,128)(2,1)S(1)} %shard_map.105), channel_id=1, replica_groups=mesh['grp'=4,'frm'=8] {'grp','frm'}, dimensions={0} | all-to-all | bytes 524288 | tf_op jit(solution)/shard_map/all_to_all | solution.py:353
  29.3 0.4 collective-permute-start
  29.7 2.1 %shard_map.106 = (f32[64,512]{1,0:T(8,128)S(1)}, bf16[512,2048]{1,0:T(8,128)(2,1)S(1)}) custom-call(s32[2]{0:T(128)S(1)} %pad_add_fusion.place_ref, bf16[32,2,2048]{2,1,0:T(2,128)(2,1)S(1)} %all_to_all.15.rows_ref.near_ref, bf16[1,2048,512]{2,1,0:T(8,128)(2,1)S(1)} %get-tuple-element.20.w_in_ref, bf16[1,512,2048]{2,1,0:T(8,128)(2,1)} %w_out_hbm.1), custom_call_target="tpu_custom_call" | custom-call | tf_op jit(solution)/shard_map/pallas_call | solution.py:286
  31.8 0.0 collective-permute-done.far_ref
  31.8 2.3 %shard_map.107 = (f32[64,1024]{1,0:T(8,128)S(1)}, bf16[64,1024]{1,0:T(8,128)(2,1)S(1)}) custom-call(s32[2]{0:T(128)S(1)} %pad_add_fusion.place_ref, bf16[32,2,2048]{2,1,0:T(2,128)(2,1)S(1)} %all_to_all.15.rows_ref.near_ref, bf16[32,2,2048]{2,1,0:T(2,128)(2,1)S(1)} %collective-permute-done.far_ref, f32[64,512]{1,0:T(8,128)S(1)} %get-tuple-element.21.pre_ref, ...), custom_call_target="tpu_custom_call" | custom-call | tf_op jit(solution)/shard_map/pallas_call | solution.py:286
  34.2 0.2 collective-permute-start.1
  34.3 1.2 %collective-permute-done.1.came_ref = bf16[64,1024]{1,0:T(8,128)(2,1)S(1)} collective-permute-done((bf16[64,1024]{1,0:T(8,128)(2,1)S(1)}, bf16[64,1024]{1,0:T(8,128)(2,1)S(1)}, u32[]{:S(2)}, u32[]{:S(2)}) %collective-permute-start.1) | collective-permute-done | bytes 131104 | tf_op jit(solution)/shard_map/ppermute | solution.py:317
  35.6 10.3 %all_to_all.16.back_ref = bf16[32,2,1024]{2,1,0:T(2,128)(2,1)S(1)} all-to-all(bf16[32,2,1024]{2,1,0:T(2,128)(2,1)S(1)} %shard_map.108), channel_id=1, replica_groups=mesh['grp'=4,'frm'=8] {'grp','frm'}, dimensions={0} | all-to-all | bytes 262144 | tf_op jit(solution)/shard_map/all_to_all | solution.py:372
  45.9 1.4 %shard_map.109 = (bf16[8,4,2048]{2,1,0:T(4,128)(2,1)}, bf16[8,4,2048]{2,1,0:T(4,128)(2,1)}, bf16[8,4,2048]{2,1,0:T(4,128)(2,1)}) custom-call(bf16[2,32,64]{2,1,0:T(8,128)(2,1)S(1)} %get-tuple-element.16.spread_ref, bf16[32,2,1024]{2,1,0:T(2,128)(2,1)S(1)} %all_to_all.16.back_ref, bf16[8,4,2048]{2,1,0:T(4,128)(2,1)S(1)} %all-to-all-done.cot_ref, ...), custom_call_target="tpu_custom_call" | custom-call | tf_op jit(solution)/shard_map/pallas_call | solution.py:286
  (1 shorter events, 0.0 us)
Async XLA Ops:
  2.2 13.1 %all-to-all-start = ((bf16[8,4,2048]{2,1,0:T(4,128)(2,1)}), bf16[8,4,2048]{2,1,0:T(4,128)(2,1)S(1)}, u32[]{:S(2)}, u32[]{:S(2)}) async-start(bf16[8,4,2048]{2,1,0:T(4,128)(2,1)} %shard_map.104), calls=%async_computation | async-start | bytes 262144 | tf_op jit(solution)/shard_map/all_to_all | solution.py:328
  29.3 2.5 %collective-permute-start = (bf16[32,2,2048]{2,1,0:T(2,128)(2,1)S(1)}, bf16[32,2,2048]{2,1,0:T(2,128)(2,1)S(1)}, u32[]{:S(2)}, u32[]{:S(2)}) collective-permute-start(bf16[32,2,2048]{2,1,0:T(2,128)(2,1)S(1)} %all_to_all.15.rows_ref.near_ref), channel_id=1, source_target_pairs={{0,1},{1,0},{2,3},{3,2},{4,5},{5,4},{6,7},{7,6},{8,9},{9,8},{10,11... | collective-permute-start | bytes 786440 | tf_op jit(solution)/shard_map/ppermute | solution.py:317
  34.2 1.4 %collective-permute-start.1 = (bf16[64,1024]{1,0:T(8,128)(2,1)S(1)}, bf16[64,1024]{1,0:T(8,128)(2,1)S(1)}, u32[]{:S(2)}, u32[]{:S(2)}) collective-permute-start(bf16[64,1024]{1,0:T(8,128)(2,1)S(1)} %get-tuple-element.24), channel_id=1, source_target_pairs={{0,1},{1,0},{2,3},{3,2},{4,5},{5,4},{6,7},{7,6},{8,9},{9,8},{10,11... | collective-permute-start | bytes 393224 | tf_op jit(solution)/shard_map/ppermute | solution.py:317

commit v8 on v7

--- a/solution.py
+++ b/solution.py
@@ -81,13 +81,13 @@
 
 def forward_kernel(
     patches_all, share, place_ref,
-    chosen_hbm, gate_hbm, query_hbm, key_hbm, value_hbm, w_in_hbm,
-    query_ref, key_ref, value_ref, w_in_ref,
-    probs_ref, picked_ref, here_ref, weight_ref, spread_ref,
-    chosen_ref, gate_ref, sems,
+    chosen_hbm, gate_hbm, query_hbm, key_hbm, value_hbm, w_in_hbm, w_out_hbm,
+    w_in_ref, w_out_ref, probs_ref, picked_ref, here_ref, weight_ref, spread_ref,
+    chosen_ref, gate_ref, query_ref, key_ref, value_ref, sems,
 ):
-    sources = [chosen_hbm, gate_hbm, query_hbm, key_hbm, value_hbm, w_in_hbm]
-    targets = [chosen_ref, gate_ref, query_ref, key_ref, value_ref, w_in_ref]
+    upper = w_out_hbm.at[0, pl.ds(0, w_out_ref.shape[0])]
+    sources = [chosen_hbm, gate_hbm, query_hbm, key_hbm, value_hbm, w_in_hbm, upper]
+    targets = [chosen_ref, gate_ref, query_ref, key_ref, value_ref, w_in_ref, w_out_ref]
     copies = [
         pltpu.make_async_copy(source, target, sems.at[i])
         for i, (source, target) in enumerate(zip(sources, targets))
@@ -185,35 +185,36 @@
     return jnp.where(mine == 0, near, far), jnp.where(mine == 0, far, near)
 
 
-def first_kernel(place_ref, rows_ref, w_in_ref, w_out_hbm, pre_ref, w_out_ref, sem):
-    copy = pltpu.make_async_copy(w_out_hbm.at[0], w_out_ref, sem)
+def first_kernel(place_ref, near_ref, w_in_ref, w_out_hbm, pre_ref, lower_ref, sem):
+    half = lower_ref.shape[0]
+    copy = pltpu.make_async_copy(w_out_hbm.at[0, pl.ds(half, half)], lower_ref, sem)
     copy.start()
-    rows = rows_ref[...].reshape(pre_ref.shape[0], -1)
-    width = rows.shape[1] // 2
+    width = near_ref.shape[1] // 2
     for c in range(CORES):
 
         @pl.when(place_ref[1] == c)
         def _():
-            pre_ref[...] = dot(rows[:, :width], w_in_ref[0, c * width : (c + 1) * width, :])
+            pre_ref[...] = dot(near_ref[:, :width], w_in_ref[0, c * width : (c + 1) * width, :])
 
     copy.wait()
 
 
 def second_kernel(
-    place_ref, near_ref, far_ref, pre_ref, w_in_ref, w_out_ref, kept_ref, sent_ref, sum_ref
+    place_ref, near_ref, far_ref, pre_ref, w_in_ref, upper_ref, lower_ref,
+    kept_ref, sent_ref, sum_ref,
 ):
-    near = near_ref[...].reshape(pre_ref.shape[0], -1)
-    far = far_ref[...].reshape(pre_ref.shape[0], -1)
-    width = near.shape[1] // 2
+    width = near_ref.shape[1] // 2
     mine = place_ref[1]
     for c in range(CORES):
 
         @pl.when(mine == 1 - c)
         def _():
-            sum_ref[...] = dot(far[:, :width], w_in_ref[0, c * width : (c + 1) * width, :])
-
-    cots = jnp.concatenate(in_order(mine, near[:, width:], far[:, width:]), axis=1)
-    back_act = dot_lanes(cots, w_out_ref[...])
+            sum_ref[...] = dot(far_ref[:, :width], w_in_ref[0, c * width : (c + 1) * width, :])
+
+    cots = jnp.concatenate(in_order(mine, near_ref[:, width:], far_ref[:, width:]), axis=1)
+    back_act = jnp.concatenate(
+        [dot_lanes(cots, upper_ref[...]), dot_lanes(cots, lower_ref[...])], axis=1
+    )
     slope = back_act * gelu_slope(pre_ref[...] + sum_ref[...])
     product = dot_lanes(slope.astype(jnp.bfloat16), w_in_ref[0])
     kept, sent = in_order(mine, product[:, :width], product[:, width:])
@@ -237,8 +238,7 @@
     query = query_ref[...].reshape(rows, features)
     key = key_ref[...].reshape(rows, features)
     value = value_ref[...].reshape(rows, features)
-    back = back_ref[...].reshape(-1, back_ref.shape[2])
-    added = jnp.concatenate([dot(spread_ref[c], back) for c in range(CORES)], axis=1)
+    added = jnp.concatenate([dot(spread_ref[c], back_ref[...]) for c in range(CORES)], axis=1)
     cot = cot_ref[...].reshape(rows, features)
     stream = (cot.astype(jnp.float32) + added).astype(jnp.bfloat16)
     probs = probs_ref[...]
@@ -326,22 +326,24 @@
         "h",
     )
     cot = lax.all_to_all(turned, "frm", split_axis=0, concat_axis=0, tiled=True)
-    query, key, value, w_in_near, probs, picked, here, weight, spread = call(
+    w_in_near, upper, probs, picked, here, weight, spread = call(
         functools.partial(forward_kernel, blocks * devices, share),
         [
-            *[(array.shape, bf16) for array in (query_in, key_in, value_in, w_in)],
+            (w_in.shape, bf16),
+            ((hidden // 2, features), bf16),
             ((rows, HEADS * rows), f32),
             ((slots, features), bf16),
             ((slots, rows), f32),
             ((slots, LANES), f32),
             ((CORES, rows, devices * MOST), bf16),
         ],
-        [place, chosen, gate_probs, query_in, key_in, value_in, w_in],
-        "shhhhhh",
+        [place, chosen, gate_probs, query_in, key_in, value_in, w_in, w_out],
+        "shhhhhhh",
         [
             pltpu.VMEM(chosen.shape, jnp.int32),
             pltpu.VMEM(gate_probs.shape, f32),
-            pltpu.SemaphoreType.DMA((6,)),
+            *[pltpu.VMEM(query_in.shape, bf16)] * 3,
+            pltpu.SemaphoreType.DMA((7,)),
         ],
     )
     (outgoing,) = call(
@@ -351,11 +353,12 @@
         "vvvv",
     )
     held = lax.all_to_all(outgoing, everyone, split_axis=0, concat_axis=0, tiled=True)
+    held = held.reshape(devices * MOST, 2 * part)
     other = swap(held)
     acts = (devices * MOST, hidden)
-    pre_act, w_out_near = call(
+    pre_act, lower = call(
         first_kernel,
-        [(acts, f32), (w_out.shape[1:], bf16)],
+        [(acts, f32), ((hidden // 2, features), bf16)],
         [place, held, w_in_near, w_out],
         "svvh",
         [pltpu.SemaphoreType.DMA],
@@ -363,17 +366,18 @@
     kept, sent = call(
         second_kernel,
         [((devices * MOST, part), f32), ((devices * MOST, part), bf16)],
-        [place, held, other, pre_act, w_in_near, w_out_near],
-        "svvvvv",
+        [place, held, other, pre_act, w_in_near, upper, lower],
+        "svvvvvv",
         [pltpu.VMEM(acts, f32)],
     )
     came = swap(sent)
     (total,) = call(sum_kernel, [((devices, MOST, part), bf16)], [kept, came], "vv")
     back = lax.all_to_all(total, everyone, split_axis=0, concat_axis=0, tiled=True)
+    back = back.reshape(devices * MOST, part)
     return call(
         backward_kernel,
         [((frames, blocks, features), bf16)] * 3,
-        [spread, back, cot, probs, query, key, value],
+        [spread, back, cot, probs, query_in, key_in, value_in],
         "vvvvvvv",
         [pltpu.VMEM((frames, blocks, features), bf16)] * 3 + [pltpu.SemaphoreType.DMA((3,))],
         "h",

time: 47.7 us -> 55.8 us (1.17)
  local copies, waits for them, and re-layouts: 0 us -> 9.19 us
  waiting for transfers between devices: 5.5 us -> 3.4 us
  blocking collectives: 24.1 us -> 25 us
    unnamed x0 -> x28, local copies, waits for them, and re-layouts: none -> 8.09 us
    all_to_all x1, waiting for transfers between devices: 4.27 us -> 2.17 us  [body(): cot = lax.all_to_all(turned, 'frm', split_axis=0, concat_axis=0, tiled=True)]
    reshape x0 -> x2, local copies, waits for them, and re-layouts: none -> 1.1 us  [the longest x1 1.05 us: body(): held = held.reshape(devices * MOST, 2 * part)]
    all_to_all x1, blocking collectives: 13.9 us -> 14.8 us  [body(): lax.all_to_all(outgoing, everyone, split_axis=0, concat_axis=0, tiled=True)]
  transfers between devices with their start and end apart: 3 -> 3, of which waited for: 2 -> 2; matrix products, arithmetic and copies ran while one was open for 0% -> 0% of each run, Pallas kernels for 10% -> 8%
where the time goes in v8:
time: 55.8 us; the launch traced here: 55.3 us
  blocking collectives  25 us (45%)
  Pallas kernels  9.89 us (18%)
  local copies, waits for them, and re-layouts  9.19 us (16%)
  starting transfers between devices  6.98 us (13%)
  waiting for transfers between devices  3.4 us (6%)
  between operations  0.72 us (1%)
    all_to_all x1, blocking collectives, body(): lax.all_to_all(outgoing, everyone, split_axis=0, concat_axis=0, tiled=True)  14.8 us
    all_to_all x1, blocking collectives, body(): lax.all_to_all(total, everyone, split_axis=0, concat_axis=0, tiled=True)  10.3 us
    pallas_call x7, Pallas kernels, call(): pl.pallas_call(kernel, out_shape=[jax.ShapeDtypeStruct(shape, dtype) for...  9.89 us
    unnamed x28, local copies, waits for them, and re-layouts  8.09 us
    all_to_all x1, starting transfers between devices, body(): cot = lax.all_to_all(turned, 'frm', split_axis=0, concat_axis=0, tiled=True)  6.34 us
    all_to_all x1, waiting for transfers between devices, body(): cot = lax.all_to_all(turned, 'frm', split_axis=0, concat_axis=0, tiled=True)  2.17 us
    ppermute x2, waiting for transfers between devices, swap(): return lax.ppermute(values, 'frm', [(i, i ^ 1) for i in range(columns)])  1.23 us
  transfers between devices with their start and end apart: 3, of which 2 were waited for; matrix products, arithmetic and copies ran while one was open for 0% of the time, Pallas kernels for 8%

profile of v8, /device:TPU:0, one launch (start us, length us, event | category | flops | bytes accessed | tf_op | source)
XLA Modules:
  0.0 55.3 jit_solution(6247058400117958540)
XLA Ops:
  0.6 1.5 %shard_map.104 = bf16[8,4,2048]{2,1,0:T(4,128)(2,1)} custom-call(bf16[1,32,2048]{2,1,0:T(8,128)(2,1)} %cot_hbm.1), custom_call_target="tpu_custom_call" | custom-call | tf_op jit(solution)/shard_map/pallas_call | solution.py:286
  2.2 6.3 %all-to-all-start = ((bf16[8,4,2048]{2,1,0:T(4,128)(2,1)}), bf16[8,4,2048]{2,1,0:T(4,128)(2,1)S(1)}, u32[]{:S(2)}, u32[]{:S(2)}) async-start(bf16[8,4,2048]{2,1,0:T(4,128)(2,1)} %shard_map.104), calls=%async_computation | async-start | bytes 262144 | tf_op jit(solution)/shard_map/all_to_all | solution.py:328
  8.5 0.1 pad_add_fusion.place_ref
  8.6 0.0 copy-start.7
  8.6 2.7 %shard_map.103 = (bf16[1,2048,512]{2,1,0:T(8,128)(2,1)S(1)}, bf16[256,2048]{1,0:T(8,128)(2,1)S(1)}, f32[32,512]{1,0:T(8,128)S(1)}, bf16[4,2048]{1,0:T(4,128)(2,1...) custom-call(s32[2]{0:T(128)S(1)} %pad_add_fusion.place_ref, s32[2,32]{1,0:T(2,128)} %chosen_hbm.1, ...), custom_call_target="tpu_custom_call" | custom-call | tf_op jit(solution)/shard_map/pallas_call | solution.py:286
  11.3 0.0 copy-done.7
  11.3 0.0 copy-start.3
  11.3 0.6 %copy-done.3 = f32[32,512]{1,0:T(8,128)} copy-done((f32[32,512]{1,0:T(8,128)}, f32[32,512]{1,0:T(8,128)S(1)}, u32[]{:S(2)}) %copy-start.3) | copy-done | bytes 65560
  11.9 0.0 copy-start.5
  11.9 0.6 %copy-done.5 = bf16[4,2048]{1,0:T(4,128)(2,1)} copy-done((bf16[4,2048]{1,0:T(4,128)(2,1)}, bf16[4,2048]{1,0:T(4,128)(2,1)S(1)}, u32[]{:S(2)}) %copy-start.5) | copy-done | bytes 16408
  12.5 0.0 copy-start.12
  12.5 0.6 %copy-done.12 = f32[4,128]{1,0:T(4,128)} copy-done((f32[4,128]{1,0:T(4,128)}, f32[4,128]{1,0:T(4,128)S(1)}, u32[]{:S(2)}) %copy-start.12) | copy-done | bytes 2072
  13.1 0.0 copy-start.10
  13.1 2.2 %all-to-all-done.cot_ref = bf16[8,4,2048]{2,1,0:T(4,128)(2,1)S(1)} async-done(((bf16[8,4,2048]{2,1,0:T(4,128)(2,1)}), bf16[8,4,2048]{2,1,0:T(4,128)(2,1)S(1)}, u32[]{:S(2)}, u32[]{:S(2)}) %all-to-all-start) | async-done | bytes 131104 | tf_op jit(solution)/shard_map/all_to_all | solution.py:328
  15.3 0.0 copy-done.10
  15.3 0.0 copy-start.6
  15.3 0.7 %copy-done.6 = bf16[4,2048]{1,0:T(4,128)(2,1)S(1)} copy-done((bf16[4,2048]{1,0:T(4,128)(2,1)S(1)}, bf16[4,2048]{1,0:T(4,128)(2,1)}, u32[]{:S(2)}) %copy-start.6) | copy-done | bytes 16408
  16.0 0.0 copy-start.11
  16.0 0.7 %copy-done.11 = f32[4,32]{1,0:T(4,128)S(1)} copy-done((f32[4,32]{1,0:T(4,128)S(1)}, f32[4,32]{1,0:T(4,128)}, u32[]{:S(2)}) %copy-start.11) | copy-done | bytes 536
  16.7 0.0 copy-start.13
  16.7 0.7 %copy-done.13 = f32[4,128]{1,0:T(4,128)S(1)} copy-done((f32[4,128]{1,0:T(4,128)S(1)}, f32[4,128]{1,0:T(4,128)}, u32[]{:S(2)}) %copy-start.13) | copy-done | bytes 2072
  17.4 0.2 shard_map.105
  17.5 14.8 %all_to_all.15 = bf16[32,2,2048]{2,1,0:T(2,128)(2,1)} all-to-all(bf16[32,2,2048]{2,1,0:T(2,128)(2,1)S(1)} %shard_map.105), channel_id=1, replica_groups=mesh['grp'=4,'frm'=8] {'grp','frm'}, dimensions={0} | all-to-all | bytes 524288 | tf_op jit(solution)/shard_map/all_to_all | solution.py:355
  32.3 1.0 %reshape.12.near_ref = bf16[64,2048]{1,0:T(8,128)(2,1)S(1)} reshape(bf16[32,2,2048]{2,1,0:T(2,128)(2,1)} %all_to_all.15) | data formatting | bytes 524288 | tf_op jit(solution)/shard_map/reshape | solution.py:356
  33.3 0.5 collective-permute-start
  33.8 0.0 copy-start.8
  33.8 0.7 %copy-done.8 = s32[2]{0:T(128)S(1)} copy-done((s32[2]{0:T(128)S(1)}, s32[2]{0:T(128)}, u32[]{:S(2)}) %copy-start.8) | copy-done | bytes 32
  34.4 0.0 copy-start.9
  34.4 1.8 %shard_map.106 = (f32[64,512]{1,0:T(8,128)S(1)}, bf16[256,2048]{1,0:T(8,128)(2,1)S(1)}) custom-call(s32[2]{0:T(128)S(1)} %copy-done.8, bf16[64,2048]{1,0:T(8,128)(2,1)S(1)} %reshape.12.near_ref, bf16[1,2048,512]{2,1,0:T(8,128)(2,1)S(1)} %get-tuple-element.18.w_in_ref, bf16[1,512,2048]{2,1,0:T(8,128)(2,1)} %w_out_hbm.3), custom_call_target="tpu_custom_call" | custom-call | tf_op jit(solution)/shard_map/pallas_call | solution.py:286
  36.2 0.0 collective-permute-done.far_ref
  36.2 0.0 copy-done.9
  36.2 2.3 %shard_map.107 = (f32[64,1024]{1,0:T(8,128)S(1)}, bf16[64,1024]{1,0:T(8,128)(2,1)S(1)}) custom-call(s32[2]{0:T(128)S(1)} %copy-done.9, bf16[64,2048]{1,0:T(8,128)(2,1)S(1)} %reshape.12.near_ref, bf16[64,2048]{1,0:T(8,128)(2,1)S(1)} %collective-permute-done.far_ref, f32[64,512]{1,0:T(8,128)S(1)} %get-tuple-element.19.pre_ref, ...), custom_call_target="tpu_custom_call" | custom-call | tf_op jit(solution)/shard_map/pallas_call | solution.py:286
  38.5 0.2 collective-permute-start.1
  38.7 1.2 %collective-permute-done.1.came_ref = bf16[64,1024]{1,0:T(8,128)(2,1)S(1)} collective-permute-done((bf16[64,1024]{1,0:T(8,128)(2,1)S(1)}, bf16[64,1024]{1,0:T(8,128)(2,1)S(1)}, u32[]{:S(2)}, u32[]{:S(2)}) %collective-permute-start.1) | collective-permute-done | bytes 131104 | tf_op jit(solution)/shard_map/ppermute | solution.py:317
  40.0 10.3 %all_to_all.16 = bf16[32,2,1024]{2,1,0:T(2,128)(2,1)S(1)} all-to-all(bf16[32,2,1024]{2,1,0:T(2,128)(2,1)S(1)} %shard_map.108), channel_id=1, replica_groups=mesh['grp'=4,'frm'=8] {'grp','frm'}, dimensions={0} | all-to-all | bytes 262144 | tf_op jit(solution)/shard_map/all_to_all | solution.py:375
  50.2 0.1 reshape.13.back_ref
  50.3 0.0 copy-start
  50.3 0.9 %copy-done = bf16[8,4,2048]{2,1,0:T(4,128)(2,1)S(1)} copy-done((bf16[8,4,2048]{2,1,0:T(4,128)(2,1)S(1)}, bf16[8,4,2048]{2,1,0:T(4,128)(2,1)}, u32[]{:S(2)}) %copy-start) | copy-done | bytes 131096
  51.2 0.0 copy-start.1
  51.2 0.9 %copy-done.1 = bf16[8,4,2048]{2,1,0:T(4,128)(2,1)S(1)} copy-done((bf16[8,4,2048]{2,1,0:T(4,128)(2,1)S(1)}, bf16[8,4,2048]{2,1,0:T(4,128)(2,1)}, u32[]{:S(2)}) %copy-start.1) | copy-done | bytes 131096
  52.1 0.0 copy-start.2
  52.1 0.9 %copy-done.2 = bf16[8,4,2048]{2,1,0:T(4,128)(2,1)S(1)} copy-done((bf16[8,4,2048]{2,1,0:T(4,128)(2,1)S(1)}, bf16[8,4,2048]{2,1,0:T(4,128)(2,1)}, u32[]{:S(2)}) %copy-start.2) | copy-done | bytes 131096
  53.0 0.0 copy-start.4
  53.0 0.8 %copy-done.4 = f32[32,512]{1,0:T(8,128)S(1)} copy-done((f32[32,512]{1,0:T(8,128)S(1)}, f32[32,512]{1,0:T(8,128)}, u32[]{:S(2)}) %copy-start.4) | copy-done | bytes 65560
  53.9 1.4 %shard_map.109 = (bf16[8,4,2048]{2,1,0:T(4,128)(2,1)}, bf16[8,4,2048]{2,1,0:T(4,128)(2,1)}, bf16[8,4,2048]{2,1,0:T(4,128)(2,1)}) custom-call(bf16[2,32,64]{2,1,0:T(8,128)(2,1)S(1)} %get-tuple-element.14.spread_ref, bf16[64,1024]{1,0:T(8,128)(2,1)S(1)} %reshape.13.back_ref, bf16[8,4,2048]{2,1,0:T(4,128)(2,1)S(1)} %all-to-all-done.cot_ref, ...), custom_call_target="tpu_custom_call" | custom-call | tf_op jit(solution)/shard_map/pallas_call | solution.py:286
  (1 shorter events, 0.0 us)
Async XLA Ops:
  2.2 13.1 %all-to-all-start = ((bf16[8,4,2048]{2,1,0:T(4,128)(2,1)}), bf16[8,4,2048]{2,1,0:T(4,128)(2,1)S(1)}, u32[]{:S(2)}, u32[]{:S(2)}) async-start(bf16[8,4,2048]{2,1,0:T(4,128)(2,1)} %shard_map.104), calls=%async_computation | async-start | bytes 262144 | tf_op jit(solution)/shard_map/all_to_all | solution.py:328
  8.6 2.7 %copy-start.7 = (s32[2]{0:T(128)}, s32[2]{0:T(128)S(1)}, u32[]{:S(2)}) copy-start(s32[2]{0:T(128)S(1)} %pad_add_fusion.place_ref) | copy-start | bytes 28
  11.3 0.6 %copy-start.3 = (f32[32,512]{1,0:T(8,128)}, f32[32,512]{1,0:T(8,128)S(1)}, u32[]{:S(2)}) copy-start(f32[32,512]{1,0:T(8,128)S(1)} %get-tuple-element.24.probs_ref) | copy-start | bytes 196612
  11.9 0.6 %copy-start.5 = (bf16[4,2048]{1,0:T(4,128)(2,1)}, bf16[4,2048]{1,0:T(4,128)(2,1)S(1)}, u32[]{:S(2)}) copy-start(bf16[4,2048]{1,0:T(4,128)(2,1)S(1)} %get-tuple-element.17.picked_ref) | copy-start | bytes 49156
  12.5 0.6 %copy-start.12 = (f32[4,128]{1,0:T(4,128)}, f32[4,128]{1,0:T(4,128)S(1)}, u32[]{:S(2)}) copy-start(f32[4,128]{1,0:T(4,128)S(1)} %get-tuple-element.16.weight_ref) | copy-start | bytes 6148
  13.1 2.2 %copy-start.10 = (f32[4,32]{1,0:T(4,128)}, f32[4,32]{1,0:T(4,128)S(1)}, u32[]{:S(2)}) copy-start(f32[4,32]{1,0:T(4,128)S(1)} %get-tuple-element.15.here_ref) | copy-start | bytes 1540
  15.3 0.7 %copy-start.6 = (bf16[4,2048]{1,0:T(4,128)(2,1)S(1)}, bf16[4,2048]{1,0:T(4,128)(2,1)}, u32[]{:S(2)}) copy-start(bf16[4,2048]{1,0:T(4,128)(2,1)} %copy-done.5) | copy-start | bytes 49156
  16.0 0.7 %copy-start.11 = (f32[4,32]{1,0:T(4,128)S(1)}, f32[4,32]{1,0:T(4,128)}, u32[]{:S(2)}) copy-start(f32[4,32]{1,0:T(4,128)} %copy-done.10) | copy-start | bytes 1540
  16.7 0.7 %copy-start.13 = (f32[4,128]{1,0:T(4,128)S(1)}, f32[4,128]{1,0:T(4,128)}, u32[]{:S(2)}) copy-start(f32[4,128]{1,0:T(4,128)} %copy-done.12) | copy-start | bytes 6148
  33.3 2.9 %collective-permute-start = (bf16[64,2048]{1,0:T(8,128)(2,1)S(1)}, bf16[64,2048]{1,0:T(8,128)(2,1)S(1)}, u32[]{:S(2)}, u32[]{:S(2)}) collective-permute-start(bf16[64,2048]{1,0:T(8,128)(2,1)S(1)} %reshape.12.near_ref), channel_id=1, source_target_pairs={{0,1},{1,0},{2,3},{3,2},{4,5},{5,4},{6,7},{7,6},{8,9},{9,8},{10,11... | collective-permute-start | bytes 786440 | tf_op jit(solution)/shard_map/ppermute | solution.py:317
  33.8 0.7 %copy-start.8 = (s32[2]{0:T(128)S(1)}, s32[2]{0:T(128)}, u32[]{:S(2)}) copy-start(s32[2]{0:T(128)} %copy-done.7) | copy-start | bytes 28
  34.4 1.8 %copy-start.9 = (s32[2]{0:T(128)S(1)}, s32[2]{0:T(128)}, u32[]{:S(2)}) copy-start(s32[2]{0:T(128)} %copy-done.7) | copy-start | bytes 28
  38.5 1.4 %collective-permute-start.1 = (bf16[64,1024]{1,0:T(8,128)(2,1)S(1)}, bf16[64,1024]{1,0:T(8,128)(2,1)S(1)}, u32[]{:S(2)}, u32[]{:S(2)}) collective-permute-start(bf16[64,1024]{1,0:T(8,128)(2,1)S(1)} %get-tuple-element.23), channel_id=1, source_target_pairs={{0,1},{1,0},{2,3},{3,2},{4,5},{5,4},{6,7},{7,6},{8,9},{9,8},{10,11... | collective-permute-start | bytes 393224 | tf_op jit(solution)/shard_map/ppermute | solution.py:317
  50.3 0.9 %copy-start = (bf16[8,4,2048]{2,1,0:T(4,128)(2,1)S(1)}, bf16[8,4,2048]{2,1,0:T(4,128)(2,1)}, u32[]{:S(2)}) copy-start(bf16[8,4,2048]{2,1,0:T(4,128)(2,1)} %query_ref.1) | copy-start | bytes 393220
  51.2 0.9 %copy-start.1 = (bf16[8,4,2048]{2,1,0:T(4,128)(2,1)S(1)}, bf16[8,4,2048]{2,1,0:T(4,128)(2,1)}, u32[]{:S(2)}) copy-start(bf16[8,4,2048]{2,1,0:T(4,128)(2,1)} %key_ref.1) | copy-start | bytes 393220
  52.1 0.9 %copy-start.2 = (bf16[8,4,2048]{2,1,0:T(4,128)(2,1)S(1)}, bf16[8,4,2048]{2,1,0:T(4,128)(2,1)}, u32[]{:S(2)}) copy-start(bf16[8,4,2048]{2,1,0:T(4,128)(2,1)} %value_ref.1) | copy-start | bytes 393220
  53.0 0.8 %copy-start.4 = (f32[32,512]{1,0:T(8,128)S(1)}, f32[32,512]{1,0:T(8,128)}, u32[]{:S(2)}) copy-start(f32[32,512]{1,0:T(8,128)} %copy-done.3) | copy-start | bytes 196612

commit v9 on v7

--- a/solution.py
+++ b/solution.py
@@ -80,14 +80,20 @@
 
 
 def forward_kernel(
-    patches_all, share, place_ref,
+    patches_all, share,
     chosen_hbm, gate_hbm, query_hbm, key_hbm, value_hbm, w_in_hbm,
     query_ref, key_ref, value_ref, w_in_ref,
     probs_ref, picked_ref, here_ref, weight_ref, spread_ref,
     chosen_ref, gate_ref, sems,
 ):
-    sources = [chosen_hbm, gate_hbm, query_hbm, key_hbm, value_hbm, w_in_hbm]
-    targets = [chosen_ref, gate_ref, query_ref, key_ref, value_ref, w_in_ref]
+    columns = lax.axis_size("frm")
+    column = lax.axis_index("frm")
+    part = w_in_ref.shape[0] // CORES
+    sources = [chosen_hbm, gate_hbm, query_hbm, key_hbm, value_hbm]
+    targets = [chosen_ref, gate_ref, query_ref, key_ref, value_ref]
+    for i in range(CORES):
+        sources.append(w_in_hbm.at[0, part_of(column % CORES ^ i, part)])
+        targets.append(w_in_ref.at[pl.ds(i * part, part)])
     copies = [
         pltpu.make_async_copy(source, target, sems.at[i])
         for i, (source, target) in enumerate(zip(sources, targets))
@@ -101,7 +107,7 @@
     for copy in copies[:2]:
         copy.wait()
     experts, cap = chosen_ref.shape
-    myself = place_ref[0]
+    myself = lax.axis_index("grp") * columns + column
     before = (
         lax.broadcasted_iota(jnp.int32, (cap, cap), 0)
         < lax.broadcasted_iota(jnp.int32, (cap, cap), 1)
@@ -181,44 +187,43 @@
             out_ref[e * share + i] = both[i % CORES][e * MOST : (e + 1) * MOST]
 
 
-def in_order(mine, near, far):
-    return jnp.where(mine == 0, near, far), jnp.where(mine == 0, far, near)
-
-
-def first_kernel(place_ref, rows_ref, w_in_ref, w_out_hbm, pre_ref, w_out_ref, sem):
-    copy = pltpu.make_async_copy(w_out_hbm.at[0], w_out_ref, sem)
-    copy.start()
-    rows = rows_ref[...].reshape(pre_ref.shape[0], -1)
-    width = rows.shape[1] // 2
-    for c in range(CORES):
-
-        @pl.when(place_ref[1] == c)
-        def _():
-            pre_ref[...] = dot(rows[:, :width], w_in_ref[0, c * width : (c + 1) * width, :])
-
-    copy.wait()
-
-
-def second_kernel(
-    place_ref, near_ref, far_ref, pre_ref, w_in_ref, w_out_ref, kept_ref, sent_ref, sum_ref
-):
-    near = near_ref[...].reshape(pre_ref.shape[0], -1)
-    far = far_ref[...].reshape(pre_ref.shape[0], -1)
-    width = near.shape[1] // 2
-    mine = place_ref[1]
-    for c in range(CORES):
-
-        @pl.when(mine == 1 - c)
-        def _():
-            sum_ref[...] = dot(far[:, :width], w_in_ref[0, c * width : (c + 1) * width, :])
-
-    cots = jnp.concatenate(in_order(mine, near[:, width:], far[:, width:]), axis=1)
-    back_act = dot_lanes(cots, w_out_ref[...])
-    slope = back_act * gelu_slope(pre_ref[...] + sum_ref[...])
-    product = dot_lanes(slope.astype(jnp.bfloat16), w_in_ref[0])
-    kept, sent = in_order(mine, product[:, :width], product[:, width:])
-    kept_ref[...] = kept
-    sent_ref[...] = sent.astype(jnp.bfloat16)
+def part_of(part, width):
+    return pl.ds(pl.multiple_of(part * width, width), width)
+
+
+def first_kernel(near_ref, w_in_ref, w_out_hbm, rows_ref, pre_ref, w_out_ref, sems):
+    width = w_in_ref.shape[0] // CORES
+    copies = [
+        pltpu.make_async_copy(
+            w_out_hbm.at[0, :, part_of(lax.axis_index("frm") % CORES ^ i, width)],
+            w_out_ref.at[:, pl.ds(i * width, width)],
+            sems.at[i],
+        )
+        for i in range(CORES)
+    ]
+    for copy in copies:
+        copy.start()
+    rows = near_ref[...].reshape(rows_ref.shape)
+    rows_ref[...] = rows
+    pre_ref[...] = dot(rows[:, :width], w_in_ref[:width, :])
+    for copy in copies:
+        copy.wait()
+
+
+def second_kernel(near_ref, far_ref, pre_ref, w_in_ref, w_out_ref, slope_ref, sent_ref):
+    width = w_in_ref.shape[0] // CORES
+    far = far_ref[...].reshape(near_ref.shape)
+    pre_act = pre_ref[...] + dot(far[:, :width], w_in_ref[width:, :])
+    back_act = dot_lanes(near_ref[:, width:], w_out_ref[:, :width])
+    back_act = back_act + dot_lanes(far[:, width:], w_out_ref[:, width:])
+    slope = (back_act * gelu_slope(pre_act)).astype(jnp.bfloat16)
+    slope_ref[...] = slope
+    sent_ref[...] = dot_lanes(slope, w_in_ref[width:, :]).astype(jnp.bfloat16)
+
+
+def third_kernel(slope_ref, w_in_ref, kept_ref):
+    width = kept_ref.shape[1]
+    kept_ref[...] = dot_lanes(slope_ref[...], w_in_ref[:width, :])
 
 
 def sum_kernel(kept_ref, came_ref, out_ref):
@@ -279,10 +284,10 @@
 
 
 def call(kernel, outs, operands, places, scratch=(), results="v"):
-    smem, vmem, hbm = (
-        pl.BlockSpec(memory_space=space) for space in (pltpu.SMEM, pltpu.VMEM, pl.ANY)
-    )
-    spaces = {"s": smem, "v": vmem, "h": hbm}
+    spaces = {
+        "v": pl.BlockSpec(memory_space=pltpu.VMEM),
+        "h": pl.BlockSpec(memory_space=pl.ANY),
+    }
     return pl.pallas_call(
         kernel,
         out_shape=[jax.ShapeDtypeStruct(shape, dtype) for shape, dtype in outs],
@@ -308,9 +313,6 @@
     slots = experts * MOST
     part = features // CORES
     hidden = w_in.shape[2]
-    column = lax.axis_index("frm")
-    place = jnp.stack([lax.axis_index("grp") * columns + column, column % CORES])
-    place = place.astype(jnp.int32)
     everyone = ("grp", "frm")
 
     def swap(values):
@@ -329,19 +331,20 @@
     query, key, value, w_in_near, probs, picked, here, weight, spread = call(
         functools.partial(forward_kernel, blocks * devices, share),
         [
-            *[(array.shape, bf16) for array in (query_in, key_in, value_in, w_in)],
+            *[(array.shape, bf16) for array in (query_in, key_in, value_in)],
+            (w_in.shape[1:], bf16),
             ((rows, HEADS * rows), f32),
             ((slots, features), bf16),
             ((slots, rows), f32),
             ((slots, LANES), f32),
             ((CORES, rows, devices * MOST), bf16),
         ],
-        [place, chosen, gate_probs, query_in, key_in, value_in, w_in],
-        "shhhhhh",
+        [chosen, gate_probs, query_in, key_in, value_in, w_in],
+        "hhhhhh",
         [
             pltpu.VMEM(chosen.shape, jnp.int32),
             pltpu.VMEM(gate_probs.shape, f32),
-            pltpu.SemaphoreType.DMA((6,)),
+            pltpu.SemaphoreType.DMA((5 + CORES,)),
         ],
     )
     (outgoing,) = call(
@@ -353,21 +356,22 @@
     held = lax.all_to_all(outgoing, everyone, split_axis=0, concat_axis=0, tiled=True)
     other = swap(held)
     acts = (devices * MOST, hidden)
-    pre_act, w_out_near = call(
+    halves = (devices * MOST, part)
+    near, pre_act, w_out_near = call(
         first_kernel,
-        [(acts, f32), (w_out.shape[1:], bf16)],
-        [place, held, w_in_near, w_out],
-        "svvh",
-        [pltpu.SemaphoreType.DMA],
-    )
-    kept, sent = call(
+        [((devices * MOST, 2 * part), bf16), (acts, f32), (w_out.shape[1:], bf16)],
+        [held, w_in_near, w_out],
+        "vvh",
+        [pltpu.SemaphoreType.DMA((CORES,))],
+    )
+    slope, sent = call(
         second_kernel,
-        [((devices * MOST, part), f32), ((devices * MOST, part), bf16)],
-        [place, held, other, pre_act, w_in_near, w_out_near],
-        "svvvvv",
-        [pltpu.VMEM(acts, f32)],
+        [(acts, bf16), (halves, bf16)],
+        [near, other, pre_act, w_in_near, w_out_near],
+        "vvvvv",
     )
     came = swap(sent)
+    (kept,) = call(third_kernel, [(halves, f32)], [slope, w_in_near], "vv")
     (total,) = call(sum_kernel, [((devices, MOST, part), bf16)], [kept, came], "vv")
     back = lax.all_to_all(total, everyone, split_axis=0, concat_axis=0, tiled=True)
     return call(

time: 47.7 us -> 46.2 us (0.969)
  Pallas kernels: 10 us -> 8.45 us
    pallas_call x7 -> x8, Pallas kernels: 10 us -> 8.45 us  [call(): pl.pallas_call(kernel, out_shape=[jax.ShapeDtypeStruct(shape, dtype) for...]
    all_to_all x1, waiting for transfers between devices: 4.27 us -> 4.93 us  [body(): cot = lax.all_to_all(turned, 'frm', split_axis=0, concat_axis=0, tiled=True)]
  transfers between devices with their start and end apart: 3 -> 3, of which waited for: 2 -> 2; matrix products, arithmetic and copies ran while one was open for 0% -> 0% of each run, Pallas kernels for 10% -> 9%
where the time goes in v9:
time: 46.2 us; the launch traced here: 45.9 us
  blocking collectives  24.1 us (52%)
  Pallas kernels  8.45 us (18%)
  starting transfers between devices  6.91 us (15%)
  waiting for transfers between devices  5.73 us (12%)
  between operations  0.67 us (1%)
    all_to_all x1, blocking collectives, body(): lax.all_to_all(outgoing, everyone, split_axis=0, concat_axis=0, tiled=True)  13.9 us
    all_to_all x1, blocking collectives, body(): lax.all_to_all(total, everyone, split_axis=0, concat_axis=0, tiled=True)  10.3 us
    pallas_call x8, Pallas kernels, call(): pl.pallas_call(kernel, out_shape=[jax.ShapeDtypeStruct(shape, dtype) for...  8.45 us
    all_to_all x1, starting transfers between devices, body(): cot = lax.all_to_all(turned, 'frm', split_axis=0, concat_axis=0, tiled=True)  6.34 us
    all_to_all x1, waiting for transfers between devices, body(): cot = lax.all_to_all(turned, 'frm', split_axis=0, concat_axis=0, tiled=True)  4.93 us
  transfers between devices with their start and end apart: 3, of which 2 were waited for; matrix products, arithmetic and copies ran while one was open for 0% of the time, Pallas kernels for 9%

profile of v9, /device:TPU:0, one launch (start us, length us, event | category | flops | bytes accessed | tf_op | source)
XLA Modules:
  0.0 45.9 jit_solution(8501528386976431992)
XLA Ops:
  0.6 1.5 %shard_map.104 = bf16[8,4,2048]{2,1,0:T(4,128)(2,1)} custom-call(bf16[1,32,2048]{2,1,0:T(8,128)(2,1)} %cot_hbm.1), custom_call_target="tpu_custom_call" | custom-call | tf_op jit(solution)/shard_map/pallas_call | solution.py:291
  2.2 6.3 %all-to-all-start = ((bf16[8,4,2048]{2,1,0:T(4,128)(2,1)}), bf16[8,4,2048]{2,1,0:T(4,128)(2,1)S(1)}, u32[]{:S(2)}, u32[]{:S(2)}) async-start(bf16[8,4,2048]{2,1,0:T(4,128)(2,1)} %shard_map.104), calls=%async_computation | async-start | bytes 262144 | tf_op jit(solution)/shard_map/all_to_all | solution.py:330
  8.5 1.8 %shard_map.103 = (bf16[8,4,2048]{2,1,0:T(4,128)(2,1)S(1)}, bf16[8,4,2048]{2,1,0:T(4,128)(2,1)S(1)}, bf16[8,4,2048]{2,1,0:T(4,128)(2,1)S(1)}, bf16[2048,512]{1,0:...) custom-call(s32[2,32]{1,0:T(2,128)} %chosen_hbm.1, ...), custom_call_target="tpu_custom_call" | custom-call | tf_op jit(solution)/shard_map/pallas_call | solution.py:291
  10.4 4.9 %all-to-all-done.cot_ref = bf16[8,4,2048]{2,1,0:T(4,128)(2,1)S(1)} async-done(((bf16[8,4,2048]{2,1,0:T(4,128)(2,1)}), bf16[8,4,2048]{2,1,0:T(4,128)(2,1)S(1)}, u32[]{:S(2)}, u32[]{:S(2)}) %all-to-all-start) | async-done | bytes 131104 | tf_op jit(solution)/shard_map/all_to_all | solution.py:330
  15.3 0.2 shard_map.105
  15.5 13.9 %all_to_all.15.near_ref = bf16[32,2,2048]{2,1,0:T(2,128)(2,1)S(1)} all-to-all(bf16[32,2,2048]{2,1,0:T(2,128)(2,1)S(1)} %shard_map.105), channel_id=1, replica_groups=mesh['grp'=4,'frm'=8] {'grp','frm'}, dimensions={0} | all-to-all | bytes 524288 | tf_op jit(solution)/shard_map/all_to_all | solution.py:356
  29.3 0.4 collective-permute-start
  29.7 1.7 %shard_map.106 = (bf16[64,2048]{1,0:T(8,128)(2,1)S(1)}, f32[64,512]{1,0:T(8,128)S(1)}, bf16[512,2048]{1,0:T(8,128)(2,1)S(1)}) custom-call(bf16[32,2,2048]{2,1,0:T(2,128)(2,1)S(1)} %all_to_all.15.near_ref, bf16[2048,512]{1,0:T(8,128)(2,1)S(1)} %get-tuple-element.21.w_in_ref, bf16[1,512,2048]{2,1,0:T(8,128)(2,1)} %w_out_hbm.1), custom_call_target="tpu_custom_call" | custom-call | tf_op jit(solution)/shard_map/pallas_call | solution.py:291
  31.4 0.0 collective-permute-done.far_ref
  31.4 1.3 %shard_map.107 = (bf16[64,512]{1,0:T(8,128)(2,1)S(1)}, bf16[64,1024]{1,0:T(8,128)(2,1)S(1)}) custom-call(bf16[64,2048]{1,0:T(8,128)(2,1)S(1)} %get-tuple-element.22.near_ref, bf16[32,2,2048]{2,1,0:T(2,128)(2,1)S(1)} %collective-permute-done.far_ref, f32[64,512]{1,0:T(8,128)S(1)} %get-tuple-element.23.pre_ref, ...), custom_call_target="tpu_custom_call" | custom-call | tf_op jit(solution)/shard_map/pallas_call | solution.py:291
  32.7 0.2 collective-permute-start.1
  32.9 0.4 shard_map.108.kept_ref
  33.3 0.8 %collective-permute-done.1.came_ref = bf16[64,1024]{1,0:T(8,128)(2,1)S(1)} collective-permute-done((bf16[64,1024]{1,0:T(8,128)(2,1)S(1)}, bf16[64,1024]{1,0:T(8,128)(2,1)S(1)}, u32[]{:S(2)}, u32[]{:S(2)}) %collective-permute-start.1) | collective-permute-done | bytes 131104 | tf_op jit(solution)/shard_map/ppermute | solution.py:319
  34.2 10.3 %all_to_all.16.back_ref = bf16[32,2,1024]{2,1,0:T(2,128)(2,1)S(1)} all-to-all(bf16[32,2,1024]{2,1,0:T(2,128)(2,1)S(1)} %shard_map.109), channel_id=1, replica_groups=mesh['grp'=4,'frm'=8] {'grp','frm'}, dimensions={0} | all-to-all | bytes 262144 | tf_op jit(solution)/shard_map/all_to_all | solution.py:376
  44.5 1.4 %shard_map.110 = (bf16[8,4,2048]{2,1,0:T(4,128)(2,1)}, bf16[8,4,2048]{2,1,0:T(4,128)(2,1)}, bf16[8,4,2048]{2,1,0:T(4,128)(2,1)}) custom-call(bf16[2,32,64]{2,1,0:T(8,128)(2,1)S(1)} %get-tuple-element.17.spread_ref, bf16[32,2,1024]{2,1,0:T(2,128)(2,1)S(1)} %all_to_all.16.back_ref, bf16[8,4,2048]{2,1,0:T(4,128)(2,1)S(1)} %all-to-all-done.cot_ref, ...), custom_call_target="tpu_custom_call" | custom-call | tf_op jit(solution)/shard_map/pallas_call | solution.py:291
  (1 shorter events, 0.0 us)
Async XLA Ops:
  2.2 13.1 %all-to-all-start = ((bf16[8,4,2048]{2,1,0:T(4,128)(2,1)}), bf16[8,4,2048]{2,1,0:T(4,128)(2,1)S(1)}, u32[]{:S(2)}, u32[]{:S(2)}) async-start(bf16[8,4,2048]{2,1,0:T(4,128)(2,1)} %shard_map.104), calls=%async_computation | async-start | bytes 262144 | tf_op jit(solution)/shard_map/all_to_all | solution.py:330
  29.3 2.1 %collective-permute-start = (bf16[32,2,2048]{2,1,0:T(2,128)(2,1)S(1)}, bf16[32,2,2048]{2,1,0:T(2,128)(2,1)S(1)}, u32[]{:S(2)}, u32[]{:S(2)}) collective-permute-start(bf16[32,2,2048]{2,1,0:T(2,128)(2,1)S(1)} %all_to_all.15.near_ref), channel_id=1, source_target_pairs={{0,1},{1,0},{2,3},{3,2},{4,5},{5,4},{6,7},{7,6},{8,9},{9,8},{10,11... | collective-permute-start | bytes 786440 | tf_op jit(solution)/shard_map/ppermute | solution.py:319
  32.7 1.4 %collective-permute-start.1 = (bf16[64,1024]{1,0:T(8,128)(2,1)S(1)}, bf16[64,1024]{1,0:T(8,128)(2,1)S(1)}, u32[]{:S(2)}, u32[]{:S(2)}) collective-permute-start(bf16[64,1024]{1,0:T(8,128)(2,1)S(1)} %get-tuple-element.26), channel_id=1, source_target_pairs={{0,1},{1,0},{2,3},{3,2},{4,5},{5,4},{6,7},{7,6},{8,9},{9,8},{10,11... | collective-permute-start | bytes 393224 | tf_op jit(solution)/shard_map/ppermute | solution.py:319

commit v10 on v9

--- a/solution.py
+++ b/solution.py
@@ -12,7 +12,6 @@
 CORES = 2
 SUBLANES = 8
 LANES = 128
-TILE = 16
 
 root_half = 0.7071067811865476
 inv_root_tau = 0.3989422804014327
@@ -52,39 +51,19 @@
     return [values[:, h * width : (h + 1) * width] for h in range(HEADS)]
 
 
-def turn_kernel(cot_hbm, out_hbm, cot_ref, turned_ref, sems):
-    _, rows, _ = cot_ref.shape
-    columns, blocks, features = turned_ref.shape
-    pieces = rows // TILE
-    span = columns // pieces
-    arrivals = [
-        pltpu.make_async_copy(
-            cot_hbm.at[:, pl.ds(i * TILE, TILE)], cot_ref.at[:, pl.ds(i * TILE, TILE)], sems.at[0, i]
-        )
-        for i in range(pieces)
-    ]
-    for copy in arrivals:
-        copy.start()
-    leaving = []
-    for i, copy in enumerate(arrivals):
-        copy.wait()
-        part = slice(i * span, (i + 1) * span)
-        turned_ref[part] = cot_ref[0, i * TILE : (i + 1) * TILE, :].reshape(span, blocks, features)
-        copy = pltpu.make_async_copy(
-            turned_ref.at[pl.ds(i * span, span)], out_hbm.at[pl.ds(i * span, span)], sems.at[1, i]
-        )
-        copy.start()
-        leaving.append(copy)
-    for copy in leaving:
-        copy.wait()
+def turn_kernel(cot_hbm, out_ref, cot_ref, sem):
+    copy = pltpu.make_async_copy(cot_hbm, cot_ref, sem)
+    copy.start()
+    copy.wait()
+    out_ref[...] = cot_ref[...].reshape(out_ref.shape)
 
 
 def forward_kernel(
     patches_all, share,
     chosen_hbm, gate_hbm, query_hbm, key_hbm, value_hbm, w_in_hbm,
-    query_ref, key_ref, value_ref, w_in_ref,
+    query_rows_ref, key_rows_ref, value_rows_ref, w_in_ref,
     probs_ref, picked_ref, here_ref, weight_ref, spread_ref,
-    chosen_ref, gate_ref, sems,
+    chosen_ref, gate_ref, query_ref, key_ref, value_ref, sems,
 ):
     columns = lax.axis_size("frm")
     column = lax.axis_index("frm")
@@ -150,6 +129,9 @@
     query = query_ref[...].reshape(rows, features)
     key = key_ref[...].reshape(rows, features)
     value = value_ref[...].reshape(rows, features)
+    query_rows_ref[...] = query
+    key_rows_ref[...] = key
+    value_rows_ref[...] = value
     scores = jnp.concatenate(
         [dot_lanes(k, q) for k, q in zip(heads_of(key), heads_of(query))], axis=1
     )
@@ -170,9 +152,11 @@
         copy.wait()
 
 
-def pick_kernel(share, here_ref, weight_ref, picked_ref, cot_ref, out_ref):
+def pick_kernel(share, here_ref, weight_ref, picked_ref, cot_ref, out_ref, cot_rows_ref):
     frames, blocks, features = cot_ref.shape
-    rows = dot(here_ref[...].astype(jnp.bfloat16), cot_ref[...].reshape(frames * blocks, features))
+    cot = cot_ref[...].reshape(frames * blocks, features)
+    cot_rows_ref[...] = cot
+    rows = dot(here_ref[...].astype(jnp.bfloat16), cot)
     rows = (rows * weight_ref[:, :1]).astype(jnp.bfloat16)
     part = features // CORES
     picked = picked_ref[...]
@@ -191,7 +175,7 @@
     return pl.ds(pl.multiple_of(part * width, width), width)
 
 
-def first_kernel(near_ref, w_in_ref, w_out_hbm, rows_ref, pre_ref, w_out_ref, sems):
+def first_kernel(near_ref, w_in_ref, w_out_hbm, pre_ref, back_ref, w_out_ref, sems):
     width = w_in_ref.shape[0] // CORES
     copies = [
         pltpu.make_async_copy(
@@ -203,19 +187,19 @@
     ]
     for copy in copies:
         copy.start()
-    rows = near_ref[...].reshape(rows_ref.shape)
-    rows_ref[...] = rows
+    rows = near_ref[...].reshape(pre_ref.shape[0], CORES * width)
     pre_ref[...] = dot(rows[:, :width], w_in_ref[:width, :])
-    for copy in copies:
-        copy.wait()
-
-
-def second_kernel(near_ref, far_ref, pre_ref, w_in_ref, w_out_ref, slope_ref, sent_ref):
+    copies[0].wait()
+    back_ref[...] = dot_lanes(rows[:, width:], w_out_ref[:, :width])
+    for copy in copies[1:]:
+        copy.wait()
+
+
+def second_kernel(far_ref, pre_ref, back_ref, w_in_ref, w_out_ref, slope_ref, sent_ref):
     width = w_in_ref.shape[0] // CORES
-    far = far_ref[...].reshape(near_ref.shape)
+    far = far_ref[...].reshape(pre_ref.shape[0], CORES * width)
     pre_act = pre_ref[...] + dot(far[:, :width], w_in_ref[width:, :])
-    back_act = dot_lanes(near_ref[:, width:], w_out_ref[:, :width])
-    back_act = back_act + dot_lanes(far[:, width:], w_out_ref[:, width:])
+    back_act = back_ref[...] + dot_lanes(far[:, width:], w_out_ref[:, width:])
     slope = (back_act * gelu_slope(pre_act)).astype(jnp.bfloat16)
     slope_ref[...] = slope
     sent_ref[...] = dot_lanes(slope, w_in_ref[width:, :]).astype(jnp.bfloat16)
@@ -236,16 +220,13 @@
     grad_query_hbm, grad_key_hbm, grad_value_hbm,
     grad_query_ref, grad_key_ref, grad_value_ref, sems,
 ):
-    frames, blocks, features = query_ref.shape
+    frames, blocks, features = grad_query_ref.shape
     rows = frames * blocks
     scaling = (features // HEADS) ** (-0.5)
-    query = query_ref[...].reshape(rows, features)
-    key = key_ref[...].reshape(rows, features)
-    value = value_ref[...].reshape(rows, features)
+    query, key, value = query_ref[...], key_ref[...], value_ref[...]
     back = back_ref[...].reshape(-1, back_ref.shape[2])
     added = jnp.concatenate([dot(spread_ref[c], back) for c in range(CORES)], axis=1)
-    cot = cot_ref[...].reshape(rows, features)
-    stream = (cot.astype(jnp.float32) + added).astype(jnp.bfloat16)
+    stream = (cot_ref[...].astype(jnp.float32) + added).astype(jnp.bfloat16)
     probs = probs_ref[...]
     weights = probs.astype(jnp.bfloat16)
     copies = []
@@ -283,14 +264,16 @@
         copy.wait()
 
 
-def call(kernel, outs, operands, places, scratch=(), results="v"):
+def call(kernel, outs, operands, places, scratch=(), results="v", pinned=False):
     spaces = {
         "v": pl.BlockSpec(memory_space=pltpu.VMEM),
         "h": pl.BlockSpec(memory_space=pl.ANY),
     }
     return pl.pallas_call(
         kernel,
-        out_shape=[jax.ShapeDtypeStruct(shape, dtype) for shape, dtype in outs],
+        out_shape=[
+            (pltpu.VMEM if pinned else jax.ShapeDtypeStruct)(shape, dtype) for shape, dtype in outs
+        ],
         in_specs=[spaces[place] for place in places],
         out_specs=[spaces[results]] * len(outs),
         scratch_shapes=list(scratch),
@@ -319,19 +302,18 @@
         return lax.ppermute(values, "frm", [(i, i ^ 1) for i in range(columns)])
 
     (turned,) = call(
-        turn_kernel, [((columns, blocks, features), bf16)], [cotangent], "h",
-        [
-            pltpu.VMEM(cotangent.shape, bf16),
-            pltpu.VMEM((columns, blocks, features), bf16),
-            pltpu.SemaphoreType.DMA((2, cotangent.shape[1] // TILE)),
-        ],
+        turn_kernel,
+        [((columns, blocks, features), bf16)],
+        [cotangent],
         "h",
+        [pltpu.VMEM(cotangent.shape, bf16), pltpu.SemaphoreType.DMA],
+        pinned=True,
     )
     cot = lax.all_to_all(turned, "frm", split_axis=0, concat_axis=0, tiled=True)
     query, key, value, w_in_near, probs, picked, here, weight, spread = call(
         functools.partial(forward_kernel, blocks * devices, share),
         [
-            *[(array.shape, bf16) for array in (query_in, key_in, value_in)],
+            *[((rows, features), bf16)] * 3,
             (w_in.shape[1:], bf16),
             ((rows, HEADS * rows), f32),
             ((slots, features), bf16),
@@ -344,12 +326,13 @@
         [
             pltpu.VMEM(chosen.shape, jnp.int32),
             pltpu.VMEM(gate_probs.shape, f32),
+            *[pltpu.VMEM(query_in.shape, bf16)] * 3,
             pltpu.SemaphoreType.DMA((5 + CORES,)),
         ],
     )
-    (outgoing,) = call(
+    outgoing, cot = call(
         functools.partial(pick_kernel, share),
-        [((devices, MOST, 2 * part), bf16)],
+        [((devices, MOST, 2 * part), bf16), ((rows, features), bf16)],
         [here, weight, picked, cot],
         "vvvv",
     )
@@ -357,9 +340,9 @@
     other = swap(held)
     acts = (devices * MOST, hidden)
     halves = (devices * MOST, part)
-    near, pre_act, w_out_near = call(
+    pre_act, back_act, w_out_near = call(
         first_kernel,
-        [((devices * MOST, 2 * part), bf16), (acts, f32), (w_out.shape[1:], bf16)],
+        [(acts, f32), (acts, f32), (w_out.shape[1:], bf16)],
         [held, w_in_near, w_out],
         "vvh",
         [pltpu.SemaphoreType.DMA((CORES,))],
@@ -367,7 +350,7 @@
     slope, sent = call(
         second_kernel,
         [(acts, bf16), (halves, bf16)],
-        [near, other, pre_act, w_in_near, w_out_near],
+        [other, pre_act, back_act, w_in_near, w_out_near],
         "vvvvv",
     )
     came = swap(sent)

time: 46.2 us -> 46 us (level)
  no operation moved by 1% of the time
where the time goes in v10:
time: 46 us; the launch traced here: 45.7 us
  blocking collectives  24.1 us (52%)
  Pallas kernels  8.28 us (18%)
  starting transfers between devices  6.91 us (15%)
  waiting for transfers between devices  5.73 us (12%)
  between operations  0.67 us (1%)
    all_to_all x1, blocking collectives, body(): lax.all_to_all(outgoing, everyone, split_axis=0, concat_axis=0, tiled=True)  13.9 us
    all_to_all x1, blocking collectives, body(): lax.all_to_all(total, everyone, split_axis=0, concat_axis=0, tiled=True)  10.3 us
    pallas_call x8, Pallas kernels, call(): pl.pallas_call(kernel, out_shape=[(pltpu.VMEM if pinned else jax.ShapeDty...  8.28 us
    all_to_all x1, starting transfers between devices, body(): cot = lax.all_to_all(turned, 'frm', split_axis=0, concat_axis=0, tiled=True)  6.34 us
    all_to_all x1, waiting for transfers between devices, body(): cot = lax.all_to_all(turned, 'frm', split_axis=0, concat_axis=0, tiled=True)  4.93 us
  transfers between devices with their start and end apart: 3, of which 2 were waited for; matrix products, arithmetic and copies ran while one was open for 0% of the time, Pallas kernels for 9%

profile of v10, /device:TPU:0, one launch (start us, length us, event | category | flops | bytes accessed | tf_op | source)
XLA Modules:
  0.0 45.7 jit_solution(11167004172651240135)
XLA Ops:
  0.6 1.6 %shard_map.104 = bf16[8,4,2048]{2,1,0:T(4,128)(2,1)} custom-call(bf16[1,32,2048]{2,1,0:T(8,128)(2,1)} %cot_hbm.1), custom_call_target="tpu_custom_call" | custom-call | tf_op jit(solution)/shard_map/pallas_call | solution.py:272
  2.2 6.3 %all-to-all-start = ((bf16[8,4,2048]{2,1,0:T(4,128)(2,1)}), bf16[8,4,2048]{2,1,0:T(4,128)(2,1)S(1)}, u32[]{:S(2)}, u32[]{:S(2)}) async-start(bf16[8,4,2048]{2,1,0:T(4,128)(2,1)} %shard_map.104), calls=%async_computation | async-start | bytes 262144 | tf_op jit(solution)/shard_map/all_to_all | solution.py:312
  8.6 1.8 %shard_map.103 = (bf16[32,2048]{1,0:T(8,128)(2,1)S(1)}, bf16[32,2048]{1,0:T(8,128)(2,1)S(1)}, bf16[32,2048]{1,0:T(8,128)(2,1)S(1)}, bf16[2048,512]{1,0:T(8,128)(...) custom-call(s32[2,32]{1,0:T(2,128)} %chosen_hbm.1, ...), custom_call_target="tpu_custom_call" | custom-call | tf_op jit(solution)/shard_map/pallas_call | solution.py:272
  10.4 4.9 %all-to-all-done.cot_ref = bf16[8,4,2048]{2,1,0:T(4,128)(2,1)S(1)} async-done(((bf16[8,4,2048]{2,1,0:T(4,128)(2,1)}), bf16[8,4,2048]{2,1,0:T(4,128)(2,1)S(1)}, u32[]{:S(2)}, u32[]{:S(2)}) %all-to-all-start) | async-done | bytes 131104 | tf_op jit(solution)/shard_map/all_to_all | solution.py:312
  15.3 0.2 shard_map.105
  15.5 13.9 %all_to_all.15.near_ref = bf16[32,2,2048]{2,1,0:T(2,128)(2,1)S(1)} all-to-all(bf16[32,2,2048]{2,1,0:T(2,128)(2,1)S(1)} %get-tuple-element.23), channel_id=1, replica_groups=mesh['grp'=4,'frm'=8] {'grp','frm'}, dimensions={0} | all-to-all | bytes 524288 | tf_op jit(solution)/shard_map/all_to_all | solution.py:339
  29.3 0.4 collective-permute-start
  29.7 1.8 %shard_map.106 = (f32[64,512]{1,0:T(8,128)S(1)}, f32[64,512]{1,0:T(8,128)S(1)}, bf16[512,2048]{1,0:T(8,128)(2,1)S(1)}) custom-call(bf16[32,2,2048]{2,1,0:T(2,128)(2,1)S(1)} %all_to_all.15.near_ref, bf16[2048,512]{1,0:T(8,128)(2,1)S(1)} %get-tuple-element.24.w_in_ref, bf16[1,512,2048]{2,1,0:T(8,128)(2,1)} %w_out_hbm.1), custom_call_target="tpu_custom_call" | custom-call | tf_op jit(solution)/shard_map/pallas_call | solution.py:272
  31.6 0.0 collective-permute-done.far_ref
  31.6 1.0 %shard_map.107 = (bf16[64,512]{1,0:T(8,128)(2,1)S(1)}, bf16[64,1024]{1,0:T(8,128)(2,1)S(1)}) custom-call(bf16[32,2,2048]{2,1,0:T(2,128)(2,1)S(1)} %collective-permute-done.far_ref, f32[64,512]{1,0:T(8,128)S(1)} %get-tuple-element.25.pre_ref, f32[64,512]{1,0:T(8,128)S(1)} %get-tuple-element.26.back_ref, bf16[2048,512]{1,0:T(8,128)(2,1)S(1)} %get-tuple-element.24.w_in_ref, ...), custom_call_target="tpu_custom_call" | custom-call | tf_op jit(solution)/shard_map/pallas_call | solution.py:272
  32.6 0.2 collective-permute-start.1
  32.8 0.4 shard_map.108.kept_ref
  33.2 0.8 %collective-permute-done.1.came_ref = bf16[64,1024]{1,0:T(8,128)(2,1)S(1)} collective-permute-done((bf16[64,1024]{1,0:T(8,128)(2,1)S(1)}, bf16[64,1024]{1,0:T(8,128)(2,1)S(1)}, u32[]{:S(2)}, u32[]{:S(2)}) %collective-permute-start.1) | collective-permute-done | bytes 131104 | tf_op jit(solution)/shard_map/ppermute | solution.py:302
  34.0 10.3 %all_to_all.16.back_ref = bf16[32,2,1024]{2,1,0:T(2,128)(2,1)S(1)} all-to-all(bf16[32,2,1024]{2,1,0:T(2,128)(2,1)S(1)} %shard_map.109), channel_id=1, replica_groups=mesh['grp'=4,'frm'=8] {'grp','frm'}, dimensions={0} | all-to-all | bytes 262144 | tf_op jit(solution)/shard_map/all_to_all | solution.py:359
  44.3 1.4 %shard_map.110 = (bf16[8,4,2048]{2,1,0:T(4,128)(2,1)}, bf16[8,4,2048]{2,1,0:T(4,128)(2,1)}, bf16[8,4,2048]{2,1,0:T(4,128)(2,1)}) custom-call(bf16[2,32,64]{2,1,0:T(8,128)(2,1)S(1)} %get-tuple-element.19.spread_ref, bf16[32,2,1024]{2,1,0:T(2,128)(2,1)S(1)} %all_to_all.16.back_ref, bf16[32,2048]{1,0:T(8,128)(2,1)S(1)} %get-tuple-element.30.cot_ref, ...), custom_call_target="tpu_custom_call" | custom-call | tf_op jit(solution)/shard_map/pallas_call | solution.py:272
  (1 shorter events, 0.0 us)
Async XLA Ops:
  2.2 13.1 %all-to-all-start = ((bf16[8,4,2048]{2,1,0:T(4,128)(2,1)}), bf16[8,4,2048]{2,1,0:T(4,128)(2,1)S(1)}, u32[]{:S(2)}, u32[]{:S(2)}) async-start(bf16[8,4,2048]{2,1,0:T(4,128)(2,1)} %shard_map.104), calls=%async_computation | async-start | bytes 262144 | tf_op jit(solution)/shard_map/all_to_all | solution.py:312
  29.3 2.2 %collective-permute-start = (bf16[32,2,2048]{2,1,0:T(2,128)(2,1)S(1)}, bf16[32,2,2048]{2,1,0:T(2,128)(2,1)S(1)}, u32[]{:S(2)}, u32[]{:S(2)}) collective-permute-start(bf16[32,2,2048]{2,1,0:T(2,128)(2,1)S(1)} %all_to_all.15.near_ref), channel_id=1, source_target_pairs={{0,1},{1,0},{2,3},{3,2},{4,5},{5,4},{6,7},{7,6},{8,9},{9,8},{10,11... | collective-permute-start | bytes 786440 | tf_op jit(solution)/shard_map/ppermute | solution.py:302
  32.6 1.4 %collective-permute-start.1 = (bf16[64,1024]{1,0:T(8,128)(2,1)S(1)}, bf16[64,1024]{1,0:T(8,128)(2,1)S(1)}, u32[]{:S(2)}, u32[]{:S(2)}) collective-permute-start(bf16[64,1024]{1,0:T(8,128)(2,1)S(1)} %get-tuple-element.29), channel_id=1, source_target_pairs={{0,1},{1,0},{2,3},{3,2},{4,5},{5,4},{6,7},{7,6},{8,9},{9,8},{10,11... | collective-permute-start | bytes 393224 | tf_op jit(solution)/shard_map/ppermute | solution.py:302

commit v11 on v10

--- a/solution.py
+++ b/solution.py
@@ -5,6 +5,7 @@
 from jax import lax
 from jax.experimental import pallas as pl
 from jax.experimental.pallas import tpu as pltpu
+from jax.sharding import Mesh
 from jax.sharding import PartitionSpec as P
 
 HEADS = 16
@@ -51,27 +52,20 @@
     return [values[:, h * width : (h + 1) * width] for h in range(HEADS)]
 
 
-def turn_kernel(cot_hbm, out_ref, cot_ref, sem):
-    copy = pltpu.make_async_copy(cot_hbm, cot_ref, sem)
-    copy.start()
-    copy.wait()
-    out_ref[...] = cot_ref[...].reshape(out_ref.shape)
-
-
 def forward_kernel(
     patches_all, share,
     chosen_hbm, gate_hbm, query_hbm, key_hbm, value_hbm, w_in_hbm,
     query_rows_ref, key_rows_ref, value_rows_ref, w_in_ref,
-    probs_ref, picked_ref, here_ref, weight_ref, spread_ref,
+    probs_ref, picked_ref, take_ref, weight_ref, spread_ref,
     chosen_ref, gate_ref, query_ref, key_ref, value_ref, sems,
 ):
-    columns = lax.axis_size("frm")
-    column = lax.axis_index("frm")
+    core = lax.axis_index("core")
+    chip = lax.axis_index("grp") * lax.axis_size("z") + lax.axis_index("z")
     part = w_in_ref.shape[0] // CORES
     sources = [chosen_hbm, gate_hbm, query_hbm, key_hbm, value_hbm]
     targets = [chosen_ref, gate_ref, query_ref, key_ref, value_ref]
     for i in range(CORES):
-        sources.append(w_in_hbm.at[0, part_of(column % CORES ^ i, part)])
+        sources.append(w_in_hbm.at[0, part_of(core ^ i, part)])
         targets.append(w_in_ref.at[pl.ds(i * part, part)])
     copies = [
         pltpu.make_async_copy(source, target, sems.at[i])
@@ -86,40 +80,53 @@
     for copy in copies[:2]:
         copy.wait()
     experts, cap = chosen_ref.shape
-    myself = lax.axis_index("grp") * columns + column
     before = (
         lax.broadcasted_iota(jnp.int32, (cap, cap), 0)
         < lax.broadcasted_iota(jnp.int32, (cap, cap), 1)
     ).astype(jnp.bfloat16)
     slot = lax.broadcasted_iota(jnp.int32, (SUBLANES, cap), 0)
     row_at = lax.broadcasted_iota(jnp.int32, (rows, cap), 0)
+    span = CORES * blocks
+    slots = experts * MOST
     found = []
     for e in range(experts):
         tokens = chosen_ref[e : e + 1, :]
         gates = gate_ref[e : e + 1, :]
         patch = tokens % patches_all
-        owned = jnp.broadcast_to((patch // blocks == myself).astype(jnp.float32), slot.shape)
-        rank = dot(owned.astype(jnp.bfloat16), before)
-        taken = jnp.where((rank == slot.astype(jnp.float32)) & (owned > 0.0), 1.0, 0.0)
-        position = (tokens // patches_all) * blocks + patch % blocks
-        at_row = (row_at == position).astype(jnp.bfloat16)
-        here = dot_lanes(taken.astype(jnp.bfloat16), at_row)
-        weight = jnp.sum(taken * gates, axis=1, keepdims=True)
-        here_ref[e * MOST : (e + 1) * MOST, :] = here[:MOST]
-        weight_ref[e * MOST : (e + 1) * MOST, :] = jnp.broadcast_to(
-            weight[:MOST], (MOST, weight_ref.shape[1])
-        )
-        found.append(here[:MOST])
+        frame = tokens // patches_all
+        for i in range(CORES):
+            owned = patch // blocks == chip * CORES + (core ^ i)
+            owned = jnp.broadcast_to(owned.astype(jnp.float32), slot.shape)
+            rank = dot(owned.astype(jnp.bfloat16), before)
+            taken = jnp.where((rank == slot.astype(jnp.float32)) & (owned > 0.0), 1.0, 0.0)
+            weight = jnp.sum(taken * gates, axis=1, keepdims=True)
+            taken = taken.astype(jnp.bfloat16)
+            place = jnp.where(
+                frame % CORES == core,
+                (frame // CORES) * span + (core ^ i) * blocks + patch % blocks,
+                -1,
+            )
+            at = slice(i * slots + e * MOST, i * slots + (e + 1) * MOST)
+            take_ref[at] = dot_lanes(taken, (row_at == place).astype(jnp.bfloat16))[:MOST]
+            weight_ref[at] = jnp.broadcast_to(weight[:MOST], (MOST, weight_ref.shape[1]))
+            if i == 0:
+                position = frame * blocks + patch % blocks
+                found.append(dot_lanes(taken, (row_at == position).astype(jnp.bfloat16))[:MOST])
+    levels = rows // span
+    want = lax.broadcasted_iota(jnp.int32, (levels * blocks, rows), 0)
+    have = lax.broadcasted_iota(jnp.int32, (levels * blocks, rows), 1)
+    source = (want // blocks) * span + (core ^ 1) * blocks + want % blocks
+    take_ref[CORES * slots :] = (source == have).astype(jnp.float32)
     here = jnp.concatenate(found, axis=0).astype(jnp.bfloat16)
-    cores, _, returns = spread_ref.shape
+    _, _, returns = spread_ref.shape
     slot_at = lax.broadcasted_iota(jnp.int32, (experts * MOST, returns), 0)
     back_at = lax.broadcasted_iota(jnp.int32, (experts * MOST, returns), 1)
     sender = back_at // MOST
     same = (sender // share == slot_at // MOST) & (back_at % MOST == slot_at % MOST)
-    for c in range(cores):
+    for c in range(CORES):
         spread_ref[c] = lax.dot_general(
             here,
-            (same & (sender % cores == c)).astype(jnp.bfloat16),
+            (same & (sender % CORES == c)).astype(jnp.bfloat16),
             FIRST_BOTH,
             preferred_element_type=jnp.float32,
         ).astype(jnp.bfloat16)
@@ -152,12 +159,19 @@
         copy.wait()
 
 
-def pick_kernel(share, here_ref, weight_ref, picked_ref, cot_ref, out_ref, cot_rows_ref):
-    frames, blocks, features = cot_ref.shape
-    cot = cot_ref[...].reshape(frames * blocks, features)
-    cot_rows_ref[...] = cot
-    rows = dot(here_ref[...].astype(jnp.bfloat16), cot)
-    rows = (rows * weight_ref[:, :1]).astype(jnp.bfloat16)
+def pick_kernel(take_ref, weight_ref, cot_ref, mine_ref, sent_ref):
+    levels, span, features = cot_ref.shape
+    slots = mine_ref.shape[0]
+    rows = dot(take_ref[...].astype(jnp.bfloat16), cot_ref[...].reshape(levels * span, features))
+    picks = (rows[: CORES * slots] * weight_ref[:, :1]).astype(jnp.bfloat16)
+    mine_ref[...] = picks[:slots]
+    away = rows[CORES * slots :].astype(jnp.bfloat16)
+    sent_ref[...] = jnp.concatenate([away, picks[slots:]], axis=0)
+
+
+def pack_kernel(share, picked_ref, mine_ref, came_ref, out_ref):
+    slots, features = mine_ref.shape
+    rows = mine_ref[...] + came_ref[came_ref.shape[0] - slots :, :]
     part = features // CORES
     picked = picked_ref[...]
     both = [
@@ -179,7 +193,7 @@
     width = w_in_ref.shape[0] // CORES
     copies = [
         pltpu.make_async_copy(
-            w_out_hbm.at[0, :, part_of(lax.axis_index("frm") % CORES ^ i, width)],
+            w_out_hbm.at[0, :, part_of(lax.axis_index("core") ^ i, width)],
             w_out_ref.at[:, pl.ds(i * width, width)],
             sems.at[i],
         )
@@ -205,7 +219,22 @@
     sent_ref[...] = dot_lanes(slope, w_in_ref[width:, :]).astype(jnp.bfloat16)
 
 
-def third_kernel(slope_ref, w_in_ref, kept_ref):
+def third_kernel(slope_ref, w_in_ref, near_ref, came_ref, kept_ref, cot_ref):
+    core = lax.axis_index("core")
+    levels, span, features = near_ref.shape
+    blocks = span // CORES
+    rows = levels * span
+    want = lax.broadcasted_iota(jnp.int32, (rows, rows), 0)
+    have = lax.broadcasted_iota(jnp.int32, (rows, rows), 1)
+    frame = want // blocks
+    source = (frame // CORES) * span + core * blocks + want % blocks
+    own = ((frame % CORES == core) & (source == have)).astype(jnp.bfloat16)
+    want, have, frame = (values[:, : levels * blocks] for values in (want, have, frame))
+    source = (frame // CORES) * blocks + want % blocks
+    others = ((frame % CORES != core) & (source == have)).astype(jnp.bfloat16)
+    cot = dot(own, near_ref[...].reshape(rows, features))
+    cot = cot + dot(others, came_ref[: levels * blocks, :])
+    cot_ref[...] = cot.astype(jnp.bfloat16)
     width = kept_ref.shape[1]
     kept_ref[...] = dot_lanes(slope_ref[...], w_in_ref[:width, :])
 
@@ -264,16 +293,14 @@
         copy.wait()
 
 
-def call(kernel, outs, operands, places, scratch=(), results="v", pinned=False):
+def call(kernel, outs, operands, places, scratch=(), results="v"):
     spaces = {
         "v": pl.BlockSpec(memory_space=pltpu.VMEM),
         "h": pl.BlockSpec(memory_space=pl.ANY),
     }
     return pl.pallas_call(
         kernel,
-        out_shape=[
-            (pltpu.VMEM if pinned else jax.ShapeDtypeStruct)(shape, dtype) for shape, dtype in outs
-        ],
+        out_shape=[jax.ShapeDtypeStruct(shape, dtype) for shape, dtype in outs],
         in_specs=[spaces[place] for place in places],
         out_specs=[spaces[results]] * len(outs),
         scratch_shapes=list(scratch),
@@ -288,7 +315,8 @@
     bf16, f32 = jnp.bfloat16, jnp.float32
     frames, blocks, features = query_in.shape
     groups = lax.axis_size("grp")
-    columns = lax.axis_size("frm")
+    levels = lax.axis_size("z")
+    columns = levels * CORES
     experts = gate_probs.shape[0]
     devices = groups * columns
     share = devices // experts
@@ -296,29 +324,24 @@
     slots = experts * MOST
     part = features // CORES
     hidden = w_in.shape[2]
-    everyone = ("grp", "frm")
+    everyone = ("grp", "z", "core")
 
     def swap(values):
-        return lax.ppermute(values, "frm", [(i, i ^ 1) for i in range(columns)])
-
-    (turned,) = call(
-        turn_kernel,
-        [((columns, blocks, features), bf16)],
-        [cotangent],
-        "h",
-        [pltpu.VMEM(cotangent.shape, bf16), pltpu.SemaphoreType.DMA],
-        pinned=True,
-    )
-    cot = lax.all_to_all(turned, "frm", split_axis=0, concat_axis=0, tiled=True)
-    query, key, value, w_in_near, probs, picked, here, weight, spread = call(
+        return lax.ppermute(values, "core", [(i, i ^ 1) for i in range(CORES)])
+
+    cot_near = lax.all_to_all(
+        cotangent.reshape(levels, CORES * blocks, features),
+        "z", split_axis=0, concat_axis=0, tiled=True,
+    )
+    query, key, value, w_in_near, probs, picked, take, weight, spread = call(
         functools.partial(forward_kernel, blocks * devices, share),
         [
             *[((rows, features), bf16)] * 3,
             (w_in.shape[1:], bf16),
             ((rows, HEADS * rows), f32),
             ((slots, features), bf16),
-            ((slots, rows), f32),
-            ((slots, LANES), f32),
+            ((CORES * slots + levels * blocks, rows), f32),
+            ((CORES * slots, LANES), f32),
             ((CORES, rows, devices * MOST), bf16),
         ],
         [chosen, gate_probs, query_in, key_in, value_in, w_in],
@@ -330,11 +353,18 @@
             pltpu.SemaphoreType.DMA((5 + CORES,)),
         ],
     )
-    outgoing, cot = call(
-        functools.partial(pick_kernel, share),
-        [((devices, MOST, 2 * part), bf16), ((rows, features), bf16)],
-        [here, weight, picked, cot],
-        "vvvv",
+    mine, sent = call(
+        pick_kernel,
+        [((slots, features), bf16), ((levels * blocks + slots, features), bf16)],
+        [take, weight, cot_near],
+        "vvv",
+    )
+    came_near = swap(sent)
+    (outgoing,) = call(
+        functools.partial(pack_kernel, share),
+        [((devices, MOST, 2 * part), bf16)],
+        [picked, mine, came_near],
+        "vvv",
     )
     held = lax.all_to_all(outgoing, everyone, split_axis=0, concat_axis=0, tiled=True)
     other = swap(held)
@@ -354,7 +384,12 @@
         "vvvvv",
     )
     came = swap(sent)
-    (kept,) = call(third_kernel, [(halves, f32)], [slope, w_in_near], "vv")
+    kept, cot = call(
+        third_kernel,
+        [(halves, f32), ((rows, features), bf16)],
+        [slope, w_in_near, cot_near, came_near],
+        "vvvv",
+    )
     (total,) = call(sum_kernel, [((devices, MOST, part), bf16)], [kept, came], "vv")
     back = lax.all_to_all(total, everyone, split_axis=0, concat_axis=0, tiled=True)
     return call(
@@ -368,23 +403,17 @@
 
 
 def solution(mesh):
+    groups, columns = mesh.devices.shape
+    split = Mesh(mesh.devices.reshape(groups, columns // CORES, CORES), ("grp", "z", "core"))
+    frm = ("z", "core")
+    patches = P(None, ("grp",) + frm, None)
     return jax.shard_map(
         body,
-        mesh=mesh,
+        mesh=split,
         in_specs=(
-            P(None, ("grp", "frm"), None),
-            P(None, ("grp", "frm"), None),
-            P(None, ("grp", "frm"), None),
-            P("frm", "grp", None),
-            P("grp", None, "frm"),
-            P("grp", "frm", None),
-            P(),
-            P(),
+            patches, patches, patches, P(frm, "grp", None), P("grp", None, frm),
+            P("grp", frm, None), P(), P(),
         ),
-        out_specs=(
-            P(None, ("grp", "frm"), None),
-            P(None, ("grp", "frm"), None),
-            P(None, ("grp", "frm"), None),
-        ),
+        out_specs=(patches, patches, patches),
         check_vma=False,
     )

time: 46 us -> 45.2 us (0.983)
  Pallas kernels: 8.28 us -> 6.94 us
    pallas_call x8, Pallas kernels: 8.28 us -> 6.94 us  [call(): pl.pallas_call(kernel, out_shape=[jax.ShapeDtypeStruct(shape, dtype) for...]
    ppermute x2 -> x3, waiting for transfers between devices: 0.8 us -> 2 us  [swap(): return lax.ppermute(values, 'core', [(i, i ^ 1) for i in range(CORES)])]
    all_to_all x1, waiting for transfers between devices: 4.93 us -> 4.1 us  [body(): lax.all_to_all(cotangent.reshape(levels, CORES * blocks, features), 'z',...]
  transfers between devices with their start and end apart: 3 -> 4, of which waited for: 2 -> 3; matrix products, arithmetic and copies ran while one was open for 0% -> 0% of each run, Pallas kernels for 9% -> 10%
where the time goes in v11:
time: 45.2 us; the launch traced here: 44.9 us
  blocking collectives  24.2 us (54%)
  starting transfers between devices  6.97 us (15%)
  Pallas kernels  6.94 us (15%)
  waiting for transfers between devices  6.1 us (13%)
  between operations  0.69 us (2%)
    all_to_all x1, blocking collectives, body(): lax.all_to_all(outgoing, everyone, split_axis=0, concat_axis=0, tiled=True)  13.9 us
    all_to_all x1, blocking collectives, body(): lax.all_to_all(total, everyone, split_axis=0, concat_axis=0, tiled=True)  10.3 us
    pallas_call x8, Pallas kernels, call(): pl.pallas_call(kernel, out_shape=[jax.ShapeDtypeStruct(shape, dtype) for...  6.94 us
    all_to_all x1, starting transfers between devices, body(): lax.all_to_all(cotangent.reshape(levels, CORES * blocks, features), 'z',...  6.33 us
    all_to_all x1, waiting for transfers between devices, body(): lax.all_to_all(cotangent.reshape(levels, CORES * blocks, features), 'z',...  4.1 us
    ppermute x3, waiting for transfers between devices, swap(): return lax.ppermute(values, 'core', [(i, i ^ 1) for i in range(CORES)])  2 us
  transfers between devices with their start and end apart: 4, of which 3 were waited for; matrix products, arithmetic and copies ran while one was open for 0% of the time, Pallas kernels for 10%

profile of v11, /device:TPU:0, one launch (start us, length us, event | category | flops | bytes accessed | tf_op | source)
XLA Modules:
  0.0 44.9 jit_solution(7734947995118345054)
XLA Ops:
  0.6 6.3 %all-to-all-start = ((bf16[4,8,2048]{2,1,0:T(8,128)(2,1)}), bf16[4,8,2048]{2,1,0:T(8,128)(2,1)S(1)}, u32[]{:S(2)}, u32[]{:S(2)}) async-start(bf16[4,8,2048]{2,1,0:T(8,128)(2,1)} %bitcast.1), calls=%async_computation | async-start | bytes 262144 | tf_op jit(solution)/shard_map/all_to_all | solution.py:332
  7.0 2.0 %shard_map.103 = (bf16[32,2048]{1,0:T(8,128)(2,1)S(1)}, bf16[32,2048]{1,0:T(8,128)(2,1)S(1)}, bf16[32,2048]{1,0:T(8,128)(2,1)S(1)}, bf16[2048,512]{1,0:T(8,128)(...) custom-call(s32[2,32]{1,0:T(2,128)} %chosen_hbm.1, ...), custom_call_target="tpu_custom_call" | custom-call | tf_op jit(solution)/shard_map/pallas_call | solution.py:301
  8.9 4.1 %all-to-all-done.cot_ref.near_ref = bf16[4,8,2048]{2,1,0:T(8,128)(2,1)S(1)} async-done(((bf16[4,8,2048]{2,1,0:T(8,128)(2,1)}), bf16[4,8,2048]{2,1,0:T(8,128)(2,1)S(1)}, u32[]{:S(2)}, u32[]{:S(2)}) %all-to-all-start) | async-done | bytes 131104 | tf_op jit(solution)/shard_map/all_to_all | solution.py:332
  13.0 0.2 shard_map.104
  13.2 0.1 collective-permute-start
  13.3 1.3 %collective-permute-done.came_ref = bf16[20,2048]{1,0:T(8,128)(2,1)S(1)} collective-permute-done((bf16[20,2048]{1,0:T(8,128)(2,1)S(1)}, bf16[20,2048]{1,0:T(8,128)(2,1)S(1)}, u32[]{:S(2)}, u32[]{:S(2)}) %collective-permute-start) | collective-permute-done | bytes 81952 | tf_op jit(solution)/shard_map/ppermute | solution.py:330
  14.6 13.9 %all_to_all.15.near_ref = bf16[32,2,2048]{2,1,0:T(2,128)(2,1)S(1)} all-to-all(bf16[32,2,2048]{2,1,0:T(2,128)(2,1)S(1)} %shard_map.105), channel_id=1, replica_groups=mesh['grp'=4,'z'=4,'core'=2] {'grp','z','core'}, dimensions={0} | all-to-all | bytes 524288 | tf_op jit(solution)/shard_map/all_to_all | solution.py:369
  28.5 0.4 collective-permute-start.1
  28.9 1.8 %shard_map.106 = (f32[64,512]{1,0:T(8,128)S(1)}, f32[64,512]{1,0:T(8,128)S(1)}, bf16[512,2048]{1,0:T(8,128)(2,1)S(1)}) custom-call(bf16[32,2,2048]{2,1,0:T(2,128)(2,1)S(1)} %all_to_all.15.near_ref, bf16[2048,512]{1,0:T(8,128)(2,1)S(1)} %get-tuple-element.27.w_in_ref, bf16[1,512,2048]{2,1,0:T(8,128)(2,1)} %w_out_hbm.1), custom_call_target="tpu_custom_call" | custom-call | tf_op jit(solution)/shard_map/pallas_call | solution.py:301
  30.7 0.0 collective-permute-done.1.far_ref
  30.7 1.0 %shard_map.107 = (bf16[64,512]{1,0:T(8,128)(2,1)S(1)}, bf16[64,1024]{1,0:T(8,128)(2,1)S(1)}) custom-call(bf16[32,2,2048]{2,1,0:T(2,128)(2,1)S(1)} %collective-permute-done.1.far_ref, f32[64,512]{1,0:T(8,128)S(1)} %get-tuple-element.28.pre_ref, f32[64,512]{1,0:T(8,128)S(1)} %get-tuple-element.29.back_ref, bf16[2048,512]{1,0:T(8,128)(2,1)S(1)} %get-tuple-element.27.w_in_ref, ...), custom_call_target="tpu_custom_call" | custom-call | tf_op jit(solution)/shard_map/pallas_call | solution.py:301
  31.7 0.2 collective-permute-start.2
  31.9 0.5 %shard_map.108 = (f32[64,1024]{1,0:T(8,128)S(1)}, bf16[32,2048]{1,0:T(8,128)(2,1)S(1)}) custom-call(bf16[64,512]{1,0:T(8,128)(2,1)S(1)} %get-tuple-element.31.slope_ref, bf16[2048,512]{1,0:T(8,128)(2,1)S(1)} %get-tuple-element.27.w_in_ref, bf16[4,8,2048]{2,1,0:T(8,128)(2,1)S(1)} %all-to-all-done.cot_ref.near_ref, ...), custom_call_target="tpu_custom_call" | custom-call | tf_op jit(solution)/shard_map/pallas_call | solution.py:301
  32.4 0.7 %collective-permute-done.2.came_ref = bf16[64,1024]{1,0:T(8,128)(2,1)S(1)} collective-permute-done((bf16[64,1024]{1,0:T(8,128)(2,1)S(1)}, bf16[64,1024]{1,0:T(8,128)(2,1)S(1)}, u32[]{:S(2)}, u32[]{:S(2)}) %collective-permute-start.2) | collective-permute-done | bytes 131104 | tf_op jit(solution)/shard_map/ppermute | solution.py:330
  33.2 10.3 %all_to_all.16.back_ref = bf16[32,2,1024]{2,1,0:T(2,128)(2,1)S(1)} all-to-all(bf16[32,2,1024]{2,1,0:T(2,128)(2,1)S(1)} %shard_map.109), channel_id=1, replica_groups=mesh['grp'=4,'z'=4,'core'=2] {'grp','z','core'}, dimensions={0} | all-to-all | bytes 262144 | tf_op jit(solution)/shard_map/all_to_all | solution.py:394
  43.5 1.4 %shard_map.110 = (bf16[8,4,2048]{2,1,0:T(4,128)(2,1)}, bf16[8,4,2048]{2,1,0:T(4,128)(2,1)}, bf16[8,4,2048]{2,1,0:T(4,128)(2,1)}) custom-call(bf16[2,32,64]{2,1,0:T(8,128)(2,1)S(1)} %get-tuple-element.21.spread_ref, bf16[32,2,1024]{2,1,0:T(2,128)(2,1)S(1)} %all_to_all.16.back_ref, bf16[32,2048]{1,0:T(8,128)(2,1)S(1)} %get-tuple-element.34.cot_ref, ...), custom_call_target="tpu_custom_call" | custom-call | tf_op jit(solution)/shard_map/pallas_call | solution.py:301
  (2 shorter events, 0.1 us)
Async XLA Ops:
  0.6 12.4 %all-to-all-start = ((bf16[4,8,2048]{2,1,0:T(8,128)(2,1)}), bf16[4,8,2048]{2,1,0:T(8,128)(2,1)S(1)}, u32[]{:S(2)}, u32[]{:S(2)}) async-start(bf16[4,8,2048]{2,1,0:T(8,128)(2,1)} %bitcast.1), calls=%async_computation | async-start | bytes 262144 | tf_op jit(solution)/shard_map/all_to_all | solution.py:332
  13.2 1.4 %collective-permute-start = (bf16[20,2048]{1,0:T(8,128)(2,1)S(1)}, bf16[20,2048]{1,0:T(8,128)(2,1)S(1)}, u32[]{:S(2)}, u32[]{:S(2)}) collective-permute-start(bf16[20,2048]{1,0:T(8,128)(2,1)S(1)} %get-tuple-element.26), channel_id=1, source_target_pairs={{0,1},{1,0},{2,3},{3,2},{4,5},{5,4},{6,7},{7,6},{8,9},{9,8},{10,11... | collective-permute-start | bytes 245768 | tf_op jit(solution)/shard_map/ppermute | solution.py:330
  28.5 2.2 %collective-permute-start.1 = (bf16[32,2,2048]{2,1,0:T(2,128)(2,1)S(1)}, bf16[32,2,2048]{2,1,0:T(2,128)(2,1)S(1)}, u32[]{:S(2)}, u32[]{:S(2)}) collective-permute-start(bf16[32,2,2048]{2,1,0:T(2,128)(2,1)S(1)} %all_to_all.15.near_ref), channel_id=1, source_target_pairs={{0,1},{1,0},{2,3},{3,2},{4,5},{5,4},{6,7},{7,6},{8,9},{9,8},{10,11... | collective-permute-start | bytes 786440 | tf_op jit(solution)/shard_map/ppermute | solution.py:330
  31.7 1.4 %collective-permute-start.2 = (bf16[64,1024]{1,0:T(8,128)(2,1)S(1)}, bf16[64,1024]{1,0:T(8,128)(2,1)S(1)}, u32[]{:S(2)}, u32[]{:S(2)}) collective-permute-start(bf16[64,1024]{1,0:T(8,128)(2,1)S(1)} %get-tuple-element.33), channel_id=1, source_target_pairs={{0,1},{1,0},{2,3},{3,2},{4,5},{5,4},{6,7},{7,6},{8,9},{9,8},{10,11... | collective-permute-start | bytes 393224 | tf_op jit(solution)/shard_map/ppermute | solution.py:330

commit v12 on v11

--- a/solution.py
+++ b/solution.py
@@ -169,7 +169,7 @@
     sent_ref[...] = jnp.concatenate([away, picks[slots:]], axis=0)
 
 
-def pack_kernel(share, picked_ref, mine_ref, came_ref, out_ref):
+def pack_kernel(share, picked_ref, mine_ref, came_ref, w_out_near_ref, out_ref):
     slots, features = mine_ref.shape
     rows = mine_ref[...] + came_ref[came_ref.shape[0] - slots :, :]
     part = features // CORES
@@ -189,31 +189,36 @@
     return pl.ds(pl.multiple_of(part * width, width), width)
 
 
-def first_kernel(near_ref, w_in_ref, w_out_hbm, pre_ref, back_ref, w_out_ref, sems):
+def half_copy(i, w_out_hbm, half_ref, sem):
+    width = half_ref.shape[1]
+    return pltpu.make_async_copy(
+        w_out_hbm.at[0, :, part_of(lax.axis_index("core") ^ i, width)], half_ref, sem
+    )
+
+
+def load_kernel(after_ref, w_out_hbm, half_ref, sem):
+    copy = half_copy(0, w_out_hbm, half_ref, sem)
+    copy.start()
+    copy.wait()
+
+
+def first_kernel(
+    near_ref, w_in_ref, w_out_near_ref, w_out_hbm, pre_ref, back_ref, w_out_far_ref, sem
+):
+    copy = half_copy(1, w_out_hbm, w_out_far_ref, sem)
+    copy.start()
     width = w_in_ref.shape[0] // CORES
-    copies = [
-        pltpu.make_async_copy(
-            w_out_hbm.at[0, :, part_of(lax.axis_index("core") ^ i, width)],
-            w_out_ref.at[:, pl.ds(i * width, width)],
-            sems.at[i],
-        )
-        for i in range(CORES)
-    ]
-    for copy in copies:
-        copy.start()
     rows = near_ref[...].reshape(pre_ref.shape[0], CORES * width)
     pre_ref[...] = dot(rows[:, :width], w_in_ref[:width, :])
-    copies[0].wait()
-    back_ref[...] = dot_lanes(rows[:, width:], w_out_ref[:, :width])
-    for copy in copies[1:]:
-        copy.wait()
-
-
-def second_kernel(far_ref, pre_ref, back_ref, w_in_ref, w_out_ref, slope_ref, sent_ref):
+    back_ref[...] = dot_lanes(rows[:, width:], w_out_near_ref[...])
+    copy.wait()
+
+
+def second_kernel(far_ref, pre_ref, back_ref, w_in_ref, w_out_far_ref, slope_ref, sent_ref):
     width = w_in_ref.shape[0] // CORES
     far = far_ref[...].reshape(pre_ref.shape[0], CORES * width)
     pre_act = pre_ref[...] + dot(far[:, :width], w_in_ref[width:, :])
-    back_act = back_ref[...] + dot_lanes(far[:, width:], w_out_ref[:, width:])
+    back_act = back_ref[...] + dot_lanes(far[:, width:], w_out_far_ref[...])
     slope = (back_act * gelu_slope(pre_act)).astype(jnp.bfloat16)
     slope_ref[...] = slope
     sent_ref[...] = dot_lanes(slope, w_in_ref[width:, :]).astype(jnp.bfloat16)
@@ -360,27 +365,31 @@
         "vvv",
     )
     came_near = swap(sent)
+    half = (hidden, part)
+    (w_out_near,) = call(
+        load_kernel, [(half, bf16)], [mine, w_out], "vh", [pltpu.SemaphoreType.DMA]
+    )
     (outgoing,) = call(
         functools.partial(pack_kernel, share),
         [((devices, MOST, 2 * part), bf16)],
-        [picked, mine, came_near],
-        "vvv",
+        [picked, mine, came_near, w_out_near],
+        "vvvv",
     )
     held = lax.all_to_all(outgoing, everyone, split_axis=0, concat_axis=0, tiled=True)
     other = swap(held)
     acts = (devices * MOST, hidden)
     halves = (devices * MOST, part)
-    pre_act, back_act, w_out_near = call(
+    pre_act, back_act, w_out_far = call(
         first_kernel,
-        [(acts, f32), (acts, f32), (w_out.shape[1:], bf16)],
-        [held, w_in_near, w_out],
-        "vvh",
-        [pltpu.SemaphoreType.DMA((CORES,))],
+        [(acts, f32), (acts, f32), (half, bf16)],
+        [held, w_in_near, w_out_near, w_out],
+        "vvvh",
+        [pltpu.SemaphoreType.DMA],
     )
     slope, sent = call(
         second_kernel,
         [(acts, bf16), (halves, bf16)],
-        [other, pre_act, back_act, w_in_near, w_out_near],
+        [other, pre_act, back_act, w_in_near, w_out_far],
         "vvvvv",
     )
     came = swap(sent)

time: 45.2 us -> 45.1 us (level)
  waiting for transfers between devices: 6.1 us -> 4.84 us
  Pallas kernels: 6.94 us -> 8.02 us
    ppermute x3, waiting for transfers between devices: 2 us -> 0.73 us  [swap(): return lax.ppermute(values, 'core', [(i, i ^ 1) for i in range(CORES)])]
    pallas_call x8 -> x9, Pallas kernels: 6.94 us -> 8.02 us  [call(): pl.pallas_call(kernel, out_shape=[jax.ShapeDtypeStruct(shape, dtype) for...]
  transfers between devices with their start and end apart: 4 -> 4, of which waited for: 3 -> 2; matrix products, arithmetic and copies ran while one was open for 0% -> 0% of each run, Pallas kernels for 10% -> 12%
where the time goes in v12:
time: 45.1 us; the launch traced here: 44.8 us
  blocking collectives  24.2 us (54%)
  Pallas kernels  8.02 us (18%)
  starting transfers between devices  6.98 us (15%)
  waiting for transfers between devices  4.84 us (11%)
  between operations  0.7 us (2%)
    all_to_all x1, blocking collectives, body(): lax.all_to_all(outgoing, everyone, split_axis=0, concat_axis=0, tiled=True)  14 us
    all_to_all x1, blocking collectives, body(): lax.all_to_all(total, everyone, split_axis=0, concat_axis=0, tiled=True)  10.3 us
    pallas_call x9, Pallas kernels, call(): pl.pallas_call(kernel, out_shape=[jax.ShapeDtypeStruct(shape, dtype) for...  8.02 us
    all_to_all x1, starting transfers between devices, body(): lax.all_to_all(cotangent.reshape(levels, CORES * blocks, features), 'z',...  6.33 us
    all_to_all x1, waiting for transfers between devices, body(): lax.all_to_all(cotangent.reshape(levels, CORES * blocks, features), 'z',...  4.1 us
  transfers between devices with their start and end apart: 4, of which 2 were waited for; matrix products, arithmetic and copies ran while one was open for 0% of the time, Pallas kernels for 12%

profile of v12, /device:TPU:0, one launch (start us, length us, event | category | flops | bytes accessed | tf_op | source)
XLA Modules:
  0.0 44.8 jit_solution(453976351563202587)
XLA Ops:
  0.6 6.3 %all-to-all-start = ((bf16[4,8,2048]{2,1,0:T(8,128)(2,1)}), bf16[4,8,2048]{2,1,0:T(8,128)(2,1)S(1)}, u32[]{:S(2)}, u32[]{:S(2)}) async-start(bf16[4,8,2048]{2,1,0:T(8,128)(2,1)} %bitcast.1), calls=%async_computation | async-start | bytes 262144 | tf_op jit(solution)/shard_map/all_to_all | solution.py:337
  7.0 2.0 %shard_map.103 = (bf16[32,2048]{1,0:T(8,128)(2,1)S(1)}, bf16[32,2048]{1,0:T(8,128)(2,1)S(1)}, bf16[32,2048]{1,0:T(8,128)(2,1)S(1)}, bf16[2048,512]{1,0:T(8,128)(...) custom-call(s32[2,32]{1,0:T(2,128)} %chosen_hbm.1, ...), custom_call_target="tpu_custom_call" | custom-call | tf_op jit(solution)/shard_map/pallas_call | solution.py:306
  8.9 4.1 %all-to-all-done.cot_ref.near_ref = bf16[4,8,2048]{2,1,0:T(8,128)(2,1)S(1)} async-done(((bf16[4,8,2048]{2,1,0:T(8,128)(2,1)}), bf16[4,8,2048]{2,1,0:T(8,128)(2,1)S(1)}, u32[]{:S(2)}, u32[]{:S(2)}) %all-to-all-start) | async-done | bytes 131104 | tf_op jit(solution)/shard_map/all_to_all | solution.py:337
  13.0 0.2 shard_map.104
  13.2 0.1 collective-permute-start
  13.3 1.2 %shard_map.105.w_out_near_ref = bf16[512,1024]{1,0:T(8,128)(2,1)S(1)} custom-call(bf16[4,2048]{1,0:T(4,128)(2,1)S(1)} %get-tuple-element.25.after_ref.mine_ref, bf16[1,512,2048]{2,1,0:T(8,128)(2,1)} %w_out_hbm.3), custom_call_target="tpu_custom_call" | custom-call | tf_op jit(solution)/shard_map/pallas_call | solution.py:306
  14.5 0.0 collective-permute-done.came_ref
  14.6 14.0 %all_to_all.15.near_ref = bf16[32,2,2048]{2,1,0:T(2,128)(2,1)S(1)} all-to-all(bf16[32,2,2048]{2,1,0:T(2,128)(2,1)S(1)} %shard_map.106), channel_id=1, replica_groups=mesh['grp'=4,'z'=4,'core'=2] {'grp','z','core'}, dimensions={0} | all-to-all | bytes 524288 | tf_op jit(solution)/shard_map/all_to_all | solution.py:378
  28.6 0.4 collective-permute-start.1
  28.9 1.7 %shard_map.107 = (f32[64,512]{1,0:T(8,128)S(1)}, f32[64,512]{1,0:T(8,128)S(1)}, bf16[512,1024]{1,0:T(8,128)(2,1)S(1)}) custom-call(bf16[32,2,2048]{2,1,0:T(2,128)(2,1)S(1)} %all_to_all.15.near_ref, bf16[2048,512]{1,0:T(8,128)(2,1)S(1)} %get-tuple-element.27.w_in_ref, bf16[512,1024]{1,0:T(8,128)(2,1)S(1)} %shard_map.105.w_out_near_ref, ...), custom_call_target="tpu_custom_call" | custom-call | tf_op jit(solution)/shard_map/pallas_call | solution.py:306
  30.6 0.0 collective-permute-done.1.far_ref
  30.6 1.0 %shard_map.108 = (bf16[64,512]{1,0:T(8,128)(2,1)S(1)}, bf16[64,1024]{1,0:T(8,128)(2,1)S(1)}) custom-call(bf16[32,2,2048]{2,1,0:T(2,128)(2,1)S(1)} %collective-permute-done.1.far_ref, f32[64,512]{1,0:T(8,128)S(1)} %get-tuple-element.28.pre_ref, f32[64,512]{1,0:T(8,128)S(1)} %get-tuple-element.29.back_ref, bf16[2048,512]{1,0:T(8,128)(2,1)S(1)} %get-tuple-element.27.w_in_ref, ...), custom_call_target="tpu_custom_call" | custom-call | tf_op jit(solution)/shard_map/pallas_call | solution.py:306
  31.6 0.2 collective-permute-start.2
  31.8 0.5 %shard_map.109 = (f32[64,1024]{1,0:T(8,128)S(1)}, bf16[32,2048]{1,0:T(8,128)(2,1)S(1)}) custom-call(bf16[64,512]{1,0:T(8,128)(2,1)S(1)} %get-tuple-element.31.slope_ref, bf16[2048,512]{1,0:T(8,128)(2,1)S(1)} %get-tuple-element.27.w_in_ref, bf16[4,8,2048]{2,1,0:T(8,128)(2,1)S(1)} %all-to-all-done.cot_ref.near_ref, ...), custom_call_target="tpu_custom_call" | custom-call | tf_op jit(solution)/shard_map/pallas_call | solution.py:306
  32.3 0.7 %collective-permute-done.2.came_ref = bf16[64,1024]{1,0:T(8,128)(2,1)S(1)} collective-permute-done((bf16[64,1024]{1,0:T(8,128)(2,1)S(1)}, bf16[64,1024]{1,0:T(8,128)(2,1)S(1)}, u32[]{:S(2)}, u32[]{:S(2)}) %collective-permute-start.2) | collective-permute-done | bytes 131104 | tf_op jit(solution)/shard_map/ppermute | solution.py:335
  33.1 10.3 %all_to_all.16.back_ref = bf16[32,2,1024]{2,1,0:T(2,128)(2,1)S(1)} all-to-all(bf16[32,2,1024]{2,1,0:T(2,128)(2,1)S(1)} %shard_map.110), channel_id=1, replica_groups=mesh['grp'=4,'z'=4,'core'=2] {'grp','z','core'}, dimensions={0} | all-to-all | bytes 262144 | tf_op jit(solution)/shard_map/all_to_all | solution.py:403
  43.4 1.4 %shard_map.111 = (bf16[8,4,2048]{2,1,0:T(4,128)(2,1)}, bf16[8,4,2048]{2,1,0:T(4,128)(2,1)}, bf16[8,4,2048]{2,1,0:T(4,128)(2,1)}) custom-call(bf16[2,32,64]{2,1,0:T(8,128)(2,1)S(1)} %get-tuple-element.21.spread_ref, bf16[32,2,1024]{2,1,0:T(2,128)(2,1)S(1)} %all_to_all.16.back_ref, bf16[32,2048]{1,0:T(8,128)(2,1)S(1)} %get-tuple-element.34.cot_ref, ...), custom_call_target="tpu_custom_call" | custom-call | tf_op jit(solution)/shard_map/pallas_call | solution.py:306
  (2 shorter events, 0.1 us)
Async XLA Ops:
  0.6 12.4 %all-to-all-start = ((bf16[4,8,2048]{2,1,0:T(8,128)(2,1)}), bf16[4,8,2048]{2,1,0:T(8,128)(2,1)S(1)}, u32[]{:S(2)}, u32[]{:S(2)}) async-start(bf16[4,8,2048]{2,1,0:T(8,128)(2,1)} %bitcast.1), calls=%async_computation | async-start | bytes 262144 | tf_op jit(solution)/shard_map/all_to_all | solution.py:337
  13.2 1.4 %collective-permute-start = (bf16[20,2048]{1,0:T(8,128)(2,1)S(1)}, bf16[20,2048]{1,0:T(8,128)(2,1)S(1)}, u32[]{:S(2)}, u32[]{:S(2)}) collective-permute-start(bf16[20,2048]{1,0:T(8,128)(2,1)S(1)} %get-tuple-element.26), channel_id=1, source_target_pairs={{0,1},{1,0},{2,3},{3,2},{4,5},{5,4},{6,7},{7,6},{8,9},{9,8},{10,11... | collective-permute-start | bytes 245768 | tf_op jit(solution)/shard_map/ppermute | solution.py:335
  28.6 2.1 %collective-permute-start.1 = (bf16[32,2,2048]{2,1,0:T(2,128)(2,1)S(1)}, bf16[32,2,2048]{2,1,0:T(2,128)(2,1)S(1)}, u32[]{:S(2)}, u32[]{:S(2)}) collective-permute-start(bf16[32,2,2048]{2,1,0:T(2,128)(2,1)S(1)} %all_to_all.15.near_ref), channel_id=1, source_target_pairs={{0,1},{1,0},{2,3},{3,2},{4,5},{5,4},{6,7},{7,6},{8,9},{9,8},{10,11... | collective-permute-start | bytes 786440 | tf_op jit(solution)/shard_map/ppermute | solution.py:335
  31.6 1.4 %collective-permute-start.2 = (bf16[64,1024]{1,0:T(8,128)(2,1)S(1)}, bf16[64,1024]{1,0:T(8,128)(2,1)S(1)}, u32[]{:S(2)}, u32[]{:S(2)}) collective-permute-start(bf16[64,1024]{1,0:T(8,128)(2,1)S(1)} %get-tuple-element.33), channel_id=1, source_target_pairs={{0,1},{1,0},{2,3},{3,2},{4,5},{5,4},{6,7},{7,6},{8,9},{9,8},{10,11... | collective-permute-start | bytes 393224 | tf_op jit(solution)/shard_map/ppermute | solution.py:335

commit v13 on v12

--- a/solution.py
+++ b/solution.py
@@ -159,30 +159,37 @@
         copy.wait()
 
 
-def pick_kernel(take_ref, weight_ref, cot_ref, mine_ref, sent_ref):
+def pick_kernel(take_ref, weight_ref, picked_ref, cot_ref, mine_ref, sent_ref):
     levels, span, features = cot_ref.shape
-    slots = mine_ref.shape[0]
+    slots = picked_ref.shape[0]
     rows = dot(take_ref[...].astype(jnp.bfloat16), cot_ref[...].reshape(levels * span, features))
     picks = (rows[: CORES * slots] * weight_ref[:, :1]).astype(jnp.bfloat16)
-    mine_ref[...] = picks[:slots]
+    mine_ref[...] = picks
     away = rows[CORES * slots :].astype(jnp.bfloat16)
-    sent_ref[...] = jnp.concatenate([away, picks[slots:]], axis=0)
+    sent_ref[...] = jnp.concatenate([away, picks[slots:], picks[:slots], picked_ref[...]], axis=0)
 
 
 def pack_kernel(share, picked_ref, mine_ref, came_ref, w_out_near_ref, out_ref):
-    slots, features = mine_ref.shape
-    rows = mine_ref[...] + came_ref[came_ref.shape[0] - slots :, :]
+    core = lax.axis_index("core")
+    slots, features = picked_ref.shape
     part = features // CORES
-    picked = picked_ref[...]
-    both = [
-        jnp.concatenate(
-            [half[:, c * part : (c + 1) * part] for half in (picked, rows)], axis=1
-        )
-        for c in range(CORES)
-    ]
+    came = came_ref[came_ref.shape[0] - 3 * slots :, :]
+    cots = mine_ref[...] + came[: 2 * slots]
+    near = jnp.concatenate([picked_ref[...], cots[:slots]], axis=1)
+    far = jnp.concatenate([came[2 * slots :], cots[slots:]], axis=1)
+
+    def columns(values):
+        quarters = [values[:, i * part : (i + 1) * part] for i in range(2 * CORES)]
+        low = jnp.concatenate(quarters[0::2], axis=1)
+        high = jnp.concatenate(quarters[1::2], axis=1)
+        return jnp.where(core == 0, low, high)
+
+    near, far = columns(near), columns(far)
+    pair = [jnp.where(core == 0, near, far), jnp.where(core == 0, far, near)]
     for e in range(out_ref.shape[0] // share):
+        both = jnp.concatenate([rows[e * MOST : (e + 1) * MOST] for rows in pair], axis=0)
         for i in range(share):
-            out_ref[e * share + i] = both[i % CORES][e * MOST : (e + 1) * MOST]
+            out_ref[e * share + i] = both
 
 
 def part_of(part, width):
@@ -360,9 +367,9 @@
     )
     mine, sent = call(
         pick_kernel,
-        [((slots, features), bf16), ((levels * blocks + slots, features), bf16)],
-        [take, weight, cot_near],
-        "vvv",
+        [((CORES * slots, features), bf16), ((levels * blocks + 3 * slots, features), bf16)],
+        [take, weight, picked, cot_near],
+        "vvvv",
     )
     came_near = swap(sent)
     half = (hidden, part)
@@ -370,12 +377,12 @@
         load_kernel, [(half, bf16)], [mine, w_out], "vh", [pltpu.SemaphoreType.DMA]
     )
     (outgoing,) = call(
-        functools.partial(pack_kernel, share),
-        [((devices, MOST, 2 * part), bf16)],
+        functools.partial(pack_kernel, share // CORES),
+        [((devices // CORES, CORES * MOST, 2 * part), bf16)],
         [picked, mine, came_near, w_out_near],
         "vvvv",
     )
-    held = lax.all_to_all(outgoing, everyone, split_axis=0, concat_axis=0, tiled=True)
+    held = lax.all_to_all(outgoing, ("grp", "z"), split_axis=0, concat_axis=0, tiled=True)
     other = swap(held)
     acts = (devices * MOST, hidden)
     halves = (devices * MOST, part)

time: 45.1 us -> 46.3 us (1.027)
  blocking collectives: 24.2 us -> 25.6 us
    all_to_all x1, blocking collectives: 14 us -> 15.7 us  [body(): lax.all_to_all(outgoing, ('grp', 'z'), split_axis=0, concat_axis=0, tiled...]
  transfers between devices with their start and end apart: 4 -> 4, of which waited for: 2 -> 3; matrix products, arithmetic and copies ran while one was open for 0% -> 0% of each run, Pallas kernels for 12% -> 12%
where the time goes in v13:
time: 46.3 us; the launch traced here: 45.9 us
  blocking collectives  25.6 us (55%)
  Pallas kernels  8.06 us (17%)
  starting transfers between devices  6.98 us (15%)
  waiting for transfers between devices  4.65 us (10%)
  between operations  0.7 us (2%)
    all_to_all x1, blocking collectives, body(): lax.all_to_all(outgoing, ('grp', 'z'), split_axis=0, concat_axis=0, tiled...  15.7 us
    all_to_all x1, blocking collectives, body(): lax.all_to_all(total, everyone, split_axis=0, concat_axis=0, tiled=True)  9.88 us
    pallas_call x9, Pallas kernels, call(): pl.pallas_call(kernel, out_shape=[jax.ShapeDtypeStruct(shape, dtype) for...  8.06 us
    all_to_all x1, starting transfers between devices, body(): lax.all_to_all(cotangent.reshape(levels, CORES * blocks, features), 'z',...  6.33 us
    all_to_all x1, waiting for transfers between devices, body(): lax.all_to_all(cotangent.reshape(levels, CORES * blocks, features), 'z',...  4.1 us
  transfers between devices with their start and end apart: 4, of which 3 were waited for; matrix products, arithmetic and copies ran while one was open for 0% of the time, Pallas kernels for 12%

profile of v13, /device:TPU:0, one launch (start us, length us, event | category | flops | bytes accessed | tf_op | source)
XLA Modules:
  0.0 45.9 jit_solution(10398574453501995631)
XLA Ops:
  0.6 6.3 %all-to-all-start = ((bf16[4,8,2048]{2,1,0:T(8,128)(2,1)}), bf16[4,8,2048]{2,1,0:T(8,128)(2,1)S(1)}, u32[]{:S(2)}, u32[]{:S(2)}) async-start(bf16[4,8,2048]{2,1,0:T(8,128)(2,1)} %bitcast.1), calls=%async_computation | async-start | bytes 262144 | tf_op jit(solution)/shard_map/all_to_all | solution.py:344
  7.0 2.0 %shard_map.103 = (bf16[32,2048]{1,0:T(8,128)(2,1)S(1)}, bf16[32,2048]{1,0:T(8,128)(2,1)S(1)}, bf16[32,2048]{1,0:T(8,128)(2,1)S(1)}, bf16[2048,512]{1,0:T(8,128)(...) custom-call(s32[2,32]{1,0:T(2,128)} %chosen_hbm.1, ...), custom_call_target="tpu_custom_call" | custom-call | tf_op jit(solution)/shard_map/pallas_call | solution.py:313
  8.9 4.1 %all-to-all-done.cot_ref.near_ref = bf16[4,8,2048]{2,1,0:T(8,128)(2,1)S(1)} async-done(((bf16[4,8,2048]{2,1,0:T(8,128)(2,1)}), bf16[4,8,2048]{2,1,0:T(8,128)(2,1)S(1)}, u32[]{:S(2)}, u32[]{:S(2)}) %all-to-all-start) | async-done | bytes 131104 | tf_op jit(solution)/shard_map/all_to_all | solution.py:344
  13.0 0.2 shard_map.104
  13.2 0.1 collective-permute-start
  13.3 1.2 %shard_map.105.w_out_near_ref = bf16[512,1024]{1,0:T(8,128)(2,1)S(1)} custom-call(bf16[8,2048]{1,0:T(8,128)(2,1)S(1)} %get-tuple-element.25.after_ref.mine_ref, bf16[1,512,2048]{2,1,0:T(8,128)(2,1)} %w_out_hbm.3), custom_call_target="tpu_custom_call" | custom-call | tf_op jit(solution)/shard_map/pallas_call | solution.py:313
  14.5 0.1 collective-permute-done.came_ref
  14.7 15.7 %all_to_all.15.near_ref = bf16[16,4,2048]{2,1,0:T(4,128)(2,1)S(1)} all-to-all(bf16[16,4,2048]{2,1,0:T(4,128)(2,1)S(1)} %shard_map.106), channel_id=1, replica_groups=mesh['grp'=4,'z'=4,'core'=2] {'grp','z'}, dimensions={0} | all-to-all | bytes 524288 | tf_op jit(solution)/shard_map/all_to_all | solution.py:385
  30.4 0.0 collective-permute-start.1
  30.4 1.7 %shard_map.107 = (f32[64,512]{1,0:T(8,128)S(1)}, f32[64,512]{1,0:T(8,128)S(1)}, bf16[512,1024]{1,0:T(8,128)(2,1)S(1)}) custom-call(bf16[16,4,2048]{2,1,0:T(4,128)(2,1)S(1)} %all_to_all.15.near_ref, bf16[2048,512]{1,0:T(8,128)(2,1)S(1)} %get-tuple-element.27.w_in_ref, bf16[512,1024]{1,0:T(8,128)(2,1)S(1)} %shard_map.105.w_out_near_ref, ...), custom_call_target="tpu_custom_call" | custom-call | tf_op jit(solution)/shard_map/pallas_call | solution.py:313
  32.1 0.0 collective-permute-done.1.far_ref
  32.1 1.0 %shard_map.108 = (bf16[64,512]{1,0:T(8,128)(2,1)S(1)}, bf16[64,1024]{1,0:T(8,128)(2,1)S(1)}) custom-call(bf16[16,4,2048]{2,1,0:T(4,128)(2,1)S(1)} %collective-permute-done.1.far_ref, f32[64,512]{1,0:T(8,128)S(1)} %get-tuple-element.28.pre_ref, f32[64,512]{1,0:T(8,128)S(1)} %get-tuple-element.29.back_ref, bf16[2048,512]{1,0:T(8,128)(2,1)S(1)} %get-tuple-element.27.w_in_ref, ...), custom_call_target="tpu_custom_call" | custom-call | tf_op jit(solution)/shard_map/pallas_call | solution.py:313
  33.0 0.6 %collective-permute-start.2 = (bf16[64,1024]{1,0:T(8,128)(2,1)S(1)}, bf16[64,1024]{1,0:T(8,128)(2,1)S(1)}, u32[]{:S(2)}, u32[]{:S(2)}) collective-permute-start(bf16[64,1024]{1,0:T(8,128)(2,1)S(1)} %get-tuple-element.33), channel_id=1, source_target_pairs={{0,1},{1,0},{2,3},{3,2},{4,5},{5,4},{6,7},{7,6},{8,9},{9,8},{10,11... | collective-permute-start | bytes 393224 | tf_op jit(solution)/shard_map/ppermute | solution.py:342
  33.6 0.5 %shard_map.109 = (f32[64,1024]{1,0:T(8,128)S(1)}, bf16[32,2048]{1,0:T(8,128)(2,1)S(1)}) custom-call(bf16[64,512]{1,0:T(8,128)(2,1)S(1)} %get-tuple-element.31.slope_ref, bf16[2048,512]{1,0:T(8,128)(2,1)S(1)} %get-tuple-element.27.w_in_ref, bf16[4,8,2048]{2,1,0:T(8,128)(2,1)S(1)} %all-to-all-done.cot_ref.near_ref, ...), custom_call_target="tpu_custom_call" | custom-call | tf_op jit(solution)/shard_map/pallas_call | solution.py:313
  34.1 0.5 %collective-permute-done.2.came_ref = bf16[64,1024]{1,0:T(8,128)(2,1)S(1)} collective-permute-done((bf16[64,1024]{1,0:T(8,128)(2,1)S(1)}, bf16[64,1024]{1,0:T(8,128)(2,1)S(1)}, u32[]{:S(2)}, u32[]{:S(2)}) %collective-permute-start.2) | collective-permute-done | bytes 131104 | tf_op jit(solution)/shard_map/ppermute | solution.py:342
  34.6 9.9 %all_to_all.16.back_ref = bf16[32,2,1024]{2,1,0:T(2,128)(2,1)S(1)} all-to-all(bf16[32,2,1024]{2,1,0:T(2,128)(2,1)S(1)} %shard_map.110), channel_id=1, replica_groups=mesh['grp'=4,'z'=4,'core'=2] {'grp','z','core'}, dimensions={0} | all-to-all | bytes 262144 | tf_op jit(solution)/shard_map/all_to_all | solution.py:410
  44.5 1.4 %shard_map.111 = (bf16[8,4,2048]{2,1,0:T(4,128)(2,1)}, bf16[8,4,2048]{2,1,0:T(4,128)(2,1)}, bf16[8,4,2048]{2,1,0:T(4,128)(2,1)}) custom-call(bf16[2,32,64]{2,1,0:T(8,128)(2,1)S(1)} %get-tuple-element.21.spread_ref, bf16[32,2,1024]{2,1,0:T(2,128)(2,1)S(1)} %all_to_all.16.back_ref, bf16[32,2048]{1,0:T(8,128)(2,1)S(1)} %get-tuple-element.34.cot_ref, ...), custom_call_target="tpu_custom_call" | custom-call | tf_op jit(solution)/shard_map/pallas_call | solution.py:313
  (2 shorter events, 0.1 us)
Async XLA Ops:
  0.6 12.4 %all-to-all-start = ((bf16[4,8,2048]{2,1,0:T(8,128)(2,1)}), bf16[4,8,2048]{2,1,0:T(8,128)(2,1)S(1)}, u32[]{:S(2)}, u32[]{:S(2)}) async-start(bf16[4,8,2048]{2,1,0:T(8,128)(2,1)} %bitcast.1), calls=%async_computation | async-start | bytes 262144 | tf_op jit(solution)/shard_map/all_to_all | solution.py:344
  13.2 1.4 %collective-permute-start = (bf16[28,2048]{1,0:T(8,128)(2,1)S(1)}, bf16[28,2048]{1,0:T(8,128)(2,1)S(1)}, u32[]{:S(2)}, u32[]{:S(2)}) collective-permute-start(bf16[28,2048]{1,0:T(8,128)(2,1)S(1)} %get-tuple-element.26), channel_id=1, source_target_pairs={{0,1},{1,0},{2,3},{3,2},{4,5},{5,4},{6,7},{7,6},{8,9},{9,8},{10,11... | collective-permute-start | bytes 344072 | tf_op jit(solution)/shard_map/ppermute | solution.py:342
  30.4 1.7 %collective-permute-start.1 = (bf16[16,4,2048]{2,1,0:T(4,128)(2,1)S(1)}, bf16[16,4,2048]{2,1,0:T(4,128)(2,1)S(1)}, u32[]{:S(2)}, u32[]{:S(2)}) collective-permute-start(bf16[16,4,2048]{2,1,0:T(4,128)(2,1)S(1)} %all_to_all.15.near_ref), channel_id=1, source_target_pairs={{0,1},{1,0},{2,3},{3,2},{4,5},{5,4},{6,7},{7,6},{8,9},{9,8},{10,11... | collective-permute-start | bytes 786440 | tf_op jit(solution)/shard_map/ppermute | solution.py:342
  33.0 1.6 %collective-permute-start.2 = (bf16[64,1024]{1,0:T(8,128)(2,1)S(1)}, bf16[64,1024]{1,0:T(8,128)(2,1)S(1)}, u32[]{:S(2)}, u32[]{:S(2)}) collective-permute-start(bf16[64,1024]{1,0:T(8,128)(2,1)S(1)} %get-tuple-element.33), channel_id=1, source_target_pairs={{0,1},{1,0},{2,3},{3,2},{4,5},{5,4},{6,7},{7,6},{8,9},{9,8},{10,11... | collective-permute-start | bytes 393224 | tf_op jit(solution)/shard_map/ppermute | solution.py:342

commit v14 on v12

--- a/solution.py
+++ b/solution.py
@@ -50,6 +50,26 @@
 def heads_of(values):
     width = values.shape[1] // HEADS
     return [values[:, h * width : (h + 1) * width] for h in range(HEADS)]
+
+
+def turn_kernel(span, cot_hbm, *refs):
+    *part_refs, cot_ref, sem = refs
+    copy = pltpu.make_async_copy(cot_hbm, cot_ref, sem)
+    copy.start()
+    rows = cot_ref.shape[1]
+    want = lax.broadcasted_iota(jnp.int32, (rows, rows), 0)
+    have = lax.broadcasted_iota(jnp.int32, (rows, rows), 1)
+    source = ((want // span) ^ lax.axis_index("z")) * span + want % span
+    order = (source == have).astype(jnp.bfloat16)
+    copy.wait()
+    turned = dot(order, cot_ref[0]).astype(jnp.bfloat16)
+    for k, part_ref in enumerate(part_refs):
+        part_ref[...] = turned[k * span : (k + 1) * span]
+
+
+def held_core(level):
+    core = lax.axis_index("core")
+    return jnp.where(level == 0, core, 1 - core)
 
 
 def forward_kernel(
@@ -94,6 +114,7 @@
         gates = gate_ref[e : e + 1, :]
         patch = tokens % patches_all
         frame = tokens // patches_all
+        level = (frame // CORES) ^ lax.axis_index("z")
         for i in range(CORES):
             owned = patch // blocks == chip * CORES + (core ^ i)
             owned = jnp.broadcast_to(owned.astype(jnp.float32), slot.shape)
@@ -102,8 +123,8 @@
             weight = jnp.sum(taken * gates, axis=1, keepdims=True)
             taken = taken.astype(jnp.bfloat16)
             place = jnp.where(
-                frame % CORES == core,
-                (frame // CORES) * span + (core ^ i) * blocks + patch % blocks,
+                frame % CORES == held_core(level),
+                level * span + (core ^ i) * blocks + patch % blocks,
                 -1,
             )
             at = slice(i * slots + e * MOST, i * slots + (e + 1) * MOST)
@@ -159,10 +180,12 @@
         copy.wait()
 
 
-def pick_kernel(take_ref, weight_ref, cot_ref, mine_ref, sent_ref):
-    levels, span, features = cot_ref.shape
+def pick_kernel(take_ref, weight_ref, *refs):
+    *part_refs, cot_ref, mine_ref, sent_ref = refs
+    cot = jnp.concatenate([part_ref[...] for part_ref in part_refs], axis=0)
+    cot_ref[...] = cot
     slots = mine_ref.shape[0]
-    rows = dot(take_ref[...].astype(jnp.bfloat16), cot_ref[...].reshape(levels * span, features))
+    rows = dot(take_ref[...].astype(jnp.bfloat16), cot)
     picks = (rows[: CORES * slots] * weight_ref[:, :1]).astype(jnp.bfloat16)
     mine_ref[...] = picks[:slots]
     away = rows[CORES * slots :].astype(jnp.bfloat16)
@@ -224,20 +247,21 @@
     sent_ref[...] = dot_lanes(slope, w_in_ref[width:, :]).astype(jnp.bfloat16)
 
 
-def third_kernel(slope_ref, w_in_ref, near_ref, came_ref, kept_ref, cot_ref):
-    core = lax.axis_index("core")
-    levels, span, features = near_ref.shape
-    blocks = span // CORES
-    rows = levels * span
+def third_kernel(blocks, slope_ref, w_in_ref, near_ref, came_ref, kept_ref, cot_ref):
+    rows = near_ref.shape[0]
+    span = CORES * blocks
+    levels = rows // span
     want = lax.broadcasted_iota(jnp.int32, (rows, rows), 0)
     have = lax.broadcasted_iota(jnp.int32, (rows, rows), 1)
     frame = want // blocks
-    source = (frame // CORES) * span + core * blocks + want % blocks
-    own = ((frame % CORES == core) & (source == have)).astype(jnp.bfloat16)
-    want, have, frame = (values[:, : levels * blocks] for values in (want, have, frame))
-    source = (frame // CORES) * blocks + want % blocks
-    others = ((frame % CORES != core) & (source == have)).astype(jnp.bfloat16)
-    cot = dot(own, near_ref[...].reshape(rows, features))
+    level = (frame // CORES) ^ lax.axis_index("z")
+    here = frame % CORES == held_core(level)
+    source = level * span + lax.axis_index("core") * blocks + want % blocks
+    own = (here & (source == have)).astype(jnp.bfloat16)
+    source = level * blocks + want % blocks
+    others = (jnp.logical_not(here) & (source == have)).astype(jnp.bfloat16)
+    others = others[:, : levels * blocks]
+    cot = dot(own, near_ref[...])
     cot = cot + dot(others, came_ref[: levels * blocks, :])
     cot_ref[...] = cot.astype(jnp.bfloat16)
     width = kept_ref.shape[1]
@@ -334,10 +358,19 @@
     def swap(values):
         return lax.ppermute(values, "core", [(i, i ^ 1) for i in range(CORES)])
 
-    cot_near = lax.all_to_all(
-        cotangent.reshape(levels, CORES * blocks, features),
-        "z", split_axis=0, concat_axis=0, tiled=True,
-    )
+    def across(values, step):
+        pairs = [(i, i ^ (CORES * step) ^ 1) for i in range(columns)]
+        return lax.ppermute(values, ("z", "core"), pairs)
+
+    span = CORES * blocks
+    parts = call(
+        functools.partial(turn_kernel, span),
+        [((span, features), bf16)] * levels,
+        [cotangent],
+        "h",
+        [pltpu.VMEM(cotangent.shape, bf16), pltpu.SemaphoreType.DMA],
+    )
+    parts = [parts[0]] + [across(parts[k], k) for k in range(1, levels)]
     query, key, value, w_in_near, probs, picked, take, weight, spread = call(
         functools.partial(forward_kernel, blocks * devices, share),
         [
@@ -358,11 +391,11 @@
             pltpu.SemaphoreType.DMA((5 + CORES,)),
         ],
     )
-    mine, sent = call(
+    cot_near, mine, sent = call(
         pick_kernel,
-        [((slots, features), bf16), ((levels * blocks + slots, features), bf16)],
-        [take, weight, cot_near],
-        "vvv",
+        [((rows, features), bf16), ((slots, features), bf16), ((levels * blocks + slots, features), bf16)],
+        [take, weight, *parts],
+        "vv" + "v" * levels,
     )
     came_near = swap(sent)
     half = (hidden, part)
@@ -394,7 +427,7 @@
     )
     came = swap(sent)
     kept, cot = call(
-        third_kernel,
+        functools.partial(third_kernel, blocks),
         [(halves, f32), ((rows, features), bf16)],
         [slope, w_in_near, cot_near, came_near],
         "vvvv",

time: 45.1 us -> 43.7 us (0.969)
  Pallas kernels: 8.02 us -> 9.09 us
  blocking collectives: 24.2 us -> 23.3 us
  starting transfers between devices: 6.98 us -> 6.15 us
  waiting for transfers between devices: 4.84 us -> 4.19 us
    all_to_all x1 -> x0, starting transfers between devices: 6.33 us -> none  [body(): lax.all_to_all(cotangent.reshape(levels, CORES * blocks, features), 'z',...]
    ppermute x0 -> x3, starting transfers between devices: none -> 5.4 us  [across(): return lax.ppermute(values, ('z', 'core'), pairs)]
    all_to_all x1 -> x0, waiting for transfers between devices: 4.1 us -> none  [body(): lax.all_to_all(cotangent.reshape(levels, CORES * blocks, features), 'z',...]
    ppermute x0 -> x3, waiting for transfers between devices: none -> 3.48 us  [across(): return lax.ppermute(values, ('z', 'core'), pairs)]
    pallas_call x9 -> x10, Pallas kernels: 8.02 us -> 9.09 us  [call(): pl.pallas_call(kernel, out_shape=[jax.ShapeDtypeStruct(shape, dtype) for...]
    all_to_all x1, blocking collectives: 14 us -> 13 us  [body(): lax.all_to_all(outgoing, everyone, split_axis=0, concat_axis=0, tiled=True)]
  transfers between devices with their start and end apart: 4 -> 6, of which waited for: 2 -> 2; matrix products, arithmetic and copies ran while one was open for 0% -> 0% of each run, Pallas kernels for 12% -> 12%
where the time goes in v14:
time: 43.7 us; the launch traced here: 43.5 us
  blocking collectives  23.3 us (53%)
  Pallas kernels  9.09 us (21%)
  starting transfers between devices  6.15 us (14%)
  waiting for transfers between devices  4.19 us (10%)
  between operations  0.72 us (2%)
    all_to_all x1, blocking collectives, body(): lax.all_to_all(outgoing, everyone, split_axis=0, concat_axis=0, tiled=True)  13 us
    all_to_all x1, blocking collectives, body(): lax.all_to_all(total, everyone, split_axis=0, concat_axis=0, tiled=True)  10.3 us
    pallas_call x10, Pallas kernels, call(): pl.pallas_call(kernel, out_shape=[jax.ShapeDtypeStruct(shape, dtype) for...  9.09 us
    ppermute x3, starting transfers between devices, across(): return lax.ppermute(values, ('z', 'core'), pairs)  5.4 us
    ppermute x3, waiting for transfers between devices, across(): return lax.ppermute(values, ('z', 'core'), pairs)  3.48 us
  transfers between devices with their start and end apart: 6, of which 2 were waited for; matrix products, arithmetic and copies ran while one was open for 0% of the time, Pallas kernels for 12%

profile of v14, /device:TPU:0, one launch (start us, length us, event | category | flops | bytes accessed | tf_op | source)
XLA Modules:
  0.0 43.5 jit_solution(10004052089413363704)
XLA Ops:
  0.6 1.1 %shard_map.104 = (bf16[8,2048]{1,0:T(8,128)(2,1)S(1)}, bf16[8,2048]{1,0:T(8,128)(2,1)S(1)}, bf16[8,2048]{1,0:T(8,128)(2,1)S(1)}, bf16[8,2048]{1,0:T(8,128)(2,1)S(1)}) custom-call(bf16[1,32,2048]{2,1,0:T(8,128)(2,1)} %cot_hbm.1), custom_call_target="tpu_custom_call" | custom-call | tf_op jit(solution)/shard_map/pallas_call | solution.py:330
  1.7 2.5 %collective-permute-start = (bf16[8,2048]{1,0:T(8,128)(2,1)S(1)}, bf16[8,2048]{1,0:T(8,128)(2,1)S(1)}, u32[]{:S(2)}, u32[]{:S(2)}) collective-permute-start(bf16[8,2048]{1,0:T(8,128)(2,1)S(1)} %get-tuple-element.31), channel_id=1, source_target_pairs={{0,3},{1,2},{2,1},{3,0},{4,7},{5,6},{6,5},{7,4},{8,11},{9,10},{10,... | collective-permute-start | bytes 98312 | tf_op jit(solution)/shard_map/ppermute | solution.py:363
  4.2 2.9 %collective-permute-start.1 = (bf16[8,2048]{1,0:T(8,128)(2,1)S(1)}, bf16[8,2048]{1,0:T(8,128)(2,1)S(1)}, u32[]{:S(2)}, u32[]{:S(2)}) collective-permute-start(bf16[8,2048]{1,0:T(8,128)(2,1)S(1)} %get-tuple-element.32), channel_id=1, source_target_pairs={{0,5},{1,4},{2,7},{3,6},{4,1},{5,0},{6,3},{7,2},{8,13},{9,12},{10,... | collective-permute-start | bytes 98312 | tf_op jit(solution)/shard_map/ppermute | solution.py:363
  7.1 0.0 collective-permute-start.2
  7.1 2.0 %shard_map.103 = (bf16[32,2048]{1,0:T(8,128)(2,1)S(1)}, bf16[32,2048]{1,0:T(8,128)(2,1)S(1)}, bf16[32,2048]{1,0:T(8,128)(2,1)S(1)}, bf16[2048,512]{1,0:T(8,128)(...) custom-call(s32[2,32]{1,0:T(2,128)} %chosen_hbm.1, ...), custom_call_target="tpu_custom_call" | custom-call | tf_op jit(solution)/shard_map/pallas_call | solution.py:330
  9.1 0.0 collective-permute-done.refs_1_
  9.1 0.0 collective-permute-done.1.refs_2_
  9.1 3.5 %collective-permute-done.2.refs_3_ = bf16[8,2048]{1,0:T(8,128)(2,1)S(1)} collective-permute-done((bf16[8,2048]{1,0:T(8,128)(2,1)S(1)}, bf16[8,2048]{1,0:T(8,128)(2,1)S(1)}, u32[]{:S(2)}, u32[]{:S(2)}) %collective-permute-start.2) | collective-permute-done | bytes 32800 | tf_op jit(solution)/shard_map/ppermute | solution.py:363
  12.6 0.2 shard_map.105
  12.8 0.2 collective-permute-start.3
  12.9 1.2 %shard_map.106.w_out_near_ref = bf16[512,1024]{1,0:T(8,128)(2,1)S(1)} custom-call(bf16[4,2048]{1,0:T(4,128)(2,1)S(1)} %get-tuple-element.34.after_ref.mine_ref, bf16[1,512,2048]{2,1,0:T(8,128)(2,1)} %w_out_hbm.3), custom_call_target="tpu_custom_call" | custom-call | tf_op jit(solution)/shard_map/pallas_call | solution.py:330
  14.2 0.0 collective-permute-done.3.came_ref
  14.2 13.0 %all_to_all.10.near_ref = bf16[32,2,2048]{2,1,0:T(2,128)(2,1)S(1)} all-to-all(bf16[32,2,2048]{2,1,0:T(2,128)(2,1)S(1)} %shard_map.107), channel_id=1, replica_groups=mesh['grp'=4,'z'=4,'core'=2] {'grp','z','core'}, dimensions={0} | all-to-all | bytes 524288 | tf_op jit(solution)/shard_map/all_to_all | solution.py:411
  27.3 0.4 collective-permute-start.4
  27.6 1.7 %shard_map.108 = (f32[64,512]{1,0:T(8,128)S(1)}, f32[64,512]{1,0:T(8,128)S(1)}, bf16[512,1024]{1,0:T(8,128)(2,1)S(1)}) custom-call(bf16[32,2,2048]{2,1,0:T(2,128)(2,1)S(1)} %all_to_all.10.near_ref, bf16[2048,512]{1,0:T(8,128)(2,1)S(1)} %get-tuple-element.36.w_in_ref, bf16[512,1024]{1,0:T(8,128)(2,1)S(1)} %shard_map.106.w_out_near_ref, ...), custom_call_target="tpu_custom_call" | custom-call | tf_op jit(solution)/shard_map/pallas_call | solution.py:330
  29.3 0.0 collective-permute-done.4.far_ref
  29.3 1.0 %shard_map.109 = (bf16[64,512]{1,0:T(8,128)(2,1)S(1)}, bf16[64,1024]{1,0:T(8,128)(2,1)S(1)}) custom-call(bf16[32,2,2048]{2,1,0:T(2,128)(2,1)S(1)} %collective-permute-done.4.far_ref, f32[64,512]{1,0:T(8,128)S(1)} %get-tuple-element.37.pre_ref, f32[64,512]{1,0:T(8,128)S(1)} %get-tuple-element.38.back_ref, bf16[2048,512]{1,0:T(8,128)(2,1)S(1)} %get-tuple-element.36.w_in_ref, ...), custom_call_target="tpu_custom_call" | custom-call | tf_op jit(solution)/shard_map/pallas_call | solution.py:330
  30.3 0.2 collective-permute-start.5
  30.5 0.5 %shard_map.110 = (f32[64,1024]{1,0:T(8,128)S(1)}, bf16[32,2048]{1,0:T(8,128)(2,1)S(1)}) custom-call(bf16[64,512]{1,0:T(8,128)(2,1)S(1)} %get-tuple-element.40.slope_ref, bf16[2048,512]{1,0:T(8,128)(2,1)S(1)} %get-tuple-element.36.w_in_ref, bf16[32,2048]{1,0:T(8,128)(2,1)S(1)} %get-tuple-element.41.near_ref, bf16[20,2048]{1,0:T(8,128)(2,1)S(1)} %collective-permute-done.3.came_ref), custom_call_target="tpu_custom_call" | custom-call | tf_op jit(solution)/shard_map/pallas_call | solution.py:330
  31.0 0.7 %collective-permute-done.5.came_ref = bf16[64,1024]{1,0:T(8,128)(2,1)S(1)} collective-permute-done((bf16[64,1024]{1,0:T(8,128)(2,1)S(1)}, bf16[64,1024]{1,0:T(8,128)(2,1)S(1)}, u32[]{:S(2)}, u32[]{:S(2)}) %collective-permute-start.5) | collective-permute-done | bytes 131104 | tf_op jit(solution)/shard_map/ppermute | solution.py:359
  31.8 10.3 %all_to_all.11.back_ref = bf16[32,2,1024]{2,1,0:T(2,128)(2,1)S(1)} all-to-all(bf16[32,2,1024]{2,1,0:T(2,128)(2,1)S(1)} %shard_map.111), channel_id=1, replica_groups=mesh['grp'=4,'z'=4,'core'=2] {'grp','z','core'}, dimensions={0} | all-to-all | bytes 262144 | tf_op jit(solution)/shard_map/all_to_all | solution.py:436
  42.1 1.4 %shard_map.112 = (bf16[8,4,2048]{2,1,0:T(4,128)(2,1)}, bf16[8,4,2048]{2,1,0:T(4,128)(2,1)}, bf16[8,4,2048]{2,1,0:T(4,128)(2,1)}) custom-call(bf16[2,32,64]{2,1,0:T(8,128)(2,1)S(1)} %get-tuple-element.26.spread_ref, bf16[32,2,1024]{2,1,0:T(2,128)(2,1)S(1)} %all_to_all.11.back_ref, bf16[32,2048]{1,0:T(8,128)(2,1)S(1)} %get-tuple-element.44.cot_ref, ...), custom_call_target="tpu_custom_call" | custom-call | tf_op jit(solution)/shard_map/pallas_call | solution.py:330
  (2 shorter events, 0.1 us)
Async XLA Ops:
  1.7 7.4 %collective-permute-start = (bf16[8,2048]{1,0:T(8,128)(2,1)S(1)}, bf16[8,2048]{1,0:T(8,128)(2,1)S(1)}, u32[]{:S(2)}, u32[]{:S(2)}) collective-permute-start(bf16[8,2048]{1,0:T(8,128)(2,1)S(1)} %get-tuple-element.31), channel_id=1, source_target_pairs={{0,3},{1,2},{2,1},{3,0},{4,7},{5,6},{6,5},{7,4},{8,11},{9,10},{10,... | collective-permute-start | bytes 98312 | tf_op jit(solution)/shard_map/ppermute | solution.py:363
  4.2 4.9 %collective-permute-start.1 = (bf16[8,2048]{1,0:T(8,128)(2,1)S(1)}, bf16[8,2048]{1,0:T(8,128)(2,1)S(1)}, u32[]{:S(2)}, u32[]{:S(2)}) collective-permute-start(bf16[8,2048]{1,0:T(8,128)(2,1)S(1)} %get-tuple-element.32), channel_id=1, source_target_pairs={{0,5},{1,4},{2,7},{3,6},{4,1},{5,0},{6,3},{7,2},{8,13},{9,12},{10,... | collective-permute-start | bytes 98312 | tf_op jit(solution)/shard_map/ppermute | solution.py:363
  7.1 5.5 %collective-permute-start.2 = (bf16[8,2048]{1,0:T(8,128)(2,1)S(1)}, bf16[8,2048]{1,0:T(8,128)(2,1)S(1)}, u32[]{:S(2)}, u32[]{:S(2)}) collective-permute-start(bf16[8,2048]{1,0:T(8,128)(2,1)S(1)} %get-tuple-element.33), channel_id=1, source_target_pairs={{0,7},{1,6},{2,5},{3,4},{4,3},{5,2},{6,1},{7,0},{8,15},{9,14},{10,... | collective-permute-start | bytes 98312 | tf_op jit(solution)/shard_map/ppermute | solution.py:363
  12.8 1.4 %collective-permute-start.3 = (bf16[20,2048]{1,0:T(8,128)(2,1)S(1)}, bf16[20,2048]{1,0:T(8,128)(2,1)S(1)}, u32[]{:S(2)}, u32[]{:S(2)}) collective-permute-start(bf16[20,2048]{1,0:T(8,128)(2,1)S(1)} %get-tuple-element.35), channel_id=1, source_target_pairs={{0,1},{1,0},{2,3},{3,2},{4,5},{5,4},{6,7},{7,6},{8,9},{9,8},{10,11... | collective-permute-start | bytes 245768 | tf_op jit(solution)/shard_map/ppermute | solution.py:359
  27.3 2.1 %collective-permute-start.4 = (bf16[32,2,2048]{2,1,0:T(2,128)(2,1)S(1)}, bf16[32,2,2048]{2,1,0:T(2,128)(2,1)S(1)}, u32[]{:S(2)}, u32[]{:S(2)}) collective-permute-start(bf16[32,2,2048]{2,1,0:T(2,128)(2,1)S(1)} %all_to_all.10.near_ref), channel_id=1, source_target_pairs={{0,1},{1,0},{2,3},{3,2},{4,5},{5,4},{6,7},{7,6},{8,9},{9,8},{10,11... | collective-permute-start | bytes 786440 | tf_op jit(solution)/shard_map/ppermute | solution.py:359
  30.3 1.4 %collective-permute-start.5 = (bf16[64,1024]{1,0:T(8,128)(2,1)S(1)}, bf16[64,1024]{1,0:T(8,128)(2,1)S(1)}, u32[]{:S(2)}, u32[]{:S(2)}) collective-permute-start(bf16[64,1024]{1,0:T(8,128)(2,1)S(1)} %get-tuple-element.43), channel_id=1, source_target_pairs={{0,1},{1,0},{2,3},{3,2},{4,5},{5,4},{6,7},{7,6},{8,9},{9,8},{10,11... | collective-permute-start | bytes 393224 | tf_op jit(solution)/shard_map/ppermute | solution.py:359

commit v15 on v14

--- a/solution.py
+++ b/solution.py
@@ -180,9 +180,10 @@
         copy.wait()
 
 
-def pick_kernel(take_ref, weight_ref, *refs):
+def pick_kernel(order, take_ref, weight_ref, *refs):
     *part_refs, cot_ref, mine_ref, sent_ref = refs
-    cot = jnp.concatenate([part_ref[...] for part_ref in part_refs], axis=0)
+    parts = [part_refs[order.index(k)][...] for k in range(len(order))]
+    cot = jnp.concatenate(parts, axis=0)
     cot_ref[...] = cot
     slots = mine_ref.shape[0]
     rows = dot(take_ref[...].astype(jnp.bfloat16), cot)
@@ -370,7 +371,8 @@
         "h",
         [pltpu.VMEM(cotangent.shape, bf16), pltpu.SemaphoreType.DMA],
     )
-    parts = [parts[0]] + [across(parts[k], k) for k in range(1, levels)]
+    order = [0] + [i ^ (i >> 1) for i in range(levels - 1, 0, -1)]
+    parts = [across(parts[k], k) if k else parts[k] for k in order]
     query, key, value, w_in_near, probs, picked, take, weight, spread = call(
         functools.partial(forward_kernel, blocks * devices, share),
         [
@@ -392,7 +394,7 @@
         ],
     )
     cot_near, mine, sent = call(
-        pick_kernel,
+        functools.partial(pick_kernel, order),
         [((rows, features), bf16), ((slots, features), bf16), ((levels * blocks + slots, features), bf16)],
         [take, weight, *parts],
         "vv" + "v" * levels,

time: 43.7 us -> 44 us (level)
  waiting for transfers between devices: 4.19 us -> 2.26 us
  blocking collectives: 23.3 us -> 25 us
  starting transfers between devices: 6.15 us -> 6.7 us
    ppermute x3, waiting for transfers between devices: 3.48 us -> 1.56 us  [across(): return lax.ppermute(values, ('z', 'core'), pairs)]
    all_to_all x1, blocking collectives: 13 us -> 14.7 us  [body(): lax.all_to_all(outgoing, everyone, split_axis=0, concat_axis=0, tiled=True)]
    ppermute x3, starting transfers between devices: 0.75 us -> 1.3 us  [swap(): return lax.ppermute(values, 'core', [(i, i ^ 1) for i in range(CORES)])]
  transfers between devices with their start and end apart: 6 -> 6, of which waited for: 2 -> 3; matrix products, arithmetic and copies ran while one was open for 0% -> 0% of each run, Pallas kernels for 12% -> 12%
where the time goes in v15:
time: 44 us; the launch traced here: 43.7 us
  blocking collectives  25 us (57%)
  Pallas kernels  9.1 us (21%)
  starting transfers between devices  6.7 us (15%)
  waiting for transfers between devices  2.26 us (5%)
  between operations  0.72 us (2%)
    all_to_all x1, blocking collectives, body(): lax.all_to_all(outgoing, everyone, split_axis=0, concat_axis=0, tiled=True)  14.7 us
    all_to_all x1, blocking collectives, body(): lax.all_to_all(total, everyone, split_axis=0, concat_axis=0, tiled=True)  10.3 us
    pallas_call x10, Pallas kernels, call(): pl.pallas_call(kernel, out_shape=[jax.ShapeDtypeStruct(shape, dtype) for...  9.1 us
    ppermute x3, starting transfers between devices, across(): return lax.ppermute(values, ('z', 'core'), pairs)  5.4 us
    ppermute x3, waiting for transfers between devices, across(): return lax.ppermute(values, ('z', 'core'), pairs)  1.56 us
    ppermute x3, starting transfers between devices, swap(): return lax.ppermute(values, 'core', [(i, i ^ 1) for i in range(CORES)])  1.3 us
  transfers between devices with their start and end apart: 6, of which 3 were waited for; matrix products, arithmetic and copies ran while one was open for 0% of the time, Pallas kernels for 12%

profile of v15, /device:TPU:0, one launch (start us, length us, event | category | flops | bytes accessed | tf_op | source)
XLA Modules:
  0.0 43.7 jit_solution(17162976047584660042)
XLA Ops:
  0.6 1.1 %shard_map.104 = (bf16[8,2048]{1,0:T(8,128)(2,1)S(1)}, bf16[8,2048]{1,0:T(8,128)(2,1)S(1)}, bf16[8,2048]{1,0:T(8,128)(2,1)S(1)}, bf16[8,2048]{1,0:T(8,128)(2,1)S(1)}) custom-call(bf16[1,32,2048]{2,1,0:T(8,128)(2,1)} %cot_hbm.1), custom_call_target="tpu_custom_call" | custom-call | tf_op jit(solution)/shard_map/pallas_call | solution.py:331
  1.7 3.5 %collective-permute-start = (bf16[8,2048]{1,0:T(8,128)(2,1)S(1)}, bf16[8,2048]{1,0:T(8,128)(2,1)S(1)}, u32[]{:S(2)}, u32[]{:S(2)}) collective-permute-start(bf16[8,2048]{1,0:T(8,128)(2,1)S(1)} %get-tuple-element.31), channel_id=1, source_target_pairs={{0,5},{1,4},{2,7},{3,6},{4,1},{5,0},{6,3},{7,2},{8,13},{9,12},{10,... | collective-permute-start | bytes 98312 | tf_op jit(solution)/shard_map/ppermute | solution.py:364
  5.3 1.6 %collective-permute-start.1 = (bf16[8,2048]{1,0:T(8,128)(2,1)S(1)}, bf16[8,2048]{1,0:T(8,128)(2,1)S(1)}, u32[]{:S(2)}, u32[]{:S(2)}) collective-permute-start(bf16[8,2048]{1,0:T(8,128)(2,1)S(1)} %get-tuple-element.32), channel_id=1, source_target_pairs={{0,7},{1,6},{2,5},{3,4},{4,3},{5,2},{6,1},{7,0},{8,15},{9,14},{10,... | collective-permute-start | bytes 98312 | tf_op jit(solution)/shard_map/ppermute | solution.py:364
  6.9 0.2 collective-permute-start.2
  7.1 2.0 %shard_map.103 = (bf16[32,2048]{1,0:T(8,128)(2,1)S(1)}, bf16[32,2048]{1,0:T(8,128)(2,1)S(1)}, bf16[32,2048]{1,0:T(8,128)(2,1)S(1)}, bf16[2048,512]{1,0:T(8,128)(...) custom-call(s32[2,32]{1,0:T(2,128)} %chosen_hbm.1, ...), custom_call_target="tpu_custom_call" | custom-call | tf_op jit(solution)/shard_map/pallas_call | solution.py:331
  9.1 0.0 collective-permute-done.refs_1_
  9.1 1.4 %collective-permute-done.1.refs_2_ = bf16[8,2048]{1,0:T(8,128)(2,1)S(1)} collective-permute-done((bf16[8,2048]{1,0:T(8,128)(2,1)S(1)}, bf16[8,2048]{1,0:T(8,128)(2,1)S(1)}, u32[]{:S(2)}, u32[]{:S(2)}) %collective-permute-start.1) | collective-permute-done | bytes 32800 | tf_op jit(solution)/shard_map/ppermute | solution.py:364
  10.5 0.2 collective-permute-done.2.refs_3_
  10.7 0.2 shard_map.105
  10.8 0.7 %collective-permute-start.3 = (bf16[20,2048]{1,0:T(8,128)(2,1)S(1)}, bf16[20,2048]{1,0:T(8,128)(2,1)S(1)}, u32[]{:S(2)}, u32[]{:S(2)}) collective-permute-start(bf16[20,2048]{1,0:T(8,128)(2,1)S(1)} %get-tuple-element.35), channel_id=1, source_target_pairs={{0,1},{1,0},{2,3},{3,2},{4,5},{5,4},{6,7},{7,6},{8,9},{9,8},{10,11... | collective-permute-start | bytes 245768 | tf_op jit(solution)/shard_map/ppermute | solution.py:360
  11.6 1.2 %shard_map.106.w_out_near_ref = bf16[512,1024]{1,0:T(8,128)(2,1)S(1)} custom-call(bf16[4,2048]{1,0:T(4,128)(2,1)S(1)} %get-tuple-element.34.after_ref.mine_ref, bf16[1,512,2048]{2,1,0:T(8,128)(2,1)} %w_out_hbm.3), custom_call_target="tpu_custom_call" | custom-call | tf_op jit(solution)/shard_map/pallas_call | solution.py:331
  12.8 0.0 collective-permute-done.3.came_ref
  12.8 14.7 %all_to_all.10.near_ref = bf16[32,2,2048]{2,1,0:T(2,128)(2,1)S(1)} all-to-all(bf16[32,2,2048]{2,1,0:T(2,128)(2,1)S(1)} %shard_map.107), channel_id=1, replica_groups=mesh['grp'=4,'z'=4,'core'=2] {'grp','z','core'}, dimensions={0} | all-to-all | bytes 524288 | tf_op jit(solution)/shard_map/all_to_all | solution.py:413
  27.5 0.4 collective-permute-start.4
  27.9 1.7 %shard_map.108 = (f32[64,512]{1,0:T(8,128)S(1)}, f32[64,512]{1,0:T(8,128)S(1)}, bf16[512,1024]{1,0:T(8,128)(2,1)S(1)}) custom-call(bf16[32,2,2048]{2,1,0:T(2,128)(2,1)S(1)} %all_to_all.10.near_ref, bf16[2048,512]{1,0:T(8,128)(2,1)S(1)} %get-tuple-element.36.w_in_ref, bf16[512,1024]{1,0:T(8,128)(2,1)S(1)} %shard_map.106.w_out_near_ref, ...), custom_call_target="tpu_custom_call" | custom-call | tf_op jit(solution)/shard_map/pallas_call | solution.py:331
  29.6 0.0 collective-permute-done.4.far_ref
  29.6 1.0 %shard_map.109 = (bf16[64,512]{1,0:T(8,128)(2,1)S(1)}, bf16[64,1024]{1,0:T(8,128)(2,1)S(1)}) custom-call(bf16[32,2,2048]{2,1,0:T(2,128)(2,1)S(1)} %collective-permute-done.4.far_ref, f32[64,512]{1,0:T(8,128)S(1)} %get-tuple-element.37.pre_ref, f32[64,512]{1,0:T(8,128)S(1)} %get-tuple-element.38.back_ref, bf16[2048,512]{1,0:T(8,128)(2,1)S(1)} %get-tuple-element.36.w_in_ref, ...), custom_call_target="tpu_custom_call" | custom-call | tf_op jit(solution)/shard_map/pallas_call | solution.py:331
  30.6 0.2 collective-permute-start.5
  30.8 0.5 %shard_map.110 = (f32[64,1024]{1,0:T(8,128)S(1)}, bf16[32,2048]{1,0:T(8,128)(2,1)S(1)}) custom-call(bf16[64,512]{1,0:T(8,128)(2,1)S(1)} %get-tuple-element.40.slope_ref, bf16[2048,512]{1,0:T(8,128)(2,1)S(1)} %get-tuple-element.36.w_in_ref, bf16[32,2048]{1,0:T(8,128)(2,1)S(1)} %get-tuple-element.41.near_ref, bf16[20,2048]{1,0:T(8,128)(2,1)S(1)} %collective-permute-done.3.came_ref), custom_call_target="tpu_custom_call" | custom-call | tf_op jit(solution)/shard_map/pallas_call | solution.py:331
  31.3 0.7 %collective-permute-done.5.came_ref = bf16[64,1024]{1,0:T(8,128)(2,1)S(1)} collective-permute-done((bf16[64,1024]{1,0:T(8,128)(2,1)S(1)}, bf16[64,1024]{1,0:T(8,128)(2,1)S(1)}, u32[]{:S(2)}, u32[]{:S(2)}) %collective-permute-start.5) | collective-permute-done | bytes 131104 | tf_op jit(solution)/shard_map/ppermute | solution.py:360
  32.0 10.3 %all_to_all.11.back_ref = bf16[32,2,1024]{2,1,0:T(2,128)(2,1)S(1)} all-to-all(bf16[32,2,1024]{2,1,0:T(2,128)(2,1)S(1)} %shard_map.111), channel_id=1, replica_groups=mesh['grp'=4,'z'=4,'core'=2] {'grp','z','core'}, dimensions={0} | all-to-all | bytes 262144 | tf_op jit(solution)/shard_map/all_to_all | solution.py:438
  42.3 1.4 %shard_map.112 = (bf16[8,4,2048]{2,1,0:T(4,128)(2,1)}, bf16[8,4,2048]{2,1,0:T(4,128)(2,1)}, bf16[8,4,2048]{2,1,0:T(4,128)(2,1)}) custom-call(bf16[2,32,64]{2,1,0:T(8,128)(2,1)S(1)} %get-tuple-element.26.spread_ref, bf16[32,2,1024]{2,1,0:T(2,128)(2,1)S(1)} %all_to_all.11.back_ref, bf16[32,2048]{1,0:T(8,128)(2,1)S(1)} %get-tuple-element.44.cot_ref, ...), custom_call_target="tpu_custom_call" | custom-call | tf_op jit(solution)/shard_map/pallas_call | solution.py:331
  (2 shorter events, 0.1 us)
Async XLA Ops:
  1.7 7.4 %collective-permute-start = (bf16[8,2048]{1,0:T(8,128)(2,1)S(1)}, bf16[8,2048]{1,0:T(8,128)(2,1)S(1)}, u32[]{:S(2)}, u32[]{:S(2)}) collective-permute-start(bf16[8,2048]{1,0:T(8,128)(2,1)S(1)} %get-tuple-element.31), channel_id=1, source_target_pairs={{0,5},{1,4},{2,7},{3,6},{4,1},{5,0},{6,3},{7,2},{8,13},{9,12},{10,... | collective-permute-start | bytes 98312 | tf_op jit(solution)/shard_map/ppermute | solution.py:364
  5.3 5.2 %collective-permute-start.1 = (bf16[8,2048]{1,0:T(8,128)(2,1)S(1)}, bf16[8,2048]{1,0:T(8,128)(2,1)S(1)}, u32[]{:S(2)}, u32[]{:S(2)}) collective-permute-start(bf16[8,2048]{1,0:T(8,128)(2,1)S(1)} %get-tuple-element.32), channel_id=1, source_target_pairs={{0,7},{1,6},{2,5},{3,4},{4,3},{5,2},{6,1},{7,0},{8,15},{9,14},{10,... | collective-permute-start | bytes 98312 | tf_op jit(solution)/shard_map/ppermute | solution.py:364
  6.9 3.8 %collective-permute-start.2 = (bf16[8,2048]{1,0:T(8,128)(2,1)S(1)}, bf16[8,2048]{1,0:T(8,128)(2,1)S(1)}, u32[]{:S(2)}, u32[]{:S(2)}) collective-permute-start(bf16[8,2048]{1,0:T(8,128)(2,1)S(1)} %get-tuple-element.33), channel_id=1, source_target_pairs={{0,3},{1,2},{2,1},{3,0},{4,7},{5,6},{6,5},{7,4},{8,11},{9,10},{10,... | collective-permute-start | bytes 98312 | tf_op jit(solution)/shard_map/ppermute | solution.py:364
  10.8 2.0 %collective-permute-start.3 = (bf16[20,2048]{1,0:T(8,128)(2,1)S(1)}, bf16[20,2048]{1,0:T(8,128)(2,1)S(1)}, u32[]{:S(2)}, u32[]{:S(2)}) collective-permute-start(bf16[20,2048]{1,0:T(8,128)(2,1)S(1)} %get-tuple-element.35), channel_id=1, source_target_pairs={{0,1},{1,0},{2,3},{3,2},{4,5},{5,4},{6,7},{7,6},{8,9},{9,8},{10,11... | collective-permute-start | bytes 245768 | tf_op jit(solution)/shard_map/ppermute | solution.py:360
  27.5 2.1 %collective-permute-start.4 = (bf16[32,2,2048]{2,1,0:T(2,128)(2,1)S(1)}, bf16[32,2,2048]{2,1,0:T(2,128)(2,1)S(1)}, u32[]{:S(2)}, u32[]{:S(2)}) collective-permute-start(bf16[32,2,2048]{2,1,0:T(2,128)(2,1)S(1)} %all_to_all.10.near_ref), channel_id=1, source_target_pairs={{0,1},{1,0},{2,3},{3,2},{4,5},{5,4},{6,7},{7,6},{8,9},{9,8},{10,11... | collective-permute-start | bytes 786440 | tf_op jit(solution)/shard_map/ppermute | solution.py:360
  30.6 1.4 %collective-permute-start.5 = (bf16[64,1024]{1,0:T(8,128)(2,1)S(1)}, bf16[64,1024]{1,0:T(8,128)(2,1)S(1)}, u32[]{:S(2)}, u32[]{:S(2)}) collective-permute-start(bf16[64,1024]{1,0:T(8,128)(2,1)S(1)} %get-tuple-element.43), channel_id=1, source_target_pairs={{0,1},{1,0},{2,3},{3,2},{4,5},{5,4},{6,7},{7,6},{8,9},{9,8},{10,11... | collective-permute-start | bytes 393224 | tf_op jit(solution)/shard_map/ppermute | solution.py:360

commit v16 on v15

--- a/solution.py
+++ b/solution.py
@@ -74,8 +74,8 @@
 
 def forward_kernel(
     patches_all, share,
-    chosen_hbm, gate_hbm, query_hbm, key_hbm, value_hbm, w_in_hbm,
-    query_rows_ref, key_rows_ref, value_rows_ref, w_in_ref,
+    chosen_hbm, gate_hbm, query_hbm, key_hbm, value_hbm, w_in_hbm, w_out_hbm,
+    query_rows_ref, key_rows_ref, value_rows_ref, w_in_ref, w_out_ref,
     probs_ref, picked_ref, take_ref, weight_ref, spread_ref,
     chosen_ref, gate_ref, query_ref, key_ref, value_ref, sems,
 ):
@@ -87,6 +87,8 @@
     for i in range(CORES):
         sources.append(w_in_hbm.at[0, part_of(core ^ i, part)])
         targets.append(w_in_ref.at[pl.ds(i * part, part)])
+        sources.append(w_out_hbm.at[0, :, part_of(core ^ i, part)])
+        targets.append(w_out_ref.at[:, pl.ds(i * part, part)])
     copies = [
         pltpu.make_async_copy(source, target, sems.at[i])
         for i, (source, target) in enumerate(zip(sources, targets))
@@ -193,7 +195,7 @@
     sent_ref[...] = jnp.concatenate([away, picks[slots:]], axis=0)
 
 
-def pack_kernel(share, picked_ref, mine_ref, came_ref, w_out_near_ref, out_ref):
+def pack_kernel(share, picked_ref, mine_ref, came_ref, out_ref):
     slots, features = mine_ref.shape
     rows = mine_ref[...] + came_ref[came_ref.shape[0] - slots :, :]
     part = features // CORES
@@ -213,36 +215,18 @@
     return pl.ds(pl.multiple_of(part * width, width), width)
 
 
-def half_copy(i, w_out_hbm, half_ref, sem):
-    width = half_ref.shape[1]
-    return pltpu.make_async_copy(
-        w_out_hbm.at[0, :, part_of(lax.axis_index("core") ^ i, width)], half_ref, sem
-    )
-
-
-def load_kernel(after_ref, w_out_hbm, half_ref, sem):
-    copy = half_copy(0, w_out_hbm, half_ref, sem)
-    copy.start()
-    copy.wait()
-
-
-def first_kernel(
-    near_ref, w_in_ref, w_out_near_ref, w_out_hbm, pre_ref, back_ref, w_out_far_ref, sem
-):
-    copy = half_copy(1, w_out_hbm, w_out_far_ref, sem)
-    copy.start()
+def first_kernel(near_ref, w_in_ref, w_out_ref, pre_ref, back_ref):
     width = w_in_ref.shape[0] // CORES
     rows = near_ref[...].reshape(pre_ref.shape[0], CORES * width)
     pre_ref[...] = dot(rows[:, :width], w_in_ref[:width, :])
-    back_ref[...] = dot_lanes(rows[:, width:], w_out_near_ref[...])
-    copy.wait()
-
-
-def second_kernel(far_ref, pre_ref, back_ref, w_in_ref, w_out_far_ref, slope_ref, sent_ref):
+    back_ref[...] = dot_lanes(rows[:, width:], w_out_ref[:, :width])
+
+
+def second_kernel(far_ref, pre_ref, back_ref, w_in_ref, w_out_ref, slope_ref, sent_ref):
     width = w_in_ref.shape[0] // CORES
     far = far_ref[...].reshape(pre_ref.shape[0], CORES * width)
     pre_act = pre_ref[...] + dot(far[:, :width], w_in_ref[width:, :])
-    back_act = back_ref[...] + dot_lanes(far[:, width:], w_out_far_ref[...])
+    back_act = back_ref[...] + dot_lanes(far[:, width:], w_out_ref[:, width:])
     slope = (back_act * gelu_slope(pre_act)).astype(jnp.bfloat16)
     slope_ref[...] = slope
     sent_ref[...] = dot_lanes(slope, w_in_ref[width:, :]).astype(jnp.bfloat16)
@@ -373,24 +357,25 @@
     )
     order = [0] + [i ^ (i >> 1) for i in range(levels - 1, 0, -1)]
     parts = [across(parts[k], k) if k else parts[k] for k in order]
-    query, key, value, w_in_near, probs, picked, take, weight, spread = call(
+    query, key, value, w_in_near, w_out_near, probs, picked, take, weight, spread = call(
         functools.partial(forward_kernel, blocks * devices, share),
         [
             *[((rows, features), bf16)] * 3,
             (w_in.shape[1:], bf16),
+            (w_out.shape[1:], bf16),
             ((rows, HEADS * rows), f32),
             ((slots, features), bf16),
             ((CORES * slots + levels * blocks, rows), f32),
             ((CORES * slots, LANES), f32),
             ((CORES, rows, devices * MOST), bf16),
         ],
-        [chosen, gate_probs, query_in, key_in, value_in, w_in],
-        "hhhhhh",
+        [chosen, gate_probs, query_in, key_in, value_in, w_in, w_out],
+        "hhhhhhh",
         [
             pltpu.VMEM(chosen.shape, jnp.int32),
             pltpu.VMEM(gate_probs.shape, f32),
             *[pltpu.VMEM(query_in.shape, bf16)] * 3,
-            pltpu.SemaphoreType.DMA((5 + CORES,)),
+            pltpu.SemaphoreType.DMA((5 + 2 * CORES,)),
         ],
     )
     cot_near, mine, sent = call(
@@ -400,31 +385,23 @@
         "vv" + "v" * levels,
     )
     came_near = swap(sent)
-    half = (hidden, part)
-    (w_out_near,) = call(
-        load_kernel, [(half, bf16)], [mine, w_out], "vh", [pltpu.SemaphoreType.DMA]
-    )
     (outgoing,) = call(
         functools.partial(pack_kernel, share),
         [((devices, MOST, 2 * part), bf16)],
-        [picked, mine, came_near, w_out_near],
-        "vvvv",
+        [picked, mine, came_near],
+        "vvv",
     )
     held = lax.all_to_all(outgoing, everyone, split_axis=0, concat_axis=0, tiled=True)
     other = swap(held)
     acts = (devices * MOST, hidden)
     halves = (devices * MOST, part)
-    pre_act, back_act, w_out_far = call(
-        first_kernel,
-        [(acts, f32), (acts, f32), (half, bf16)],
-        [held, w_in_near, w_out_near, w_out],
-        "vvvh",
-        [pltpu.SemaphoreType.DMA],
+    pre_act, back_act = call(
+        first_kernel, [(acts, f32), (acts, f32)], [held, w_in_near, w_out_near], "vvv"
     )
     slope, sent = call(
         second_kernel,
         [(acts, bf16), (halves, bf16)],
-        [other, pre_act, back_act, w_in_near, w_out_far],
+        [other, pre_act, back_act, w_in_near, w_out_near],
         "vvvvv",
     )
     came = swap(sent)

time: 44 us -> 43.5 us (0.989)
  Pallas kernels: 9.1 us -> 7.3 us
  waiting for transfers between devices: 2.26 us -> 3.01 us
    pallas_call x10 -> x9, Pallas kernels: 9.1 us -> 7.3 us  [call(): pl.pallas_call(kernel, out_shape=[jax.ShapeDtypeStruct(shape, dtype) for...]
    ppermute x3, waiting for transfers between devices: 0.7 us -> 1.96 us  [swap(): return lax.ppermute(values, 'core', [(i, i ^ 1) for i in range(CORES)])]
    ppermute x3, waiting for transfers between devices: 1.56 us -> 1.05 us  [across(): return lax.ppermute(values, ('z', 'core'), pairs)]
  transfers between devices with their start and end apart: 6 -> 6, of which waited for: 3 -> 5; matrix products, arithmetic and copies ran while one was open for 0% -> 0% of each run, Pallas kernels for 12% -> 8%
where the time goes in v16:
time: 43.5 us; the launch traced here: 43.3 us
  blocking collectives  25.4 us (58%)
  Pallas kernels  7.3 us (17%)
  starting transfers between devices  6.94 us (16%)
  waiting for transfers between devices  3.01 us (7%)
  between operations  0.69 us (2%)
    all_to_all x1, blocking collectives, body(): lax.all_to_all(outgoing, everyone, split_axis=0, concat_axis=0, tiled=True)  14.9 us
    all_to_all x1, blocking collectives, body(): lax.all_to_all(total, everyone, split_axis=0, concat_axis=0, tiled=True)  10.5 us
    pallas_call x9, Pallas kernels, call(): pl.pallas_call(kernel, out_shape=[jax.ShapeDtypeStruct(shape, dtype) for...  7.3 us
    ppermute x3, starting transfers between devices, across(): return lax.ppermute(values, ('z', 'core'), pairs)  5.4 us
    ppermute x3, waiting for transfers between devices, swap(): return lax.ppermute(values, 'core', [(i, i ^ 1) for i in range(CORES)])  1.96 us
    ppermute x3, starting transfers between devices, swap(): return lax.ppermute(values, 'core', [(i, i ^ 1) for i in range(CORES)])  1.54 us
    ppermute x3, waiting for transfers between devices, across(): return lax.ppermute(values, ('z', 'core'), pairs)  1.05 us
  transfers between devices with their start and end apart: 6, of which 5 were waited for; matrix products, arithmetic and copies ran while one was open for 0% of the time, Pallas kernels for 8%

profile of v16, /device:TPU:0, one launch (start us, length us, event | category | flops | bytes accessed | tf_op | source)
XLA Modules:
  0.0 43.3 jit_solution(4436900843051735669)
XLA Ops:
  0.6 1.1 %shard_map.104 = (bf16[8,2048]{1,0:T(8,128)(2,1)S(1)}, bf16[8,2048]{1,0:T(8,128)(2,1)S(1)}, bf16[8,2048]{1,0:T(8,128)(2,1)S(1)}, bf16[8,2048]{1,0:T(8,128)(2,1)S(1)}) custom-call(bf16[1,32,2048]{2,1,0:T(8,128)(2,1)} %cot_hbm.1), custom_call_target="tpu_custom_call" | custom-call | tf_op jit(solution)/shard_map/pallas_call | solution.py:315
  1.7 3.5 %collective-permute-start = (bf16[8,2048]{1,0:T(8,128)(2,1)S(1)}, bf16[8,2048]{1,0:T(8,128)(2,1)S(1)}, u32[]{:S(2)}, u32[]{:S(2)}) collective-permute-start(bf16[8,2048]{1,0:T(8,128)(2,1)S(1)} %get-tuple-element.31), channel_id=1, source_target_pairs={{0,5},{1,4},{2,7},{3,6},{4,1},{5,0},{6,3},{7,2},{8,13},{9,12},{10,... | collective-permute-start | bytes 98312 | tf_op jit(solution)/shard_map/ppermute | solution.py:348
  5.3 1.6 %collective-permute-start.1 = (bf16[8,2048]{1,0:T(8,128)(2,1)S(1)}, bf16[8,2048]{1,0:T(8,128)(2,1)S(1)}, u32[]{:S(2)}, u32[]{:S(2)}) collective-permute-start(bf16[8,2048]{1,0:T(8,128)(2,1)S(1)} %get-tuple-element.32), channel_id=1, source_target_pairs={{0,7},{1,6},{2,5},{3,4},{4,3},{5,2},{6,1},{7,0},{8,15},{9,14},{10,... | collective-permute-start | bytes 98312 | tf_op jit(solution)/shard_map/ppermute | solution.py:348
  6.9 0.2 collective-permute-start.2
  7.1 2.5 %shard_map.103 = (bf16[32,2048]{1,0:T(8,128)(2,1)S(1)}, bf16[32,2048]{1,0:T(8,128)(2,1)S(1)}, bf16[32,2048]{1,0:T(8,128)(2,1)S(1)}, bf16[2048,512]{1,0:T(8,128)(...) custom-call(s32[2,32]{1,0:T(2,128)} %chosen_hbm.1, ...), custom_call_target="tpu_custom_call" | custom-call | tf_op jit(solution)/shard_map/pallas_call | solution.py:315
  9.6 0.0 collective-permute-done.refs_1_
  9.6 0.9 %collective-permute-done.1.refs_2_ = bf16[8,2048]{1,0:T(8,128)(2,1)S(1)} collective-permute-done((bf16[8,2048]{1,0:T(8,128)(2,1)S(1)}, bf16[8,2048]{1,0:T(8,128)(2,1)S(1)}, u32[]{:S(2)}, u32[]{:S(2)}) %collective-permute-start.1) | collective-permute-done | bytes 32800 | tf_op jit(solution)/shard_map/ppermute | solution.py:348
  10.5 0.2 collective-permute-done.2.refs_3_
  10.7 0.2 shard_map.105
  10.8 0.7 %collective-permute-start.3 = (bf16[20,2048]{1,0:T(8,128)(2,1)S(1)}, bf16[20,2048]{1,0:T(8,128)(2,1)S(1)}, u32[]{:S(2)}, u32[]{:S(2)}) collective-permute-start(bf16[20,2048]{1,0:T(8,128)(2,1)S(1)} %get-tuple-element.35), channel_id=1, source_target_pairs={{0,1},{1,0},{2,3},{3,2},{4,5},{5,4},{6,7},{7,6},{8,9},{9,8},{10,11... | collective-permute-start | bytes 245768 | tf_op jit(solution)/shard_map/ppermute | solution.py:344
  11.6 0.9 %collective-permute-done.3.came_ref = bf16[20,2048]{1,0:T(8,128)(2,1)S(1)} collective-permute-done((bf16[20,2048]{1,0:T(8,128)(2,1)S(1)}, bf16[20,2048]{1,0:T(8,128)(2,1)S(1)}, u32[]{:S(2)}, u32[]{:S(2)}) %collective-permute-start.3) | collective-permute-done | bytes 81952 | tf_op jit(solution)/shard_map/ppermute | solution.py:344
  12.5 14.9 %all_to_all.10.near_ref = bf16[32,2,2048]{2,1,0:T(2,128)(2,1)S(1)} all-to-all(bf16[32,2,2048]{2,1,0:T(2,128)(2,1)S(1)} %shard_map.106), channel_id=1, replica_groups=mesh['grp'=4,'z'=4,'core'=2] {'grp','z','core'}, dimensions={0} | all-to-all | bytes 524288 | tf_op jit(solution)/shard_map/all_to_all | solution.py:394
  27.4 0.4 collective-permute-start.4
  27.8 0.6 %shard_map.107 = (f32[64,512]{1,0:T(8,128)S(1)}, f32[64,512]{1,0:T(8,128)S(1)}) custom-call(bf16[32,2,2048]{2,1,0:T(2,128)(2,1)S(1)} %all_to_all.10.near_ref, bf16[2048,512]{1,0:T(8,128)(2,1)S(1)} %get-tuple-element.36.w_in_ref, bf16[512,2048]{1,0:T(8,128)(2,1)S(1)} %get-tuple-element.37.w_out_ref), custom_call_target="tpu_custom_call" | custom-call | tf_op jit(solution)/shard_map/pallas_call | solution.py:315
  28.4 0.6 %collective-permute-done.4.far_ref = bf16[32,2,2048]{2,1,0:T(2,128)(2,1)S(1)} collective-permute-done((bf16[32,2,2048]{2,1,0:T(2,128)(2,1)S(1)}, bf16[32,2,2048]{2,1,0:T(2,128)(2,1)S(1)}, u32[]{:S(2)}, u32[]{:S(2)}) %collective-permute-start.4) | collective-permute-done | bytes 262176 | tf_op jit(solution)/shard_map/ppermute | solution.py:344
  29.0 1.0 %shard_map.108 = (bf16[64,512]{1,0:T(8,128)(2,1)S(1)}, bf16[64,1024]{1,0:T(8,128)(2,1)S(1)}) custom-call(bf16[32,2,2048]{2,1,0:T(2,128)(2,1)S(1)} %collective-permute-done.4.far_ref, f32[64,512]{1,0:T(8,128)S(1)} %get-tuple-element.38.pre_ref, f32[64,512]{1,0:T(8,128)S(1)} %get-tuple-element.39.back_ref, bf16[2048,512]{1,0:T(8,128)(2,1)S(1)} %get-tuple-element.36.w_in_ref, ...), custom_call_target="tpu_custom_call" | custom-call | tf_op jit(solution)/shard_map/pallas_call | solution.py:315
  30.0 0.4 collective-permute-start.5
  30.4 0.5 %shard_map.109 = (f32[64,1024]{1,0:T(8,128)S(1)}, bf16[32,2048]{1,0:T(8,128)(2,1)S(1)}) custom-call(bf16[64,512]{1,0:T(8,128)(2,1)S(1)} %get-tuple-element.40.slope_ref, bf16[2048,512]{1,0:T(8,128)(2,1)S(1)} %get-tuple-element.36.w_in_ref, bf16[32,2048]{1,0:T(8,128)(2,1)S(1)} %get-tuple-element.41.near_ref, bf16[20,2048]{1,0:T(8,128)(2,1)S(1)} %collective-permute-done.3.came_ref), custom_call_target="tpu_custom_call" | custom-call | tf_op jit(solution)/shard_map/pallas_call | solution.py:315
  30.9 0.5 %collective-permute-done.5.came_ref = bf16[64,1024]{1,0:T(8,128)(2,1)S(1)} collective-permute-done((bf16[64,1024]{1,0:T(8,128)(2,1)S(1)}, bf16[64,1024]{1,0:T(8,128)(2,1)S(1)}, u32[]{:S(2)}, u32[]{:S(2)}) %collective-permute-start.5) | collective-permute-done | bytes 131104 | tf_op jit(solution)/shard_map/ppermute | solution.py:344
  31.4 10.5 %all_to_all.11.back_ref = bf16[32,2,1024]{2,1,0:T(2,128)(2,1)S(1)} all-to-all(bf16[32,2,1024]{2,1,0:T(2,128)(2,1)S(1)} %shard_map.110), channel_id=1, replica_groups=mesh['grp'=4,'z'=4,'core'=2] {'grp','z','core'}, dimensions={0} | all-to-all | bytes 262144 | tf_op jit(solution)/shard_map/all_to_all | solution.py:415
  41.9 1.4 %shard_map.111 = (bf16[8,4,2048]{2,1,0:T(4,128)(2,1)}, bf16[8,4,2048]{2,1,0:T(4,128)(2,1)}, bf16[8,4,2048]{2,1,0:T(4,128)(2,1)}) custom-call(bf16[2,32,64]{2,1,0:T(8,128)(2,1)S(1)} %get-tuple-element.26.spread_ref, bf16[32,2,1024]{2,1,0:T(2,128)(2,1)S(1)} %all_to_all.11.back_ref, bf16[32,2048]{1,0:T(8,128)(2,1)S(1)} %get-tuple-element.44.cot_ref, ...), custom_call_target="tpu_custom_call" | custom-call | tf_op jit(solution)/shard_map/pallas_call | solution.py:315
  (2 shorter events, 0.1 us)
Async XLA Ops:
  1.7 7.9 %collective-permute-start = (bf16[8,2048]{1,0:T(8,128)(2,1)S(1)}, bf16[8,2048]{1,0:T(8,128)(2,1)S(1)}, u32[]{:S(2)}, u32[]{:S(2)}) collective-permute-start(bf16[8,2048]{1,0:T(8,128)(2,1)S(1)} %get-tuple-element.31), channel_id=1, source_target_pairs={{0,5},{1,4},{2,7},{3,6},{4,1},{5,0},{6,3},{7,2},{8,13},{9,12},{10,... | collective-permute-start | bytes 98312 | tf_op jit(solution)/shard_map/ppermute | solution.py:348
  5.3 5.2 %collective-permute-start.1 = (bf16[8,2048]{1,0:T(8,128)(2,1)S(1)}, bf16[8,2048]{1,0:T(8,128)(2,1)S(1)}, u32[]{:S(2)}, u32[]{:S(2)}) collective-permute-start(bf16[8,2048]{1,0:T(8,128)(2,1)S(1)} %get-tuple-element.32), channel_id=1, source_target_pairs={{0,7},{1,6},{2,5},{3,4},{4,3},{5,2},{6,1},{7,0},{8,15},{9,14},{10,... | collective-permute-start | bytes 98312 | tf_op jit(solution)/shard_map/ppermute | solution.py:348
  6.9 3.8 %collective-permute-start.2 = (bf16[8,2048]{1,0:T(8,128)(2,1)S(1)}, bf16[8,2048]{1,0:T(8,128)(2,1)S(1)}, u32[]{:S(2)}, u32[]{:S(2)}) collective-permute-start(bf16[8,2048]{1,0:T(8,128)(2,1)S(1)} %get-tuple-element.33), channel_id=1, source_target_pairs={{0,3},{1,2},{2,1},{3,0},{4,7},{5,6},{6,5},{7,4},{8,11},{9,10},{10,... | collective-permute-start | bytes 98312 | tf_op jit(solution)/shard_map/ppermute | solution.py:348
  10.8 1.7 %collective-permute-start.3 = (bf16[20,2048]{1,0:T(8,128)(2,1)S(1)}, bf16[20,2048]{1,0:T(8,128)(2,1)S(1)}, u32[]{:S(2)}, u32[]{:S(2)}) collective-permute-start(bf16[20,2048]{1,0:T(8,128)(2,1)S(1)} %get-tuple-element.35), channel_id=1, source_target_pairs={{0,1},{1,0},{2,3},{3,2},{4,5},{5,4},{6,7},{7,6},{8,9},{9,8},{10,11... | collective-permute-start | bytes 245768 | tf_op jit(solution)/shard_map/ppermute | solution.py:344
  27.4 1.5 %collective-permute-start.4 = (bf16[32,2,2048]{2,1,0:T(2,128)(2,1)S(1)}, bf16[32,2,2048]{2,1,0:T(2,128)(2,1)S(1)}, u32[]{:S(2)}, u32[]{:S(2)}) collective-permute-start(bf16[32,2,2048]{2,1,0:T(2,128)(2,1)S(1)} %all_to_all.10.near_ref), channel_id=1, source_target_pairs={{0,1},{1,0},{2,3},{3,2},{4,5},{5,4},{6,7},{7,6},{8,9},{9,8},{10,11... | collective-permute-start | bytes 786440 | tf_op jit(solution)/shard_map/ppermute | solution.py:344
  30.0 1.4 %collective-permute-start.5 = (bf16[64,1024]{1,0:T(8,128)(2,1)S(1)}, bf16[64,1024]{1,0:T(8,128)(2,1)S(1)}, u32[]{:S(2)}, u32[]{:S(2)}) collective-permute-start(bf16[64,1024]{1,0:T(8,128)(2,1)S(1)} %get-tuple-element.43), channel_id=1, source_target_pairs={{0,1},{1,0},{2,3},{3,2},{4,5},{5,4},{6,7},{7,6},{8,9},{9,8},{10,11... | collective-permute-start | bytes 393224 | tf_op jit(solution)/shard_map/ppermute | solution.py:344

commit v17 on v16

--- a/solution.py
+++ b/solution.py
@@ -355,7 +355,7 @@
         "h",
         [pltpu.VMEM(cotangent.shape, bf16), pltpu.SemaphoreType.DMA],
     )
-    order = [0] + [i ^ (i >> 1) for i in range(levels - 1, 0, -1)]
+    order = [0] + [i ^ (i >> 1) for i in range(1, levels)]
     parts = [across(parts[k], k) if k else parts[k] for k in order]
     query, key, value, w_in_near, w_out_near, probs, picked, take, weight, spread = call(
         functools.partial(forward_kernel, blocks * devices, share),

time: 43.5 us -> 44 us (1.011)
  waiting for transfers between devices: 3.01 us -> 4.67 us
  blocking collectives: 25.4 us -> 24.7 us
  starting transfers between devices: 6.94 us -> 6.41 us
    ppermute x3, waiting for transfers between devices: 1.05 us -> 2.47 us  [across(): return lax.ppermute(values, ('z', 'core'), pairs)]
    all_to_all x1, blocking collectives: 14.9 us -> 14.2 us  [body(): lax.all_to_all(outgoing, everyone, split_axis=0, concat_axis=0, tiled=True)]
    ppermute x3, starting transfers between devices: 1.54 us -> 1.01 us  [swap(): return lax.ppermute(values, 'core', [(i, i ^ 1) for i in range(CORES)])]
  transfers between devices with their start and end apart: 6 -> 6, of which waited for: 5 -> 4; matrix products, arithmetic and copies ran while one was open for 0% -> 0% of each run, Pallas kernels for 8% -> 8%
where the time goes in v17:
time: 44 us; the launch traced here: 43.8 us
  blocking collectives  24.7 us (56%)
  Pallas kernels  7.3 us (17%)
  starting transfers between devices  6.41 us (15%)
  waiting for transfers between devices  4.67 us (11%)
  between operations  0.7 us (2%)
    all_to_all x1, blocking collectives, body(): lax.all_to_all(outgoing, everyone, split_axis=0, concat_axis=0, tiled=True)  14.2 us
    all_to_all x1, blocking collectives, body(): lax.all_to_all(total, everyone, split_axis=0, concat_axis=0, tiled=True)  10.5 us
    pallas_call x9, Pallas kernels, call(): pl.pallas_call(kernel, out_shape=[jax.ShapeDtypeStruct(shape, dtype) for...  7.3 us
    ppermute x3, starting transfers between devices, across(): return lax.ppermute(values, ('z', 'core'), pairs)  5.4 us
    ppermute x3, waiting for transfers between devices, across(): return lax.ppermute(values, ('z', 'core'), pairs)  2.47 us
    ppermute x3, waiting for transfers between devices, swap(): return lax.ppermute(values, 'core', [(i, i ^ 1) for i in range(CORES)])  2.2 us
    ppermute x3, starting transfers between devices, swap(): return lax.ppermute(values, 'core', [(i, i ^ 1) for i in range(CORES)])  1.01 us
  transfers between devices with their start and end apart: 6, of which 4 were waited for; matrix products, arithmetic and copies ran while one was open for 0% of the time, Pallas kernels for 8%

profile of v17, /device:TPU:0, one launch (start us, length us, event | category | flops | bytes accessed | tf_op | source)
XLA Modules:
  0.0 43.8 jit_solution(7788673510960153111)
XLA Ops:
  0.6 1.1 %shard_map.104 = (bf16[8,2048]{1,0:T(8,128)(2,1)S(1)}, bf16[8,2048]{1,0:T(8,128)(2,1)S(1)}, bf16[8,2048]{1,0:T(8,128)(2,1)S(1)}, bf16[8,2048]{1,0:T(8,128)(2,1)S(1)}) custom-call(bf16[1,32,2048]{2,1,0:T(8,128)(2,1)} %cot_hbm.1), custom_call_target="tpu_custom_call" | custom-call | tf_op jit(solution)/shard_map/pallas_call | solution.py:315
  1.7 2.5 %collective-permute-start = (bf16[8,2048]{1,0:T(8,128)(2,1)S(1)}, bf16[8,2048]{1,0:T(8,128)(2,1)S(1)}, u32[]{:S(2)}, u32[]{:S(2)}) collective-permute-start(bf16[8,2048]{1,0:T(8,128)(2,1)S(1)} %get-tuple-element.31), channel_id=1, source_target_pairs={{0,3},{1,2},{2,1},{3,0},{4,7},{5,6},{6,5},{7,4},{8,11},{9,10},{10,... | collective-permute-start | bytes 98312 | tf_op jit(solution)/shard_map/ppermute | solution.py:348
  4.2 2.8 %collective-permute-start.1 = (bf16[8,2048]{1,0:T(8,128)(2,1)S(1)}, bf16[8,2048]{1,0:T(8,128)(2,1)S(1)}, u32[]{:S(2)}, u32[]{:S(2)}) collective-permute-start(bf16[8,2048]{1,0:T(8,128)(2,1)S(1)} %get-tuple-element.32), channel_id=1, source_target_pairs={{0,7},{1,6},{2,5},{3,4},{4,3},{5,2},{6,1},{7,0},{8,15},{9,14},{10,... | collective-permute-start | bytes 98312 | tf_op jit(solution)/shard_map/ppermute | solution.py:348
  7.0 0.1 collective-permute-start.2
  7.1 2.5 %shard_map.103 = (bf16[32,2048]{1,0:T(8,128)(2,1)S(1)}, bf16[32,2048]{1,0:T(8,128)(2,1)S(1)}, bf16[32,2048]{1,0:T(8,128)(2,1)S(1)}, bf16[2048,512]{1,0:T(8,128)(...) custom-call(s32[2,32]{1,0:T(2,128)} %chosen_hbm.1, ...), custom_call_target="tpu_custom_call" | custom-call | tf_op jit(solution)/shard_map/pallas_call | solution.py:315
  9.6 0.0 collective-permute-done.refs_1_
  9.6 0.0 collective-permute-done.1.refs_2_
  9.6 2.5 %collective-permute-done.2.refs_3_ = bf16[8,2048]{1,0:T(8,128)(2,1)S(1)} collective-permute-done((bf16[8,2048]{1,0:T(8,128)(2,1)S(1)}, bf16[8,2048]{1,0:T(8,128)(2,1)S(1)}, u32[]{:S(2)}, u32[]{:S(2)}) %collective-permute-start.2) | collective-permute-done | bytes 32800 | tf_op jit(solution)/shard_map/ppermute | solution.py:348
  12.1 0.2 shard_map.105
  12.3 0.2 collective-permute-start.3
  12.4 1.2 %collective-permute-done.3.came_ref = bf16[20,2048]{1,0:T(8,128)(2,1)S(1)} collective-permute-done((bf16[20,2048]{1,0:T(8,128)(2,1)S(1)}, bf16[20,2048]{1,0:T(8,128)(2,1)S(1)}, u32[]{:S(2)}, u32[]{:S(2)}) %collective-permute-start.3) | collective-permute-done | bytes 81952 | tf_op jit(solution)/shard_map/ppermute | solution.py:344
  13.7 14.2 %all_to_all.10.near_ref = bf16[32,2,2048]{2,1,0:T(2,128)(2,1)S(1)} all-to-all(bf16[32,2,2048]{2,1,0:T(2,128)(2,1)S(1)} %shard_map.106), channel_id=1, replica_groups=mesh['grp'=4,'z'=4,'core'=2] {'grp','z','core'}, dimensions={0} | all-to-all | bytes 524288 | tf_op jit(solution)/shard_map/all_to_all | solution.py:394
  27.9 0.4 collective-permute-start.4
  28.3 0.6 %shard_map.107 = (f32[64,512]{1,0:T(8,128)S(1)}, f32[64,512]{1,0:T(8,128)S(1)}) custom-call(bf16[32,2,2048]{2,1,0:T(2,128)(2,1)S(1)} %all_to_all.10.near_ref, bf16[2048,512]{1,0:T(8,128)(2,1)S(1)} %get-tuple-element.36.w_in_ref, bf16[512,2048]{1,0:T(8,128)(2,1)S(1)} %get-tuple-element.37.w_out_ref), custom_call_target="tpu_custom_call" | custom-call | tf_op jit(solution)/shard_map/pallas_call | solution.py:315
  28.9 0.6 %collective-permute-done.4.far_ref = bf16[32,2,2048]{2,1,0:T(2,128)(2,1)S(1)} collective-permute-done((bf16[32,2,2048]{2,1,0:T(2,128)(2,1)S(1)}, bf16[32,2,2048]{2,1,0:T(2,128)(2,1)S(1)}, u32[]{:S(2)}, u32[]{:S(2)}) %collective-permute-start.4) | collective-permute-done | bytes 262176 | tf_op jit(solution)/shard_map/ppermute | solution.py:344
  29.5 1.0 %shard_map.108 = (bf16[64,512]{1,0:T(8,128)(2,1)S(1)}, bf16[64,1024]{1,0:T(8,128)(2,1)S(1)}) custom-call(bf16[32,2,2048]{2,1,0:T(2,128)(2,1)S(1)} %collective-permute-done.4.far_ref, f32[64,512]{1,0:T(8,128)S(1)} %get-tuple-element.38.pre_ref, f32[64,512]{1,0:T(8,128)S(1)} %get-tuple-element.39.back_ref, bf16[2048,512]{1,0:T(8,128)(2,1)S(1)} %get-tuple-element.36.w_in_ref, ...), custom_call_target="tpu_custom_call" | custom-call | tf_op jit(solution)/shard_map/pallas_call | solution.py:315
  30.4 0.4 %collective-permute-start.5 = (bf16[64,1024]{1,0:T(8,128)(2,1)S(1)}, bf16[64,1024]{1,0:T(8,128)(2,1)S(1)}, u32[]{:S(2)}, u32[]{:S(2)}) collective-permute-start(bf16[64,1024]{1,0:T(8,128)(2,1)S(1)} %get-tuple-element.43), channel_id=1, source_target_pairs={{0,1},{1,0},{2,3},{3,2},{4,5},{5,4},{6,7},{7,6},{8,9},{9,8},{10,11... | collective-permute-start | bytes 393224 | tf_op jit(solution)/shard_map/ppermute | solution.py:344
  30.9 0.5 %shard_map.109 = (f32[64,1024]{1,0:T(8,128)S(1)}, bf16[32,2048]{1,0:T(8,128)(2,1)S(1)}) custom-call(bf16[64,512]{1,0:T(8,128)(2,1)S(1)} %get-tuple-element.40.slope_ref, bf16[2048,512]{1,0:T(8,128)(2,1)S(1)} %get-tuple-element.36.w_in_ref, bf16[32,2048]{1,0:T(8,128)(2,1)S(1)} %get-tuple-element.41.near_ref, bf16[20,2048]{1,0:T(8,128)(2,1)S(1)} %collective-permute-done.3.came_ref), custom_call_target="tpu_custom_call" | custom-call | tf_op jit(solution)/shard_map/pallas_call | solution.py:315
  31.4 0.5 %collective-permute-done.5.came_ref = bf16[64,1024]{1,0:T(8,128)(2,1)S(1)} collective-permute-done((bf16[64,1024]{1,0:T(8,128)(2,1)S(1)}, bf16[64,1024]{1,0:T(8,128)(2,1)S(1)}, u32[]{:S(2)}, u32[]{:S(2)}) %collective-permute-start.5) | collective-permute-done | bytes 131104 | tf_op jit(solution)/shard_map/ppermute | solution.py:344
  31.9 10.5 %all_to_all.11.back_ref = bf16[32,2,1024]{2,1,0:T(2,128)(2,1)S(1)} all-to-all(bf16[32,2,1024]{2,1,0:T(2,128)(2,1)S(1)} %shard_map.110), channel_id=1, replica_groups=mesh['grp'=4,'z'=4,'core'=2] {'grp','z','core'}, dimensions={0} | all-to-all | bytes 262144 | tf_op jit(solution)/shard_map/all_to_all | solution.py:415
  42.4 1.4 %shard_map.111 = (bf16[8,4,2048]{2,1,0:T(4,128)(2,1)}, bf16[8,4,2048]{2,1,0:T(4,128)(2,1)}, bf16[8,4,2048]{2,1,0:T(4,128)(2,1)}) custom-call(bf16[2,32,64]{2,1,0:T(8,128)(2,1)S(1)} %get-tuple-element.26.spread_ref, bf16[32,2,1024]{2,1,0:T(2,128)(2,1)S(1)} %all_to_all.11.back_ref, bf16[32,2048]{1,0:T(8,128)(2,1)S(1)} %get-tuple-element.44.cot_ref, ...), custom_call_target="tpu_custom_call" | custom-call | tf_op jit(solution)/shard_map/pallas_call | solution.py:315
  (2 shorter events, 0.1 us)
Async XLA Ops:
  1.7 7.9 %collective-permute-start = (bf16[8,2048]{1,0:T(8,128)(2,1)S(1)}, bf16[8,2048]{1,0:T(8,128)(2,1)S(1)}, u32[]{:S(2)}, u32[]{:S(2)}) collective-permute-start(bf16[8,2048]{1,0:T(8,128)(2,1)S(1)} %get-tuple-element.31), channel_id=1, source_target_pairs={{0,3},{1,2},{2,1},{3,0},{4,7},{5,6},{6,5},{7,4},{8,11},{9,10},{10,... | collective-permute-start | bytes 98312 | tf_op jit(solution)/shard_map/ppermute | solution.py:348
  4.2 5.4 %collective-permute-start.1 = (bf16[8,2048]{1,0:T(8,128)(2,1)S(1)}, bf16[8,2048]{1,0:T(8,128)(2,1)S(1)}, u32[]{:S(2)}, u32[]{:S(2)}) collective-permute-start(bf16[8,2048]{1,0:T(8,128)(2,1)S(1)} %get-tuple-element.32), channel_id=1, source_target_pairs={{0,7},{1,6},{2,5},{3,4},{4,3},{5,2},{6,1},{7,0},{8,15},{9,14},{10,... | collective-permute-start | bytes 98312 | tf_op jit(solution)/shard_map/ppermute | solution.py:348
  7.0 5.1 %collective-permute-start.2 = (bf16[8,2048]{1,0:T(8,128)(2,1)S(1)}, bf16[8,2048]{1,0:T(8,128)(2,1)S(1)}, u32[]{:S(2)}, u32[]{:S(2)}) collective-permute-start(bf16[8,2048]{1,0:T(8,128)(2,1)S(1)} %get-tuple-element.33), channel_id=1, source_target_pairs={{0,5},{1,4},{2,7},{3,6},{4,1},{5,0},{6,3},{7,2},{8,13},{9,12},{10,... | collective-permute-start | bytes 98312 | tf_op jit(solution)/shard_map/ppermute | solution.py:348
  12.3 1.4 %collective-permute-start.3 = (bf16[20,2048]{1,0:T(8,128)(2,1)S(1)}, bf16[20,2048]{1,0:T(8,128)(2,1)S(1)}, u32[]{:S(2)}, u32[]{:S(2)}) collective-permute-start(bf16[20,2048]{1,0:T(8,128)(2,1)S(1)} %get-tuple-element.35), channel_id=1, source_target_pairs={{0,1},{1,0},{2,3},{3,2},{4,5},{5,4},{6,7},{7,6},{8,9},{9,8},{10,11... | collective-permute-start | bytes 245768 | tf_op jit(solution)/shard_map/ppermute | solution.py:344
  27.9 1.5 %collective-permute-start.4 = (bf16[32,2,2048]{2,1,0:T(2,128)(2,1)S(1)}, bf16[32,2,2048]{2,1,0:T(2,128)(2,1)S(1)}, u32[]{:S(2)}, u32[]{:S(2)}) collective-permute-start(bf16[32,2,2048]{2,1,0:T(2,128)(2,1)S(1)} %all_to_all.10.near_ref), channel_id=1, source_target_pairs={{0,1},{1,0},{2,3},{3,2},{4,5},{5,4},{6,7},{7,6},{8,9},{9,8},{10,11... | collective-permute-start | bytes 786440 | tf_op jit(solution)/shard_map/ppermute | solution.py:344
  30.4 1.4 %collective-permute-start.5 = (bf16[64,1024]{1,0:T(8,128)(2,1)S(1)}, bf16[64,1024]{1,0:T(8,128)(2,1)S(1)}, u32[]{:S(2)}, u32[]{:S(2)}) collective-permute-start(bf16[64,1024]{1,0:T(8,128)(2,1)S(1)} %get-tuple-element.43), channel_id=1, source_target_pairs={{0,1},{1,0},{2,3},{3,2},{4,5},{5,4},{6,7},{7,6},{8,9},{9,8},{10,11... | collective-permute-start | bytes 393224 | tf_op jit(solution)/shard_map/ppermute | solution.py:344

commit v18 on v16

--- a/solution.py
+++ b/solution.py
@@ -13,6 +13,7 @@
 CORES = 2
 SUBLANES = 8
 LANES = 128
+PIECE = 256
 
 root_half = 0.7071067811865476
 inv_root_tau = 0.3989422804014327
@@ -76,19 +77,14 @@
     patches_all, share,
     chosen_hbm, gate_hbm, query_hbm, key_hbm, value_hbm, w_in_hbm, w_out_hbm,
     query_rows_ref, key_rows_ref, value_rows_ref, w_in_ref, w_out_ref,
-    probs_ref, picked_ref, take_ref, weight_ref, spread_ref,
+    probs_ref, picked_ref, take_ref, weight_ref, spread_ref, join_ref,
     chosen_ref, gate_ref, query_ref, key_ref, value_ref, sems,
 ):
     core = lax.axis_index("core")
     chip = lax.axis_index("grp") * lax.axis_size("z") + lax.axis_index("z")
-    part = w_in_ref.shape[0] // CORES
     sources = [chosen_hbm, gate_hbm, query_hbm, key_hbm, value_hbm]
-    targets = [chosen_ref, gate_ref, query_ref, key_ref, value_ref]
-    for i in range(CORES):
-        sources.append(w_in_hbm.at[0, part_of(core ^ i, part)])
-        targets.append(w_in_ref.at[pl.ds(i * part, part)])
-        sources.append(w_out_hbm.at[0, :, part_of(core ^ i, part)])
-        targets.append(w_out_ref.at[:, pl.ds(i * part, part)])
+    sources += [w_in_hbm.at[0], w_out_hbm.at[0]]
+    targets = [chosen_ref, gate_ref, query_ref, key_ref, value_ref, w_in_ref, w_out_ref]
     copies = [
         pltpu.make_async_copy(source, target, sems.at[i])
         for i, (source, target) in enumerate(zip(sources, targets))
@@ -141,18 +137,27 @@
     source = (want // blocks) * span + (core ^ 1) * blocks + want % blocks
     take_ref[CORES * slots :] = (source == have).astype(jnp.float32)
     here = jnp.concatenate(found, axis=0).astype(jnp.bfloat16)
-    _, _, returns = spread_ref.shape
-    slot_at = lax.broadcasted_iota(jnp.int32, (experts * MOST, returns), 0)
-    back_at = lax.broadcasted_iota(jnp.int32, (experts * MOST, returns), 1)
-    sender = back_at // MOST
-    same = (sender // share == slot_at // MOST) & (back_at % MOST == slot_at % MOST)
-    for c in range(CORES):
-        spread_ref[c] = lax.dot_general(
-            here,
-            (same & (sender % CORES == c)).astype(jnp.bfloat16),
-            FIRST_BOTH,
-            preferred_element_type=jnp.float32,
-        ).astype(jnp.bfloat16)
+    pieces = spread_ref.shape[0] // rows
+    returns = spread_ref.shape[1]
+    slot_at = lax.broadcasted_iota(jnp.int32, (slots, returns), 0)
+    sender = lax.broadcasted_iota(jnp.int32, (slots, returns), 1) // pieces
+    same = (sender // share == slot_at // MOST) & (sender % CORES == slot_at % MOST)
+    back = lax.dot_general(
+        here, same.astype(jnp.bfloat16), FIRST_BOTH, preferred_element_type=jnp.float32
+    )
+    piece = lax.broadcasted_iota(jnp.int32, (rows, returns), 1) % pieces
+    for j in range(pieces):
+        spread_ref[j * rows : (j + 1) * rows, :] = jnp.where(piece == j, back, 0.0).astype(
+            jnp.bfloat16
+        )
+    want = lax.broadcasted_iota(jnp.int32, join_ref.shape, 0)
+    have = lax.broadcasted_iota(jnp.int32, join_ref.shape, 1)
+    frame = want // blocks
+    level = (frame // CORES) ^ lax.axis_index("z")
+    mine = level * span + core * blocks + want % blocks
+    others = rows + level * blocks + want % blocks
+    source = jnp.where(frame % CORES == held_core(level), mine, others)
+    join_ref[...] = (source == have).astype(jnp.bfloat16)
 
     for copy in copies[2:5]:
         copy.wait()
@@ -198,68 +203,53 @@
 def pack_kernel(share, picked_ref, mine_ref, came_ref, out_ref):
     slots, features = mine_ref.shape
     rows = mine_ref[...] + came_ref[came_ref.shape[0] - slots :, :]
-    part = features // CORES
-    picked = picked_ref[...]
-    both = [
-        jnp.concatenate(
-            [half[:, c * part : (c + 1) * part] for half in (picked, rows)], axis=1
-        )
-        for c in range(CORES)
-    ]
+    rows = [values.astype(jnp.float32) for values in (picked_ref[...], rows)]
     for e in range(out_ref.shape[0] // share):
-        for i in range(share):
-            out_ref[e * share + i] = both[i % CORES][e * MOST : (e + 1) * MOST]
-
-
-def part_of(part, width):
-    return pl.ds(pl.multiple_of(part * width, width), width)
-
-
-def first_kernel(near_ref, w_in_ref, w_out_ref, pre_ref, back_ref):
-    width = w_in_ref.shape[0] // CORES
-    rows = near_ref[...].reshape(pre_ref.shape[0], CORES * width)
-    pre_ref[...] = dot(rows[:, :width], w_in_ref[:width, :])
-    back_ref[...] = dot_lanes(rows[:, width:], w_out_ref[:, :width])
-
-
-def second_kernel(far_ref, pre_ref, back_ref, w_in_ref, w_out_ref, slope_ref, sent_ref):
-    width = w_in_ref.shape[0] // CORES
-    far = far_ref[...].reshape(pre_ref.shape[0], CORES * width)
-    pre_act = pre_ref[...] + dot(far[:, :width], w_in_ref[width:, :])
-    back_act = back_ref[...] + dot_lanes(far[:, width:], w_out_ref[:, width:])
-    slope = (back_act * gelu_slope(pre_act)).astype(jnp.bfloat16)
-    slope_ref[...] = slope
-    sent_ref[...] = dot_lanes(slope, w_in_ref[width:, :]).astype(jnp.bfloat16)
-
-
-def third_kernel(blocks, slope_ref, w_in_ref, near_ref, came_ref, kept_ref, cot_ref):
-    rows = near_ref.shape[0]
-    span = CORES * blocks
-    levels = rows // span
-    want = lax.broadcasted_iota(jnp.int32, (rows, rows), 0)
-    have = lax.broadcasted_iota(jnp.int32, (rows, rows), 1)
-    frame = want // blocks
-    level = (frame // CORES) ^ lax.axis_index("z")
-    here = frame % CORES == held_core(level)
-    source = level * span + lax.axis_index("core") * blocks + want % blocks
-    own = (here & (source == have)).astype(jnp.bfloat16)
-    source = level * blocks + want % blocks
-    others = (jnp.logical_not(here) & (source == have)).astype(jnp.bfloat16)
-    others = others[:, : levels * blocks]
-    cot = dot(own, near_ref[...])
-    cot = cot + dot(others, came_ref[: levels * blocks, :])
-    cot_ref[...] = cot.astype(jnp.bfloat16)
-    width = kept_ref.shape[1]
-    kept_ref[...] = dot_lanes(slope_ref[...], w_in_ref[:width, :])
-
-
-def sum_kernel(kept_ref, came_ref, out_ref):
-    total = kept_ref[...] + came_ref[...].astype(jnp.float32)
-    out_ref[...] = total.astype(jnp.bfloat16).reshape(out_ref.shape)
+        for m in range(MOST):
+            at = e * MOST + m
+            pieces = [
+                values[at : at + 1, start : start + PIECE]
+                for values in rows
+                for start in range(0, features, PIECE)
+            ]
+            message = jnp.concatenate(pieces, axis=0).astype(jnp.bfloat16)
+            for i in range(m, share, CORES):
+                out_ref[e * share + i] = message
+
+
+def expert_kernel(
+    held_ref, w_in_ref, w_out_ref, w_in_far_ref, w_out_far_ref, out_ref, came_ref, sent_ref
+):
+    devices, count, width = held_ref.shape
+    held = held_ref[...].reshape(devices * count, width).astype(jnp.float32)
+    for i in range(came_ref.shape[0]):
+        came_ref[i] = held[:, i * LANES : (i + 1) * LANES]
+
+    def rows_from(first):
+        parts = [
+            came_ref[i, pl.ds(first + j, devices, stride=count), :]
+            for j in range(count // 2)
+            for i in range(came_ref.shape[0])
+        ]
+        return jnp.concatenate(parts, axis=1).astype(jnp.bfloat16)
+
+    rows_in, rows_cot = rows_from(0), rows_from(count // 2)
+    product = None
+    for w_in, w_out in ((w_in_ref, w_out_ref), (w_in_far_ref, w_out_far_ref)):
+        back_act = dot_lanes(rows_cot, w_out[...])
+        slope = back_act * gelu_slope(dot(rows_in, w_in[...]))
+        part = dot_lanes(slope.astype(jnp.bfloat16), w_in[...])
+        product = part if product is None else product + part
+    for j in range(count // 2):
+        for i in range(sent_ref.shape[0]):
+            start = j * width + i * LANES
+            sent_ref[i, pl.ds(j, devices, stride=count // 2), :] = product[:, start : start + LANES]
+    sent = jnp.concatenate([sent_ref[i] for i in range(sent_ref.shape[0])], axis=1)
+    out_ref[...] = sent.astype(jnp.bfloat16).reshape(out_ref.shape)
 
 
 def backward_kernel(
-    spread_ref, back_ref, cot_ref, probs_ref, query_ref, key_ref, value_ref,
+    spread_ref, back_ref, join_ref, cot_near_ref, came_ref, probs_ref, query_ref, key_ref, value_ref,
     grad_query_hbm, grad_key_hbm, grad_value_hbm,
     grad_query_ref, grad_key_ref, grad_value_ref, sems,
 ):
@@ -267,9 +257,12 @@
     rows = frames * blocks
     scaling = (features // HEADS) ** (-0.5)
     query, key, value = query_ref[...], key_ref[...], value_ref[...]
-    back = back_ref[...].reshape(-1, back_ref.shape[2])
-    added = jnp.concatenate([dot(spread_ref[c], back) for c in range(CORES)], axis=1)
-    stream = (cot_ref[...].astype(jnp.float32) + added).astype(jnp.bfloat16)
+    back = dot(spread_ref[...], back_ref[...].reshape(-1, back_ref.shape[2]))
+    added = jnp.concatenate(
+        [back[start : start + rows] for start in range(0, back.shape[0], rows)], axis=1
+    )
+    cot = jnp.concatenate([cot_near_ref[...], came_ref[: join_ref.shape[1] - rows, :]], axis=0)
+    stream = (dot(join_ref[...], cot) + added).astype(jnp.bfloat16)
     probs = probs_ref[...]
     weights = probs.astype(jnp.bfloat16)
     copies = []
@@ -336,8 +329,6 @@
     share = devices // experts
     rows = frames * blocks
     slots = experts * MOST
-    part = features // CORES
-    hidden = w_in.shape[2]
     everyone = ("grp", "z", "core")
 
     def swap(values):
@@ -357,7 +348,7 @@
     )
     order = [0] + [i ^ (i >> 1) for i in range(levels - 1, 0, -1)]
     parts = [across(parts[k], k) if k else parts[k] for k in order]
-    query, key, value, w_in_near, w_out_near, probs, picked, take, weight, spread = call(
+    query, key, value, w_in_near, w_out_near, probs, picked, take, weight, spread, join = call(
         functools.partial(forward_kernel, blocks * devices, share),
         [
             *[((rows, features), bf16)] * 3,
@@ -367,7 +358,8 @@
             ((slots, features), bf16),
             ((CORES * slots + levels * blocks, rows), f32),
             ((CORES * slots, LANES), f32),
-            ((CORES, rows, devices * MOST), bf16),
+            ((rows * features // PIECE, devices * features // PIECE), bf16),
+            ((rows, rows + levels * blocks), bf16),
         ],
         [chosen, gate_probs, query_in, key_in, value_in, w_in, w_out],
         "hhhhhhh",
@@ -375,7 +367,7 @@
             pltpu.VMEM(chosen.shape, jnp.int32),
             pltpu.VMEM(gate_probs.shape, f32),
             *[pltpu.VMEM(query_in.shape, bf16)] * 3,
-            pltpu.SemaphoreType.DMA((5 + 2 * CORES,)),
+            pltpu.SemaphoreType.DMA((7,)),
         ],
     )
     cot_near, mine, sent = call(
@@ -387,37 +379,29 @@
     came_near = swap(sent)
     (outgoing,) = call(
         functools.partial(pack_kernel, share),
-        [((devices, MOST, 2 * part), bf16)],
+        [((devices, 2 * features // PIECE, PIECE), bf16)],
         [picked, mine, came_near],
         "vvv",
     )
+    outgoing, w_in_near, w_out_near = lax.optimization_barrier((outgoing, w_in_near, w_out_near))
+    w_in_far, w_out_far = swap(w_in_near), swap(w_out_near)
     held = lax.all_to_all(outgoing, everyone, split_axis=0, concat_axis=0, tiled=True)
-    other = swap(held)
-    acts = (devices * MOST, hidden)
-    halves = (devices * MOST, part)
-    pre_act, back_act = call(
-        first_kernel, [(acts, f32), (acts, f32)], [held, w_in_near, w_out_near], "vvv"
-    )
-    slope, sent = call(
-        second_kernel,
-        [(acts, bf16), (halves, bf16)],
-        [other, pre_act, back_act, w_in_near, w_out_near],
+    (sent_back,) = call(
+        expert_kernel,
+        [((devices, features // PIECE, PIECE), bf16)],
+        [held, w_in_near, w_out_near, w_in_far, w_out_far],
         "vvvvv",
-    )
-    came = swap(sent)
-    kept, cot = call(
-        functools.partial(third_kernel, blocks),
-        [(halves, f32), ((rows, features), bf16)],
-        [slope, w_in_near, cot_near, came_near],
-        "vvvv",
-    )
-    (total,) = call(sum_kernel, [((devices, MOST, part), bf16)], [kept, came], "vv")
-    back = lax.all_to_all(total, everyone, split_axis=0, concat_axis=0, tiled=True)
+        [
+            pltpu.VMEM((PIECE // LANES, devices * 2 * features // PIECE, LANES), f32),
+            pltpu.VMEM((PIECE // LANES, devices * features // PIECE, LANES), f32),
+        ],
+    )
+    back = lax.all_to_all(sent_back, everyone, split_axis=0, concat_axis=0, tiled=True)
     return call(
         backward_kernel,
         [((frames, blocks, features), bf16)] * 3,
-        [spread, back, cot, probs, query, key, value],
-        "vvvvvvv",
+        [spread, back, join, cot_near, came_near, probs, query, key, value],
+        "vvvvvvvvv",
         [pltpu.VMEM((frames, blocks, features), bf16)] * 3 + [pltpu.SemaphoreType.DMA((3,))],
         "h",
     )

time: 43.5 us -> 43.6 us (level)
  Pallas kernels: 7.3 us -> 8.71 us
  waiting for transfers between devices: 3.01 us -> 1.95 us
    pallas_call x9 -> x6, Pallas kernels: 7.3 us -> 8.71 us  [call(): pl.pallas_call(kernel, out_shape=[jax.ShapeDtypeStruct(shape, dtype) for...]
    ppermute x3, waiting for transfers between devices: 1.96 us -> 0.95 us  [swap(): return lax.ppermute(values, 'core', [(i, i ^ 1) for i in range(CORES)])]
  transfers between devices with their start and end apart: 6 -> 6, of which waited for: 5 -> 3; matrix products, arithmetic and copies ran while one was open for 0% -> 0% of each run, Pallas kernels for 8% -> 6%
where the time goes in v18:
time: 43.6 us; the launch traced here: 43.4 us
  blocking collectives  25.4 us (58%)
  Pallas kernels  8.71 us (20%)
  starting transfers between devices  6.7 us (15%)
  waiting for transfers between devices  1.95 us (4%)
  between operations  0.68 us (2%)
    all_to_all x1, blocking collectives, body(): lax.all_to_all(outgoing, everyone, split_axis=0, concat_axis=0, tiled=True)  14.9 us
    all_to_all x1, blocking collectives, body(): lax.all_to_all(sent_back, everyone, split_axis=0, concat_axis=0, tiled=True)  10.5 us
    pallas_call x6, Pallas kernels, call(): pl.pallas_call(kernel, out_shape=[jax.ShapeDtypeStruct(shape, dtype) for...  8.71 us
    ppermute x3, starting transfers between devices, across(): return lax.ppermute(values, ('z', 'core'), pairs)  5.4 us
    ppermute x3, starting transfers between devices, swap(): return lax.ppermute(values, 'core', [(i, i ^ 1) for i in range(CORES)])  1.3 us
    ppermute x3, waiting for transfers between devices, across(): return lax.ppermute(values, ('z', 'core'), pairs)  1 us
    ppermute x3, waiting for transfers between devices, swap(): return lax.ppermute(values, 'core', [(i, i ^ 1) for i in range(CORES)])  0.95 us
  transfers between devices with their start and end apart: 6, of which 3 were waited for; matrix products, arithmetic and copies ran while one was open for 0% of the time, Pallas kernels for 6%

profile of v18, /device:TPU:0, one launch (start us, length us, event | category | flops | bytes accessed | tf_op | source)
XLA Modules:
  0.0 43.4 jit_solution(14527341536998590925)
XLA Ops:
  0.6 1.1 %shard_map.104 = (bf16[8,2048]{1,0:T(8,128)(2,1)S(1)}, bf16[8,2048]{1,0:T(8,128)(2,1)S(1)}, bf16[8,2048]{1,0:T(8,128)(2,1)S(1)}, bf16[8,2048]{1,0:T(8,128)(2,1)S(1)}) custom-call(bf16[1,32,2048]{2,1,0:T(8,128)(2,1)} %cot_hbm.1), custom_call_target="tpu_custom_call" | custom-call | tf_op jit(solution)/shard_map/pallas_call | solution.py:308
  1.7 3.5 %collective-permute-start = (bf16[8,2048]{1,0:T(8,128)(2,1)S(1)}, bf16[8,2048]{1,0:T(8,128)(2,1)S(1)}, u32[]{:S(2)}, u32[]{:S(2)}) collective-permute-start(bf16[8,2048]{1,0:T(8,128)(2,1)S(1)} %get-tuple-element.29), channel_id=1, source_target_pairs={{0,5},{1,4},{2,7},{3,6},{4,1},{5,0},{6,3},{7,2},{8,13},{9,12},{10,... | collective-permute-start | bytes 98312 | tf_op jit(solution)/shard_map/ppermute | solution.py:339
  5.3 1.6 %collective-permute-start.1 = (bf16[8,2048]{1,0:T(8,128)(2,1)S(1)}, bf16[8,2048]{1,0:T(8,128)(2,1)S(1)}, u32[]{:S(2)}, u32[]{:S(2)}) collective-permute-start(bf16[8,2048]{1,0:T(8,128)(2,1)S(1)} %get-tuple-element.30), channel_id=1, source_target_pairs={{0,7},{1,6},{2,5},{3,4},{4,3},{5,2},{6,1},{7,0},{8,15},{9,14},{10,... | collective-permute-start | bytes 98312 | tf_op jit(solution)/shard_map/ppermute | solution.py:339
  6.9 0.2 collective-permute-start.2
  7.1 2.5 %shard_map.103 = (bf16[32,2048]{1,0:T(8,128)(2,1)S(1)}, bf16[32,2048]{1,0:T(8,128)(2,1)S(1)}, bf16[32,2048]{1,0:T(8,128)(2,1)S(1)}, bf16[2048,512]{1,0:T(8,128)(...) custom-call(s32[2,32]{1,0:T(2,128)} %chosen_hbm.1, ...), custom_call_target="tpu_custom_call" | custom-call | tf_op jit(solution)/shard_map/pallas_call | solution.py:308
  9.6 0.0 collective-permute-done.refs_1_
  9.7 0.8 %collective-permute-done.1.refs_2_ = bf16[8,2048]{1,0:T(8,128)(2,1)S(1)} collective-permute-done((bf16[8,2048]{1,0:T(8,128)(2,1)S(1)}, bf16[8,2048]{1,0:T(8,128)(2,1)S(1)}, u32[]{:S(2)}, u32[]{:S(2)}) %collective-permute-start.1) | collective-permute-done | bytes 32800 | tf_op jit(solution)/shard_map/ppermute | solution.py:339
  10.5 0.2 collective-permute-done.2.refs_3_
  10.7 0.2 shard_map.105
  10.8 0.7 %collective-permute-start.3 = (bf16[20,2048]{1,0:T(8,128)(2,1)S(1)}, bf16[20,2048]{1,0:T(8,128)(2,1)S(1)}, u32[]{:S(2)}, u32[]{:S(2)}) collective-permute-start(bf16[20,2048]{1,0:T(8,128)(2,1)S(1)} %get-tuple-element.33), channel_id=1, source_target_pairs={{0,1},{1,0},{2,3},{3,2},{4,5},{5,4},{6,7},{7,6},{8,9},{9,8},{10,11... | collective-permute-start | bytes 245768 | tf_op jit(solution)/shard_map/ppermute | solution.py:335
  11.6 0.9 %collective-permute-done.3.came_ref = bf16[20,2048]{1,0:T(8,128)(2,1)S(1)} collective-permute-done((bf16[20,2048]{1,0:T(8,128)(2,1)S(1)}, bf16[20,2048]{1,0:T(8,128)(2,1)S(1)}, u32[]{:S(2)}, u32[]{:S(2)}) %collective-permute-start.3) | collective-permute-done | bytes 81952 | tf_op jit(solution)/shard_map/ppermute | solution.py:335
  12.5 0.4 collective-permute-start.4
  13.0 0.2 collective-permute-start.5
  13.1 14.9 %all_to_all.10.held_ref = bf16[32,16,256]{2,1,0:T(8,128)(2,1)S(1)} all-to-all(bf16[32,16,256]{2,1,0:T(8,128)(2,1)S(1)} %shard_map.106), channel_id=1, replica_groups=mesh['grp'=4,'z'=4,'core'=2] {'grp','z','core'}, dimensions={0} | all-to-all | bytes 524288 | tf_op jit(solution)/shard_map/all_to_all | solution.py:388
  28.0 0.0 collective-permute-done.4.w_in_far_ref
  28.0 0.0 collective-permute-done.5.w_out_far_ref
  28.0 3.4 %shard_map.107 = bf16[32,8,256]{2,1,0:T(8,128)(2,1)S(1)} custom-call(bf16[32,16,256]{2,1,0:T(8,128)(2,1)S(1)} %all_to_all.10.held_ref, bf16[2048,512]{1,0:T(8,128)(2,1)S(1)} %get-tuple-element.37.w_in_ref, bf16[512,2048]{1,0:T(8,128)(2,1)S(1)} %get-tuple-element.38.w_out_ref, bf16[2048,512]{1,0:T(8,128)(2,1)S(1)} %collective-permute-done.4.w_in_far_ref, ...), custom_call_target="tpu_custom_call" | custom-call | tf_op jit(solution)/shard_map/pallas_call | solution.py:308
  31.4 10.5 %all_to_all.11.back_ref = bf16[32,8,256]{2,1,0:T(8,128)(2,1)S(1)} all-to-all(bf16[32,8,256]{2,1,0:T(8,128)(2,1)S(1)} %shard_map.107), channel_id=1, replica_groups=mesh['grp'=4,'z'=4,'core'=2] {'grp','z','core'}, dimensions={0} | all-to-all | bytes 262144 | tf_op jit(solution)/shard_map/all_to_all | solution.py:399
  41.9 1.6 %shard_map.108 = (bf16[8,4,2048]{2,1,0:T(4,128)(2,1)}, bf16[8,4,2048]{2,1,0:T(4,128)(2,1)}, bf16[8,4,2048]{2,1,0:T(4,128)(2,1)}) custom-call(bf16[256,256]{1,0:T(8,128)(2,1)S(1)} %get-tuple-element.24.spread_ref, bf16[32,8,256]{2,1,0:T(8,128)(2,1)S(1)} %all_to_all.11.back_ref, bf16[32,48]{1,0:T(8,128)(2,1)S(1)} %get-tuple-element.39.join_ref, ...), custom_call_target="tpu_custom_call" | custom-call | tf_op jit(solution)/shard_map/pallas_call | solution.py:308
  (1 shorter events, 0.0 us)
Async XLA Ops:
  1.7 7.9 %collective-permute-start = (bf16[8,2048]{1,0:T(8,128)(2,1)S(1)}, bf16[8,2048]{1,0:T(8,128)(2,1)S(1)}, u32[]{:S(2)}, u32[]{:S(2)}) collective-permute-start(bf16[8,2048]{1,0:T(8,128)(2,1)S(1)} %get-tuple-element.29), channel_id=1, source_target_pairs={{0,5},{1,4},{2,7},{3,6},{4,1},{5,0},{6,3},{7,2},{8,13},{9,12},{10,... | collective-permute-start | bytes 98312 | tf_op jit(solution)/shard_map/ppermute | solution.py:339
  5.3 5.2 %collective-permute-start.1 = (bf16[8,2048]{1,0:T(8,128)(2,1)S(1)}, bf16[8,2048]{1,0:T(8,128)(2,1)S(1)}, u32[]{:S(2)}, u32[]{:S(2)}) collective-permute-start(bf16[8,2048]{1,0:T(8,128)(2,1)S(1)} %get-tuple-element.30), channel_id=1, source_target_pairs={{0,7},{1,6},{2,5},{3,4},{4,3},{5,2},{6,1},{7,0},{8,15},{9,14},{10,... | collective-permute-start | bytes 98312 | tf_op jit(solution)/shard_map/ppermute | solution.py:339
  6.9 3.8 %collective-permute-start.2 = (bf16[8,2048]{1,0:T(8,128)(2,1)S(1)}, bf16[8,2048]{1,0:T(8,128)(2,1)S(1)}, u32[]{:S(2)}, u32[]{:S(2)}) collective-permute-start(bf16[8,2048]{1,0:T(8,128)(2,1)S(1)} %get-tuple-element.31), channel_id=1, source_target_pairs={{0,3},{1,2},{2,1},{3,0},{4,7},{5,6},{6,5},{7,4},{8,11},{9,10},{10,... | collective-permute-start | bytes 98312 | tf_op jit(solution)/shard_map/ppermute | solution.py:339
  10.8 1.7 %collective-permute-start.3 = (bf16[20,2048]{1,0:T(8,128)(2,1)S(1)}, bf16[20,2048]{1,0:T(8,128)(2,1)S(1)}, u32[]{:S(2)}, u32[]{:S(2)}) collective-permute-start(bf16[20,2048]{1,0:T(8,128)(2,1)S(1)} %get-tuple-element.33), channel_id=1, source_target_pairs={{0,1},{1,0},{2,3},{3,2},{4,5},{5,4},{6,7},{7,6},{8,9},{9,8},{10,11... | collective-permute-start | bytes 245768 | tf_op jit(solution)/shard_map/ppermute | solution.py:335
  12.5 15.5 %collective-permute-start.4 = (bf16[2048,512]{1,0:T(8,128)(2,1)S(1)}, bf16[2048,512]{1,0:T(8,128)(2,1)S(1)}, u32[]{:S(2)}, u32[]{:S(2)}) collective-permute-start(bf16[2048,512]{1,0:T(8,128)(2,1)S(1)} %get-tuple-element.37.w_in_ref), channel_id=1, source_target_pairs={{0,1},{1,0},{2,3},{3,2},{4,5},{5,4},{6,7},{7,6},{8,9},{9,8},{10,11... | collective-permute-start | bytes 6291464 | tf_op jit(solution)/shard_map/ppermute | solution.py:335
  13.0 15.0 %collective-permute-start.5 = (bf16[512,2048]{1,0:T(8,128)(2,1)S(1)}, bf16[512,2048]{1,0:T(8,128)(2,1)S(1)}, u32[]{:S(2)}, u32[]{:S(2)}) collective-permute-start(bf16[512,2048]{1,0:T(8,128)(2,1)S(1)} %get-tuple-element.38.w_out_ref), channel_id=1, source_target_pairs={{0,1},{1,0},{2,3},{3,2},{4,5},{5,4},{6,7},{7,6},{8,9},{9,8},{10,11... | collective-permute-start | bytes 6291464 | tf_op jit(solution)/shard_map/ppermute | solution.py:335

commit v19 on v16

--- a/solution.py
+++ b/solution.py
@@ -13,6 +13,7 @@
 CORES = 2
 SUBLANES = 8
 LANES = 128
+PIECE = 256
 
 root_half = 0.7071067811865476
 inv_root_tau = 0.3989422804014327
@@ -56,15 +57,16 @@
     *part_refs, cot_ref, sem = refs
     copy = pltpu.make_async_copy(cot_hbm, cot_ref, sem)
     copy.start()
-    rows = cot_ref.shape[1]
-    want = lax.broadcasted_iota(jnp.int32, (rows, rows), 0)
-    have = lax.broadcasted_iota(jnp.int32, (rows, rows), 1)
-    source = ((want // span) ^ lax.axis_index("z")) * span + want % span
-    order = (source == have).astype(jnp.bfloat16)
+    level = lax.axis_index("z")
     copy.wait()
-    turned = dot(order, cot_ref[0]).astype(jnp.bfloat16)
-    for k, part_ref in enumerate(part_refs):
-        part_ref[...] = turned[k * span : (k + 1) * span]
+    parts = [cot_ref[0, k * span : (k + 1) * span, :] for k in range(len(part_refs))]
+    bit = 1
+    while bit < len(parts):
+        turn = (level // bit) % 2 == 1
+        parts = [jnp.where(turn, parts[k ^ bit], parts[k]) for k in range(len(parts))]
+        bit *= 2
+    for part_ref, part in zip(part_refs, parts):
+        part_ref[...] = part
 
 
 def held_core(level):
@@ -141,18 +143,20 @@
     source = (want // blocks) * span + (core ^ 1) * blocks + want % blocks
     take_ref[CORES * slots :] = (source == have).astype(jnp.float32)
     here = jnp.concatenate(found, axis=0).astype(jnp.bfloat16)
-    _, _, returns = spread_ref.shape
-    slot_at = lax.broadcasted_iota(jnp.int32, (experts * MOST, returns), 0)
-    back_at = lax.broadcasted_iota(jnp.int32, (experts * MOST, returns), 1)
-    sender = back_at // MOST
-    same = (sender // share == slot_at // MOST) & (back_at % MOST == slot_at % MOST)
-    for c in range(CORES):
-        spread_ref[c] = lax.dot_general(
-            here,
-            (same & (sender % CORES == c)).astype(jnp.bfloat16),
-            FIRST_BOTH,
-            preferred_element_type=jnp.float32,
-        ).astype(jnp.bfloat16)
+    pieces = spread_ref.shape[0] // (rows * CORES)
+    returns = spread_ref.shape[1]
+    slot_at = lax.broadcasted_iota(jnp.int32, (slots, returns), 0)
+    back_at = lax.broadcasted_iota(jnp.int32, (slots, returns), 1) // pieces
+    same = (back_at // MOST // share == slot_at // MOST) & (back_at % MOST == slot_at % MOST)
+    back = lax.dot_general(
+        here, same.astype(jnp.bfloat16), FIRST_BOTH, preferred_element_type=jnp.float32
+    )
+    back_at = lax.broadcasted_iota(jnp.int32, (rows, returns), 1)
+    piece = back_at // (MOST * pieces) % CORES * pieces + back_at % pieces
+    for j in range(CORES * pieces):
+        spread_ref[j * rows : (j + 1) * rows, :] = jnp.where(piece == j, back, 0.0).astype(
+            jnp.bfloat16
+        )
 
     for copy in copies[2:5]:
         copy.wait()
@@ -253,8 +257,16 @@
     kept_ref[...] = dot_lanes(slope_ref[...], w_in_ref[:width, :])
 
 
-def sum_kernel(kept_ref, came_ref, out_ref):
+def sum_kernel(kept_ref, came_ref, out_ref, piece_ref):
     total = kept_ref[...] + came_ref[...].astype(jnp.float32)
+    count, width = total.shape
+    pieces = width // PIECE
+    parts = piece_ref.shape[0]
+    for j in range(pieces):
+        for i in range(parts):
+            start = j * PIECE + i * LANES
+            piece_ref[i, pl.ds(j, count, stride=pieces), :] = total[:, start : start + LANES]
+    total = jnp.concatenate([piece_ref[i] for i in range(parts)], axis=1)
     out_ref[...] = total.astype(jnp.bfloat16).reshape(out_ref.shape)
 
 
@@ -267,8 +279,10 @@
     rows = frames * blocks
     scaling = (features // HEADS) ** (-0.5)
     query, key, value = query_ref[...], key_ref[...], value_ref[...]
-    back = back_ref[...].reshape(-1, back_ref.shape[2])
-    added = jnp.concatenate([dot(spread_ref[c], back) for c in range(CORES)], axis=1)
+    back = dot(spread_ref[...], back_ref[...].reshape(-1, PIECE))
+    added = jnp.concatenate(
+        [back[start : start + rows] for start in range(0, back.shape[0], rows)], axis=1
+    )
     stream = (cot_ref[...].astype(jnp.float32) + added).astype(jnp.bfloat16)
     probs = probs_ref[...]
     weights = probs.astype(jnp.bfloat16)
@@ -367,7 +381,7 @@
             ((slots, features), bf16),
             ((CORES * slots + levels * blocks, rows), f32),
             ((CORES * slots, LANES), f32),
-            ((CORES, rows, devices * MOST), bf16),
+            ((rows * features // PIECE, devices * MOST * part // PIECE), bf16),
         ],
         [chosen, gate_probs, query_in, key_in, value_in, w_in, w_out],
         "hhhhhhh",
@@ -411,7 +425,14 @@
         [slope, w_in_near, cot_near, came_near],
         "vvvv",
     )
-    (total,) = call(sum_kernel, [((devices, MOST, part), bf16)], [kept, came], "vv")
+    pieces = MOST * part // PIECE
+    (total,) = call(
+        sum_kernel,
+        [((devices, pieces, PIECE), bf16)],
+        [kept, came],
+        "vv",
+        [pltpu.VMEM((PIECE // LANES, devices * pieces, LANES), f32)],
+    )
     back = lax.all_to_all(total, everyone, split_axis=0, concat_axis=0, tiled=True)
     return call(
         backward_kernel,

time: 43.5 us -> 43.4 us (level)
  no operation moved by 1% of the time
where the time goes in v19:
time: 43.4 us; the launch traced here: 43.2 us
  blocking collectives  25.4 us (59%)
  Pallas kernels  7.21 us (17%)
  starting transfers between devices  6.95 us (16%)
  waiting for transfers between devices  3 us (7%)
  between operations  0.69 us (2%)
    all_to_all x1, blocking collectives, body(): lax.all_to_all(outgoing, everyone, split_axis=0, concat_axis=0, tiled=True)  14.9 us
    all_to_all x1, blocking collectives, body(): lax.all_to_all(total, everyone, split_axis=0, concat_axis=0, tiled=True)  10.5 us
    pallas_call x9, Pallas kernels, call(): pl.pallas_call(kernel, out_shape=[jax.ShapeDtypeStruct(shape, dtype) for...  7.21 us
    ppermute x3, starting transfers between devices, across(): return lax.ppermute(values, ('z', 'core'), pairs)  5.4 us
    ppermute x3, waiting for transfers between devices, swap(): return lax.ppermute(values, 'core', [(i, i ^ 1) for i in range(CORES)])  1.95 us
    ppermute x3, starting transfers between devices, swap(): return lax.ppermute(values, 'core', [(i, i ^ 1) for i in range(CORES)])  1.55 us
    ppermute x3, waiting for transfers between devices, across(): return lax.ppermute(values, ('z', 'core'), pairs)  1.05 us
  transfers between devices with their start and end apart: 6, of which 5 were waited for; matrix products, arithmetic and copies ran while one was open for 0% of the time, Pallas kernels for 8%

profile of v19, /device:TPU:0, one launch (start us, length us, event | category | flops | bytes accessed | tf_op | source)
XLA Modules:
  0.0 43.2 jit_solution(16674690595223579109)
XLA Ops:
  0.6 0.9 %shard_map.104 = (bf16[8,2048]{1,0:T(8,128)(2,1)S(1)}, bf16[8,2048]{1,0:T(8,128)(2,1)S(1)}, bf16[8,2048]{1,0:T(8,128)(2,1)S(1)}, bf16[8,2048]{1,0:T(8,128)(2,1)S(1)}) custom-call(bf16[1,32,2048]{2,1,0:T(8,128)(2,1)} %cot_hbm.1), custom_call_target="tpu_custom_call" | custom-call | tf_op jit(solution)/shard_map/pallas_call | solution.py:329
  1.6 3.5 %collective-permute-start = (bf16[8,2048]{1,0:T(8,128)(2,1)S(1)}, bf16[8,2048]{1,0:T(8,128)(2,1)S(1)}, u32[]{:S(2)}, u32[]{:S(2)}) collective-permute-start(bf16[8,2048]{1,0:T(8,128)(2,1)S(1)} %get-tuple-element.31), channel_id=1, source_target_pairs={{0,5},{1,4},{2,7},{3,6},{4,1},{5,0},{6,3},{7,2},{8,13},{9,12},{10,... | collective-permute-start | bytes 98312 | tf_op jit(solution)/shard_map/ppermute | solution.py:362
  5.1 1.6 %collective-permute-start.1 = (bf16[8,2048]{1,0:T(8,128)(2,1)S(1)}, bf16[8,2048]{1,0:T(8,128)(2,1)S(1)}, u32[]{:S(2)}, u32[]{:S(2)}) collective-permute-start(bf16[8,2048]{1,0:T(8,128)(2,1)S(1)} %get-tuple-element.32), channel_id=1, source_target_pairs={{0,7},{1,6},{2,5},{3,4},{4,3},{5,2},{6,1},{7,0},{8,15},{9,14},{10,... | collective-permute-start | bytes 98312 | tf_op jit(solution)/shard_map/ppermute | solution.py:362
  6.7 0.2 collective-permute-start.2
  7.0 2.5 %shard_map.103 = (bf16[32,2048]{1,0:T(8,128)(2,1)S(1)}, bf16[32,2048]{1,0:T(8,128)(2,1)S(1)}, bf16[32,2048]{1,0:T(8,128)(2,1)S(1)}, bf16[2048,512]{1,0:T(8,128)(...) custom-call(s32[2,32]{1,0:T(2,128)} %chosen_hbm.1, ...), custom_call_target="tpu_custom_call" | custom-call | tf_op jit(solution)/shard_map/pallas_call | solution.py:329
  9.5 0.0 collective-permute-done.refs_1_
  9.5 0.9 %collective-permute-done.1.refs_2_ = bf16[8,2048]{1,0:T(8,128)(2,1)S(1)} collective-permute-done((bf16[8,2048]{1,0:T(8,128)(2,1)S(1)}, bf16[8,2048]{1,0:T(8,128)(2,1)S(1)}, u32[]{:S(2)}, u32[]{:S(2)}) %collective-permute-start.1) | collective-permute-done | bytes 32800 | tf_op jit(solution)/shard_map/ppermute | solution.py:362
  10.4 0.2 collective-permute-done.2.refs_3_
  10.5 0.2 shard_map.105
  10.7 0.7 %collective-permute-start.3 = (bf16[20,2048]{1,0:T(8,128)(2,1)S(1)}, bf16[20,2048]{1,0:T(8,128)(2,1)S(1)}, u32[]{:S(2)}, u32[]{:S(2)}) collective-permute-start(bf16[20,2048]{1,0:T(8,128)(2,1)S(1)} %get-tuple-element.35), channel_id=1, source_target_pairs={{0,1},{1,0},{2,3},{3,2},{4,5},{5,4},{6,7},{7,6},{8,9},{9,8},{10,11... | collective-permute-start | bytes 245768 | tf_op jit(solution)/shard_map/ppermute | solution.py:358
  11.4 0.9 %collective-permute-done.3.came_ref = bf16[20,2048]{1,0:T(8,128)(2,1)S(1)} collective-permute-done((bf16[20,2048]{1,0:T(8,128)(2,1)S(1)}, bf16[20,2048]{1,0:T(8,128)(2,1)S(1)}, u32[]{:S(2)}, u32[]{:S(2)}) %collective-permute-start.3) | collective-permute-done | bytes 81952 | tf_op jit(solution)/shard_map/ppermute | solution.py:358
  12.4 14.9 %all_to_all.10.near_ref = bf16[32,2,2048]{2,1,0:T(2,128)(2,1)S(1)} all-to-all(bf16[32,2,2048]{2,1,0:T(2,128)(2,1)S(1)} %shard_map.106), channel_id=1, replica_groups=mesh['grp'=4,'z'=4,'core'=2] {'grp','z','core'}, dimensions={0} | all-to-all | bytes 524288 | tf_op jit(solution)/shard_map/all_to_all | solution.py:408
  27.3 0.4 collective-permute-start.4
  27.7 0.6 %shard_map.107 = (f32[64,512]{1,0:T(8,128)S(1)}, f32[64,512]{1,0:T(8,128)S(1)}) custom-call(bf16[32,2,2048]{2,1,0:T(2,128)(2,1)S(1)} %all_to_all.10.near_ref, bf16[2048,512]{1,0:T(8,128)(2,1)S(1)} %get-tuple-element.36.w_in_ref, bf16[512,2048]{1,0:T(8,128)(2,1)S(1)} %get-tuple-element.37.w_out_ref), custom_call_target="tpu_custom_call" | custom-call | tf_op jit(solution)/shard_map/pallas_call | solution.py:329
  28.3 0.6 %collective-permute-done.4.far_ref = bf16[32,2,2048]{2,1,0:T(2,128)(2,1)S(1)} collective-permute-done((bf16[32,2,2048]{2,1,0:T(2,128)(2,1)S(1)}, bf16[32,2,2048]{2,1,0:T(2,128)(2,1)S(1)}, u32[]{:S(2)}, u32[]{:S(2)}) %collective-permute-start.4) | collective-permute-done | bytes 262176 | tf_op jit(solution)/shard_map/ppermute | solution.py:358
  28.8 1.0 %shard_map.108 = (bf16[64,512]{1,0:T(8,128)(2,1)S(1)}, bf16[64,1024]{1,0:T(8,128)(2,1)S(1)}) custom-call(bf16[32,2,2048]{2,1,0:T(2,128)(2,1)S(1)} %collective-permute-done.4.far_ref, f32[64,512]{1,0:T(8,128)S(1)} %get-tuple-element.38.pre_ref, f32[64,512]{1,0:T(8,128)S(1)} %get-tuple-element.39.back_ref, bf16[2048,512]{1,0:T(8,128)(2,1)S(1)} %get-tuple-element.36.w_in_ref, ...), custom_call_target="tpu_custom_call" | custom-call | tf_op jit(solution)/shard_map/pallas_call | solution.py:329
  29.8 0.4 %collective-permute-start.5 = (bf16[64,1024]{1,0:T(8,128)(2,1)S(1)}, bf16[64,1024]{1,0:T(8,128)(2,1)S(1)}, u32[]{:S(2)}, u32[]{:S(2)}) collective-permute-start(bf16[64,1024]{1,0:T(8,128)(2,1)S(1)} %get-tuple-element.43), channel_id=1, source_target_pairs={{0,1},{1,0},{2,3},{3,2},{4,5},{5,4},{6,7},{7,6},{8,9},{9,8},{10,11... | collective-permute-start | bytes 393224 | tf_op jit(solution)/shard_map/ppermute | solution.py:358
  30.2 0.5 %shard_map.109 = (f32[64,1024]{1,0:T(8,128)S(1)}, bf16[32,2048]{1,0:T(8,128)(2,1)S(1)}) custom-call(bf16[64,512]{1,0:T(8,128)(2,1)S(1)} %get-tuple-element.40.slope_ref, bf16[2048,512]{1,0:T(8,128)(2,1)S(1)} %get-tuple-element.36.w_in_ref, bf16[32,2048]{1,0:T(8,128)(2,1)S(1)} %get-tuple-element.41.near_ref, bf16[20,2048]{1,0:T(8,128)(2,1)S(1)} %collective-permute-done.3.came_ref), custom_call_target="tpu_custom_call" | custom-call | tf_op jit(solution)/shard_map/pallas_call | solution.py:329
  30.8 0.5 %collective-permute-done.5.came_ref = bf16[64,1024]{1,0:T(8,128)(2,1)S(1)} collective-permute-done((bf16[64,1024]{1,0:T(8,128)(2,1)S(1)}, bf16[64,1024]{1,0:T(8,128)(2,1)S(1)}, u32[]{:S(2)}, u32[]{:S(2)}) %collective-permute-start.5) | collective-permute-done | bytes 131104 | tf_op jit(solution)/shard_map/ppermute | solution.py:358
  31.3 10.5 %all_to_all.11.back_ref = bf16[32,8,256]{2,1,0:T(8,128)(2,1)S(1)} all-to-all(bf16[32,8,256]{2,1,0:T(8,128)(2,1)S(1)} %shard_map.110), channel_id=1, replica_groups=mesh['grp'=4,'z'=4,'core'=2] {'grp','z','core'}, dimensions={0} | all-to-all | bytes 262144 | tf_op jit(solution)/shard_map/all_to_all | solution.py:436
  41.8 1.5 %shard_map.111 = (bf16[8,4,2048]{2,1,0:T(4,128)(2,1)}, bf16[8,4,2048]{2,1,0:T(4,128)(2,1)}, bf16[8,4,2048]{2,1,0:T(4,128)(2,1)}) custom-call(bf16[256,256]{1,0:T(8,128)(2,1)S(1)} %get-tuple-element.26.spread_ref, bf16[32,8,256]{2,1,0:T(8,128)(2,1)S(1)} %all_to_all.11.back_ref, bf16[32,2048]{1,0:T(8,128)(2,1)S(1)} %get-tuple-element.44.cot_ref, ...), custom_call_target="tpu_custom_call" | custom-call | tf_op jit(solution)/shard_map/pallas_call | solution.py:329
  (2 shorter events, 0.1 us)
Async XLA Ops:
  1.6 7.9 %collective-permute-start = (bf16[8,2048]{1,0:T(8,128)(2,1)S(1)}, bf16[8,2048]{1,0:T(8,128)(2,1)S(1)}, u32[]{:S(2)}, u32[]{:S(2)}) collective-permute-start(bf16[8,2048]{1,0:T(8,128)(2,1)S(1)} %get-tuple-element.31), channel_id=1, source_target_pairs={{0,5},{1,4},{2,7},{3,6},{4,1},{5,0},{6,3},{7,2},{8,13},{9,12},{10,... | collective-permute-start | bytes 98312 | tf_op jit(solution)/shard_map/ppermute | solution.py:362
  5.1 5.2 %collective-permute-start.1 = (bf16[8,2048]{1,0:T(8,128)(2,1)S(1)}, bf16[8,2048]{1,0:T(8,128)(2,1)S(1)}, u32[]{:S(2)}, u32[]{:S(2)}) collective-permute-start(bf16[8,2048]{1,0:T(8,128)(2,1)S(1)} %get-tuple-element.32), channel_id=1, source_target_pairs={{0,7},{1,6},{2,5},{3,4},{4,3},{5,2},{6,1},{7,0},{8,15},{9,14},{10,... | collective-permute-start | bytes 98312 | tf_op jit(solution)/shard_map/ppermute | solution.py:362
  6.7 3.8 %collective-permute-start.2 = (bf16[8,2048]{1,0:T(8,128)(2,1)S(1)}, bf16[8,2048]{1,0:T(8,128)(2,1)S(1)}, u32[]{:S(2)}, u32[]{:S(2)}) collective-permute-start(bf16[8,2048]{1,0:T(8,128)(2,1)S(1)} %get-tuple-element.33), channel_id=1, source_target_pairs={{0,3},{1,2},{2,1},{3,0},{4,7},{5,6},{6,5},{7,4},{8,11},{9,10},{10,... | collective-permute-start | bytes 98312 | tf_op jit(solution)/shard_map/ppermute | solution.py:362
  10.7 1.7 %collective-permute-start.3 = (bf16[20,2048]{1,0:T(8,128)(2,1)S(1)}, bf16[20,2048]{1,0:T(8,128)(2,1)S(1)}, u32[]{:S(2)}, u32[]{:S(2)}) collective-permute-start(bf16[20,2048]{1,0:T(8,128)(2,1)S(1)} %get-tuple-element.35), channel_id=1, source_target_pairs={{0,1},{1,0},{2,3},{3,2},{4,5},{5,4},{6,7},{7,6},{8,9},{9,8},{10,11... | collective-permute-start | bytes 245768 | tf_op jit(solution)/shard_map/ppermute | solution.py:358
  27.3 1.5 %collective-permute-start.4 = (bf16[32,2,2048]{2,1,0:T(2,128)(2,1)S(1)}, bf16[32,2,2048]{2,1,0:T(2,128)(2,1)S(1)}, u32[]{:S(2)}, u32[]{:S(2)}) collective-permute-start(bf16[32,2,2048]{2,1,0:T(2,128)(2,1)S(1)} %all_to_all.10.near_ref), channel_id=1, source_target_pairs={{0,1},{1,0},{2,3},{3,2},{4,5},{5,4},{6,7},{7,6},{8,9},{9,8},{10,11... | collective-permute-start | bytes 786440 | tf_op jit(solution)/shard_map/ppermute | solution.py:358
  29.8 1.4 %collective-permute-start.5 = (bf16[64,1024]{1,0:T(8,128)(2,1)S(1)}, bf16[64,1024]{1,0:T(8,128)(2,1)S(1)}, u32[]{:S(2)}, u32[]{:S(2)}) collective-permute-start(bf16[64,1024]{1,0:T(8,128)(2,1)S(1)} %get-tuple-element.43), channel_id=1, source_target_pairs={{0,1},{1,0},{2,3},{3,2},{4,5},{5,4},{6,7},{7,6},{8,9},{9,8},{10,11... | collective-permute-start | bytes 393224 | tf_op jit(solution)/shard_map/ppermute | solution.py:358

commit v20 on v19

--- a/solution.py
+++ b/solution.py
@@ -53,25 +53,20 @@
     return [values[:, h * width : (h + 1) * width] for h in range(HEADS)]
 
 
-def turn_kernel(span, cot_hbm, *refs):
+def turn_kernel(blocks, cot_hbm, *refs):
     *part_refs, cot_ref, sem = refs
     copy = pltpu.make_async_copy(cot_hbm, cot_ref, sem)
     copy.start()
-    level = lax.axis_index("z")
+    column = lax.axis_index("z") * CORES + lax.axis_index("core")
     copy.wait()
-    parts = [cot_ref[0, k * span : (k + 1) * span, :] for k in range(len(part_refs))]
+    parts = [cot_ref[0, k * blocks : (k + 1) * blocks, :] for k in range(len(part_refs))]
     bit = 1
     while bit < len(parts):
-        turn = (level // bit) % 2 == 1
+        turn = (column // bit) % 2 == 1
         parts = [jnp.where(turn, parts[k ^ bit], parts[k]) for k in range(len(parts))]
         bit *= 2
     for part_ref, part in zip(part_refs, parts):
         part_ref[...] = part
-
-
-def held_core(level):
-    core = lax.axis_index("core")
-    return jnp.where(level == 0, core, 1 - core)
 
 
 def forward_kernel(
@@ -110,7 +105,7 @@
     ).astype(jnp.bfloat16)
     slot = lax.broadcasted_iota(jnp.int32, (SUBLANES, cap), 0)
     row_at = lax.broadcasted_iota(jnp.int32, (rows, cap), 0)
-    span = CORES * blocks
+    column = lax.axis_index("z") * CORES + core
     slots = experts * MOST
     found = []
     for e in range(experts):
@@ -118,30 +113,18 @@
         gates = gate_ref[e : e + 1, :]
         patch = tokens % patches_all
         frame = tokens // patches_all
-        level = (frame // CORES) ^ lax.axis_index("z")
-        for i in range(CORES):
-            owned = patch // blocks == chip * CORES + (core ^ i)
-            owned = jnp.broadcast_to(owned.astype(jnp.float32), slot.shape)
-            rank = dot(owned.astype(jnp.bfloat16), before)
-            taken = jnp.where((rank == slot.astype(jnp.float32)) & (owned > 0.0), 1.0, 0.0)
-            weight = jnp.sum(taken * gates, axis=1, keepdims=True)
-            taken = taken.astype(jnp.bfloat16)
-            place = jnp.where(
-                frame % CORES == held_core(level),
-                level * span + (core ^ i) * blocks + patch % blocks,
-                -1,
-            )
-            at = slice(i * slots + e * MOST, i * slots + (e + 1) * MOST)
-            take_ref[at] = dot_lanes(taken, (row_at == place).astype(jnp.bfloat16))[:MOST]
-            weight_ref[at] = jnp.broadcast_to(weight[:MOST], (MOST, weight_ref.shape[1]))
-            if i == 0:
-                position = frame * blocks + patch % blocks
-                found.append(dot_lanes(taken, (row_at == position).astype(jnp.bfloat16))[:MOST])
-    levels = rows // span
-    want = lax.broadcasted_iota(jnp.int32, (levels * blocks, rows), 0)
-    have = lax.broadcasted_iota(jnp.int32, (levels * blocks, rows), 1)
-    source = (want // blocks) * span + (core ^ 1) * blocks + want % blocks
-    take_ref[CORES * slots :] = (source == have).astype(jnp.float32)
+        owned = patch // blocks == chip * CORES + core
+        owned = jnp.broadcast_to(owned.astype(jnp.float32), slot.shape)
+        rank = dot(owned.astype(jnp.bfloat16), before)
+        taken = jnp.where((rank == slot.astype(jnp.float32)) & (owned > 0.0), 1.0, 0.0)
+        weight = jnp.sum(taken * gates, axis=1, keepdims=True)
+        taken = taken.astype(jnp.bfloat16)
+        at = slice(e * MOST, (e + 1) * MOST)
+        place = (frame ^ column) * blocks + patch % blocks
+        take_ref[at] = dot_lanes(taken, (row_at == place).astype(jnp.bfloat16))[:MOST]
+        weight_ref[at] = jnp.broadcast_to(weight[:MOST], (MOST, weight_ref.shape[1]))
+        position = frame * blocks + patch % blocks
+        found.append(dot_lanes(taken, (row_at == position).astype(jnp.bfloat16))[:MOST])
     here = jnp.concatenate(found, axis=0).astype(jnp.bfloat16)
     pieces = spread_ref.shape[0] // (rows * CORES)
     returns = spread_ref.shape[1]
@@ -186,23 +169,14 @@
         copy.wait()
 
 
-def pick_kernel(order, take_ref, weight_ref, *refs):
-    *part_refs, cot_ref, mine_ref, sent_ref = refs
+def pick_kernel(share, order, take_ref, weight_ref, picked_ref, *refs):
+    *part_refs, cot_ref, out_ref = refs
     parts = [part_refs[order.index(k)][...] for k in range(len(order))]
     cot = jnp.concatenate(parts, axis=0)
     cot_ref[...] = cot
-    slots = mine_ref.shape[0]
     rows = dot(take_ref[...].astype(jnp.bfloat16), cot)
-    picks = (rows[: CORES * slots] * weight_ref[:, :1]).astype(jnp.bfloat16)
-    mine_ref[...] = picks[:slots]
-    away = rows[CORES * slots :].astype(jnp.bfloat16)
-    sent_ref[...] = jnp.concatenate([away, picks[slots:]], axis=0)
-
-
-def pack_kernel(share, picked_ref, mine_ref, came_ref, out_ref):
-    slots, features = mine_ref.shape
-    rows = mine_ref[...] + came_ref[came_ref.shape[0] - slots :, :]
-    part = features // CORES
+    rows = (rows * weight_ref[:, :1]).astype(jnp.bfloat16)
+    part = rows.shape[1] // CORES
     picked = picked_ref[...]
     both = [
         jnp.concatenate(
@@ -236,22 +210,13 @@
     sent_ref[...] = dot_lanes(slope, w_in_ref[width:, :]).astype(jnp.bfloat16)
 
 
-def third_kernel(blocks, slope_ref, w_in_ref, near_ref, came_ref, kept_ref, cot_ref):
+def third_kernel(blocks, slope_ref, w_in_ref, near_ref, kept_ref, cot_ref):
     rows = near_ref.shape[0]
-    span = CORES * blocks
-    levels = rows // span
     want = lax.broadcasted_iota(jnp.int32, (rows, rows), 0)
     have = lax.broadcasted_iota(jnp.int32, (rows, rows), 1)
-    frame = want // blocks
-    level = (frame // CORES) ^ lax.axis_index("z")
-    here = frame % CORES == held_core(level)
-    source = level * span + lax.axis_index("core") * blocks + want % blocks
-    own = (here & (source == have)).astype(jnp.bfloat16)
-    source = level * blocks + want % blocks
-    others = (jnp.logical_not(here) & (source == have)).astype(jnp.bfloat16)
-    others = others[:, : levels * blocks]
-    cot = dot(own, near_ref[...])
-    cot = cot + dot(others, came_ref[: levels * blocks, :])
+    column = lax.axis_index("z") * CORES + lax.axis_index("core")
+    source = ((want // blocks) ^ column) * blocks + want % blocks
+    cot = dot((source == have).astype(jnp.bfloat16), near_ref[...])
     cot_ref[...] = cot.astype(jnp.bfloat16)
     width = kept_ref.shape[1]
     kept_ref[...] = dot_lanes(slope_ref[...], w_in_ref[:width, :])
@@ -358,18 +323,18 @@
         return lax.ppermute(values, "core", [(i, i ^ 1) for i in range(CORES)])
 
     def across(values, step):
-        pairs = [(i, i ^ (CORES * step) ^ 1) for i in range(columns)]
+        pairs = [(i, i ^ step) for i in range(columns)]
         return lax.ppermute(values, ("z", "core"), pairs)
 
-    span = CORES * blocks
     parts = call(
-        functools.partial(turn_kernel, span),
-        [((span, features), bf16)] * levels,
+        functools.partial(turn_kernel, blocks),
+        [((blocks, features), bf16)] * columns,
         [cotangent],
         "h",
         [pltpu.VMEM(cotangent.shape, bf16), pltpu.SemaphoreType.DMA],
     )
-    order = [0] + [i ^ (i >> 1) for i in range(levels - 1, 0, -1)]
+    order = [i ^ (i >> 1) for i in range(levels - 1, 0, -1)]
+    order = [0] + [CORES * k + c for k in order for c in (1, 0)] + [1]
     parts = [across(parts[k], k) if k else parts[k] for k in order]
     query, key, value, w_in_near, w_out_near, probs, picked, take, weight, spread = call(
         functools.partial(forward_kernel, blocks * devices, share),
@@ -379,8 +344,8 @@
             (w_out.shape[1:], bf16),
             ((rows, HEADS * rows), f32),
             ((slots, features), bf16),
-            ((CORES * slots + levels * blocks, rows), f32),
-            ((CORES * slots, LANES), f32),
+            ((slots, rows), f32),
+            ((slots, LANES), f32),
             ((rows * features // PIECE, devices * MOST * part // PIECE), bf16),
         ],
         [chosen, gate_probs, query_in, key_in, value_in, w_in, w_out],
@@ -392,18 +357,11 @@
             pltpu.SemaphoreType.DMA((5 + 2 * CORES,)),
         ],
     )
-    cot_near, mine, sent = call(
-        functools.partial(pick_kernel, order),
-        [((rows, features), bf16), ((slots, features), bf16), ((levels * blocks + slots, features), bf16)],
-        [take, weight, *parts],
-        "vv" + "v" * levels,
-    )
-    came_near = swap(sent)
-    (outgoing,) = call(
-        functools.partial(pack_kernel, share),
-        [((devices, MOST, 2 * part), bf16)],
-        [picked, mine, came_near],
-        "vvv",
+    cot_near, outgoing = call(
+        functools.partial(pick_kernel, share, order),
+        [((rows, features), bf16), ((devices, MOST, 2 * part), bf16)],
+        [take, weight, picked, *parts],
+        "vvv" + "v" * columns,
     )
     held = lax.all_to_all(outgoing, everyone, split_axis=0, concat_axis=0, tiled=True)
     other = swap(held)
@@ -422,8 +380,8 @@
     kept, cot = call(
         functools.partial(third_kernel, blocks),
         [(halves, f32), ((rows, features), bf16)],
-        [slope, w_in_near, cot_near, came_near],
-        "vvvv",
+        [slope, w_in_near, cot_near],
+        "vvv",
     )
     pieces = MOST * part // PIECE
     (total,) = call(

time: 43.4 us -> 46.1 us (1.062)
  starting transfers between devices: 6.95 us -> 10.3 us
  waiting for transfers between devices: 3 us -> 2.1 us
    ppermute x3 -> x7, starting transfers between devices: 5.4 us -> 9.51 us  [across(): return lax.ppermute(values, ('z', 'core'), pairs)]
    ppermute x3 -> x2, waiting for transfers between devices: 1.95 us -> 1.05 us  [swap(): return lax.ppermute(values, 'core', [(i, i ^ 1) for i in range(CORES)])]
    ppermute x3 -> x2, starting transfers between devices: 1.55 us -> 0.82 us  [swap(): return lax.ppermute(values, 'core', [(i, i ^ 1) for i in range(CORES)])]
    pallas_call x9 -> x8, Pallas kernels: 7.21 us -> 7.2 us  [call(): pl.pallas_call(kernel, out_shape=[jax.ShapeDtypeStruct(shape, dtype) for...]
    ppermute x3 -> x7, waiting for transfers between devices: 1.05 us -> 1.05 us  [across(): return lax.ppermute(values, ('z', 'core'), pairs)]
  transfers between devices with their start and end apart: 6 -> 9, of which waited for: 5 -> 3; matrix products, arithmetic and copies ran while one was open for 0% -> 0% of each run, Pallas kernels for 8% -> 8%
where the time goes in v20:
time: 46.1 us; the launch traced here: 45.9 us
  blocking collectives  25.6 us (56%)
  starting transfers between devices  10.3 us (22%)
  Pallas kernels  7.2 us (16%)
  waiting for transfers between devices  2.1 us (5%)
  between operations  0.69 us (1%)
    all_to_all x1, blocking collectives, body(): lax.all_to_all(outgoing, everyone, split_axis=0, concat_axis=0, tiled=True)  15.1 us
    all_to_all x1, blocking collectives, body(): lax.all_to_all(total, everyone, split_axis=0, concat_axis=0, tiled=True)  10.5 us
    ppermute x7, starting transfers between devices, across(): return lax.ppermute(values, ('z', 'core'), pairs)  9.51 us
    pallas_call x8, Pallas kernels, call(): pl.pallas_call(kernel, out_shape=[jax.ShapeDtypeStruct(shape, dtype) for...  7.2 us
    ppermute x2, waiting for transfers between devices, swap(): return lax.ppermute(values, 'core', [(i, i ^ 1) for i in range(CORES)])  1.05 us
    ppermute x7, waiting for transfers between devices, across(): return lax.ppermute(values, ('z', 'core'), pairs)  1.05 us
  transfers between devices with their start and end apart: 9, of which 3 were waited for; matrix products, arithmetic and copies ran while one was open for 0% of the time, Pallas kernels for 8%

profile of v20, /device:TPU:0, one launch (start us, length us, event | category | flops | bytes accessed | tf_op | source)
XLA Modules:
  0.0 45.9 jit_solution(17795519812031592916)
XLA Ops:
  0.6 1.0 %shard_map.104 = (bf16[4,2048]{1,0:T(4,128)(2,1)S(1)}, bf16[4,2048]{1,0:T(4,128)(2,1)S(1)}, bf16[4,2048]{1,0:T(4,128)(2,1)S(1)}, bf16[4,2048]{1,0:T(4,128)(2,1)S...) custom-call(bf16[1,32,2048]{2,1,0:T(8,128)(2,1)} %cot_hbm.1), custom_call_target="tpu_custom_call" | custom-call | tf_op jit(solution)/shard_map/pallas_call | solution.py:294
  1.6 3.5 %collective-permute-start = (bf16[4,2048]{1,0:T(4,128)(2,1)S(1)}, bf16[4,2048]{1,0:T(4,128)(2,1)S(1)}, u32[]{:S(2)}, u32[]{:S(2)}) collective-permute-start(bf16[4,2048]{1,0:T(4,128)(2,1)S(1)} %get-tuple-element.34), channel_id=1, source_target_pairs={{0,5},{1,4},{2,7},{3,6},{4,1},{5,0},{6,3},{7,2},{8,13},{9,12},{10,... | collective-permute-start | bytes 49160 | tf_op jit(solution)/shard_map/ppermute | solution.py:327
  5.2 0.6 %collective-permute-start.1 = (bf16[4,2048]{1,0:T(4,128)(2,1)S(1)}, bf16[4,2048]{1,0:T(4,128)(2,1)S(1)}, u32[]{:S(2)}, u32[]{:S(2)}) collective-permute-start(bf16[4,2048]{1,0:T(4,128)(2,1)S(1)} %get-tuple-element.35), channel_id=1, source_target_pairs={{0,4},{1,5},{2,6},{3,7},{4,0},{5,1},{6,2},{7,3},{8,12},{9,13},{10,... | collective-permute-start | bytes 49160 | tf_op jit(solution)/shard_map/ppermute | solution.py:327
  5.8 3.3 %collective-permute-start.2 = (bf16[4,2048]{1,0:T(4,128)(2,1)S(1)}, bf16[4,2048]{1,0:T(4,128)(2,1)S(1)}, u32[]{:S(2)}, u32[]{:S(2)}) collective-permute-start(bf16[4,2048]{1,0:T(4,128)(2,1)S(1)} %get-tuple-element.36), channel_id=1, source_target_pairs={{0,7},{1,6},{2,5},{3,4},{4,3},{5,2},{6,1},{7,0},{8,15},{9,14},{10,... | collective-permute-start | bytes 49160 | tf_op jit(solution)/shard_map/ppermute | solution.py:327
  9.1 0.1 collective-permute-start.3
  9.3 0.0 collective-permute-start.4
  9.3 0.0 collective-permute-done.refs_1_
  9.3 1.8 %collective-permute-start.5 = (bf16[4,2048]{1,0:T(4,128)(2,1)S(1)}, bf16[4,2048]{1,0:T(4,128)(2,1)S(1)}, u32[]{:S(2)}, u32[]{:S(2)}) collective-permute-start(bf16[4,2048]{1,0:T(4,128)(2,1)S(1)} %get-tuple-element.39), channel_id=1, source_target_pairs={{0,2},{1,3},{2,0},{3,1},{4,6},{5,7},{6,4},{7,5},{8,10},{9,11},{10,... | collective-permute-start | bytes 49160 | tf_op jit(solution)/shard_map/ppermute | solution.py:327
  11.1 0.0 collective-permute-done.1.refs_2_
  11.1 0.0 collective-permute-start.6
  11.1 2.5 %shard_map.103 = (bf16[32,2048]{1,0:T(8,128)(2,1)S(1)}, bf16[32,2048]{1,0:T(8,128)(2,1)S(1)}, bf16[32,2048]{1,0:T(8,128)(2,1)S(1)}, bf16[2048,512]{1,0:T(8,128)(...) custom-call(s32[2,32]{1,0:T(2,128)} %chosen_hbm.1, ...), custom_call_target="tpu_custom_call" | custom-call | tf_op jit(solution)/shard_map/pallas_call | solution.py:294
  13.6 0.0 collective-permute-done.2.refs_3_
  13.6 1.0 %collective-permute-done.3.refs_4_ = bf16[4,2048]{1,0:T(4,128)(2,1)S(1)} collective-permute-done((bf16[4,2048]{1,0:T(4,128)(2,1)S(1)}, bf16[4,2048]{1,0:T(4,128)(2,1)S(1)}, u32[]{:S(2)}, u32[]{:S(2)}) %collective-permute-start.3) | collective-permute-done | bytes 16416 | tf_op jit(solution)/shard_map/ppermute | solution.py:327
  14.7 0.0 collective-permute-done.4.refs_5_
  14.7 0.0 collective-permute-done.5.refs_6_
  14.7 0.0 collective-permute-done.6.refs_7_
  14.7 0.2 shard_map.105
  14.9 15.1 %all_to_all.10.near_ref = bf16[32,2,2048]{2,1,0:T(2,128)(2,1)S(1)} all-to-all(bf16[32,2,2048]{2,1,0:T(2,128)(2,1)S(1)} %get-tuple-element.41), channel_id=1, replica_groups=mesh['grp'=4,'z'=4,'core'=2] {'grp','z','core'}, dimensions={0} | all-to-all | bytes 524288 | tf_op jit(solution)/shard_map/all_to_all | solution.py:366
  30.0 0.4 collective-permute-start.7
  30.4 0.6 %shard_map.106 = (f32[64,512]{1,0:T(8,128)S(1)}, f32[64,512]{1,0:T(8,128)S(1)}) custom-call(bf16[32,2,2048]{2,1,0:T(2,128)(2,1)S(1)} %all_to_all.10.near_ref, bf16[2048,512]{1,0:T(8,128)(2,1)S(1)} %get-tuple-element.42.w_in_ref, bf16[512,2048]{1,0:T(8,128)(2,1)S(1)} %get-tuple-element.43.w_out_ref), custom_call_target="tpu_custom_call" | custom-call | tf_op jit(solution)/shard_map/pallas_call | solution.py:294
  31.0 0.6 %collective-permute-done.7.far_ref = bf16[32,2,2048]{2,1,0:T(2,128)(2,1)S(1)} collective-permute-done((bf16[32,2,2048]{2,1,0:T(2,128)(2,1)S(1)}, bf16[32,2,2048]{2,1,0:T(2,128)(2,1)S(1)}, u32[]{:S(2)}, u32[]{:S(2)}) %collective-permute-start.7) | collective-permute-done | bytes 262176 | tf_op jit(solution)/shard_map/ppermute | solution.py:323
  31.5 1.0 %shard_map.107 = (bf16[64,512]{1,0:T(8,128)(2,1)S(1)}, bf16[64,1024]{1,0:T(8,128)(2,1)S(1)}) custom-call(bf16[32,2,2048]{2,1,0:T(2,128)(2,1)S(1)} %collective-permute-done.7.far_ref, f32[64,512]{1,0:T(8,128)S(1)} %get-tuple-element.44.pre_ref, f32[64,512]{1,0:T(8,128)S(1)} %get-tuple-element.45.back_ref, bf16[2048,512]{1,0:T(8,128)(2,1)S(1)} %get-tuple-element.42.w_in_ref, ...), custom_call_target="tpu_custom_call" | custom-call | tf_op jit(solution)/shard_map/pallas_call | solution.py:294
  32.5 0.4 collective-permute-start.8
  32.9 0.5 %shard_map.108 = (f32[64,1024]{1,0:T(8,128)S(1)}, bf16[32,2048]{1,0:T(8,128)(2,1)S(1)}) custom-call(bf16[64,512]{1,0:T(8,128)(2,1)S(1)} %get-tuple-element.46.slope_ref, bf16[2048,512]{1,0:T(8,128)(2,1)S(1)} %get-tuple-element.42.w_in_ref, bf16[32,2048]{1,0:T(8,128)(2,1)S(1)} %get-tuple-element.47.near_ref), custom_call_target="tpu_custom_call" | custom-call | tf_op jit(solution)/shard_map/pallas_call | solution.py:294
  33.4 0.5 %collective-permute-done.8.came_ref = bf16[64,1024]{1,0:T(8,128)(2,1)S(1)} collective-permute-done((bf16[64,1024]{1,0:T(8,128)(2,1)S(1)}, bf16[64,1024]{1,0:T(8,128)(2,1)S(1)}, u32[]{:S(2)}, u32[]{:S(2)}) %collective-permute-start.8) | collective-permute-done | bytes 131104 | tf_op jit(solution)/shard_map/ppermute | solution.py:323
  34.0 10.5 %all_to_all.11.back_ref = bf16[32,8,256]{2,1,0:T(8,128)(2,1)S(1)} all-to-all(bf16[32,8,256]{2,1,0:T(8,128)(2,1)S(1)} %shard_map.109), channel_id=1, replica_groups=mesh['grp'=4,'z'=4,'core'=2] {'grp','z','core'}, dimensions={0} | all-to-all | bytes 262144 | tf_op jit(solution)/shard_map/all_to_all | solution.py:394
  44.5 1.5 %shard_map.110 = (bf16[8,4,2048]{2,1,0:T(4,128)(2,1)}, bf16[8,4,2048]{2,1,0:T(4,128)(2,1)}, bf16[8,4,2048]{2,1,0:T(4,128)(2,1)}) custom-call(bf16[256,256]{1,0:T(8,128)(2,1)S(1)} %get-tuple-element.29.spread_ref, bf16[32,8,256]{2,1,0:T(8,128)(2,1)S(1)} %all_to_all.11.back_ref, bf16[32,2048]{1,0:T(8,128)(2,1)S(1)} %get-tuple-element.50.cot_ref, ...), custom_call_target="tpu_custom_call" | custom-call | tf_op jit(solution)/shard_map/pallas_call | solution.py:294
  (1 shorter events, 0.0 us)
Async XLA Ops:
  1.6 7.7 %collective-permute-start = (bf16[4,2048]{1,0:T(4,128)(2,1)S(1)}, bf16[4,2048]{1,0:T(4,128)(2,1)S(1)}, u32[]{:S(2)}, u32[]{:S(2)}) collective-permute-start(bf16[4,2048]{1,0:T(4,128)(2,1)S(1)} %get-tuple-element.34), channel_id=1, source_target_pairs={{0,5},{1,4},{2,7},{3,6},{4,1},{5,0},{6,3},{7,2},{8,13},{9,12},{10,... | collective-permute-start | bytes 49160 | tf_op jit(solution)/shard_map/ppermute | solution.py:327
  5.2 5.9 %collective-permute-start.1 = (bf16[4,2048]{1,0:T(4,128)(2,1)S(1)}, bf16[4,2048]{1,0:T(4,128)(2,1)S(1)}, u32[]{:S(2)}, u32[]{:S(2)}) collective-permute-start(bf16[4,2048]{1,0:T(4,128)(2,1)S(1)} %get-tuple-element.35), channel_id=1, source_target_pairs={{0,4},{1,5},{2,6},{3,7},{4,0},{5,1},{6,2},{7,3},{8,12},{9,13},{10,... | collective-permute-start | bytes 49160 | tf_op jit(solution)/shard_map/ppermute | solution.py:327
  5.8 7.8 %collective-permute-start.2 = (bf16[4,2048]{1,0:T(4,128)(2,1)S(1)}, bf16[4,2048]{1,0:T(4,128)(2,1)S(1)}, u32[]{:S(2)}, u32[]{:S(2)}) collective-permute-start(bf16[4,2048]{1,0:T(4,128)(2,1)S(1)} %get-tuple-element.36), channel_id=1, source_target_pairs={{0,7},{1,6},{2,5},{3,4},{4,3},{5,2},{6,1},{7,0},{8,15},{9,14},{10,... | collective-permute-start | bytes 49160 | tf_op jit(solution)/shard_map/ppermute | solution.py:327
  9.1 5.5 %collective-permute-start.3 = (bf16[4,2048]{1,0:T(4,128)(2,1)S(1)}, bf16[4,2048]{1,0:T(4,128)(2,1)S(1)}, u32[]{:S(2)}, u32[]{:S(2)}) collective-permute-start(bf16[4,2048]{1,0:T(4,128)(2,1)S(1)} %get-tuple-element.37), channel_id=1, source_target_pairs={{0,6},{1,7},{2,4},{3,5},{4,2},{5,3},{6,0},{7,1},{8,14},{9,15},{10,... | collective-permute-start | bytes 49160 | tf_op jit(solution)/shard_map/ppermute | solution.py:327
  9.3 5.4 %collective-permute-start.4 = (bf16[4,2048]{1,0:T(4,128)(2,1)S(1)}, bf16[4,2048]{1,0:T(4,128)(2,1)S(1)}, u32[]{:S(2)}, u32[]{:S(2)}) collective-permute-start(bf16[4,2048]{1,0:T(4,128)(2,1)S(1)} %get-tuple-element.38), channel_id=1, source_target_pairs={{0,3},{1,2},{2,1},{3,0},{4,7},{5,6},{6,5},{7,4},{8,11},{9,10},{10,... | collective-permute-start | bytes 49160 | tf_op jit(solution)/shard_map/ppermute | solution.py:327
  9.3 5.4 %collective-permute-start.5 = (bf16[4,2048]{1,0:T(4,128)(2,1)S(1)}, bf16[4,2048]{1,0:T(4,128)(2,1)S(1)}, u32[]{:S(2)}, u32[]{:S(2)}) collective-permute-start(bf16[4,2048]{1,0:T(4,128)(2,1)S(1)} %get-tuple-element.39), channel_id=1, source_target_pairs={{0,2},{1,3},{2,0},{3,1},{4,6},{5,7},{6,4},{7,5},{8,10},{9,11},{10,... | collective-permute-start | bytes 49160 | tf_op jit(solution)/shard_map/ppermute | solution.py:327
  11.1 3.6 %collective-permute-start.6 = (bf16[4,2048]{1,0:T(4,128)(2,1)S(1)}, bf16[4,2048]{1,0:T(4,128)(2,1)S(1)}, u32[]{:S(2)}, u32[]{:S(2)}) collective-permute-start(bf16[4,2048]{1,0:T(4,128)(2,1)S(1)} %get-tuple-element.40), channel_id=1, source_target_pairs={{0,1},{1,0},{2,3},{3,2},{4,5},{5,4},{6,7},{7,6},{8,9},{9,8},{10,11... | collective-permute-start | bytes 49160 | tf_op jit(solution)/shard_map/ppermute | solution.py:327
  30.0 1.5 %collective-permute-start.7 = (bf16[32,2,2048]{2,1,0:T(2,128)(2,1)S(1)}, bf16[32,2,2048]{2,1,0:T(2,128)(2,1)S(1)}, u32[]{:S(2)}, u32[]{:S(2)}) collective-permute-start(bf16[32,2,2048]{2,1,0:T(2,128)(2,1)S(1)} %all_to_all.10.near_ref), channel_id=1, source_target_pairs={{0,1},{1,0},{2,3},{3,2},{4,5},{5,4},{6,7},{7,6},{8,9},{9,8},{10,11... | collective-permute-start | bytes 786440 | tf_op jit(solution)/shard_map/ppermute | solution.py:323
  32.5 1.4 %collective-permute-start.8 = (bf16[64,1024]{1,0:T(8,128)(2,1)S(1)}, bf16[64,1024]{1,0:T(8,128)(2,1)S(1)}, u32[]{:S(2)}, u32[]{:S(2)}) collective-permute-start(bf16[64,1024]{1,0:T(8,128)(2,1)S(1)} %get-tuple-element.49), channel_id=1, source_target_pairs={{0,1},{1,0},{2,3},{3,2},{4,5},{5,4},{6,7},{7,6},{8,9},{9,8},{10,11... | collective-permute-start | bytes 393224 | tf_op jit(solution)/shard_map/ppermute | solution.py:323

commit v21 on v19

--- a/solution.py
+++ b/solution.py
@@ -295,13 +295,13 @@
         copy.start()
         copies.append(copy)
 
+    grad_prob = jnp.concatenate(
+        [dot_lanes(v, g) for v, g in zip(heads_of(value), heads_of(stream))], axis=1
+    )
     put(
         grad_value_ref,
         grad_value_hbm,
         [dot(w, g) for w, g in zip(heads_of(weights), heads_of(stream))],
-    )
-    grad_prob = jnp.concatenate(
-        [dot_lanes(v, g) for v, g in zip(heads_of(value), heads_of(stream))], axis=1
     )
     centre = over_frames(probs * grad_prob, jnp.add, blocks)
     grad_score = probs * (grad_prob - centre)

time: 43.4 us -> 43.4 us (level)
  no operation moved by 1% of the time
where the time goes in v21:
time: 43.4 us; the launch traced here: 43.2 us
  blocking collectives  25.4 us (59%)
  Pallas kernels  7.17 us (17%)
  starting transfers between devices  6.95 us (16%)
  waiting for transfers between devices  3 us (7%)
  between operations  0.69 us (2%)
    all_to_all x1, blocking collectives, body(): lax.all_to_all(outgoing, everyone, split_axis=0, concat_axis=0, tiled=True)  14.9 us
    all_to_all x1, blocking collectives, body(): lax.all_to_all(total, everyone, split_axis=0, concat_axis=0, tiled=True)  10.5 us
    pallas_call x9, Pallas kernels, call(): pl.pallas_call(kernel, out_shape=[jax.ShapeDtypeStruct(shape, dtype) for...  7.17 us
    ppermute x3, starting transfers between devices, across(): return lax.ppermute(values, ('z', 'core'), pairs)  5.4 us
    ppermute x3, waiting for transfers between devices, swap(): return lax.ppermute(values, 'core', [(i, i ^ 1) for i in range(CORES)])  1.95 us
    ppermute x3, starting transfers between devices, swap(): return lax.ppermute(values, 'core', [(i, i ^ 1) for i in range(CORES)])  1.55 us
    ppermute x3, waiting for transfers between devices, across(): return lax.ppermute(values, ('z', 'core'), pairs)  1.05 us
  transfers between devices with their start and end apart: 6, of which 5 were waited for; matrix products, arithmetic and copies ran while one was open for 0% of the time, Pallas kernels for 8%

profile of v21, /device:TPU:0, one launch (start us, length us, event | category | flops | bytes accessed | tf_op | source)
XLA Modules:
  0.0 43.2 jit_solution(8713458714131911255)
XLA Ops:
  0.6 0.9 %shard_map.104 = (bf16[8,2048]{1,0:T(8,128)(2,1)S(1)}, bf16[8,2048]{1,0:T(8,128)(2,1)S(1)}, bf16[8,2048]{1,0:T(8,128)(2,1)S(1)}, bf16[8,2048]{1,0:T(8,128)(2,1)S(1)}) custom-call(bf16[1,32,2048]{2,1,0:T(8,128)(2,1)} %cot_hbm.1), custom_call_target="tpu_custom_call" | custom-call | tf_op jit(solution)/shard_map/pallas_call | solution.py:329
  1.6 3.5 %collective-permute-start = (bf16[8,2048]{1,0:T(8,128)(2,1)S(1)}, bf16[8,2048]{1,0:T(8,128)(2,1)S(1)}, u32[]{:S(2)}, u32[]{:S(2)}) collective-permute-start(bf16[8,2048]{1,0:T(8,128)(2,1)S(1)} %get-tuple-element.31), channel_id=1, source_target_pairs={{0,5},{1,4},{2,7},{3,6},{4,1},{5,0},{6,3},{7,2},{8,13},{9,12},{10,... | collective-permute-start | bytes 98312 | tf_op jit(solution)/shard_map/ppermute | solution.py:362
  5.1 1.6 %collective-permute-start.1 = (bf16[8,2048]{1,0:T(8,128)(2,1)S(1)}, bf16[8,2048]{1,0:T(8,128)(2,1)S(1)}, u32[]{:S(2)}, u32[]{:S(2)}) collective-permute-start(bf16[8,2048]{1,0:T(8,128)(2,1)S(1)} %get-tuple-element.32), channel_id=1, source_target_pairs={{0,7},{1,6},{2,5},{3,4},{4,3},{5,2},{6,1},{7,0},{8,15},{9,14},{10,... | collective-permute-start | bytes 98312 | tf_op jit(solution)/shard_map/ppermute | solution.py:362
  6.7 0.2 collective-permute-start.2
  7.0 2.5 %shard_map.103 = (bf16[32,2048]{1,0:T(8,128)(2,1)S(1)}, bf16[32,2048]{1,0:T(8,128)(2,1)S(1)}, bf16[32,2048]{1,0:T(8,128)(2,1)S(1)}, bf16[2048,512]{1,0:T(8,128)(...) custom-call(s32[2,32]{1,0:T(2,128)} %chosen_hbm.1, ...), custom_call_target="tpu_custom_call" | custom-call | tf_op jit(solution)/shard_map/pallas_call | solution.py:329
  9.5 0.0 collective-permute-done.refs_1_
  9.5 0.9 %collective-permute-done.1.refs_2_ = bf16[8,2048]{1,0:T(8,128)(2,1)S(1)} collective-permute-done((bf16[8,2048]{1,0:T(8,128)(2,1)S(1)}, bf16[8,2048]{1,0:T(8,128)(2,1)S(1)}, u32[]{:S(2)}, u32[]{:S(2)}) %collective-permute-start.1) | collective-permute-done | bytes 32800 | tf_op jit(solution)/shard_map/ppermute | solution.py:362
  10.4 0.2 collective-permute-done.2.refs_3_
  10.5 0.2 shard_map.105
  10.7 0.7 %collective-permute-start.3 = (bf16[20,2048]{1,0:T(8,128)(2,1)S(1)}, bf16[20,2048]{1,0:T(8,128)(2,1)S(1)}, u32[]{:S(2)}, u32[]{:S(2)}) collective-permute-start(bf16[20,2048]{1,0:T(8,128)(2,1)S(1)} %get-tuple-element.35), channel_id=1, source_target_pairs={{0,1},{1,0},{2,3},{3,2},{4,5},{5,4},{6,7},{7,6},{8,9},{9,8},{10,11... | collective-permute-start | bytes 245768 | tf_op jit(solution)/shard_map/ppermute | solution.py:358
  11.4 0.9 %collective-permute-done.3.came_ref = bf16[20,2048]{1,0:T(8,128)(2,1)S(1)} collective-permute-done((bf16[20,2048]{1,0:T(8,128)(2,1)S(1)}, bf16[20,2048]{1,0:T(8,128)(2,1)S(1)}, u32[]{:S(2)}, u32[]{:S(2)}) %collective-permute-start.3) | collective-permute-done | bytes 81952 | tf_op jit(solution)/shard_map/ppermute | solution.py:358
  12.4 14.9 %all_to_all.10.near_ref = bf16[32,2,2048]{2,1,0:T(2,128)(2,1)S(1)} all-to-all(bf16[32,2,2048]{2,1,0:T(2,128)(2,1)S(1)} %shard_map.106), channel_id=1, replica_groups=mesh['grp'=4,'z'=4,'core'=2] {'grp','z','core'}, dimensions={0} | all-to-all | bytes 524288 | tf_op jit(solution)/shard_map/all_to_all | solution.py:408
  27.3 0.4 collective-permute-start.4
  27.7 0.6 %shard_map.107 = (f32[64,512]{1,0:T(8,128)S(1)}, f32[64,512]{1,0:T(8,128)S(1)}) custom-call(bf16[32,2,2048]{2,1,0:T(2,128)(2,1)S(1)} %all_to_all.10.near_ref, bf16[2048,512]{1,0:T(8,128)(2,1)S(1)} %get-tuple-element.36.w_in_ref, bf16[512,2048]{1,0:T(8,128)(2,1)S(1)} %get-tuple-element.37.w_out_ref), custom_call_target="tpu_custom_call" | custom-call | tf_op jit(solution)/shard_map/pallas_call | solution.py:329
  28.3 0.6 %collective-permute-done.4.far_ref = bf16[32,2,2048]{2,1,0:T(2,128)(2,1)S(1)} collective-permute-done((bf16[32,2,2048]{2,1,0:T(2,128)(2,1)S(1)}, bf16[32,2,2048]{2,1,0:T(2,128)(2,1)S(1)}, u32[]{:S(2)}, u32[]{:S(2)}) %collective-permute-start.4) | collective-permute-done | bytes 262176 | tf_op jit(solution)/shard_map/ppermute | solution.py:358
  28.8 1.0 %shard_map.108 = (bf16[64,512]{1,0:T(8,128)(2,1)S(1)}, bf16[64,1024]{1,0:T(8,128)(2,1)S(1)}) custom-call(bf16[32,2,2048]{2,1,0:T(2,128)(2,1)S(1)} %collective-permute-done.4.far_ref, f32[64,512]{1,0:T(8,128)S(1)} %get-tuple-element.38.pre_ref, f32[64,512]{1,0:T(8,128)S(1)} %get-tuple-element.39.back_ref, bf16[2048,512]{1,0:T(8,128)(2,1)S(1)} %get-tuple-element.36.w_in_ref, ...), custom_call_target="tpu_custom_call" | custom-call | tf_op jit(solution)/shard_map/pallas_call | solution.py:329
  29.8 0.4 %collective-permute-start.5 = (bf16[64,1024]{1,0:T(8,128)(2,1)S(1)}, bf16[64,1024]{1,0:T(8,128)(2,1)S(1)}, u32[]{:S(2)}, u32[]{:S(2)}) collective-permute-start(bf16[64,1024]{1,0:T(8,128)(2,1)S(1)} %get-tuple-element.43), channel_id=1, source_target_pairs={{0,1},{1,0},{2,3},{3,2},{4,5},{5,4},{6,7},{7,6},{8,9},{9,8},{10,11... | collective-permute-start | bytes 393224 | tf_op jit(solution)/shard_map/ppermute | solution.py:358
  30.2 0.5 %shard_map.109 = (f32[64,1024]{1,0:T(8,128)S(1)}, bf16[32,2048]{1,0:T(8,128)(2,1)S(1)}) custom-call(bf16[64,512]{1,0:T(8,128)(2,1)S(1)} %get-tuple-element.40.slope_ref, bf16[2048,512]{1,0:T(8,128)(2,1)S(1)} %get-tuple-element.36.w_in_ref, bf16[32,2048]{1,0:T(8,128)(2,1)S(1)} %get-tuple-element.41.near_ref, bf16[20,2048]{1,0:T(8,128)(2,1)S(1)} %collective-permute-done.3.came_ref), custom_call_target="tpu_custom_call" | custom-call | tf_op jit(solution)/shard_map/pallas_call | solution.py:329
  30.8 0.5 %collective-permute-done.5.came_ref = bf16[64,1024]{1,0:T(8,128)(2,1)S(1)} collective-permute-done((bf16[64,1024]{1,0:T(8,128)(2,1)S(1)}, bf16[64,1024]{1,0:T(8,128)(2,1)S(1)}, u32[]{:S(2)}, u32[]{:S(2)}) %collective-permute-start.5) | collective-permute-done | bytes 131104 | tf_op jit(solution)/shard_map/ppermute | solution.py:358
  31.3 10.5 %all_to_all.11.back_ref = bf16[32,8,256]{2,1,0:T(8,128)(2,1)S(1)} all-to-all(bf16[32,8,256]{2,1,0:T(8,128)(2,1)S(1)} %shard_map.110), channel_id=1, replica_groups=mesh['grp'=4,'z'=4,'core'=2] {'grp','z','core'}, dimensions={0} | all-to-all | bytes 262144 | tf_op jit(solution)/shard_map/all_to_all | solution.py:436
  41.8 1.4 %shard_map.111 = (bf16[8,4,2048]{2,1,0:T(4,128)(2,1)}, bf16[8,4,2048]{2,1,0:T(4,128)(2,1)}, bf16[8,4,2048]{2,1,0:T(4,128)(2,1)}) custom-call(bf16[256,256]{1,0:T(8,128)(2,1)S(1)} %get-tuple-element.26.spread_ref, bf16[32,8,256]{2,1,0:T(8,128)(2,1)S(1)} %all_to_all.11.back_ref, bf16[32,2048]{1,0:T(8,128)(2,1)S(1)} %get-tuple-element.44.cot_ref, ...), custom_call_target="tpu_custom_call" | custom-call | tf_op jit(solution)/shard_map/pallas_call | solution.py:329
  (2 shorter events, 0.1 us)
Async XLA Ops:
  1.6 7.9 %collective-permute-start = (bf16[8,2048]{1,0:T(8,128)(2,1)S(1)}, bf16[8,2048]{1,0:T(8,128)(2,1)S(1)}, u32[]{:S(2)}, u32[]{:S(2)}) collective-permute-start(bf16[8,2048]{1,0:T(8,128)(2,1)S(1)} %get-tuple-element.31), channel_id=1, source_target_pairs={{0,5},{1,4},{2,7},{3,6},{4,1},{5,0},{6,3},{7,2},{8,13},{9,12},{10,... | collective-permute-start | bytes 98312 | tf_op jit(solution)/shard_map/ppermute | solution.py:362
  5.1 5.2 %collective-permute-start.1 = (bf16[8,2048]{1,0:T(8,128)(2,1)S(1)}, bf16[8,2048]{1,0:T(8,128)(2,1)S(1)}, u32[]{:S(2)}, u32[]{:S(2)}) collective-permute-start(bf16[8,2048]{1,0:T(8,128)(2,1)S(1)} %get-tuple-element.32), channel_id=1, source_target_pairs={{0,7},{1,6},{2,5},{3,4},{4,3},{5,2},{6,1},{7,0},{8,15},{9,14},{10,... | collective-permute-start | bytes 98312 | tf_op jit(solution)/shard_map/ppermute | solution.py:362
  6.7 3.8 %collective-permute-start.2 = (bf16[8,2048]{1,0:T(8,128)(2,1)S(1)}, bf16[8,2048]{1,0:T(8,128)(2,1)S(1)}, u32[]{:S(2)}, u32[]{:S(2)}) collective-permute-start(bf16[8,2048]{1,0:T(8,128)(2,1)S(1)} %get-tuple-element.33), channel_id=1, source_target_pairs={{0,3},{1,2},{2,1},{3,0},{4,7},{5,6},{6,5},{7,4},{8,11},{9,10},{10,... | collective-permute-start | bytes 98312 | tf_op jit(solution)/shard_map/ppermute | solution.py:362
  10.7 1.7 %collective-permute-start.3 = (bf16[20,2048]{1,0:T(8,128)(2,1)S(1)}, bf16[20,2048]{1,0:T(8,128)(2,1)S(1)}, u32[]{:S(2)}, u32[]{:S(2)}) collective-permute-start(bf16[20,2048]{1,0:T(8,128)(2,1)S(1)} %get-tuple-element.35), channel_id=1, source_target_pairs={{0,1},{1,0},{2,3},{3,2},{4,5},{5,4},{6,7},{7,6},{8,9},{9,8},{10,11... | collective-permute-start | bytes 245768 | tf_op jit(solution)/shard_map/ppermute | solution.py:358
  27.3 1.5 %collective-permute-start.4 = (bf16[32,2,2048]{2,1,0:T(2,128)(2,1)S(1)}, bf16[32,2,2048]{2,1,0:T(2,128)(2,1)S(1)}, u32[]{:S(2)}, u32[]{:S(2)}) collective-permute-start(bf16[32,2,2048]{2,1,0:T(2,128)(2,1)S(1)} %all_to_all.10.near_ref), channel_id=1, source_target_pairs={{0,1},{1,0},{2,3},{3,2},{4,5},{5,4},{6,7},{7,6},{8,9},{9,8},{10,11... | collective-permute-start | bytes 786440 | tf_op jit(solution)/shard_map/ppermute | solution.py:358
  29.8 1.4 %collective-permute-start.5 = (bf16[64,1024]{1,0:T(8,128)(2,1)S(1)}, bf16[64,1024]{1,0:T(8,128)(2,1)S(1)}, u32[]{:S(2)}, u32[]{:S(2)}) collective-permute-start(bf16[64,1024]{1,0:T(8,128)(2,1)S(1)} %get-tuple-element.43), channel_id=1, source_target_pairs={{0,1},{1,0},{2,3},{3,2},{4,5},{5,4},{6,7},{7,6},{8,9},{9,8},{10,11... | collective-permute-start | bytes 393224 | tf_op jit(solution)/shard_map/ppermute | solution.py:358

commit v22 on v21

--- a/solution.py
+++ b/solution.py
@@ -152,7 +152,8 @@
         here, same.astype(jnp.bfloat16), FIRST_BOTH, preferred_element_type=jnp.float32
     )
     back_at = lax.broadcasted_iota(jnp.int32, (rows, returns), 1)
-    piece = back_at // (MOST * pieces) % CORES * pieces + back_at % pieces
+    sender = back_at // (MOST * pieces)
+    piece = sender // lax.axis_size("z") % CORES * pieces + back_at % pieces
     for j in range(CORES * pieces):
         spread_ref[j * rows : (j + 1) * rows, :] = jnp.where(piece == j, back, 0.0).astype(
             jnp.bfloat16
@@ -200,6 +201,7 @@
 
 
 def pack_kernel(share, picked_ref, mine_ref, came_ref, out_ref):
+    levels = lax.axis_size("z")
     slots, features = mine_ref.shape
     rows = mine_ref[...] + came_ref[came_ref.shape[0] - slots :, :]
     part = features // CORES
@@ -212,7 +214,8 @@
     ]
     for e in range(out_ref.shape[0] // share):
         for i in range(share):
-            out_ref[e * share + i] = both[i % CORES][e * MOST : (e + 1) * MOST]
+            core = i // levels % CORES
+            out_ref[e * share + i] = both[core][e * MOST : (e + 1) * MOST]
 
 
 def part_of(part, width):
@@ -352,7 +355,7 @@
     slots = experts * MOST
     part = features // CORES
     hidden = w_in.shape[2]
-    everyone = ("grp", "z", "core")
+    everyone = ("grp", "core", "z")
 
     def swap(values):
         return lax.ppermute(values, "core", [(i, i ^ 1) for i in range(CORES)])

time: 43.4 us -> 43.6 us (level)
  no operation moved by 1% of the time
where the time goes in v22:
time: 43.6 us; the launch traced here: 43.4 us
  blocking collectives  25.6 us (59%)
  Pallas kernels  7.17 us (16%)
  starting transfers between devices  6.96 us (16%)
  waiting for transfers between devices  3 us (7%)
  between operations  0.69 us (2%)
    all_to_all x1, blocking collectives, body(): lax.all_to_all(outgoing, everyone, split_axis=0, concat_axis=0, tiled=True)  14.7 us
    all_to_all x1, blocking collectives, body(): lax.all_to_all(total, everyone, split_axis=0, concat_axis=0, tiled=True)  10.9 us
    pallas_call x9, Pallas kernels, call(): pl.pallas_call(kernel, out_shape=[jax.ShapeDtypeStruct(shape, dtype) for...  7.17 us
    ppermute x3, starting transfers between devices, across(): return lax.ppermute(values, ('z', 'core'), pairs)  5.4 us
    ppermute x3, waiting for transfers between devices, swap(): return lax.ppermute(values, 'core', [(i, i ^ 1) for i in range(CORES)])  1.95 us
    ppermute x3, starting transfers between devices, swap(): return lax.ppermute(values, 'core', [(i, i ^ 1) for i in range(CORES)])  1.56 us
    ppermute x3, waiting for transfers between devices, across(): return lax.ppermute(values, ('z', 'core'), pairs)  1.05 us
  transfers between devices with their start and end apart: 6, of which 5 were waited for; matrix products, arithmetic and copies ran while one was open for 0% of the time, Pallas kernels for 8%

profile of v22, /device:TPU:0, one launch (start us, length us, event | category | flops | bytes accessed | tf_op | source)
XLA Modules:
  0.0 43.4 jit_solution(13866046965516578952)
XLA Ops:
  0.6 0.9 %shard_map.104 = (bf16[8,2048]{1,0:T(8,128)(2,1)S(1)}, bf16[8,2048]{1,0:T(8,128)(2,1)S(1)}, bf16[8,2048]{1,0:T(8,128)(2,1)S(1)}, bf16[8,2048]{1,0:T(8,128)(2,1)S(1)}) custom-call(bf16[1,32,2048]{2,1,0:T(8,128)(2,1)} %cot_hbm.1), custom_call_target="tpu_custom_call" | custom-call | tf_op jit(solution)/shard_map/pallas_call | solution.py:332
  1.6 3.5 %collective-permute-start = (bf16[8,2048]{1,0:T(8,128)(2,1)S(1)}, bf16[8,2048]{1,0:T(8,128)(2,1)S(1)}, u32[]{:S(2)}, u32[]{:S(2)}) collective-permute-start(bf16[8,2048]{1,0:T(8,128)(2,1)S(1)} %get-tuple-element.31), channel_id=1, source_target_pairs={{0,5},{1,4},{2,7},{3,6},{4,1},{5,0},{6,3},{7,2},{8,13},{9,12},{10,... | collective-permute-start | bytes 98312 | tf_op jit(solution)/shard_map/ppermute | solution.py:365
  5.1 1.6 %collective-permute-start.1 = (bf16[8,2048]{1,0:T(8,128)(2,1)S(1)}, bf16[8,2048]{1,0:T(8,128)(2,1)S(1)}, u32[]{:S(2)}, u32[]{:S(2)}) collective-permute-start(bf16[8,2048]{1,0:T(8,128)(2,1)S(1)} %get-tuple-element.32), channel_id=1, source_target_pairs={{0,7},{1,6},{2,5},{3,4},{4,3},{5,2},{6,1},{7,0},{8,15},{9,14},{10,... | collective-permute-start | bytes 98312 | tf_op jit(solution)/shard_map/ppermute | solution.py:365
  6.7 0.2 collective-permute-start.2
  7.0 2.5 %shard_map.103 = (bf16[32,2048]{1,0:T(8,128)(2,1)S(1)}, bf16[32,2048]{1,0:T(8,128)(2,1)S(1)}, bf16[32,2048]{1,0:T(8,128)(2,1)S(1)}, bf16[2048,512]{1,0:T(8,128)(...) custom-call(s32[2,32]{1,0:T(2,128)} %chosen_hbm.1, ...), custom_call_target="tpu_custom_call" | custom-call | tf_op jit(solution)/shard_map/pallas_call | solution.py:332
  9.5 0.0 collective-permute-done.refs_1_
  9.5 0.9 %collective-permute-done.1.refs_2_ = bf16[8,2048]{1,0:T(8,128)(2,1)S(1)} collective-permute-done((bf16[8,2048]{1,0:T(8,128)(2,1)S(1)}, bf16[8,2048]{1,0:T(8,128)(2,1)S(1)}, u32[]{:S(2)}, u32[]{:S(2)}) %collective-permute-start.1) | collective-permute-done | bytes 32800 | tf_op jit(solution)/shard_map/ppermute | solution.py:365
  10.4 0.2 collective-permute-done.2.refs_3_
  10.5 0.2 shard_map.105
  10.7 0.7 %collective-permute-start.3 = (bf16[20,2048]{1,0:T(8,128)(2,1)S(1)}, bf16[20,2048]{1,0:T(8,128)(2,1)S(1)}, u32[]{:S(2)}, u32[]{:S(2)}) collective-permute-start(bf16[20,2048]{1,0:T(8,128)(2,1)S(1)} %get-tuple-element.35), channel_id=1, source_target_pairs={{0,1},{1,0},{2,3},{3,2},{4,5},{5,4},{6,7},{7,6},{8,9},{9,8},{10,11... | collective-permute-start | bytes 245768 | tf_op jit(solution)/shard_map/ppermute | solution.py:361
  11.4 0.9 %collective-permute-done.3.came_ref = bf16[20,2048]{1,0:T(8,128)(2,1)S(1)} collective-permute-done((bf16[20,2048]{1,0:T(8,128)(2,1)S(1)}, bf16[20,2048]{1,0:T(8,128)(2,1)S(1)}, u32[]{:S(2)}, u32[]{:S(2)}) %collective-permute-start.3) | collective-permute-done | bytes 81952 | tf_op jit(solution)/shard_map/ppermute | solution.py:361
  12.4 14.7 %all_to_all.10.near_ref = bf16[32,2,2048]{2,1,0:T(2,128)(2,1)S(1)} all-to-all(bf16[32,2,2048]{2,1,0:T(2,128)(2,1)S(1)} %shard_map.106), channel_id=1, replica_groups=mesh['grp'=4,'z'=4,'core'=2] {'grp','core','z'}, dimensions={0} | all-to-all | bytes 524288 | tf_op jit(solution)/shard_map/all_to_all | solution.py:411
  27.1 0.4 collective-permute-start.4
  27.5 0.6 %shard_map.107 = (f32[64,512]{1,0:T(8,128)S(1)}, f32[64,512]{1,0:T(8,128)S(1)}) custom-call(bf16[32,2,2048]{2,1,0:T(2,128)(2,1)S(1)} %all_to_all.10.near_ref, bf16[2048,512]{1,0:T(8,128)(2,1)S(1)} %get-tuple-element.36.w_in_ref, bf16[512,2048]{1,0:T(8,128)(2,1)S(1)} %get-tuple-element.37.w_out_ref), custom_call_target="tpu_custom_call" | custom-call | tf_op jit(solution)/shard_map/pallas_call | solution.py:332
  28.1 0.6 %collective-permute-done.4.far_ref = bf16[32,2,2048]{2,1,0:T(2,128)(2,1)S(1)} collective-permute-done((bf16[32,2,2048]{2,1,0:T(2,128)(2,1)S(1)}, bf16[32,2,2048]{2,1,0:T(2,128)(2,1)S(1)}, u32[]{:S(2)}, u32[]{:S(2)}) %collective-permute-start.4) | collective-permute-done | bytes 262176 | tf_op jit(solution)/shard_map/ppermute | solution.py:361
  28.7 1.0 %shard_map.108 = (bf16[64,512]{1,0:T(8,128)(2,1)S(1)}, bf16[64,1024]{1,0:T(8,128)(2,1)S(1)}) custom-call(bf16[32,2,2048]{2,1,0:T(2,128)(2,1)S(1)} %collective-permute-done.4.far_ref, f32[64,512]{1,0:T(8,128)S(1)} %get-tuple-element.38.pre_ref, f32[64,512]{1,0:T(8,128)S(1)} %get-tuple-element.39.back_ref, bf16[2048,512]{1,0:T(8,128)(2,1)S(1)} %get-tuple-element.36.w_in_ref, ...), custom_call_target="tpu_custom_call" | custom-call | tf_op jit(solution)/shard_map/pallas_call | solution.py:332
  29.6 0.4 %collective-permute-start.5 = (bf16[64,1024]{1,0:T(8,128)(2,1)S(1)}, bf16[64,1024]{1,0:T(8,128)(2,1)S(1)}, u32[]{:S(2)}, u32[]{:S(2)}) collective-permute-start(bf16[64,1024]{1,0:T(8,128)(2,1)S(1)} %get-tuple-element.43), channel_id=1, source_target_pairs={{0,1},{1,0},{2,3},{3,2},{4,5},{5,4},{6,7},{7,6},{8,9},{9,8},{10,11... | collective-permute-start | bytes 393224 | tf_op jit(solution)/shard_map/ppermute | solution.py:361
  30.1 0.5 %shard_map.109 = (f32[64,1024]{1,0:T(8,128)S(1)}, bf16[32,2048]{1,0:T(8,128)(2,1)S(1)}) custom-call(bf16[64,512]{1,0:T(8,128)(2,1)S(1)} %get-tuple-element.40.slope_ref, bf16[2048,512]{1,0:T(8,128)(2,1)S(1)} %get-tuple-element.36.w_in_ref, bf16[32,2048]{1,0:T(8,128)(2,1)S(1)} %get-tuple-element.41.near_ref, bf16[20,2048]{1,0:T(8,128)(2,1)S(1)} %collective-permute-done.3.came_ref), custom_call_target="tpu_custom_call" | custom-call | tf_op jit(solution)/shard_map/pallas_call | solution.py:332
  30.6 0.5 %collective-permute-done.5.came_ref = bf16[64,1024]{1,0:T(8,128)(2,1)S(1)} collective-permute-done((bf16[64,1024]{1,0:T(8,128)(2,1)S(1)}, bf16[64,1024]{1,0:T(8,128)(2,1)S(1)}, u32[]{:S(2)}, u32[]{:S(2)}) %collective-permute-start.5) | collective-permute-done | bytes 131104 | tf_op jit(solution)/shard_map/ppermute | solution.py:361
  31.1 10.9 %all_to_all.11.back_ref = bf16[32,8,256]{2,1,0:T(8,128)(2,1)S(1)} all-to-all(bf16[32,8,256]{2,1,0:T(8,128)(2,1)S(1)} %shard_map.110), channel_id=1, replica_groups=mesh['grp'=4,'z'=4,'core'=2] {'grp','core','z'}, dimensions={0} | all-to-all | bytes 262144 | tf_op jit(solution)/shard_map/all_to_all | solution.py:439
  42.0 1.4 %shard_map.111 = (bf16[8,4,2048]{2,1,0:T(4,128)(2,1)}, bf16[8,4,2048]{2,1,0:T(4,128)(2,1)}, bf16[8,4,2048]{2,1,0:T(4,128)(2,1)}) custom-call(bf16[256,256]{1,0:T(8,128)(2,1)S(1)} %get-tuple-element.26.spread_ref, bf16[32,8,256]{2,1,0:T(8,128)(2,1)S(1)} %all_to_all.11.back_ref, bf16[32,2048]{1,0:T(8,128)(2,1)S(1)} %get-tuple-element.44.cot_ref, ...), custom_call_target="tpu_custom_call" | custom-call | tf_op jit(solution)/shard_map/pallas_call | solution.py:332
  (2 shorter events, 0.1 us)
Async XLA Ops:
  1.6 7.9 %collective-permute-start = (bf16[8,2048]{1,0:T(8,128)(2,1)S(1)}, bf16[8,2048]{1,0:T(8,128)(2,1)S(1)}, u32[]{:S(2)}, u32[]{:S(2)}) collective-permute-start(bf16[8,2048]{1,0:T(8,128)(2,1)S(1)} %get-tuple-element.31), channel_id=1, source_target_pairs={{0,5},{1,4},{2,7},{3,6},{4,1},{5,0},{6,3},{7,2},{8,13},{9,12},{10,... | collective-permute-start | bytes 98312 | tf_op jit(solution)/shard_map/ppermute | solution.py:365
  5.1 5.2 %collective-permute-start.1 = (bf16[8,2048]{1,0:T(8,128)(2,1)S(1)}, bf16[8,2048]{1,0:T(8,128)(2,1)S(1)}, u32[]{:S(2)}, u32[]{:S(2)}) collective-permute-start(bf16[8,2048]{1,0:T(8,128)(2,1)S(1)} %get-tuple-element.32), channel_id=1, source_target_pairs={{0,7},{1,6},{2,5},{3,4},{4,3},{5,2},{6,1},{7,0},{8,15},{9,14},{10,... | collective-permute-start | bytes 98312 | tf_op jit(solution)/shard_map/ppermute | solution.py:365
  6.7 3.8 %collective-permute-start.2 = (bf16[8,2048]{1,0:T(8,128)(2,1)S(1)}, bf16[8,2048]{1,0:T(8,128)(2,1)S(1)}, u32[]{:S(2)}, u32[]{:S(2)}) collective-permute-start(bf16[8,2048]{1,0:T(8,128)(2,1)S(1)} %get-tuple-element.33), channel_id=1, source_target_pairs={{0,3},{1,2},{2,1},{3,0},{4,7},{5,6},{6,5},{7,4},{8,11},{9,10},{10,... | collective-permute-start | bytes 98312 | tf_op jit(solution)/shard_map/ppermute | solution.py:365
  10.7 1.7 %collective-permute-start.3 = (bf16[20,2048]{1,0:T(8,128)(2,1)S(1)}, bf16[20,2048]{1,0:T(8,128)(2,1)S(1)}, u32[]{:S(2)}, u32[]{:S(2)}) collective-permute-start(bf16[20,2048]{1,0:T(8,128)(2,1)S(1)} %get-tuple-element.35), channel_id=1, source_target_pairs={{0,1},{1,0},{2,3},{3,2},{4,5},{5,4},{6,7},{7,6},{8,9},{9,8},{10,11... | collective-permute-start | bytes 245768 | tf_op jit(solution)/shard_map/ppermute | solution.py:361
  27.1 1.6 %collective-permute-start.4 = (bf16[32,2,2048]{2,1,0:T(2,128)(2,1)S(1)}, bf16[32,2,2048]{2,1,0:T(2,128)(2,1)S(1)}, u32[]{:S(2)}, u32[]{:S(2)}) collective-permute-start(bf16[32,2,2048]{2,1,0:T(2,128)(2,1)S(1)} %all_to_all.10.near_ref), channel_id=1, source_target_pairs={{0,1},{1,0},{2,3},{3,2},{4,5},{5,4},{6,7},{7,6},{8,9},{9,8},{10,11... | collective-permute-start | bytes 786440 | tf_op jit(solution)/shard_map/ppermute | solution.py:361
  29.6 1.4 %collective-permute-start.5 = (bf16[64,1024]{1,0:T(8,128)(2,1)S(1)}, bf16[64,1024]{1,0:T(8,128)(2,1)S(1)}, u32[]{:S(2)}, u32[]{:S(2)}) collective-permute-start(bf16[64,1024]{1,0:T(8,128)(2,1)S(1)} %get-tuple-element.43), channel_id=1, source_target_pairs={{0,1},{1,0},{2,3},{3,2},{4,5},{5,4},{6,7},{7,6},{8,9},{9,8},{10,11... | collective-permute-start | bytes 393224 | tf_op jit(solution)/shard_map/ppermute | solution.py:361

commit v23 on v21

--- a/solution.py
+++ b/solution.py
@@ -147,12 +147,14 @@
     returns = spread_ref.shape[1]
     slot_at = lax.broadcasted_iota(jnp.int32, (slots, returns), 0)
     back_at = lax.broadcasted_iota(jnp.int32, (slots, returns), 1) // pieces
-    same = (back_at // MOST // share == slot_at // MOST) & (back_at % MOST == slot_at % MOST)
+    levels, groups = lax.axis_size("z"), lax.axis_size("grp")
+    expert_of = back_at // MOST // levels % groups // share
+    same = (expert_of == slot_at // MOST) & (back_at % MOST == slot_at % MOST)
     back = lax.dot_general(
         here, same.astype(jnp.bfloat16), FIRST_BOTH, preferred_element_type=jnp.float32
     )
     back_at = lax.broadcasted_iota(jnp.int32, (rows, returns), 1)
-    piece = back_at // (MOST * pieces) % CORES * pieces + back_at % pieces
+    piece = back_at // (MOST * pieces * levels * groups) * pieces + back_at % pieces
     for j in range(CORES * pieces):
         spread_ref[j * rows : (j + 1) * rows, :] = jnp.where(piece == j, back, 0.0).astype(
             jnp.bfloat16
@@ -200,6 +202,7 @@
 
 
 def pack_kernel(share, picked_ref, mine_ref, came_ref, out_ref):
+    levels, groups = lax.axis_size("z"), lax.axis_size("grp")
     slots, features = mine_ref.shape
     rows = mine_ref[...] + came_ref[came_ref.shape[0] - slots :, :]
     part = features // CORES
@@ -210,9 +213,9 @@
         )
         for c in range(CORES)
     ]
-    for e in range(out_ref.shape[0] // share):
-        for i in range(share):
-            out_ref[e * share + i] = both[i % CORES][e * MOST : (e + 1) * MOST]
+    for i in range(out_ref.shape[0]):
+        e = i // levels % groups // share
+        out_ref[i] = both[i // (levels * groups)][e * MOST : (e + 1) * MOST]
 
 
 def part_of(part, width):
@@ -347,12 +350,12 @@
     columns = levels * CORES
     experts = gate_probs.shape[0]
     devices = groups * columns
-    share = devices // experts
+    share = groups // experts
     rows = frames * blocks
     slots = experts * MOST
     part = features // CORES
     hidden = w_in.shape[2]
-    everyone = ("grp", "z", "core")
+    everyone = ("core", "grp", "z")
 
     def swap(values):
         return lax.ppermute(values, "core", [(i, i ^ 1) for i in range(CORES)])

time: 43.4 us -> 43.1 us (level)
  starting transfers between devices: 6.95 us -> 6.34 us
  waiting for transfers between devices: 3 us -> 3.59 us
    all_to_all x1, blocking collectives: 10.5 us -> 9.69 us  [body(): lax.all_to_all(total, everyone, split_axis=0, concat_axis=0, tiled=True)]
    ppermute x3, starting transfers between devices: 1.55 us -> 0.93 us  [swap(): return lax.ppermute(values, 'core', [(i, i ^ 1) for i in range(CORES)])]
    ppermute x3, waiting for transfers between devices: 1.95 us -> 2.54 us  [swap(): return lax.ppermute(values, 'core', [(i, i ^ 1) for i in range(CORES)])]
    all_to_all x1, blocking collectives: 14.9 us -> 15.5 us  [body(): lax.all_to_all(outgoing, everyone, split_axis=0, concat_axis=0, tiled=True)]
where the time goes in v23:
time: 43.1 us; the launch traced here: 42.9 us
  blocking collectives  25.1 us (58%)
  Pallas kernels  7.17 us (17%)
  starting transfers between devices  6.34 us (15%)
  waiting for transfers between devices  3.59 us (8%)
  between operations  0.69 us (2%)
    all_to_all x1, blocking collectives, body(): lax.all_to_all(outgoing, everyone, split_axis=0, concat_axis=0, tiled=True)  15.5 us
    all_to_all x1, blocking collectives, body(): lax.all_to_all(total, everyone, split_axis=0, concat_axis=0, tiled=True)  9.69 us
    pallas_call x9, Pallas kernels, call(): pl.pallas_call(kernel, out_shape=[jax.ShapeDtypeStruct(shape, dtype) for...  7.17 us
    ppermute x3, starting transfers between devices, across(): return lax.ppermute(values, ('z', 'core'), pairs)  5.4 us
    ppermute x3, waiting for transfers between devices, swap(): return lax.ppermute(values, 'core', [(i, i ^ 1) for i in range(CORES)])  2.54 us
    ppermute x3, waiting for transfers between devices, across(): return lax.ppermute(values, ('z', 'core'), pairs)  1.05 us
    ppermute x3, starting transfers between devices, swap(): return lax.ppermute(values, 'core', [(i, i ^ 1) for i in range(CORES)])  0.93 us
  transfers between devices with their start and end apart: 6, of which 5 were waited for; matrix products, arithmetic and copies ran while one was open for 0% of the time, Pallas kernels for 8%

profile of v23, /device:TPU:0, one launch (start us, length us, event | category | flops | bytes accessed | tf_op | source)
XLA Modules:
  0.0 42.9 jit_solution(3623871073073249166)
XLA Ops:
  0.6 0.9 %shard_map.104 = (bf16[8,2048]{1,0:T(8,128)(2,1)S(1)}, bf16[8,2048]{1,0:T(8,128)(2,1)S(1)}, bf16[8,2048]{1,0:T(8,128)(2,1)S(1)}, bf16[8,2048]{1,0:T(8,128)(2,1)S(1)}) custom-call(bf16[1,32,2048]{2,1,0:T(8,128)(2,1)} %cot_hbm.1), custom_call_target="tpu_custom_call" | custom-call | tf_op jit(solution)/shard_map/pallas_call | solution.py:332
  1.6 3.5 %collective-permute-start = (bf16[8,2048]{1,0:T(8,128)(2,1)S(1)}, bf16[8,2048]{1,0:T(8,128)(2,1)S(1)}, u32[]{:S(2)}, u32[]{:S(2)}) collective-permute-start(bf16[8,2048]{1,0:T(8,128)(2,1)S(1)} %get-tuple-element.31), channel_id=1, source_target_pairs={{0,5},{1,4},{2,7},{3,6},{4,1},{5,0},{6,3},{7,2},{8,13},{9,12},{10,... | collective-permute-start | bytes 98312 | tf_op jit(solution)/shard_map/ppermute | solution.py:365
  5.1 1.6 %collective-permute-start.1 = (bf16[8,2048]{1,0:T(8,128)(2,1)S(1)}, bf16[8,2048]{1,0:T(8,128)(2,1)S(1)}, u32[]{:S(2)}, u32[]{:S(2)}) collective-permute-start(bf16[8,2048]{1,0:T(8,128)(2,1)S(1)} %get-tuple-element.32), channel_id=1, source_target_pairs={{0,7},{1,6},{2,5},{3,4},{4,3},{5,2},{6,1},{7,0},{8,15},{9,14},{10,... | collective-permute-start | bytes 98312 | tf_op jit(solution)/shard_map/ppermute | solution.py:365
  6.7 0.2 collective-permute-start.2
  7.0 2.5 %shard_map.103 = (bf16[32,2048]{1,0:T(8,128)(2,1)S(1)}, bf16[32,2048]{1,0:T(8,128)(2,1)S(1)}, bf16[32,2048]{1,0:T(8,128)(2,1)S(1)}, bf16[2048,512]{1,0:T(8,128)(...) custom-call(s32[2,32]{1,0:T(2,128)} %chosen_hbm.1, ...), custom_call_target="tpu_custom_call" | custom-call | tf_op jit(solution)/shard_map/pallas_call | solution.py:332
  9.5 0.0 collective-permute-done.refs_1_
  9.5 0.9 %collective-permute-done.1.refs_2_ = bf16[8,2048]{1,0:T(8,128)(2,1)S(1)} collective-permute-done((bf16[8,2048]{1,0:T(8,128)(2,1)S(1)}, bf16[8,2048]{1,0:T(8,128)(2,1)S(1)}, u32[]{:S(2)}, u32[]{:S(2)}) %collective-permute-start.1) | collective-permute-done | bytes 32800 | tf_op jit(solution)/shard_map/ppermute | solution.py:365
  10.4 0.2 collective-permute-done.2.refs_3_
  10.5 0.2 shard_map.105
  10.7 0.7 %collective-permute-start.3 = (bf16[20,2048]{1,0:T(8,128)(2,1)S(1)}, bf16[20,2048]{1,0:T(8,128)(2,1)S(1)}, u32[]{:S(2)}, u32[]{:S(2)}) collective-permute-start(bf16[20,2048]{1,0:T(8,128)(2,1)S(1)} %get-tuple-element.35), channel_id=1, source_target_pairs={{0,1},{1,0},{2,3},{3,2},{4,5},{5,4},{6,7},{7,6},{8,9},{9,8},{10,11... | collective-permute-start | bytes 245768 | tf_op jit(solution)/shard_map/ppermute | solution.py:361
  11.4 0.9 %collective-permute-done.3.came_ref = bf16[20,2048]{1,0:T(8,128)(2,1)S(1)} collective-permute-done((bf16[20,2048]{1,0:T(8,128)(2,1)S(1)}, bf16[20,2048]{1,0:T(8,128)(2,1)S(1)}, u32[]{:S(2)}, u32[]{:S(2)}) %collective-permute-start.3) | collective-permute-done | bytes 81952 | tf_op jit(solution)/shard_map/ppermute | solution.py:361
  12.4 15.5 %all_to_all.10.near_ref = bf16[32,2,2048]{2,1,0:T(2,128)(2,1)S(1)} all-to-all(bf16[32,2,2048]{2,1,0:T(2,128)(2,1)S(1)} %shard_map.106), channel_id=1, replica_groups=mesh['grp'=4,'z'=4,'core'=2] {'core','grp','z'}, dimensions={0} | all-to-all | bytes 524288 | tf_op jit(solution)/shard_map/all_to_all | solution.py:411
  27.8 0.0 collective-permute-start.4
  27.8 0.6 %shard_map.107 = (f32[64,512]{1,0:T(8,128)S(1)}, f32[64,512]{1,0:T(8,128)S(1)}) custom-call(bf16[32,2,2048]{2,1,0:T(2,128)(2,1)S(1)} %all_to_all.10.near_ref, bf16[2048,512]{1,0:T(8,128)(2,1)S(1)} %get-tuple-element.36.w_in_ref, bf16[512,2048]{1,0:T(8,128)(2,1)S(1)} %get-tuple-element.37.w_out_ref), custom_call_target="tpu_custom_call" | custom-call | tf_op jit(solution)/shard_map/pallas_call | solution.py:332
  28.5 0.9 %collective-permute-done.4.far_ref = bf16[32,2,2048]{2,1,0:T(2,128)(2,1)S(1)} collective-permute-done((bf16[32,2,2048]{2,1,0:T(2,128)(2,1)S(1)}, bf16[32,2,2048]{2,1,0:T(2,128)(2,1)S(1)}, u32[]{:S(2)}, u32[]{:S(2)}) %collective-permute-start.4) | collective-permute-done | bytes 262176 | tf_op jit(solution)/shard_map/ppermute | solution.py:361
  29.4 1.0 %shard_map.108 = (bf16[64,512]{1,0:T(8,128)(2,1)S(1)}, bf16[64,1024]{1,0:T(8,128)(2,1)S(1)}) custom-call(bf16[32,2,2048]{2,1,0:T(2,128)(2,1)S(1)} %collective-permute-done.4.far_ref, f32[64,512]{1,0:T(8,128)S(1)} %get-tuple-element.38.pre_ref, f32[64,512]{1,0:T(8,128)S(1)} %get-tuple-element.39.back_ref, bf16[2048,512]{1,0:T(8,128)(2,1)S(1)} %get-tuple-element.36.w_in_ref, ...), custom_call_target="tpu_custom_call" | custom-call | tf_op jit(solution)/shard_map/pallas_call | solution.py:332
  30.4 0.2 collective-permute-start.5
  30.6 0.5 %shard_map.109 = (f32[64,1024]{1,0:T(8,128)S(1)}, bf16[32,2048]{1,0:T(8,128)(2,1)S(1)}) custom-call(bf16[64,512]{1,0:T(8,128)(2,1)S(1)} %get-tuple-element.40.slope_ref, bf16[2048,512]{1,0:T(8,128)(2,1)S(1)} %get-tuple-element.36.w_in_ref, bf16[32,2048]{1,0:T(8,128)(2,1)S(1)} %get-tuple-element.41.near_ref, bf16[20,2048]{1,0:T(8,128)(2,1)S(1)} %collective-permute-done.3.came_ref), custom_call_target="tpu_custom_call" | custom-call | tf_op jit(solution)/shard_map/pallas_call | solution.py:332
  31.1 0.7 %collective-permute-done.5.came_ref = bf16[64,1024]{1,0:T(8,128)(2,1)S(1)} collective-permute-done((bf16[64,1024]{1,0:T(8,128)(2,1)S(1)}, bf16[64,1024]{1,0:T(8,128)(2,1)S(1)}, u32[]{:S(2)}, u32[]{:S(2)}) %collective-permute-start.5) | collective-permute-done | bytes 131104 | tf_op jit(solution)/shard_map/ppermute | solution.py:361
  31.8 9.7 %all_to_all.11.back_ref = bf16[32,8,256]{2,1,0:T(8,128)(2,1)S(1)} all-to-all(bf16[32,8,256]{2,1,0:T(8,128)(2,1)S(1)} %shard_map.110), channel_id=1, replica_groups=mesh['grp'=4,'z'=4,'core'=2] {'core','grp','z'}, dimensions={0} | all-to-all | bytes 262144 | tf_op jit(solution)/shard_map/all_to_all | solution.py:439
  41.5 1.4 %shard_map.111 = (bf16[8,4,2048]{2,1,0:T(4,128)(2,1)}, bf16[8,4,2048]{2,1,0:T(4,128)(2,1)}, bf16[8,4,2048]{2,1,0:T(4,128)(2,1)}) custom-call(bf16[256,256]{1,0:T(8,128)(2,1)S(1)} %get-tuple-element.26.spread_ref, bf16[32,8,256]{2,1,0:T(8,128)(2,1)S(1)} %all_to_all.11.back_ref, bf16[32,2048]{1,0:T(8,128)(2,1)S(1)} %get-tuple-element.44.cot_ref, ...), custom_call_target="tpu_custom_call" | custom-call | tf_op jit(solution)/shard_map/pallas_call | solution.py:332
  (2 shorter events, 0.1 us)
Async XLA Ops:
  1.6 7.9 %collective-permute-start = (bf16[8,2048]{1,0:T(8,128)(2,1)S(1)}, bf16[8,2048]{1,0:T(8,128)(2,1)S(1)}, u32[]{:S(2)}, u32[]{:S(2)}) collective-permute-start(bf16[8,2048]{1,0:T(8,128)(2,1)S(1)} %get-tuple-element.31), channel_id=1, source_target_pairs={{0,5},{1,4},{2,7},{3,6},{4,1},{5,0},{6,3},{7,2},{8,13},{9,12},{10,... | collective-permute-start | bytes 98312 | tf_op jit(solution)/shard_map/ppermute | solution.py:365
  5.1 5.2 %collective-permute-start.1 = (bf16[8,2048]{1,0:T(8,128)(2,1)S(1)}, bf16[8,2048]{1,0:T(8,128)(2,1)S(1)}, u32[]{:S(2)}, u32[]{:S(2)}) collective-permute-start(bf16[8,2048]{1,0:T(8,128)(2,1)S(1)} %get-tuple-element.32), channel_id=1, source_target_pairs={{0,7},{1,6},{2,5},{3,4},{4,3},{5,2},{6,1},{7,0},{8,15},{9,14},{10,... | collective-permute-start | bytes 98312 | tf_op jit(solution)/shard_map/ppermute | solution.py:365
  6.7 3.8 %collective-permute-start.2 = (bf16[8,2048]{1,0:T(8,128)(2,1)S(1)}, bf16[8,2048]{1,0:T(8,128)(2,1)S(1)}, u32[]{:S(2)}, u32[]{:S(2)}) collective-permute-start(bf16[8,2048]{1,0:T(8,128)(2,1)S(1)} %get-tuple-element.33), channel_id=1, source_target_pairs={{0,3},{1,2},{2,1},{3,0},{4,7},{5,6},{6,5},{7,4},{8,11},{9,10},{10,... | collective-permute-start | bytes 98312 | tf_op jit(solution)/shard_map/ppermute | solution.py:365
  10.7 1.7 %collective-permute-start.3 = (bf16[20,2048]{1,0:T(8,128)(2,1)S(1)}, bf16[20,2048]{1,0:T(8,128)(2,1)S(1)}, u32[]{:S(2)}, u32[]{:S(2)}) collective-permute-start(bf16[20,2048]{1,0:T(8,128)(2,1)S(1)} %get-tuple-element.35), channel_id=1, source_target_pairs={{0,1},{1,0},{2,3},{3,2},{4,5},{5,4},{6,7},{7,6},{8,9},{9,8},{10,11... | collective-permute-start | bytes 245768 | tf_op jit(solution)/shard_map/ppermute | solution.py:361
  27.8 1.5 %collective-permute-start.4 = (bf16[32,2,2048]{2,1,0:T(2,128)(2,1)S(1)}, bf16[32,2,2048]{2,1,0:T(2,128)(2,1)S(1)}, u32[]{:S(2)}, u32[]{:S(2)}) collective-permute-start(bf16[32,2,2048]{2,1,0:T(2,128)(2,1)S(1)} %all_to_all.10.near_ref), channel_id=1, source_target_pairs={{0,1},{1,0},{2,3},{3,2},{4,5},{5,4},{6,7},{7,6},{8,9},{9,8},{10,11... | collective-permute-start | bytes 786440 | tf_op jit(solution)/shard_map/ppermute | solution.py:361
  30.4 1.4 %collective-permute-start.5 = (bf16[64,1024]{1,0:T(8,128)(2,1)S(1)}, bf16[64,1024]{1,0:T(8,128)(2,1)S(1)}, u32[]{:S(2)}, u32[]{:S(2)}) collective-permute-start(bf16[64,1024]{1,0:T(8,128)(2,1)S(1)} %get-tuple-element.43), channel_id=1, source_target_pairs={{0,1},{1,0},{2,3},{3,2},{4,5},{5,4},{6,7},{7,6},{8,9},{9,8},{10,11... | collective-permute-start | bytes 393224 | tf_op jit(solution)/shard_map/ppermute | solution.py:361

commit v24 on v23

--- a/solution.py
+++ b/solution.py
@@ -148,7 +148,7 @@
     slot_at = lax.broadcasted_iota(jnp.int32, (slots, returns), 0)
     back_at = lax.broadcasted_iota(jnp.int32, (slots, returns), 1) // pieces
     levels, groups = lax.axis_size("z"), lax.axis_size("grp")
-    expert_of = back_at // MOST // levels % groups // share
+    expert_of = back_at // MOST % groups // share
     same = (expert_of == slot_at // MOST) & (back_at % MOST == slot_at % MOST)
     back = lax.dot_general(
         here, same.astype(jnp.bfloat16), FIRST_BOTH, preferred_element_type=jnp.float32
@@ -214,7 +214,7 @@
         for c in range(CORES)
     ]
     for i in range(out_ref.shape[0]):
-        e = i // levels % groups // share
+        e = i % groups // share
         out_ref[i] = both[i // (levels * groups)][e * MOST : (e + 1) * MOST]
 
 
@@ -355,7 +355,7 @@
     slots = experts * MOST
     part = features // CORES
     hidden = w_in.shape[2]
-    everyone = ("core", "grp", "z")
+    everyone = ("core", "z", "grp")
 
     def swap(values):
         return lax.ppermute(values, "core", [(i, i ^ 1) for i in range(CORES)])

time: 43.1 us -> 43.3 us (level)
  no operation moved by 1% of the time
where the time goes in v24:
time: 43.3 us; the launch traced here: 43.1 us
  blocking collectives  25.3 us (58%)
  Pallas kernels  7.16 us (17%)
  starting transfers between devices  6.33 us (15%)
  waiting for transfers between devices  3.61 us (8%)
  between operations  0.69 us (2%)
    all_to_all x1, blocking collectives, body(): lax.all_to_all(outgoing, everyone, split_axis=0, concat_axis=0, tiled=True)  15.7 us
    all_to_all x1, blocking collectives, body(): lax.all_to_all(total, everyone, split_axis=0, concat_axis=0, tiled=True)  9.62 us
    pallas_call x9, Pallas kernels, call(): pl.pallas_call(kernel, out_shape=[jax.ShapeDtypeStruct(shape, dtype) for...  7.16 us
    ppermute x3, starting transfers between devices, across(): return lax.ppermute(values, ('z', 'core'), pairs)  5.4 us
    ppermute x3, waiting for transfers between devices, swap(): return lax.ppermute(values, 'core', [(i, i ^ 1) for i in range(CORES)])  2.56 us
    ppermute x3, waiting for transfers between devices, across(): return lax.ppermute(values, ('z', 'core'), pairs)  1.05 us
    ppermute x3, starting transfers between devices, swap(): return lax.ppermute(values, 'core', [(i, i ^ 1) for i in range(CORES)])  0.93 us
  transfers between devices with their start and end apart: 6, of which 5 were waited for; matrix products, arithmetic and copies ran while one was open for 0% of the time, Pallas kernels for 8%

profile of v24, /device:TPU:0, one launch (start us, length us, event | category | flops | bytes accessed | tf_op | source)
XLA Modules:
  0.0 43.1 jit_solution(15101104853312127887)
XLA Ops:
  0.6 0.9 %shard_map.104 = (bf16[8,2048]{1,0:T(8,128)(2,1)S(1)}, bf16[8,2048]{1,0:T(8,128)(2,1)S(1)}, bf16[8,2048]{1,0:T(8,128)(2,1)S(1)}, bf16[8,2048]{1,0:T(8,128)(2,1)S(1)}) custom-call(bf16[1,32,2048]{2,1,0:T(8,128)(2,1)} %cot_hbm.1), custom_call_target="tpu_custom_call" | custom-call | tf_op jit(solution)/shard_map/pallas_call | solution.py:332
  1.6 3.5 %collective-permute-start = (bf16[8,2048]{1,0:T(8,128)(2,1)S(1)}, bf16[8,2048]{1,0:T(8,128)(2,1)S(1)}, u32[]{:S(2)}, u32[]{:S(2)}) collective-permute-start(bf16[8,2048]{1,0:T(8,128)(2,1)S(1)} %get-tuple-element.31), channel_id=1, source_target_pairs={{0,5},{1,4},{2,7},{3,6},{4,1},{5,0},{6,3},{7,2},{8,13},{9,12},{10,... | collective-permute-start | bytes 98312 | tf_op jit(solution)/shard_map/ppermute | solution.py:365
  5.1 1.6 %collective-permute-start.1 = (bf16[8,2048]{1,0:T(8,128)(2,1)S(1)}, bf16[8,2048]{1,0:T(8,128)(2,1)S(1)}, u32[]{:S(2)}, u32[]{:S(2)}) collective-permute-start(bf16[8,2048]{1,0:T(8,128)(2,1)S(1)} %get-tuple-element.32), channel_id=1, source_target_pairs={{0,7},{1,6},{2,5},{3,4},{4,3},{5,2},{6,1},{7,0},{8,15},{9,14},{10,... | collective-permute-start | bytes 98312 | tf_op jit(solution)/shard_map/ppermute | solution.py:365
  6.7 0.2 collective-permute-start.2
  7.0 2.5 %shard_map.103 = (bf16[32,2048]{1,0:T(8,128)(2,1)S(1)}, bf16[32,2048]{1,0:T(8,128)(2,1)S(1)}, bf16[32,2048]{1,0:T(8,128)(2,1)S(1)}, bf16[2048,512]{1,0:T(8,128)(...) custom-call(s32[2,32]{1,0:T(2,128)} %chosen_hbm.1, ...), custom_call_target="tpu_custom_call" | custom-call | tf_op jit(solution)/shard_map/pallas_call | solution.py:332
  9.5 0.0 collective-permute-done.refs_1_
  9.5 0.9 %collective-permute-done.1.refs_2_ = bf16[8,2048]{1,0:T(8,128)(2,1)S(1)} collective-permute-done((bf16[8,2048]{1,0:T(8,128)(2,1)S(1)}, bf16[8,2048]{1,0:T(8,128)(2,1)S(1)}, u32[]{:S(2)}, u32[]{:S(2)}) %collective-permute-start.1) | collective-permute-done | bytes 32800 | tf_op jit(solution)/shard_map/ppermute | solution.py:365
  10.4 0.2 collective-permute-done.2.refs_3_
  10.5 0.2 shard_map.105
  10.7 0.7 %collective-permute-start.3 = (bf16[20,2048]{1,0:T(8,128)(2,1)S(1)}, bf16[20,2048]{1,0:T(8,128)(2,1)S(1)}, u32[]{:S(2)}, u32[]{:S(2)}) collective-permute-start(bf16[20,2048]{1,0:T(8,128)(2,1)S(1)} %get-tuple-element.35), channel_id=1, source_target_pairs={{0,1},{1,0},{2,3},{3,2},{4,5},{5,4},{6,7},{7,6},{8,9},{9,8},{10,11... | collective-permute-start | bytes 245768 | tf_op jit(solution)/shard_map/ppermute | solution.py:361
  11.4 0.9 %collective-permute-done.3.came_ref = bf16[20,2048]{1,0:T(8,128)(2,1)S(1)} collective-permute-done((bf16[20,2048]{1,0:T(8,128)(2,1)S(1)}, bf16[20,2048]{1,0:T(8,128)(2,1)S(1)}, u32[]{:S(2)}, u32[]{:S(2)}) %collective-permute-start.3) | collective-permute-done | bytes 81952 | tf_op jit(solution)/shard_map/ppermute | solution.py:361
  12.4 15.7 %all_to_all.10.near_ref = bf16[32,2,2048]{2,1,0:T(2,128)(2,1)S(1)} all-to-all(bf16[32,2,2048]{2,1,0:T(2,128)(2,1)S(1)} %shard_map.106), channel_id=1, replica_groups=mesh['grp'=4,'z'=4,'core'=2] {'core','z','grp'}, dimensions={0} | all-to-all | bytes 524288 | tf_op jit(solution)/shard_map/all_to_all | solution.py:411
  28.1 0.0 collective-permute-start.4
  28.1 0.6 %shard_map.107 = (f32[64,512]{1,0:T(8,128)S(1)}, f32[64,512]{1,0:T(8,128)S(1)}) custom-call(bf16[32,2,2048]{2,1,0:T(2,128)(2,1)S(1)} %all_to_all.10.near_ref, bf16[2048,512]{1,0:T(8,128)(2,1)S(1)} %get-tuple-element.36.w_in_ref, bf16[512,2048]{1,0:T(8,128)(2,1)S(1)} %get-tuple-element.37.w_out_ref), custom_call_target="tpu_custom_call" | custom-call | tf_op jit(solution)/shard_map/pallas_call | solution.py:332
  28.7 0.9 %collective-permute-done.4.far_ref = bf16[32,2,2048]{2,1,0:T(2,128)(2,1)S(1)} collective-permute-done((bf16[32,2,2048]{2,1,0:T(2,128)(2,1)S(1)}, bf16[32,2,2048]{2,1,0:T(2,128)(2,1)S(1)}, u32[]{:S(2)}, u32[]{:S(2)}) %collective-permute-start.4) | collective-permute-done | bytes 262176 | tf_op jit(solution)/shard_map/ppermute | solution.py:361
  29.6 1.0 %shard_map.108 = (bf16[64,512]{1,0:T(8,128)(2,1)S(1)}, bf16[64,1024]{1,0:T(8,128)(2,1)S(1)}) custom-call(bf16[32,2,2048]{2,1,0:T(2,128)(2,1)S(1)} %collective-permute-done.4.far_ref, f32[64,512]{1,0:T(8,128)S(1)} %get-tuple-element.38.pre_ref, f32[64,512]{1,0:T(8,128)S(1)} %get-tuple-element.39.back_ref, bf16[2048,512]{1,0:T(8,128)(2,1)S(1)} %get-tuple-element.36.w_in_ref, ...), custom_call_target="tpu_custom_call" | custom-call | tf_op jit(solution)/shard_map/pallas_call | solution.py:332
  30.6 0.2 collective-permute-start.5
  30.8 0.5 %shard_map.109 = (f32[64,1024]{1,0:T(8,128)S(1)}, bf16[32,2048]{1,0:T(8,128)(2,1)S(1)}) custom-call(bf16[64,512]{1,0:T(8,128)(2,1)S(1)} %get-tuple-element.40.slope_ref, bf16[2048,512]{1,0:T(8,128)(2,1)S(1)} %get-tuple-element.36.w_in_ref, bf16[32,2048]{1,0:T(8,128)(2,1)S(1)} %get-tuple-element.41.near_ref, bf16[20,2048]{1,0:T(8,128)(2,1)S(1)} %collective-permute-done.3.came_ref), custom_call_target="tpu_custom_call" | custom-call | tf_op jit(solution)/shard_map/pallas_call | solution.py:332
  31.3 0.7 %collective-permute-done.5.came_ref = bf16[64,1024]{1,0:T(8,128)(2,1)S(1)} collective-permute-done((bf16[64,1024]{1,0:T(8,128)(2,1)S(1)}, bf16[64,1024]{1,0:T(8,128)(2,1)S(1)}, u32[]{:S(2)}, u32[]{:S(2)}) %collective-permute-start.5) | collective-permute-done | bytes 131104 | tf_op jit(solution)/shard_map/ppermute | solution.py:361
  32.1 9.6 %all_to_all.11.back_ref = bf16[32,8,256]{2,1,0:T(8,128)(2,1)S(1)} all-to-all(bf16[32,8,256]{2,1,0:T(8,128)(2,1)S(1)} %shard_map.110), channel_id=1, replica_groups=mesh['grp'=4,'z'=4,'core'=2] {'core','z','grp'}, dimensions={0} | all-to-all | bytes 262144 | tf_op jit(solution)/shard_map/all_to_all | solution.py:439
  41.7 1.4 %shard_map.111 = (bf16[8,4,2048]{2,1,0:T(4,128)(2,1)}, bf16[8,4,2048]{2,1,0:T(4,128)(2,1)}, bf16[8,4,2048]{2,1,0:T(4,128)(2,1)}) custom-call(bf16[256,256]{1,0:T(8,128)(2,1)S(1)} %get-tuple-element.26.spread_ref, bf16[32,8,256]{2,1,0:T(8,128)(2,1)S(1)} %all_to_all.11.back_ref, bf16[32,2048]{1,0:T(8,128)(2,1)S(1)} %get-tuple-element.44.cot_ref, ...), custom_call_target="tpu_custom_call" | custom-call | tf_op jit(solution)/shard_map/pallas_call | solution.py:332
  (2 shorter events, 0.1 us)
Async XLA Ops:
  1.6 7.9 %collective-permute-start = (bf16[8,2048]{1,0:T(8,128)(2,1)S(1)}, bf16[8,2048]{1,0:T(8,128)(2,1)S(1)}, u32[]{:S(2)}, u32[]{:S(2)}) collective-permute-start(bf16[8,2048]{1,0:T(8,128)(2,1)S(1)} %get-tuple-element.31), channel_id=1, source_target_pairs={{0,5},{1,4},{2,7},{3,6},{4,1},{5,0},{6,3},{7,2},{8,13},{9,12},{10,... | collective-permute-start | bytes 98312 | tf_op jit(solution)/shard_map/ppermute | solution.py:365
  5.1 5.2 %collective-permute-start.1 = (bf16[8,2048]{1,0:T(8,128)(2,1)S(1)}, bf16[8,2048]{1,0:T(8,128)(2,1)S(1)}, u32[]{:S(2)}, u32[]{:S(2)}) collective-permute-start(bf16[8,2048]{1,0:T(8,128)(2,1)S(1)} %get-tuple-element.32), channel_id=1, source_target_pairs={{0,7},{1,6},{2,5},{3,4},{4,3},{5,2},{6,1},{7,0},{8,15},{9,14},{10,... | collective-permute-start | bytes 98312 | tf_op jit(solution)/shard_map/ppermute | solution.py:365
  6.7 3.8 %collective-permute-start.2 = (bf16[8,2048]{1,0:T(8,128)(2,1)S(1)}, bf16[8,2048]{1,0:T(8,128)(2,1)S(1)}, u32[]{:S(2)}, u32[]{:S(2)}) collective-permute-start(bf16[8,2048]{1,0:T(8,128)(2,1)S(1)} %get-tuple-element.33), channel_id=1, source_target_pairs={{0,3},{1,2},{2,1},{3,0},{4,7},{5,6},{6,5},{7,4},{8,11},{9,10},{10,... | collective-permute-start | bytes 98312 | tf_op jit(solution)/shard_map/ppermute | solution.py:365
  10.7 1.7 %collective-permute-start.3 = (bf16[20,2048]{1,0:T(8,128)(2,1)S(1)}, bf16[20,2048]{1,0:T(8,128)(2,1)S(1)}, u32[]{:S(2)}, u32[]{:S(2)}) collective-permute-start(bf16[20,2048]{1,0:T(8,128)(2,1)S(1)} %get-tuple-element.35), channel_id=1, source_target_pairs={{0,1},{1,0},{2,3},{3,2},{4,5},{5,4},{6,7},{7,6},{8,9},{9,8},{10,11... | collective-permute-start | bytes 245768 | tf_op jit(solution)/shard_map/ppermute | solution.py:361
  28.1 1.5 %collective-permute-start.4 = (bf16[32,2,2048]{2,1,0:T(2,128)(2,1)S(1)}, bf16[32,2,2048]{2,1,0:T(2,128)(2,1)S(1)}, u32[]{:S(2)}, u32[]{:S(2)}) collective-permute-start(bf16[32,2,2048]{2,1,0:T(2,128)(2,1)S(1)} %all_to_all.10.near_ref), channel_id=1, source_target_pairs={{0,1},{1,0},{2,3},{3,2},{4,5},{5,4},{6,7},{7,6},{8,9},{9,8},{10,11... | collective-permute-start | bytes 786440 | tf_op jit(solution)/shard_map/ppermute | solution.py:361
  30.6 1.4 %collective-permute-start.5 = (bf16[64,1024]{1,0:T(8,128)(2,1)S(1)}, bf16[64,1024]{1,0:T(8,128)(2,1)S(1)}, u32[]{:S(2)}, u32[]{:S(2)}) collective-permute-start(bf16[64,1024]{1,0:T(8,128)(2,1)S(1)} %get-tuple-element.43), channel_id=1, source_target_pairs={{0,1},{1,0},{2,3},{3,2},{4,5},{5,4},{6,7},{7,6},{8,9},{9,8},{10,11... | collective-permute-start | bytes 393224 | tf_op jit(solution)/shard_map/ppermute | solution.py:361

commit v25 on v23

--- a/solution.py
+++ b/solution.py
@@ -202,7 +202,7 @@
 
 
 def pack_kernel(share, picked_ref, mine_ref, came_ref, out_ref):
-    levels, groups = lax.axis_size("z"), lax.axis_size("grp")
+    levels = lax.axis_size("z")
     slots, features = mine_ref.shape
     rows = mine_ref[...] + came_ref[came_ref.shape[0] - slots :, :]
     part = features // CORES
@@ -214,8 +214,8 @@
         for c in range(CORES)
     ]
     for i in range(out_ref.shape[0]):
-        e = i // levels % groups // share
-        out_ref[i] = both[i // (levels * groups)][e * MOST : (e + 1) * MOST]
+        e = i // (CORES * levels) // share
+        out_ref[i] = both[i % CORES][e * MOST : (e + 1) * MOST]
 
 
 def part_of(part, width):
@@ -270,7 +270,10 @@
             start = j * PIECE + i * LANES
             piece_ref[i, pl.ds(j, count, stride=pieces), :] = total[:, start : start + LANES]
     total = jnp.concatenate([piece_ref[i] for i in range(parts)], axis=1)
-    out_ref[...] = total.astype(jnp.bfloat16).reshape(out_ref.shape)
+    devices, pieces, _ = out_ref.shape
+    total = total.astype(jnp.bfloat16).reshape(devices // CORES, CORES, pieces, PIECE)
+    for c in range(CORES):
+        out_ref[c * (devices // CORES) : (c + 1) * (devices // CORES)] = total[:, c]
 
 
 def backward_kernel(
@@ -355,7 +358,6 @@
     slots = experts * MOST
     part = features // CORES
     hidden = w_in.shape[2]
-    everyone = ("core", "grp", "z")
 
     def swap(values):
         return lax.ppermute(values, "core", [(i, i ^ 1) for i in range(CORES)])
@@ -408,7 +410,7 @@
         [picked, mine, came_near],
         "vvv",
     )
-    held = lax.all_to_all(outgoing, everyone, split_axis=0, concat_axis=0, tiled=True)
+    held = lax.all_to_all(outgoing, ("grp", "z", "core"), split_axis=0, concat_axis=0, tiled=True)
     other = swap(held)
     acts = (devices * MOST, hidden)
     halves = (devices * MOST, part)
@@ -436,7 +438,7 @@
         "vv",
         [pltpu.VMEM((PIECE // LANES, devices * pieces, LANES), f32)],
     )
-    back = lax.all_to_all(total, everyone, split_axis=0, concat_axis=0, tiled=True)
+    back = lax.all_to_all(total, ("core", "grp", "z"), split_axis=0, concat_axis=0, tiled=True)
     return call(
         backward_kernel,
         [((frames, blocks, features), bf16)] * 3,

time: 43.1 us -> 43.1 us (level)
  starting transfers between devices: 6.34 us -> 6.95 us
  waiting for transfers between devices: 3.59 us -> 3 us
    ppermute x3, starting transfers between devices: 0.93 us -> 1.55 us  [swap(): return lax.ppermute(values, 'core', [(i, i ^ 1) for i in range(CORES)])]
    ppermute x3, waiting for transfers between devices: 2.54 us -> 1.95 us  [swap(): return lax.ppermute(values, 'core', [(i, i ^ 1) for i in range(CORES)])]
where the time goes in v25:
time: 43.1 us; the launch traced here: 42.9 us
  blocking collectives  25.1 us (58%)
  Pallas kernels  7.17 us (17%)
  starting transfers between devices  6.95 us (16%)
  waiting for transfers between devices  3 us (7%)
  between operations  0.69 us (2%)
    all_to_all x1, blocking collectives, body(): lax.all_to_all(outgoing, ('grp', 'z', 'core'), split_axis=0, concat_axis=...  14.9 us
    all_to_all x1, blocking collectives, body(): lax.all_to_all(total, ('core', 'grp', 'z'), split_axis=0, concat_axis=0,...  10.2 us
    pallas_call x9, Pallas kernels, call(): pl.pallas_call(kernel, out_shape=[jax.ShapeDtypeStruct(shape, dtype) for...  7.17 us
    ppermute x3, starting transfers between devices, across(): return lax.ppermute(values, ('z', 'core'), pairs)  5.4 us
    ppermute x3, waiting for transfers between devices, swap(): return lax.ppermute(values, 'core', [(i, i ^ 1) for i in range(CORES)])  1.95 us
    ppermute x3, starting transfers between devices, swap(): return lax.ppermute(values, 'core', [(i, i ^ 1) for i in range(CORES)])  1.55 us
    ppermute x3, waiting for transfers between devices, across(): return lax.ppermute(values, ('z', 'core'), pairs)  1.05 us
  transfers between devices with their start and end apart: 6, of which 5 were waited for; matrix products, arithmetic and copies ran while one was open for 0% of the time, Pallas kernels for 8%

profile of v25, /device:TPU:0, one launch (start us, length us, event | category | flops | bytes accessed | tf_op | source)
XLA Modules:
  0.0 42.9 jit_solution(17012381979581042653)
XLA Ops:
  0.6 0.9 %shard_map.104 = (bf16[8,2048]{1,0:T(8,128)(2,1)S(1)}, bf16[8,2048]{1,0:T(8,128)(2,1)S(1)}, bf16[8,2048]{1,0:T(8,128)(2,1)S(1)}, bf16[8,2048]{1,0:T(8,128)(2,1)S(1)}) custom-call(bf16[1,32,2048]{2,1,0:T(8,128)(2,1)} %cot_hbm.1), custom_call_target="tpu_custom_call" | custom-call | tf_op jit(solution)/shard_map/pallas_call | solution.py:335
  1.6 3.5 %collective-permute-start = (bf16[8,2048]{1,0:T(8,128)(2,1)S(1)}, bf16[8,2048]{1,0:T(8,128)(2,1)S(1)}, u32[]{:S(2)}, u32[]{:S(2)}) collective-permute-start(bf16[8,2048]{1,0:T(8,128)(2,1)S(1)} %get-tuple-element.31), channel_id=1, source_target_pairs={{0,5},{1,4},{2,7},{3,6},{4,1},{5,0},{6,3},{7,2},{8,13},{9,12},{10,... | collective-permute-start | bytes 98312 | tf_op jit(solution)/shard_map/ppermute | solution.py:367
  5.1 1.6 %collective-permute-start.1 = (bf16[8,2048]{1,0:T(8,128)(2,1)S(1)}, bf16[8,2048]{1,0:T(8,128)(2,1)S(1)}, u32[]{:S(2)}, u32[]{:S(2)}) collective-permute-start(bf16[8,2048]{1,0:T(8,128)(2,1)S(1)} %get-tuple-element.32), channel_id=1, source_target_pairs={{0,7},{1,6},{2,5},{3,4},{4,3},{5,2},{6,1},{7,0},{8,15},{9,14},{10,... | collective-permute-start | bytes 98312 | tf_op jit(solution)/shard_map/ppermute | solution.py:367
  6.7 0.2 collective-permute-start.2
  7.0 2.5 %shard_map.103 = (bf16[32,2048]{1,0:T(8,128)(2,1)S(1)}, bf16[32,2048]{1,0:T(8,128)(2,1)S(1)}, bf16[32,2048]{1,0:T(8,128)(2,1)S(1)}, bf16[2048,512]{1,0:T(8,128)(...) custom-call(s32[2,32]{1,0:T(2,128)} %chosen_hbm.1, ...), custom_call_target="tpu_custom_call" | custom-call | tf_op jit(solution)/shard_map/pallas_call | solution.py:335
  9.5 0.0 collective-permute-done.refs_1_
  9.5 0.9 %collective-permute-done.1.refs_2_ = bf16[8,2048]{1,0:T(8,128)(2,1)S(1)} collective-permute-done((bf16[8,2048]{1,0:T(8,128)(2,1)S(1)}, bf16[8,2048]{1,0:T(8,128)(2,1)S(1)}, u32[]{:S(2)}, u32[]{:S(2)}) %collective-permute-start.1) | collective-permute-done | bytes 32800 | tf_op jit(solution)/shard_map/ppermute | solution.py:367
  10.4 0.2 collective-permute-done.2.refs_3_
  10.5 0.2 shard_map.105
  10.7 0.7 %collective-permute-start.3 = (bf16[20,2048]{1,0:T(8,128)(2,1)S(1)}, bf16[20,2048]{1,0:T(8,128)(2,1)S(1)}, u32[]{:S(2)}, u32[]{:S(2)}) collective-permute-start(bf16[20,2048]{1,0:T(8,128)(2,1)S(1)} %get-tuple-element.35), channel_id=1, source_target_pairs={{0,1},{1,0},{2,3},{3,2},{4,5},{5,4},{6,7},{7,6},{8,9},{9,8},{10,11... | collective-permute-start | bytes 245768 | tf_op jit(solution)/shard_map/ppermute | solution.py:363
  11.4 0.9 %collective-permute-done.3.came_ref = bf16[20,2048]{1,0:T(8,128)(2,1)S(1)} collective-permute-done((bf16[20,2048]{1,0:T(8,128)(2,1)S(1)}, bf16[20,2048]{1,0:T(8,128)(2,1)S(1)}, u32[]{:S(2)}, u32[]{:S(2)}) %collective-permute-start.3) | collective-permute-done | bytes 81952 | tf_op jit(solution)/shard_map/ppermute | solution.py:363
  12.4 14.9 %all_to_all.10.near_ref = bf16[32,2,2048]{2,1,0:T(2,128)(2,1)S(1)} all-to-all(bf16[32,2,2048]{2,1,0:T(2,128)(2,1)S(1)} %shard_map.106), channel_id=1, replica_groups=mesh['grp'=4,'z'=4,'core'=2] {'grp','z','core'}, dimensions={0} | all-to-all | bytes 524288 | tf_op jit(solution)/shard_map/all_to_all | solution.py:413
  27.3 0.4 collective-permute-start.4
  27.7 0.6 %shard_map.107 = (f32[64,512]{1,0:T(8,128)S(1)}, f32[64,512]{1,0:T(8,128)S(1)}) custom-call(bf16[32,2,2048]{2,1,0:T(2,128)(2,1)S(1)} %all_to_all.10.near_ref, bf16[2048,512]{1,0:T(8,128)(2,1)S(1)} %get-tuple-element.36.w_in_ref, bf16[512,2048]{1,0:T(8,128)(2,1)S(1)} %get-tuple-element.37.w_out_ref), custom_call_target="tpu_custom_call" | custom-call | tf_op jit(solution)/shard_map/pallas_call | solution.py:335
  28.3 0.6 %collective-permute-done.4.far_ref = bf16[32,2,2048]{2,1,0:T(2,128)(2,1)S(1)} collective-permute-done((bf16[32,2,2048]{2,1,0:T(2,128)(2,1)S(1)}, bf16[32,2,2048]{2,1,0:T(2,128)(2,1)S(1)}, u32[]{:S(2)}, u32[]{:S(2)}) %collective-permute-start.4) | collective-permute-done | bytes 262176 | tf_op jit(solution)/shard_map/ppermute | solution.py:363
  28.8 1.0 %shard_map.108 = (bf16[64,512]{1,0:T(8,128)(2,1)S(1)}, bf16[64,1024]{1,0:T(8,128)(2,1)S(1)}) custom-call(bf16[32,2,2048]{2,1,0:T(2,128)(2,1)S(1)} %collective-permute-done.4.far_ref, f32[64,512]{1,0:T(8,128)S(1)} %get-tuple-element.38.pre_ref, f32[64,512]{1,0:T(8,128)S(1)} %get-tuple-element.39.back_ref, bf16[2048,512]{1,0:T(8,128)(2,1)S(1)} %get-tuple-element.36.w_in_ref, ...), custom_call_target="tpu_custom_call" | custom-call | tf_op jit(solution)/shard_map/pallas_call | solution.py:335
  29.8 0.4 %collective-permute-start.5 = (bf16[64,1024]{1,0:T(8,128)(2,1)S(1)}, bf16[64,1024]{1,0:T(8,128)(2,1)S(1)}, u32[]{:S(2)}, u32[]{:S(2)}) collective-permute-start(bf16[64,1024]{1,0:T(8,128)(2,1)S(1)} %get-tuple-element.43), channel_id=1, source_target_pairs={{0,1},{1,0},{2,3},{3,2},{4,5},{5,4},{6,7},{7,6},{8,9},{9,8},{10,11... | collective-permute-start | bytes 393224 | tf_op jit(solution)/shard_map/ppermute | solution.py:363
  30.2 0.5 %shard_map.109 = (f32[64,1024]{1,0:T(8,128)S(1)}, bf16[32,2048]{1,0:T(8,128)(2,1)S(1)}) custom-call(bf16[64,512]{1,0:T(8,128)(2,1)S(1)} %get-tuple-element.40.slope_ref, bf16[2048,512]{1,0:T(8,128)(2,1)S(1)} %get-tuple-element.36.w_in_ref, bf16[32,2048]{1,0:T(8,128)(2,1)S(1)} %get-tuple-element.41.near_ref, bf16[20,2048]{1,0:T(8,128)(2,1)S(1)} %collective-permute-done.3.came_ref), custom_call_target="tpu_custom_call" | custom-call | tf_op jit(solution)/shard_map/pallas_call | solution.py:335
  30.8 0.5 %collective-permute-done.5.came_ref = bf16[64,1024]{1,0:T(8,128)(2,1)S(1)} collective-permute-done((bf16[64,1024]{1,0:T(8,128)(2,1)S(1)}, bf16[64,1024]{1,0:T(8,128)(2,1)S(1)}, u32[]{:S(2)}, u32[]{:S(2)}) %collective-permute-start.5) | collective-permute-done | bytes 131104 | tf_op jit(solution)/shard_map/ppermute | solution.py:363
  31.3 10.2 %all_to_all.11.back_ref = bf16[32,8,256]{2,1,0:T(8,128)(2,1)S(1)} all-to-all(bf16[32,8,256]{2,1,0:T(8,128)(2,1)S(1)} %shard_map.110), channel_id=1, replica_groups=mesh['grp'=4,'z'=4,'core'=2] {'core','grp','z'}, dimensions={0} | all-to-all | bytes 262144 | tf_op jit(solution)/shard_map/all_to_all | solution.py:441
  41.5 1.4 %shard_map.111 = (bf16[8,4,2048]{2,1,0:T(4,128)(2,1)}, bf16[8,4,2048]{2,1,0:T(4,128)(2,1)}, bf16[8,4,2048]{2,1,0:T(4,128)(2,1)}) custom-call(bf16[256,256]{1,0:T(8,128)(2,1)S(1)} %get-tuple-element.26.spread_ref, bf16[32,8,256]{2,1,0:T(8,128)(2,1)S(1)} %all_to_all.11.back_ref, bf16[32,2048]{1,0:T(8,128)(2,1)S(1)} %get-tuple-element.44.cot_ref, ...), custom_call_target="tpu_custom_call" | custom-call | tf_op jit(solution)/shard_map/pallas_call | solution.py:335
  (2 shorter events, 0.1 us)
Async XLA Ops:
  1.6 7.9 %collective-permute-start = (bf16[8,2048]{1,0:T(8,128)(2,1)S(1)}, bf16[8,2048]{1,0:T(8,128)(2,1)S(1)}, u32[]{:S(2)}, u32[]{:S(2)}) collective-permute-start(bf16[8,2048]{1,0:T(8,128)(2,1)S(1)} %get-tuple-element.31), channel_id=1, source_target_pairs={{0,5},{1,4},{2,7},{3,6},{4,1},{5,0},{6,3},{7,2},{8,13},{9,12},{10,... | collective-permute-start | bytes 98312 | tf_op jit(solution)/shard_map/ppermute | solution.py:367
  5.1 5.2 %collective-permute-start.1 = (bf16[8,2048]{1,0:T(8,128)(2,1)S(1)}, bf16[8,2048]{1,0:T(8,128)(2,1)S(1)}, u32[]{:S(2)}, u32[]{:S(2)}) collective-permute-start(bf16[8,2048]{1,0:T(8,128)(2,1)S(1)} %get-tuple-element.32), channel_id=1, source_target_pairs={{0,7},{1,6},{2,5},{3,4},{4,3},{5,2},{6,1},{7,0},{8,15},{9,14},{10,... | collective-permute-start | bytes 98312 | tf_op jit(solution)/shard_map/ppermute | solution.py:367
  6.7 3.8 %collective-permute-start.2 = (bf16[8,2048]{1,0:T(8,128)(2,1)S(1)}, bf16[8,2048]{1,0:T(8,128)(2,1)S(1)}, u32[]{:S(2)}, u32[]{:S(2)}) collective-permute-start(bf16[8,2048]{1,0:T(8,128)(2,1)S(1)} %get-tuple-element.33), channel_id=1, source_target_pairs={{0,3},{1,2},{2,1},{3,0},{4,7},{5,6},{6,5},{7,4},{8,11},{9,10},{10,... | collective-permute-start | bytes 98312 | tf_op jit(solution)/shard_map/ppermute | solution.py:367
  10.7 1.7 %collective-permute-start.3 = (bf16[20,2048]{1,0:T(8,128)(2,1)S(1)}, bf16[20,2048]{1,0:T(8,128)(2,1)S(1)}, u32[]{:S(2)}, u32[]{:S(2)}) collective-permute-start(bf16[20,2048]{1,0:T(8,128)(2,1)S(1)} %get-tuple-element.35), channel_id=1, source_target_pairs={{0,1},{1,0},{2,3},{3,2},{4,5},{5,4},{6,7},{7,6},{8,9},{9,8},{10,11... | collective-permute-start | bytes 245768 | tf_op jit(solution)/shard_map/ppermute | solution.py:363
  27.3 1.5 %collective-permute-start.4 = (bf16[32,2,2048]{2,1,0:T(2,128)(2,1)S(1)}, bf16[32,2,2048]{2,1,0:T(2,128)(2,1)S(1)}, u32[]{:S(2)}, u32[]{:S(2)}) collective-permute-start(bf16[32,2,2048]{2,1,0:T(2,128)(2,1)S(1)} %all_to_all.10.near_ref), channel_id=1, source_target_pairs={{0,1},{1,0},{2,3},{3,2},{4,5},{5,4},{6,7},{7,6},{8,9},{9,8},{10,11... | collective-permute-start | bytes 786440 | tf_op jit(solution)/shard_map/ppermute | solution.py:363
  29.8 1.4 %collective-permute-start.5 = (bf16[64,1024]{1,0:T(8,128)(2,1)S(1)}, bf16[64,1024]{1,0:T(8,128)(2,1)S(1)}, u32[]{:S(2)}, u32[]{:S(2)}) collective-permute-start(bf16[64,1024]{1,0:T(8,128)(2,1)S(1)} %get-tuple-element.43), channel_id=1, source_target_pairs={{0,1},{1,0},{2,3},{3,2},{4,5},{5,4},{6,7},{7,6},{8,9},{9,8},{10,11... | collective-permute-start | bytes 393224 | tf_op jit(solution)/shard_map/ppermute | solution.py:363

commit v26 on v23

--- a/solution.py
+++ b/solution.py
@@ -189,7 +189,7 @@
 
 
 def pick_kernel(order, take_ref, weight_ref, *refs):
-    *part_refs, cot_ref, mine_ref, sent_ref = refs
+    *part_refs, cot_ref, mine_ref, sent_ref, away_ref = refs
     parts = [part_refs[order.index(k)][...] for k in range(len(order))]
     cot = jnp.concatenate(parts, axis=0)
     cot_ref[...] = cot
@@ -197,14 +197,14 @@
     rows = dot(take_ref[...].astype(jnp.bfloat16), cot)
     picks = (rows[: CORES * slots] * weight_ref[:, :1]).astype(jnp.bfloat16)
     mine_ref[...] = picks[:slots]
-    away = rows[CORES * slots :].astype(jnp.bfloat16)
-    sent_ref[...] = jnp.concatenate([away, picks[slots:]], axis=0)
+    sent_ref[...] = picks[slots:]
+    away_ref[...] = rows[CORES * slots :].astype(jnp.bfloat16)
 
 
 def pack_kernel(share, picked_ref, mine_ref, came_ref, out_ref):
     levels, groups = lax.axis_size("z"), lax.axis_size("grp")
     slots, features = mine_ref.shape
-    rows = mine_ref[...] + came_ref[came_ref.shape[0] - slots :, :]
+    rows = mine_ref[...] + came_ref[...]
     part = features // CORES
     picked = picked_ref[...]
     both = [
@@ -222,7 +222,8 @@
     return pl.ds(pl.multiple_of(part * width, width), width)
 
 
-def first_kernel(near_ref, w_in_ref, w_out_ref, pre_ref, back_ref):
+def first_kernel(near_ref, w_in_ref, w_out_ref, away_ref, pre_ref, back_ref, later_ref):
+    later_ref[...] = away_ref[...]
     width = w_in_ref.shape[0] // CORES
     rows = near_ref[...].reshape(pre_ref.shape[0], CORES * width)
     pre_ref[...] = dot(rows[:, :width], w_in_ref[:width, :])
@@ -239,7 +240,7 @@
     sent_ref[...] = dot_lanes(slope, w_in_ref[width:, :]).astype(jnp.bfloat16)
 
 
-def third_kernel(blocks, slope_ref, w_in_ref, near_ref, came_ref, kept_ref, cot_ref):
+def cot_kernel(blocks, near_ref, came_ref, after_ref, cot_ref):
     rows = near_ref.shape[0]
     span = CORES * blocks
     levels = rows // span
@@ -256,6 +257,9 @@
     cot = dot(own, near_ref[...])
     cot = cot + dot(others, came_ref[: levels * blocks, :])
     cot_ref[...] = cot.astype(jnp.bfloat16)
+
+
+def third_kernel(slope_ref, w_in_ref, kept_ref):
     width = kept_ref.shape[1]
     kept_ref[...] = dot_lanes(slope_ref[...], w_in_ref[:width, :])
 
@@ -395,26 +399,35 @@
             pltpu.SemaphoreType.DMA((5 + 2 * CORES,)),
         ],
     )
-    cot_near, mine, sent = call(
+    cot_near, mine, sent, away = call(
         functools.partial(pick_kernel, order),
-        [((rows, features), bf16), ((slots, features), bf16), ((levels * blocks + slots, features), bf16)],
+        [
+            ((rows, features), bf16),
+            ((slots, features), bf16),
+            ((slots, features), bf16),
+            ((levels * blocks, features), bf16),
+        ],
         [take, weight, *parts],
         "vv" + "v" * levels,
     )
-    came_near = swap(sent)
+    came_picks = swap(sent)
     (outgoing,) = call(
         functools.partial(pack_kernel, share),
         [((devices, MOST, 2 * part), bf16)],
-        [picked, mine, came_near],
+        [picked, mine, came_picks],
         "vvv",
     )
     held = lax.all_to_all(outgoing, everyone, split_axis=0, concat_axis=0, tiled=True)
     other = swap(held)
     acts = (devices * MOST, hidden)
     halves = (devices * MOST, part)
-    pre_act, back_act = call(
-        first_kernel, [(acts, f32), (acts, f32)], [held, w_in_near, w_out_near], "vvv"
-    )
+    pre_act, back_act, away = call(
+        first_kernel,
+        [(acts, f32), (acts, f32), ((levels * blocks, features), bf16)],
+        [held, w_in_near, w_out_near, away],
+        "vvvv",
+    )
+    came_near = swap(away)
     slope, sent = call(
         second_kernel,
         [(acts, bf16), (halves, bf16)],
@@ -422,11 +435,12 @@
         "vvvvv",
     )
     came = swap(sent)
-    kept, cot = call(
-        functools.partial(third_kernel, blocks),
-        [(halves, f32), ((rows, features), bf16)],
-        [slope, w_in_near, cot_near, came_near],
-        "vvvv",
+    (kept,) = call(third_kernel, [(halves, f32)], [slope, w_in_near], "vv")
+    (cot,) = call(
+        functools.partial(cot_kernel, blocks),
+        [((rows, features), bf16)],
+        [cot_near, came_near, kept],
+        "vvv",
     )
     pieces = MOST * part // PIECE
     (total,) = call(

time: 43.1 us -> 44.5 us (1.032)
  blocking collectives: 25.1 us -> 15.4 us
  waiting for transfers between devices: 3.59 us -> 11.1 us
  starting transfers between devices: 6.34 us -> 9.09 us
  Pallas kernels: 7.17 us -> 7.94 us
    all_to_all x1 -> x0, blocking collectives: 9.69 us -> none  [body(): lax.all_to_all(total, everyone, split_axis=0, concat_axis=0, tiled=True)]
    all_to_all x0 -> x1, waiting for transfers between devices: none -> 6.38 us  [body(): lax.all_to_all(total, everyone, split_axis=0, concat_axis=0, tiled=True)]
    all_to_all x0 -> x1, starting transfers between devices: none -> 2.58 us  [body(): lax.all_to_all(total, everyone, split_axis=0, concat_axis=0, tiled=True)]
    ppermute x3 -> x4, waiting for transfers between devices: 2.54 us -> 3.67 us  [swap(): return lax.ppermute(values, 'core', [(i, i ^ 1) for i in range(CORES)])]
    pallas_call x9 -> x10, Pallas kernels: 7.17 us -> 7.94 us  [call(): pl.pallas_call(kernel, out_shape=[jax.ShapeDtypeStruct(shape, dtype) for...]
    ppermute x3 -> x4, starting transfers between devices: 0.93 us -> 1.11 us  [swap(): return lax.ppermute(values, 'core', [(i, i ^ 1) for i in range(CORES)])]
  transfers between devices with their start and end apart: 6 -> 8, of which waited for: 5 -> 7; matrix products, arithmetic and copies ran while one was open for 0% -> 0% of each run, Pallas kernels for 8% -> 8%
where the time goes in v26:
time: 44.5 us; the launch traced here: 44.3 us
  blocking collectives  15.4 us (35%)
  waiting for transfers between devices  11.1 us (25%)
  starting transfers between devices  9.09 us (20%)
  Pallas kernels  7.94 us (18%)
  between operations  0.7 us (2%)
    all_to_all x1, blocking collectives, body(): lax.all_to_all(outgoing, everyone, split_axis=0, concat_axis=0, tiled=True)  15.4 us
    pallas_call x10, Pallas kernels, call(): pl.pallas_call(kernel, out_shape=[jax.ShapeDtypeStruct(shape, dtype) for...  7.94 us
    all_to_all x1, waiting for transfers between devices, body(): lax.all_to_all(total, everyone, split_axis=0, concat_axis=0, tiled=True)  6.38 us
    ppermute x3, starting transfers between devices, across(): return lax.ppermute(values, ('z', 'core'), pairs)  5.4 us
    ppermute x4, waiting for transfers between devices, swap(): return lax.ppermute(values, 'core', [(i, i ^ 1) for i in range(CORES)])  3.67 us
    all_to_all x1, starting transfers between devices, body(): lax.all_to_all(total, everyone, split_axis=0, concat_axis=0, tiled=True)  2.58 us
    ppermute x4, starting transfers between devices, swap(): return lax.ppermute(values, 'core', [(i, i ^ 1) for i in range(CORES)])  1.11 us
    ppermute x3, waiting for transfers between devices, across(): return lax.ppermute(values, ('z', 'core'), pairs)  1.05 us
  transfers between devices with their start and end apart: 8, of which 7 were waited for; matrix products, arithmetic and copies ran while one was open for 0% of the time, Pallas kernels for 8%

profile of v26, /device:TPU:0, one launch (start us, length us, event | category | flops | bytes accessed | tf_op | source)
XLA Modules:
  0.0 44.3 jit_solution(5373889834482288025)
XLA Ops:
  0.6 0.9 %shard_map.104 = (bf16[8,2048]{1,0:T(8,128)(2,1)S(1)}, bf16[8,2048]{1,0:T(8,128)(2,1)S(1)}, bf16[8,2048]{1,0:T(8,128)(2,1)S(1)}, bf16[8,2048]{1,0:T(8,128)(2,1)S(1)}) custom-call(bf16[1,32,2048]{2,1,0:T(8,128)(2,1)} %cot_hbm.1), custom_call_target="tpu_custom_call" | custom-call | tf_op jit(solution)/shard_map/pallas_call | solution.py:336
  1.6 3.5 %collective-permute-start = (bf16[8,2048]{1,0:T(8,128)(2,1)S(1)}, bf16[8,2048]{1,0:T(8,128)(2,1)S(1)}, u32[]{:S(2)}, u32[]{:S(2)}) collective-permute-start(bf16[8,2048]{1,0:T(8,128)(2,1)S(1)} %get-tuple-element.31), channel_id=1, source_target_pairs={{0,5},{1,4},{2,7},{3,6},{4,1},{5,0},{6,3},{7,2},{8,13},{9,12},{10,... | collective-permute-start | bytes 98312 | tf_op jit(solution)/shard_map/ppermute | solution.py:369
  5.1 1.6 %collective-permute-start.1 = (bf16[8,2048]{1,0:T(8,128)(2,1)S(1)}, bf16[8,2048]{1,0:T(8,128)(2,1)S(1)}, u32[]{:S(2)}, u32[]{:S(2)}) collective-permute-start(bf16[8,2048]{1,0:T(8,128)(2,1)S(1)} %get-tuple-element.32), channel_id=1, source_target_pairs={{0,7},{1,6},{2,5},{3,4},{4,3},{5,2},{6,1},{7,0},{8,15},{9,14},{10,... | collective-permute-start | bytes 98312 | tf_op jit(solution)/shard_map/ppermute | solution.py:369
  6.7 0.2 collective-permute-start.2
  7.0 2.5 %shard_map.103 = (bf16[32,2048]{1,0:T(8,128)(2,1)S(1)}, bf16[32,2048]{1,0:T(8,128)(2,1)S(1)}, bf16[32,2048]{1,0:T(8,128)(2,1)S(1)}, bf16[2048,512]{1,0:T(8,128)(...) custom-call(s32[2,32]{1,0:T(2,128)} %chosen_hbm.1, ...), custom_call_target="tpu_custom_call" | custom-call | tf_op jit(solution)/shard_map/pallas_call | solution.py:336
  9.5 0.0 collective-permute-done.refs_1_
  9.5 0.9 %collective-permute-done.1.refs_2_ = bf16[8,2048]{1,0:T(8,128)(2,1)S(1)} collective-permute-done((bf16[8,2048]{1,0:T(8,128)(2,1)S(1)}, bf16[8,2048]{1,0:T(8,128)(2,1)S(1)}, u32[]{:S(2)}, u32[]{:S(2)}) %collective-permute-start.1) | collective-permute-done | bytes 32800 | tf_op jit(solution)/shard_map/ppermute | solution.py:369
  10.4 0.2 collective-permute-done.2.refs_3_
  10.5 0.2 shard_map.105
  10.7 0.7 %collective-permute-start.3 = (bf16[4,2048]{1,0:T(4,128)(2,1)S(1)}, bf16[4,2048]{1,0:T(4,128)(2,1)S(1)}, u32[]{:S(2)}, u32[]{:S(2)}) collective-permute-start(bf16[4,2048]{1,0:T(4,128)(2,1)S(1)} %get-tuple-element.35), channel_id=1, source_target_pairs={{0,1},{1,0},{2,3},{3,2},{4,5},{5,4},{6,7},{7,6},{8,9},{9,8},{10,11... | collective-permute-start | bytes 49160 | tf_op jit(solution)/shard_map/ppermute | solution.py:365
  11.4 0.8 %collective-permute-done.3.came_ref = bf16[4,2048]{1,0:T(4,128)(2,1)S(1)} collective-permute-done((bf16[4,2048]{1,0:T(4,128)(2,1)S(1)}, bf16[4,2048]{1,0:T(4,128)(2,1)S(1)}, u32[]{:S(2)}, u32[]{:S(2)}) %collective-permute-start.3) | collective-permute-done | bytes 16416 | tf_op jit(solution)/shard_map/ppermute | solution.py:365
  12.3 15.4 %all_to_all.10.near_ref = bf16[32,2,2048]{2,1,0:T(2,128)(2,1)S(1)} all-to-all(bf16[32,2,2048]{2,1,0:T(2,128)(2,1)S(1)} %shard_map.106), channel_id=1, replica_groups=mesh['grp'=4,'z'=4,'core'=2] {'core','grp','z'}, dimensions={0} | all-to-all | bytes 524288 | tf_op jit(solution)/shard_map/all_to_all | solution.py:420
  27.7 0.0 collective-permute-start.4
  27.7 0.6 %shard_map.107 = (f32[64,512]{1,0:T(8,128)S(1)}, f32[64,512]{1,0:T(8,128)S(1)}, bf16[16,2048]{1,0:T(8,128)(2,1)S(1)}) custom-call(bf16[32,2,2048]{2,1,0:T(2,128)(2,1)S(1)} %all_to_all.10.near_ref, bf16[2048,512]{1,0:T(8,128)(2,1)S(1)} %get-tuple-element.36.w_in_ref, bf16[512,2048]{1,0:T(8,128)(2,1)S(1)} %get-tuple-element.37.w_out_ref, ...), custom_call_target="tpu_custom_call" | custom-call | tf_op jit(solution)/shard_map/pallas_call | solution.py:336
  28.3 0.9 %collective-permute-done.4.far_ref = bf16[32,2,2048]{2,1,0:T(2,128)(2,1)S(1)} collective-permute-done((bf16[32,2,2048]{2,1,0:T(2,128)(2,1)S(1)}, bf16[32,2,2048]{2,1,0:T(2,128)(2,1)S(1)}, u32[]{:S(2)}, u32[]{:S(2)}) %collective-permute-start.4) | collective-permute-done | bytes 262176 | tf_op jit(solution)/shard_map/ppermute | solution.py:365
  29.3 1.0 %shard_map.108 = (bf16[64,512]{1,0:T(8,128)(2,1)S(1)}, bf16[64,1024]{1,0:T(8,128)(2,1)S(1)}) custom-call(bf16[32,2,2048]{2,1,0:T(2,128)(2,1)S(1)} %collective-permute-done.4.far_ref, f32[64,512]{1,0:T(8,128)S(1)} %get-tuple-element.39.pre_ref, f32[64,512]{1,0:T(8,128)S(1)} %get-tuple-element.40.back_ref, bf16[2048,512]{1,0:T(8,128)(2,1)S(1)} %get-tuple-element.36.w_in_ref, ...), custom_call_target="tpu_custom_call" | custom-call | tf_op jit(solution)/shard_map/pallas_call | solution.py:336
  30.2 0.2 collective-permute-start.5
  30.4 0.4 shard_map.109.kept_ref.after_ref
  30.9 0.8 %collective-permute-done.5.came_ref = bf16[64,1024]{1,0:T(8,128)(2,1)S(1)} collective-permute-done((bf16[64,1024]{1,0:T(8,128)(2,1)S(1)}, bf16[64,1024]{1,0:T(8,128)(2,1)S(1)}, u32[]{:S(2)}, u32[]{:S(2)}) %collective-permute-start.5) | collective-permute-done | bytes 131104 | tf_op jit(solution)/shard_map/ppermute | solution.py:365
  31.7 0.7 %shard_map.110 = bf16[32,8,256]{2,1,0:T(8,128)(2,1)} custom-call(f32[64,1024]{1,0:T(8,128)S(1)} %shard_map.109.kept_ref.after_ref, bf16[64,1024]{1,0:T(8,128)(2,1)S(1)} %collective-permute-done.5.came_ref), custom_call_target="tpu_custom_call" | custom-call | tf_op jit(solution)/shard_map/pallas_call | solution.py:336
  32.3 2.6 %all-to-all-start.1 = ((bf16[32,8,256]{2,1,0:T(8,128)(2,1)}), bf16[32,8,256]{2,1,0:T(8,128)(2,1)S(1)}, u32[]{:S(2)}, u32[]{:S(2)}) async-start(bf16[32,8,256]{2,1,0:T(8,128)(2,1)} %shard_map.110), calls=%async_computation.1 | async-start | bytes 262144 | tf_op jit(solution)/shard_map/all_to_all | solution.py:453
  34.9 0.2 collective-permute-start.6
  35.1 1.1 %collective-permute-done.6.came_ref = bf16[16,2048]{1,0:T(8,128)(2,1)S(1)} collective-permute-done((bf16[16,2048]{1,0:T(8,128)(2,1)S(1)}, bf16[16,2048]{1,0:T(8,128)(2,1)S(1)}, u32[]{:S(2)}, u32[]{:S(2)}) %collective-permute-start.6) | collective-permute-done | bytes 65568 | tf_op jit(solution)/shard_map/ppermute | solution.py:365
  36.2 0.2 shard_map.111.cot_ref
  36.5 6.4 %all-to-all-done.1.back_ref = bf16[32,8,256]{2,1,0:T(8,128)(2,1)S(1)} async-done(((bf16[32,8,256]{2,1,0:T(8,128)(2,1)}), bf16[32,8,256]{2,1,0:T(8,128)(2,1)S(1)}, u32[]{:S(2)}, u32[]{:S(2)}) %all-to-all-start.1) | async-done | bytes 131104 | tf_op jit(solution)/shard_map/all_to_all | solution.py:453
  42.8 1.4 %shard_map.112 = (bf16[8,4,2048]{2,1,0:T(4,128)(2,1)}, bf16[8,4,2048]{2,1,0:T(4,128)(2,1)}, bf16[8,4,2048]{2,1,0:T(4,128)(2,1)}) custom-call(bf16[256,256]{1,0:T(8,128)(2,1)S(1)} %get-tuple-element.26.spread_ref, bf16[32,8,256]{2,1,0:T(8,128)(2,1)S(1)} %all-to-all-done.1.back_ref, bf16[32,2048]{1,0:T(8,128)(2,1)S(1)} %shard_map.111.cot_ref, ...), custom_call_target="tpu_custom_call" | custom-call | tf_op jit(solution)/shard_map/pallas_call | solution.py:336
  (1 shorter events, 0.0 us)
Async XLA Ops:
  1.6 7.9 %collective-permute-start = (bf16[8,2048]{1,0:T(8,128)(2,1)S(1)}, bf16[8,2048]{1,0:T(8,128)(2,1)S(1)}, u32[]{:S(2)}, u32[]{:S(2)}) collective-permute-start(bf16[8,2048]{1,0:T(8,128)(2,1)S(1)} %get-tuple-element.31), channel_id=1, source_target_pairs={{0,5},{1,4},{2,7},{3,6},{4,1},{5,0},{6,3},{7,2},{8,13},{9,12},{10,... | collective-permute-start | bytes 98312 | tf_op jit(solution)/shard_map/ppermute | solution.py:369
  5.1 5.2 %collective-permute-start.1 = (bf16[8,2048]{1,0:T(8,128)(2,1)S(1)}, bf16[8,2048]{1,0:T(8,128)(2,1)S(1)}, u32[]{:S(2)}, u32[]{:S(2)}) collective-permute-start(bf16[8,2048]{1,0:T(8,128)(2,1)S(1)} %get-tuple-element.32), channel_id=1, source_target_pairs={{0,7},{1,6},{2,5},{3,4},{4,3},{5,2},{6,1},{7,0},{8,15},{9,14},{10,... | collective-permute-start | bytes 98312 | tf_op jit(solution)/shard_map/ppermute | solution.py:369
  6.7 3.8 %collective-permute-start.2 = (bf16[8,2048]{1,0:T(8,128)(2,1)S(1)}, bf16[8,2048]{1,0:T(8,128)(2,1)S(1)}, u32[]{:S(2)}, u32[]{:S(2)}) collective-permute-start(bf16[8,2048]{1,0:T(8,128)(2,1)S(1)} %get-tuple-element.33), channel_id=1, source_target_pairs={{0,3},{1,2},{2,1},{3,0},{4,7},{5,6},{6,5},{7,4},{8,11},{9,10},{10,... | collective-permute-start | bytes 98312 | tf_op jit(solution)/shard_map/ppermute | solution.py:369
  10.7 1.6 %collective-permute-start.3 = (bf16[4,2048]{1,0:T(4,128)(2,1)S(1)}, bf16[4,2048]{1,0:T(4,128)(2,1)S(1)}, u32[]{:S(2)}, u32[]{:S(2)}) collective-permute-start(bf16[4,2048]{1,0:T(4,128)(2,1)S(1)} %get-tuple-element.35), channel_id=1, source_target_pairs={{0,1},{1,0},{2,3},{3,2},{4,5},{5,4},{6,7},{7,6},{8,9},{9,8},{10,11... | collective-permute-start | bytes 49160 | tf_op jit(solution)/shard_map/ppermute | solution.py:365
  27.7 1.5 %collective-permute-start.4 = (bf16[32,2,2048]{2,1,0:T(2,128)(2,1)S(1)}, bf16[32,2,2048]{2,1,0:T(2,128)(2,1)S(1)}, u32[]{:S(2)}, u32[]{:S(2)}) collective-permute-start(bf16[32,2,2048]{2,1,0:T(2,128)(2,1)S(1)} %all_to_all.10.near_ref), channel_id=1, source_target_pairs={{0,1},{1,0},{2,3},{3,2},{4,5},{5,4},{6,7},{7,6},{8,9},{9,8},{10,11... | collective-permute-start | bytes 786440 | tf_op jit(solution)/shard_map/ppermute | solution.py:365
  30.2 1.4 %collective-permute-start.5 = (bf16[64,1024]{1,0:T(8,128)(2,1)S(1)}, bf16[64,1024]{1,0:T(8,128)(2,1)S(1)}, u32[]{:S(2)}, u32[]{:S(2)}) collective-permute-start(bf16[64,1024]{1,0:T(8,128)(2,1)S(1)} %get-tuple-element.42), channel_id=1, source_target_pairs={{0,1},{1,0},{2,3},{3,2},{4,5},{5,4},{6,7},{7,6},{8,9},{9,8},{10,11... | collective-permute-start | bytes 393224 | tf_op jit(solution)/shard_map/ppermute | solution.py:365
  32.3 10.5 %all-to-all-start.1 = ((bf16[32,8,256]{2,1,0:T(8,128)(2,1)}), bf16[32,8,256]{2,1,0:T(8,128)(2,1)S(1)}, u32[]{:S(2)}, u32[]{:S(2)}) async-start(bf16[32,8,256]{2,1,0:T(8,128)(2,1)} %shard_map.110), calls=%async_computation.1 | async-start | bytes 262144 | tf_op jit(solution)/shard_map/all_to_all | solution.py:453
  34.9 1.3 %collective-permute-start.6 = (bf16[16,2048]{1,0:T(8,128)(2,1)S(1)}, bf16[16,2048]{1,0:T(8,128)(2,1)S(1)}, u32[]{:S(2)}, u32[]{:S(2)}) collective-permute-start(bf16[16,2048]{1,0:T(8,128)(2,1)S(1)} %get-tuple-element.44), channel_id=1, source_target_pairs={{0,1},{1,0},{2,3},{3,2},{4,5},{5,4},{6,7},{7,6},{8,9},{9,8},{10,11... | collective-permute-start | bytes 196616 | tf_op jit(solution)/shard_map/ppermute | solution.py:365

commit v27 on v23

--- a/solution.py
+++ b/solution.py
@@ -14,6 +14,7 @@
 SUBLANES = 8
 LANES = 128
 PIECE = 256
+TILE = 16
 
 root_half = 0.7071067811865476
 inv_root_tau = 0.3989422804014327
@@ -54,11 +55,18 @@
 
 
 def turn_kernel(span, cot_hbm, *refs):
-    *part_refs, cot_ref, sem = refs
-    copy = pltpu.make_async_copy(cot_hbm, cot_ref, sem)
-    copy.start()
+    *part_refs, cot_ref, sems = refs
+    copies = [
+        pltpu.make_async_copy(
+            cot_hbm.at[:, pl.ds(i * TILE, TILE)], cot_ref.at[:, pl.ds(i * TILE, TILE)], sems.at[i]
+        )
+        for i in range(cot_ref.shape[1] // TILE)
+    ]
+    for copy in copies:
+        copy.start()
     level = lax.axis_index("z")
-    copy.wait()
+    for copy in copies:
+        copy.wait()
     parts = [cot_ref[0, k * span : (k + 1) * span, :] for k in range(len(part_refs))]
     bit = 1
     while bit < len(parts):
@@ -293,10 +301,14 @@
 
     def put(ref, hbm, parts):
         joined = jnp.concatenate(parts, axis=1).astype(jnp.bfloat16)
-        ref[...] = joined.reshape(frames, blocks, features)
-        copy = pltpu.make_async_copy(ref, hbm, sems.at[len(copies)])
-        copy.start()
-        copies.append(copy)
+        half = frames // 2
+        for i in range(2):
+            part = joined[i * half * blocks : (i + 1) * half * blocks]
+            ref[i * half : (i + 1) * half] = part.reshape(half, blocks, features)
+            at = pl.ds(i * half, half)
+            copy = pltpu.make_async_copy(ref.at[at], hbm.at[at], sems.at[len(copies)])
+            copy.start()
+            copies.append(copy)
 
     grad_prob = jnp.concatenate(
         [dot_lanes(v, g) for v, g in zip(heads_of(value), heads_of(stream))], axis=1
@@ -370,7 +382,10 @@
         [((span, features), bf16)] * levels,
         [cotangent],
         "h",
-        [pltpu.VMEM(cotangent.shape, bf16), pltpu.SemaphoreType.DMA],
+        [
+            pltpu.VMEM(cotangent.shape, bf16),
+            pltpu.SemaphoreType.DMA((cotangent.shape[1] // TILE,)),
+        ],
     )
     order = [0] + [i ^ (i >> 1) for i in range(levels - 1, 0, -1)]
     parts = [across(parts[k], k) if k else parts[k] for k in order]
@@ -442,7 +457,7 @@
         [((frames, blocks, features), bf16)] * 3,
         [spread, back, cot, probs, query, key, value],
         "vvvvvvv",
-        [pltpu.VMEM((frames, blocks, features), bf16)] * 3 + [pltpu.SemaphoreType.DMA((3,))],
+        [pltpu.VMEM((frames, blocks, features), bf16)] * 3 + [pltpu.SemaphoreType.DMA((6,))],
         "h",
     )
 

time: 43.1 us -> 43.1 us (level)
  no operation moved by 1% of the time
where the time goes in v27:
time: 43.1 us; the launch traced here: 42.9 us
  blocking collectives  25.1 us (58%)
  Pallas kernels  7.15 us (17%)
  starting transfers between devices  6.33 us (15%)
  waiting for transfers between devices  3.6 us (8%)
  between operations  0.69 us (2%)
    all_to_all x1, blocking collectives, body(): lax.all_to_all(outgoing, everyone, split_axis=0, concat_axis=0, tiled=True)  15.5 us
    all_to_all x1, blocking collectives, body(): lax.all_to_all(total, everyone, split_axis=0, concat_axis=0, tiled=True)  9.69 us
    pallas_call x9, Pallas kernels, call(): pl.pallas_call(kernel, out_shape=[jax.ShapeDtypeStruct(shape, dtype) for...  7.15 us
    ppermute x3, starting transfers between devices, across(): return lax.ppermute(values, ('z', 'core'), pairs)  5.4 us
    ppermute x3, waiting for transfers between devices, swap(): return lax.ppermute(values, 'core', [(i, i ^ 1) for i in range(CORES)])  2.56 us
    ppermute x3, waiting for transfers between devices, across(): return lax.ppermute(values, ('z', 'core'), pairs)  1.05 us
    ppermute x3, starting transfers between devices, swap(): return lax.ppermute(values, 'core', [(i, i ^ 1) for i in range(CORES)])  0.93 us
  transfers between devices with their start and end apart: 6, of which 5 were waited for; matrix products, arithmetic and copies ran while one was open for 0% of the time, Pallas kernels for 8%

profile of v27, /device:TPU:0, one launch (start us, length us, event | category | flops | bytes accessed | tf_op | source)
XLA Modules:
  0.0 42.9 jit_solution(5128764211527358582)
XLA Ops:
  0.6 0.9 %shard_map.104 = (bf16[8,2048]{1,0:T(8,128)(2,1)S(1)}, bf16[8,2048]{1,0:T(8,128)(2,1)S(1)}, bf16[8,2048]{1,0:T(8,128)(2,1)S(1)}, bf16[8,2048]{1,0:T(8,128)(2,1)S(1)}) custom-call(bf16[1,32,2048]{2,1,0:T(8,128)(2,1)} %cot_hbm.1), custom_call_target="tpu_custom_call" | custom-call | tf_op jit(solution)/shard_map/pallas_call | solution.py:344
  1.5 3.5 %collective-permute-start = (bf16[8,2048]{1,0:T(8,128)(2,1)S(1)}, bf16[8,2048]{1,0:T(8,128)(2,1)S(1)}, u32[]{:S(2)}, u32[]{:S(2)}) collective-permute-start(bf16[8,2048]{1,0:T(8,128)(2,1)S(1)} %get-tuple-element.31), channel_id=1, source_target_pairs={{0,5},{1,4},{2,7},{3,6},{4,1},{5,0},{6,3},{7,2},{8,13},{9,12},{10,... | collective-permute-start | bytes 98312 | tf_op jit(solution)/shard_map/ppermute | solution.py:377
  5.1 1.6 %collective-permute-start.1 = (bf16[8,2048]{1,0:T(8,128)(2,1)S(1)}, bf16[8,2048]{1,0:T(8,128)(2,1)S(1)}, u32[]{:S(2)}, u32[]{:S(2)}) collective-permute-start(bf16[8,2048]{1,0:T(8,128)(2,1)S(1)} %get-tuple-element.32), channel_id=1, source_target_pairs={{0,7},{1,6},{2,5},{3,4},{4,3},{5,2},{6,1},{7,0},{8,15},{9,14},{10,... | collective-permute-start | bytes 98312 | tf_op jit(solution)/shard_map/ppermute | solution.py:377
  6.7 0.2 collective-permute-start.2
  7.0 2.5 %shard_map.103 = (bf16[32,2048]{1,0:T(8,128)(2,1)S(1)}, bf16[32,2048]{1,0:T(8,128)(2,1)S(1)}, bf16[32,2048]{1,0:T(8,128)(2,1)S(1)}, bf16[2048,512]{1,0:T(8,128)(...) custom-call(s32[2,32]{1,0:T(2,128)} %chosen_hbm.1, ...), custom_call_target="tpu_custom_call" | custom-call | tf_op jit(solution)/shard_map/pallas_call | solution.py:344
  9.4 0.0 collective-permute-done.refs_1_
  9.4 0.9 %collective-permute-done.1.refs_2_ = bf16[8,2048]{1,0:T(8,128)(2,1)S(1)} collective-permute-done((bf16[8,2048]{1,0:T(8,128)(2,1)S(1)}, bf16[8,2048]{1,0:T(8,128)(2,1)S(1)}, u32[]{:S(2)}, u32[]{:S(2)}) %collective-permute-start.1) | collective-permute-done | bytes 32800 | tf_op jit(solution)/shard_map/ppermute | solution.py:377
  10.3 0.2 collective-permute-done.2.refs_3_
  10.5 0.2 shard_map.105
  10.7 0.7 %collective-permute-start.3 = (bf16[20,2048]{1,0:T(8,128)(2,1)S(1)}, bf16[20,2048]{1,0:T(8,128)(2,1)S(1)}, u32[]{:S(2)}, u32[]{:S(2)}) collective-permute-start(bf16[20,2048]{1,0:T(8,128)(2,1)S(1)} %get-tuple-element.35), channel_id=1, source_target_pairs={{0,1},{1,0},{2,3},{3,2},{4,5},{5,4},{6,7},{7,6},{8,9},{9,8},{10,11... | collective-permute-start | bytes 245768 | tf_op jit(solution)/shard_map/ppermute | solution.py:373
  11.4 0.9 %collective-permute-done.3.came_ref = bf16[20,2048]{1,0:T(8,128)(2,1)S(1)} collective-permute-done((bf16[20,2048]{1,0:T(8,128)(2,1)S(1)}, bf16[20,2048]{1,0:T(8,128)(2,1)S(1)}, u32[]{:S(2)}, u32[]{:S(2)}) %collective-permute-start.3) | collective-permute-done | bytes 81952 | tf_op jit(solution)/shard_map/ppermute | solution.py:373
  12.4 15.5 %all_to_all.10.near_ref = bf16[32,2,2048]{2,1,0:T(2,128)(2,1)S(1)} all-to-all(bf16[32,2,2048]{2,1,0:T(2,128)(2,1)S(1)} %shard_map.106), channel_id=1, replica_groups=mesh['grp'=4,'z'=4,'core'=2] {'core','grp','z'}, dimensions={0} | all-to-all | bytes 524288 | tf_op jit(solution)/shard_map/all_to_all | solution.py:426
  27.8 0.0 collective-permute-start.4
  27.8 0.6 %shard_map.107 = (f32[64,512]{1,0:T(8,128)S(1)}, f32[64,512]{1,0:T(8,128)S(1)}) custom-call(bf16[32,2,2048]{2,1,0:T(2,128)(2,1)S(1)} %all_to_all.10.near_ref, bf16[2048,512]{1,0:T(8,128)(2,1)S(1)} %get-tuple-element.36.w_in_ref, bf16[512,2048]{1,0:T(8,128)(2,1)S(1)} %get-tuple-element.37.w_out_ref), custom_call_target="tpu_custom_call" | custom-call | tf_op jit(solution)/shard_map/pallas_call | solution.py:344
  28.4 0.9 %collective-permute-done.4.far_ref = bf16[32,2,2048]{2,1,0:T(2,128)(2,1)S(1)} collective-permute-done((bf16[32,2,2048]{2,1,0:T(2,128)(2,1)S(1)}, bf16[32,2,2048]{2,1,0:T(2,128)(2,1)S(1)}, u32[]{:S(2)}, u32[]{:S(2)}) %collective-permute-start.4) | collective-permute-done | bytes 262176 | tf_op jit(solution)/shard_map/ppermute | solution.py:373
  29.4 1.0 %shard_map.108 = (bf16[64,512]{1,0:T(8,128)(2,1)S(1)}, bf16[64,1024]{1,0:T(8,128)(2,1)S(1)}) custom-call(bf16[32,2,2048]{2,1,0:T(2,128)(2,1)S(1)} %collective-permute-done.4.far_ref, f32[64,512]{1,0:T(8,128)S(1)} %get-tuple-element.38.pre_ref, f32[64,512]{1,0:T(8,128)S(1)} %get-tuple-element.39.back_ref, bf16[2048,512]{1,0:T(8,128)(2,1)S(1)} %get-tuple-element.36.w_in_ref, ...), custom_call_target="tpu_custom_call" | custom-call | tf_op jit(solution)/shard_map/pallas_call | solution.py:344
  30.3 0.2 collective-permute-start.5
  30.5 0.5 %shard_map.109 = (f32[64,1024]{1,0:T(8,128)S(1)}, bf16[32,2048]{1,0:T(8,128)(2,1)S(1)}) custom-call(bf16[64,512]{1,0:T(8,128)(2,1)S(1)} %get-tuple-element.40.slope_ref, bf16[2048,512]{1,0:T(8,128)(2,1)S(1)} %get-tuple-element.36.w_in_ref, bf16[32,2048]{1,0:T(8,128)(2,1)S(1)} %get-tuple-element.41.near_ref, bf16[20,2048]{1,0:T(8,128)(2,1)S(1)} %collective-permute-done.3.came_ref), custom_call_target="tpu_custom_call" | custom-call | tf_op jit(solution)/shard_map/pallas_call | solution.py:344
  31.1 0.7 %collective-permute-done.5.came_ref = bf16[64,1024]{1,0:T(8,128)(2,1)S(1)} collective-permute-done((bf16[64,1024]{1,0:T(8,128)(2,1)S(1)}, bf16[64,1024]{1,0:T(8,128)(2,1)S(1)}, u32[]{:S(2)}, u32[]{:S(2)}) %collective-permute-start.5) | collective-permute-done | bytes 131104 | tf_op jit(solution)/shard_map/ppermute | solution.py:373
  31.8 9.7 %all_to_all.11.back_ref = bf16[32,8,256]{2,1,0:T(8,128)(2,1)S(1)} all-to-all(bf16[32,8,256]{2,1,0:T(8,128)(2,1)S(1)} %shard_map.110), channel_id=1, replica_groups=mesh['grp'=4,'z'=4,'core'=2] {'core','grp','z'}, dimensions={0} | all-to-all | bytes 262144 | tf_op jit(solution)/shard_map/all_to_all | solution.py:454
  41.5 1.4 %shard_map.111 = (bf16[8,4,2048]{2,1,0:T(4,128)(2,1)}, bf16[8,4,2048]{2,1,0:T(4,128)(2,1)}, bf16[8,4,2048]{2,1,0:T(4,128)(2,1)}) custom-call(bf16[256,256]{1,0:T(8,128)(2,1)S(1)} %get-tuple-element.26.spread_ref, bf16[32,8,256]{2,1,0:T(8,128)(2,1)S(1)} %all_to_all.11.back_ref, bf16[32,2048]{1,0:T(8,128)(2,1)S(1)} %get-tuple-element.44.cot_ref, ...), custom_call_target="tpu_custom_call" | custom-call | tf_op jit(solution)/shard_map/pallas_call | solution.py:344
  (2 shorter events, 0.1 us)
Async XLA Ops:
  1.5 7.9 %collective-permute-start = (bf16[8,2048]{1,0:T(8,128)(2,1)S(1)}, bf16[8,2048]{1,0:T(8,128)(2,1)S(1)}, u32[]{:S(2)}, u32[]{:S(2)}) collective-permute-start(bf16[8,2048]{1,0:T(8,128)(2,1)S(1)} %get-tuple-element.31), channel_id=1, source_target_pairs={{0,5},{1,4},{2,7},{3,6},{4,1},{5,0},{6,3},{7,2},{8,13},{9,12},{10,... | collective-permute-start | bytes 98312 | tf_op jit(solution)/shard_map/ppermute | solution.py:377
  5.1 5.2 %collective-permute-start.1 = (bf16[8,2048]{1,0:T(8,128)(2,1)S(1)}, bf16[8,2048]{1,0:T(8,128)(2,1)S(1)}, u32[]{:S(2)}, u32[]{:S(2)}) collective-permute-start(bf16[8,2048]{1,0:T(8,128)(2,1)S(1)} %get-tuple-element.32), channel_id=1, source_target_pairs={{0,7},{1,6},{2,5},{3,4},{4,3},{5,2},{6,1},{7,0},{8,15},{9,14},{10,... | collective-permute-start | bytes 98312 | tf_op jit(solution)/shard_map/ppermute | solution.py:377
  6.7 3.8 %collective-permute-start.2 = (bf16[8,2048]{1,0:T(8,128)(2,1)S(1)}, bf16[8,2048]{1,0:T(8,128)(2,1)S(1)}, u32[]{:S(2)}, u32[]{:S(2)}) collective-permute-start(bf16[8,2048]{1,0:T(8,128)(2,1)S(1)} %get-tuple-element.33), channel_id=1, source_target_pairs={{0,3},{1,2},{2,1},{3,0},{4,7},{5,6},{6,5},{7,4},{8,11},{9,10},{10,... | collective-permute-start | bytes 98312 | tf_op jit(solution)/shard_map/ppermute | solution.py:377
  10.7 1.7 %collective-permute-start.3 = (bf16[20,2048]{1,0:T(8,128)(2,1)S(1)}, bf16[20,2048]{1,0:T(8,128)(2,1)S(1)}, u32[]{:S(2)}, u32[]{:S(2)}) collective-permute-start(bf16[20,2048]{1,0:T(8,128)(2,1)S(1)} %get-tuple-element.35), channel_id=1, source_target_pairs={{0,1},{1,0},{2,3},{3,2},{4,5},{5,4},{6,7},{7,6},{8,9},{9,8},{10,11... | collective-permute-start | bytes 245768 | tf_op jit(solution)/shard_map/ppermute | solution.py:373
  27.8 1.5 %collective-permute-start.4 = (bf16[32,2,2048]{2,1,0:T(2,128)(2,1)S(1)}, bf16[32,2,2048]{2,1,0:T(2,128)(2,1)S(1)}, u32[]{:S(2)}, u32[]{:S(2)}) collective-permute-start(bf16[32,2,2048]{2,1,0:T(2,128)(2,1)S(1)} %all_to_all.10.near_ref), channel_id=1, source_target_pairs={{0,1},{1,0},{2,3},{3,2},{4,5},{5,4},{6,7},{7,6},{8,9},{9,8},{10,11... | collective-permute-start | bytes 786440 | tf_op jit(solution)/shard_map/ppermute | solution.py:373
  30.3 1.4 %collective-permute-start.5 = (bf16[64,1024]{1,0:T(8,128)(2,1)S(1)}, bf16[64,1024]{1,0:T(8,128)(2,1)S(1)}, u32[]{:S(2)}, u32[]{:S(2)}) collective-permute-start(bf16[64,1024]{1,0:T(8,128)(2,1)S(1)} %get-tuple-element.43), channel_id=1, source_target_pairs={{0,1},{1,0},{2,3},{3,2},{4,5},{5,4},{6,7},{7,6},{8,9},{9,8},{10,11... | collective-permute-start | bytes 393224 | tf_op jit(solution)/shard_map/ppermute | solution.py:373

commit v28 on v25

--- a/solution.py
+++ b/solution.py
@@ -14,6 +14,7 @@
 SUBLANES = 8
 LANES = 128
 PIECE = 256
+TILE = 16
 
 root_half = 0.7071067811865476
 inv_root_tau = 0.3989422804014327
@@ -54,11 +55,18 @@
 
 
 def turn_kernel(span, cot_hbm, *refs):
-    *part_refs, cot_ref, sem = refs
-    copy = pltpu.make_async_copy(cot_hbm, cot_ref, sem)
-    copy.start()
+    *part_refs, cot_ref, sems = refs
+    copies = [
+        pltpu.make_async_copy(
+            cot_hbm.at[:, pl.ds(i * TILE, TILE)], cot_ref.at[:, pl.ds(i * TILE, TILE)], sems.at[i]
+        )
+        for i in range(cot_ref.shape[1] // TILE)
+    ]
+    for copy in copies:
+        copy.start()
     level = lax.axis_index("z")
-    copy.wait()
+    for copy in copies:
+        copy.wait()
     parts = [cot_ref[0, k * span : (k + 1) * span, :] for k in range(len(part_refs))]
     bit = 1
     while bit < len(parts):
@@ -215,7 +223,7 @@
     ]
     for i in range(out_ref.shape[0]):
         e = i // (CORES * levels) // share
-        out_ref[i] = both[i % CORES][e * MOST : (e + 1) * MOST]
+        out_ref[i] = both[i // levels % CORES][e * MOST : (e + 1) * MOST]
 
 
 def part_of(part, width):
@@ -271,9 +279,12 @@
             piece_ref[i, pl.ds(j, count, stride=pieces), :] = total[:, start : start + LANES]
     total = jnp.concatenate([piece_ref[i] for i in range(parts)], axis=1)
     devices, pieces, _ = out_ref.shape
-    total = total.astype(jnp.bfloat16).reshape(devices // CORES, CORES, pieces, PIECE)
+    levels = lax.axis_size("z")
+    total = total.astype(jnp.bfloat16).reshape(-1, CORES, levels, pieces, PIECE)
     for c in range(CORES):
-        out_ref[c * (devices // CORES) : (c + 1) * (devices // CORES)] = total[:, c]
+        out_ref[c * (devices // CORES) : (c + 1) * (devices // CORES)] = (
+            total[:, c].reshape(devices // CORES, pieces, PIECE)
+        )
 
 
 def backward_kernel(
@@ -372,7 +383,10 @@
         [((span, features), bf16)] * levels,
         [cotangent],
         "h",
-        [pltpu.VMEM(cotangent.shape, bf16), pltpu.SemaphoreType.DMA],
+        [
+            pltpu.VMEM(cotangent.shape, bf16),
+            pltpu.SemaphoreType.DMA((cotangent.shape[1] // TILE,)),
+        ],
     )
     order = [0] + [i ^ (i >> 1) for i in range(levels - 1, 0, -1)]
     parts = [across(parts[k], k) if k else parts[k] for k in order]
@@ -410,7 +424,7 @@
         [picked, mine, came_near],
         "vvv",
     )
-    held = lax.all_to_all(outgoing, ("grp", "z", "core"), split_axis=0, concat_axis=0, tiled=True)
+    held = lax.all_to_all(outgoing, ("grp", "core", "z"), split_axis=0, concat_axis=0, tiled=True)
     other = swap(held)
     acts = (devices * MOST, hidden)
     halves = (devices * MOST, part)

time: 43.1 us -> 43.1 us (level)
  no operation moved by 1% of the time
where the time goes in v28:
time: 43.1 us; the launch traced here: 42.9 us
  blocking collectives  25.1 us (58%)
  Pallas kernels  7.14 us (17%)
  starting transfers between devices  6.96 us (16%)
  waiting for transfers between devices  3 us (7%)
  between operations  0.69 us (2%)
    all_to_all x1, blocking collectives, body(): lax.all_to_all(outgoing, ('grp', 'core', 'z'), split_axis=0, concat_axis=...  14.7 us
    all_to_all x1, blocking collectives, body(): lax.all_to_all(total, ('core', 'grp', 'z'), split_axis=0, concat_axis=0,...  10.4 us
    pallas_call x9, Pallas kernels, call(): pl.pallas_call(kernel, out_shape=[jax.ShapeDtypeStruct(shape, dtype) for...  7.14 us
    ppermute x3, starting transfers between devices, across(): return lax.ppermute(values, ('z', 'core'), pairs)  5.4 us
    ppermute x3, waiting for transfers between devices, swap(): return lax.ppermute(values, 'core', [(i, i ^ 1) for i in range(CORES)])  1.95 us
    ppermute x3, starting transfers between devices, swap(): return lax.ppermute(values, 'core', [(i, i ^ 1) for i in range(CORES)])  1.56 us
    ppermute x3, waiting for transfers between devices, across(): return lax.ppermute(values, ('z', 'core'), pairs)  1.05 us
  transfers between devices with their start and end apart: 6, of which 5 were waited for; matrix products, arithmetic and copies ran while one was open for 0% of the time, Pallas kernels for 8%

profile of v28, /device:TPU:0, one launch (start us, length us, event | category | flops | bytes accessed | tf_op | source)
XLA Modules:
  0.0 42.9 jit_solution(12844083649161546633)
XLA Ops:
  0.6 0.9 %shard_map.104 = (bf16[8,2048]{1,0:T(8,128)(2,1)S(1)}, bf16[8,2048]{1,0:T(8,128)(2,1)S(1)}, bf16[8,2048]{1,0:T(8,128)(2,1)S(1)}, bf16[8,2048]{1,0:T(8,128)(2,1)S(1)}) custom-call(bf16[1,32,2048]{2,1,0:T(8,128)(2,1)} %cot_hbm.1), custom_call_target="tpu_custom_call" | custom-call | tf_op jit(solution)/shard_map/pallas_call | solution.py:346
  1.5 3.5 %collective-permute-start = (bf16[8,2048]{1,0:T(8,128)(2,1)S(1)}, bf16[8,2048]{1,0:T(8,128)(2,1)S(1)}, u32[]{:S(2)}, u32[]{:S(2)}) collective-permute-start(bf16[8,2048]{1,0:T(8,128)(2,1)S(1)} %get-tuple-element.31), channel_id=1, source_target_pairs={{0,5},{1,4},{2,7},{3,6},{4,1},{5,0},{6,3},{7,2},{8,13},{9,12},{10,... | collective-permute-start | bytes 98312 | tf_op jit(solution)/shard_map/ppermute | solution.py:378
  5.1 1.6 %collective-permute-start.1 = (bf16[8,2048]{1,0:T(8,128)(2,1)S(1)}, bf16[8,2048]{1,0:T(8,128)(2,1)S(1)}, u32[]{:S(2)}, u32[]{:S(2)}) collective-permute-start(bf16[8,2048]{1,0:T(8,128)(2,1)S(1)} %get-tuple-element.32), channel_id=1, source_target_pairs={{0,7},{1,6},{2,5},{3,4},{4,3},{5,2},{6,1},{7,0},{8,15},{9,14},{10,... | collective-permute-start | bytes 98312 | tf_op jit(solution)/shard_map/ppermute | solution.py:378
  6.7 0.2 collective-permute-start.2
  7.0 2.5 %shard_map.103 = (bf16[32,2048]{1,0:T(8,128)(2,1)S(1)}, bf16[32,2048]{1,0:T(8,128)(2,1)S(1)}, bf16[32,2048]{1,0:T(8,128)(2,1)S(1)}, bf16[2048,512]{1,0:T(8,128)(...) custom-call(s32[2,32]{1,0:T(2,128)} %chosen_hbm.1, ...), custom_call_target="tpu_custom_call" | custom-call | tf_op jit(solution)/shard_map/pallas_call | solution.py:346
  9.4 0.0 collective-permute-done.refs_1_
  9.4 0.9 %collective-permute-done.1.refs_2_ = bf16[8,2048]{1,0:T(8,128)(2,1)S(1)} collective-permute-done((bf16[8,2048]{1,0:T(8,128)(2,1)S(1)}, bf16[8,2048]{1,0:T(8,128)(2,1)S(1)}, u32[]{:S(2)}, u32[]{:S(2)}) %collective-permute-start.1) | collective-permute-done | bytes 32800 | tf_op jit(solution)/shard_map/ppermute | solution.py:378
  10.3 0.2 collective-permute-done.2.refs_3_
  10.5 0.2 shard_map.105
  10.7 0.7 %collective-permute-start.3 = (bf16[20,2048]{1,0:T(8,128)(2,1)S(1)}, bf16[20,2048]{1,0:T(8,128)(2,1)S(1)}, u32[]{:S(2)}, u32[]{:S(2)}) collective-permute-start(bf16[20,2048]{1,0:T(8,128)(2,1)S(1)} %get-tuple-element.35), channel_id=1, source_target_pairs={{0,1},{1,0},{2,3},{3,2},{4,5},{5,4},{6,7},{7,6},{8,9},{9,8},{10,11... | collective-permute-start | bytes 245768 | tf_op jit(solution)/shard_map/ppermute | solution.py:374
  11.4 0.9 %collective-permute-done.3.came_ref = bf16[20,2048]{1,0:T(8,128)(2,1)S(1)} collective-permute-done((bf16[20,2048]{1,0:T(8,128)(2,1)S(1)}, bf16[20,2048]{1,0:T(8,128)(2,1)S(1)}, u32[]{:S(2)}, u32[]{:S(2)}) %collective-permute-start.3) | collective-permute-done | bytes 81952 | tf_op jit(solution)/shard_map/ppermute | solution.py:374
  12.4 14.7 %all_to_all.10.near_ref = bf16[32,2,2048]{2,1,0:T(2,128)(2,1)S(1)} all-to-all(bf16[32,2,2048]{2,1,0:T(2,128)(2,1)S(1)} %shard_map.106), channel_id=1, replica_groups=mesh['grp'=4,'z'=4,'core'=2] {'grp','core','z'}, dimensions={0} | all-to-all | bytes 524288 | tf_op jit(solution)/shard_map/all_to_all | solution.py:427
  27.1 0.4 collective-permute-start.4
  27.5 0.6 %shard_map.107 = (f32[64,512]{1,0:T(8,128)S(1)}, f32[64,512]{1,0:T(8,128)S(1)}) custom-call(bf16[32,2,2048]{2,1,0:T(2,128)(2,1)S(1)} %all_to_all.10.near_ref, bf16[2048,512]{1,0:T(8,128)(2,1)S(1)} %get-tuple-element.36.w_in_ref, bf16[512,2048]{1,0:T(8,128)(2,1)S(1)} %get-tuple-element.37.w_out_ref), custom_call_target="tpu_custom_call" | custom-call | tf_op jit(solution)/shard_map/pallas_call | solution.py:346
  28.1 0.6 %collective-permute-done.4.far_ref = bf16[32,2,2048]{2,1,0:T(2,128)(2,1)S(1)} collective-permute-done((bf16[32,2,2048]{2,1,0:T(2,128)(2,1)S(1)}, bf16[32,2,2048]{2,1,0:T(2,128)(2,1)S(1)}, u32[]{:S(2)}, u32[]{:S(2)}) %collective-permute-start.4) | collective-permute-done | bytes 262176 | tf_op jit(solution)/shard_map/ppermute | solution.py:374
  28.6 1.0 %shard_map.108 = (bf16[64,512]{1,0:T(8,128)(2,1)S(1)}, bf16[64,1024]{1,0:T(8,128)(2,1)S(1)}) custom-call(bf16[32,2,2048]{2,1,0:T(2,128)(2,1)S(1)} %collective-permute-done.4.far_ref, f32[64,512]{1,0:T(8,128)S(1)} %get-tuple-element.38.pre_ref, f32[64,512]{1,0:T(8,128)S(1)} %get-tuple-element.39.back_ref, bf16[2048,512]{1,0:T(8,128)(2,1)S(1)} %get-tuple-element.36.w_in_ref, ...), custom_call_target="tpu_custom_call" | custom-call | tf_op jit(solution)/shard_map/pallas_call | solution.py:346
  29.6 0.4 %collective-permute-start.5 = (bf16[64,1024]{1,0:T(8,128)(2,1)S(1)}, bf16[64,1024]{1,0:T(8,128)(2,1)S(1)}, u32[]{:S(2)}, u32[]{:S(2)}) collective-permute-start(bf16[64,1024]{1,0:T(8,128)(2,1)S(1)} %get-tuple-element.43), channel_id=1, source_target_pairs={{0,1},{1,0},{2,3},{3,2},{4,5},{5,4},{6,7},{7,6},{8,9},{9,8},{10,11... | collective-permute-start | bytes 393224 | tf_op jit(solution)/shard_map/ppermute | solution.py:374
  30.0 0.5 %shard_map.109 = (f32[64,1024]{1,0:T(8,128)S(1)}, bf16[32,2048]{1,0:T(8,128)(2,1)S(1)}) custom-call(bf16[64,512]{1,0:T(8,128)(2,1)S(1)} %get-tuple-element.40.slope_ref, bf16[2048,512]{1,0:T(8,128)(2,1)S(1)} %get-tuple-element.36.w_in_ref, bf16[32,2048]{1,0:T(8,128)(2,1)S(1)} %get-tuple-element.41.near_ref, bf16[20,2048]{1,0:T(8,128)(2,1)S(1)} %collective-permute-done.3.came_ref), custom_call_target="tpu_custom_call" | custom-call | tf_op jit(solution)/shard_map/pallas_call | solution.py:346
  30.6 0.5 %collective-permute-done.5.came_ref = bf16[64,1024]{1,0:T(8,128)(2,1)S(1)} collective-permute-done((bf16[64,1024]{1,0:T(8,128)(2,1)S(1)}, bf16[64,1024]{1,0:T(8,128)(2,1)S(1)}, u32[]{:S(2)}, u32[]{:S(2)}) %collective-permute-start.5) | collective-permute-done | bytes 131104 | tf_op jit(solution)/shard_map/ppermute | solution.py:374
  31.1 10.4 %all_to_all.11.back_ref = bf16[32,8,256]{2,1,0:T(8,128)(2,1)S(1)} all-to-all(bf16[32,8,256]{2,1,0:T(8,128)(2,1)S(1)} %shard_map.110), channel_id=1, replica_groups=mesh['grp'=4,'z'=4,'core'=2] {'core','grp','z'}, dimensions={0} | all-to-all | bytes 262144 | tf_op jit(solution)/shard_map/all_to_all | solution.py:455
  41.5 1.4 %shard_map.111 = (bf16[8,4,2048]{2,1,0:T(4,128)(2,1)}, bf16[8,4,2048]{2,1,0:T(4,128)(2,1)}, bf16[8,4,2048]{2,1,0:T(4,128)(2,1)}) custom-call(bf16[256,256]{1,0:T(8,128)(2,1)S(1)} %get-tuple-element.26.spread_ref, bf16[32,8,256]{2,1,0:T(8,128)(2,1)S(1)} %all_to_all.11.back_ref, bf16[32,2048]{1,0:T(8,128)(2,1)S(1)} %get-tuple-element.44.cot_ref, ...), custom_call_target="tpu_custom_call" | custom-call | tf_op jit(solution)/shard_map/pallas_call | solution.py:346
  (2 shorter events, 0.1 us)
Async XLA Ops:
  1.5 7.9 %collective-permute-start = (bf16[8,2048]{1,0:T(8,128)(2,1)S(1)}, bf16[8,2048]{1,0:T(8,128)(2,1)S(1)}, u32[]{:S(2)}, u32[]{:S(2)}) collective-permute-start(bf16[8,2048]{1,0:T(8,128)(2,1)S(1)} %get-tuple-element.31), channel_id=1, source_target_pairs={{0,5},{1,4},{2,7},{3,6},{4,1},{5,0},{6,3},{7,2},{8,13},{9,12},{10,... | collective-permute-start | bytes 98312 | tf_op jit(solution)/shard_map/ppermute | solution.py:378
  5.1 5.2 %collective-permute-start.1 = (bf16[8,2048]{1,0:T(8,128)(2,1)S(1)}, bf16[8,2048]{1,0:T(8,128)(2,1)S(1)}, u32[]{:S(2)}, u32[]{:S(2)}) collective-permute-start(bf16[8,2048]{1,0:T(8,128)(2,1)S(1)} %get-tuple-element.32), channel_id=1, source_target_pairs={{0,7},{1,6},{2,5},{3,4},{4,3},{5,2},{6,1},{7,0},{8,15},{9,14},{10,... | collective-permute-start | bytes 98312 | tf_op jit(solution)/shard_map/ppermute | solution.py:378
  6.7 3.8 %collective-permute-start.2 = (bf16[8,2048]{1,0:T(8,128)(2,1)S(1)}, bf16[8,2048]{1,0:T(8,128)(2,1)S(1)}, u32[]{:S(2)}, u32[]{:S(2)}) collective-permute-start(bf16[8,2048]{1,0:T(8,128)(2,1)S(1)} %get-tuple-element.33), channel_id=1, source_target_pairs={{0,3},{1,2},{2,1},{3,0},{4,7},{5,6},{6,5},{7,4},{8,11},{9,10},{10,... | collective-permute-start | bytes 98312 | tf_op jit(solution)/shard_map/ppermute | solution.py:378
  10.7 1.7 %collective-permute-start.3 = (bf16[20,2048]{1,0:T(8,128)(2,1)S(1)}, bf16[20,2048]{1,0:T(8,128)(2,1)S(1)}, u32[]{:S(2)}, u32[]{:S(2)}) collective-permute-start(bf16[20,2048]{1,0:T(8,128)(2,1)S(1)} %get-tuple-element.35), channel_id=1, source_target_pairs={{0,1},{1,0},{2,3},{3,2},{4,5},{5,4},{6,7},{7,6},{8,9},{9,8},{10,11... | collective-permute-start | bytes 245768 | tf_op jit(solution)/shard_map/ppermute | solution.py:374
  27.1 1.6 %collective-permute-start.4 = (bf16[32,2,2048]{2,1,0:T(2,128)(2,1)S(1)}, bf16[32,2,2048]{2,1,0:T(2,128)(2,1)S(1)}, u32[]{:S(2)}, u32[]{:S(2)}) collective-permute-start(bf16[32,2,2048]{2,1,0:T(2,128)(2,1)S(1)} %all_to_all.10.near_ref), channel_id=1, source_target_pairs={{0,1},{1,0},{2,3},{3,2},{4,5},{5,4},{6,7},{7,6},{8,9},{9,8},{10,11... | collective-permute-start | bytes 786440 | tf_op jit(solution)/shard_map/ppermute | solution.py:374
  29.6 1.4 %collective-permute-start.5 = (bf16[64,1024]{1,0:T(8,128)(2,1)S(1)}, bf16[64,1024]{1,0:T(8,128)(2,1)S(1)}, u32[]{:S(2)}, u32[]{:S(2)}) collective-permute-start(bf16[64,1024]{1,0:T(8,128)(2,1)S(1)} %get-tuple-element.43), channel_id=1, source_target_pairs={{0,1},{1,0},{2,3},{3,2},{4,5},{5,4},{6,7},{7,6},{8,9},{9,8},{10,11... | collective-permute-start | bytes 393224 | tf_op jit(solution)/shard_map/ppermute | solution.py:374

commit v29 on v27

--- a/solution.py
+++ b/solution.py
@@ -301,14 +301,10 @@
 
     def put(ref, hbm, parts):
         joined = jnp.concatenate(parts, axis=1).astype(jnp.bfloat16)
-        half = frames // 2
-        for i in range(2):
-            part = joined[i * half * blocks : (i + 1) * half * blocks]
-            ref[i * half : (i + 1) * half] = part.reshape(half, blocks, features)
-            at = pl.ds(i * half, half)
-            copy = pltpu.make_async_copy(ref.at[at], hbm.at[at], sems.at[len(copies)])
-            copy.start()
-            copies.append(copy)
+        ref[...] = joined.reshape(frames, blocks, features)
+        copy = pltpu.make_async_copy(ref, hbm, sems.at[len(copies)])
+        copy.start()
+        copies.append(copy)
 
     grad_prob = jnp.concatenate(
         [dot_lanes(v, g) for v, g in zip(heads_of(value), heads_of(stream))], axis=1
@@ -457,7 +453,7 @@
         [((frames, blocks, features), bf16)] * 3,
         [spread, back, cot, probs, query, key, value],
         "vvvvvvv",
-        [pltpu.VMEM((frames, blocks, features), bf16)] * 3 + [pltpu.SemaphoreType.DMA((6,))],
+        [pltpu.VMEM((frames, blocks, features), bf16)] * 3 + [pltpu.SemaphoreType.DMA((3,))],
         "h",
     )
 

time: 43.1 us -> 43.1 us (level)
  no operation moved by 1% of the time
where the time goes in v29:
time: 43.1 us; the launch traced here: 42.9 us
  blocking collectives  25.1 us (58%)
  Pallas kernels  7.13 us (17%)
  starting transfers between devices  6.33 us (15%)
  waiting for transfers between devices  3.6 us (8%)
  between operations  0.69 us (2%)
    all_to_all x1, blocking collectives, body(): lax.all_to_all(outgoing, everyone, split_axis=0, concat_axis=0, tiled=True)  15.5 us
    all_to_all x1, blocking collectives, body(): lax.all_to_all(total, everyone, split_axis=0, concat_axis=0, tiled=True)  9.69 us
    pallas_call x9, Pallas kernels, call(): pl.pallas_call(kernel, out_shape=[jax.ShapeDtypeStruct(shape, dtype) for...  7.13 us
    ppermute x3, starting transfers between devices, across(): return lax.ppermute(values, ('z', 'core'), pairs)  5.4 us
    ppermute x3, waiting for transfers between devices, swap(): return lax.ppermute(values, 'core', [(i, i ^ 1) for i in range(CORES)])  2.56 us
    ppermute x3, waiting for transfers between devices, across(): return lax.ppermute(values, ('z', 'core'), pairs)  1.05 us
    ppermute x3, starting transfers between devices, swap(): return lax.ppermute(values, 'core', [(i, i ^ 1) for i in range(CORES)])  0.93 us
  transfers between devices with their start and end apart: 6, of which 5 were waited for; matrix products, arithmetic and copies ran while one was open for 0% of the time, Pallas kernels for 8%

profile of v29, /device:TPU:0, one launch (start us, length us, event | category | flops | bytes accessed | tf_op | source)
XLA Modules:
  0.0 42.9 jit_solution(12694048397746219382)
XLA Ops:
  0.6 0.9 %shard_map.104 = (bf16[8,2048]{1,0:T(8,128)(2,1)S(1)}, bf16[8,2048]{1,0:T(8,128)(2,1)S(1)}, bf16[8,2048]{1,0:T(8,128)(2,1)S(1)}, bf16[8,2048]{1,0:T(8,128)(2,1)S(1)}) custom-call(bf16[1,32,2048]{2,1,0:T(8,128)(2,1)} %cot_hbm.1), custom_call_target="tpu_custom_call" | custom-call | tf_op jit(solution)/shard_map/pallas_call | solution.py:340
  1.5 3.5 %collective-permute-start = (bf16[8,2048]{1,0:T(8,128)(2,1)S(1)}, bf16[8,2048]{1,0:T(8,128)(2,1)S(1)}, u32[]{:S(2)}, u32[]{:S(2)}) collective-permute-start(bf16[8,2048]{1,0:T(8,128)(2,1)S(1)} %get-tuple-element.31), channel_id=1, source_target_pairs={{0,5},{1,4},{2,7},{3,6},{4,1},{5,0},{6,3},{7,2},{8,13},{9,12},{10,... | collective-permute-start | bytes 98312 | tf_op jit(solution)/shard_map/ppermute | solution.py:373
  5.1 1.6 %collective-permute-start.1 = (bf16[8,2048]{1,0:T(8,128)(2,1)S(1)}, bf16[8,2048]{1,0:T(8,128)(2,1)S(1)}, u32[]{:S(2)}, u32[]{:S(2)}) collective-permute-start(bf16[8,2048]{1,0:T(8,128)(2,1)S(1)} %get-tuple-element.32), channel_id=1, source_target_pairs={{0,7},{1,6},{2,5},{3,4},{4,3},{5,2},{6,1},{7,0},{8,15},{9,14},{10,... | collective-permute-start | bytes 98312 | tf_op jit(solution)/shard_map/ppermute | solution.py:373
  6.7 0.2 collective-permute-start.2
  7.0 2.5 %shard_map.103 = (bf16[32,2048]{1,0:T(8,128)(2,1)S(1)}, bf16[32,2048]{1,0:T(8,128)(2,1)S(1)}, bf16[32,2048]{1,0:T(8,128)(2,1)S(1)}, bf16[2048,512]{1,0:T(8,128)(...) custom-call(s32[2,32]{1,0:T(2,128)} %chosen_hbm.1, ...), custom_call_target="tpu_custom_call" | custom-call | tf_op jit(solution)/shard_map/pallas_call | solution.py:340
  9.4 0.0 collective-permute-done.refs_1_
  9.4 0.9 %collective-permute-done.1.refs_2_ = bf16[8,2048]{1,0:T(8,128)(2,1)S(1)} collective-permute-done((bf16[8,2048]{1,0:T(8,128)(2,1)S(1)}, bf16[8,2048]{1,0:T(8,128)(2,1)S(1)}, u32[]{:S(2)}, u32[]{:S(2)}) %collective-permute-start.1) | collective-permute-done | bytes 32800 | tf_op jit(solution)/shard_map/ppermute | solution.py:373
  10.3 0.2 collective-permute-done.2.refs_3_
  10.5 0.2 shard_map.105
  10.7 0.7 %collective-permute-start.3 = (bf16[20,2048]{1,0:T(8,128)(2,1)S(1)}, bf16[20,2048]{1,0:T(8,128)(2,1)S(1)}, u32[]{:S(2)}, u32[]{:S(2)}) collective-permute-start(bf16[20,2048]{1,0:T(8,128)(2,1)S(1)} %get-tuple-element.35), channel_id=1, source_target_pairs={{0,1},{1,0},{2,3},{3,2},{4,5},{5,4},{6,7},{7,6},{8,9},{9,8},{10,11... | collective-permute-start | bytes 245768 | tf_op jit(solution)/shard_map/ppermute | solution.py:369
  11.4 0.9 %collective-permute-done.3.came_ref = bf16[20,2048]{1,0:T(8,128)(2,1)S(1)} collective-permute-done((bf16[20,2048]{1,0:T(8,128)(2,1)S(1)}, bf16[20,2048]{1,0:T(8,128)(2,1)S(1)}, u32[]{:S(2)}, u32[]{:S(2)}) %collective-permute-start.3) | collective-permute-done | bytes 81952 | tf_op jit(solution)/shard_map/ppermute | solution.py:369
  12.4 15.5 %all_to_all.10.near_ref = bf16[32,2,2048]{2,1,0:T(2,128)(2,1)S(1)} all-to-all(bf16[32,2,2048]{2,1,0:T(2,128)(2,1)S(1)} %shard_map.106), channel_id=1, replica_groups=mesh['grp'=4,'z'=4,'core'=2] {'core','grp','z'}, dimensions={0} | all-to-all | bytes 524288 | tf_op jit(solution)/shard_map/all_to_all | solution.py:422
  27.8 0.0 collective-permute-start.4
  27.8 0.6 %shard_map.107 = (f32[64,512]{1,0:T(8,128)S(1)}, f32[64,512]{1,0:T(8,128)S(1)}) custom-call(bf16[32,2,2048]{2,1,0:T(2,128)(2,1)S(1)} %all_to_all.10.near_ref, bf16[2048,512]{1,0:T(8,128)(2,1)S(1)} %get-tuple-element.36.w_in_ref, bf16[512,2048]{1,0:T(8,128)(2,1)S(1)} %get-tuple-element.37.w_out_ref), custom_call_target="tpu_custom_call" | custom-call | tf_op jit(solution)/shard_map/pallas_call | solution.py:340
  28.4 0.9 %collective-permute-done.4.far_ref = bf16[32,2,2048]{2,1,0:T(2,128)(2,1)S(1)} collective-permute-done((bf16[32,2,2048]{2,1,0:T(2,128)(2,1)S(1)}, bf16[32,2,2048]{2,1,0:T(2,128)(2,1)S(1)}, u32[]{:S(2)}, u32[]{:S(2)}) %collective-permute-start.4) | collective-permute-done | bytes 262176 | tf_op jit(solution)/shard_map/ppermute | solution.py:369
  29.4 1.0 %shard_map.108 = (bf16[64,512]{1,0:T(8,128)(2,1)S(1)}, bf16[64,1024]{1,0:T(8,128)(2,1)S(1)}) custom-call(bf16[32,2,2048]{2,1,0:T(2,128)(2,1)S(1)} %collective-permute-done.4.far_ref, f32[64,512]{1,0:T(8,128)S(1)} %get-tuple-element.38.pre_ref, f32[64,512]{1,0:T(8,128)S(1)} %get-tuple-element.39.back_ref, bf16[2048,512]{1,0:T(8,128)(2,1)S(1)} %get-tuple-element.36.w_in_ref, ...), custom_call_target="tpu_custom_call" | custom-call | tf_op jit(solution)/shard_map/pallas_call | solution.py:340
  30.3 0.2 collective-permute-start.5
  30.5 0.5 %shard_map.109 = (f32[64,1024]{1,0:T(8,128)S(1)}, bf16[32,2048]{1,0:T(8,128)(2,1)S(1)}) custom-call(bf16[64,512]{1,0:T(8,128)(2,1)S(1)} %get-tuple-element.40.slope_ref, bf16[2048,512]{1,0:T(8,128)(2,1)S(1)} %get-tuple-element.36.w_in_ref, bf16[32,2048]{1,0:T(8,128)(2,1)S(1)} %get-tuple-element.41.near_ref, bf16[20,2048]{1,0:T(8,128)(2,1)S(1)} %collective-permute-done.3.came_ref), custom_call_target="tpu_custom_call" | custom-call | tf_op jit(solution)/shard_map/pallas_call | solution.py:340
  31.1 0.7 %collective-permute-done.5.came_ref = bf16[64,1024]{1,0:T(8,128)(2,1)S(1)} collective-permute-done((bf16[64,1024]{1,0:T(8,128)(2,1)S(1)}, bf16[64,1024]{1,0:T(8,128)(2,1)S(1)}, u32[]{:S(2)}, u32[]{:S(2)}) %collective-permute-start.5) | collective-permute-done | bytes 131104 | tf_op jit(solution)/shard_map/ppermute | solution.py:369
  31.8 9.7 %all_to_all.11.back_ref = bf16[32,8,256]{2,1,0:T(8,128)(2,1)S(1)} all-to-all(bf16[32,8,256]{2,1,0:T(8,128)(2,1)S(1)} %shard_map.110), channel_id=1, replica_groups=mesh['grp'=4,'z'=4,'core'=2] {'core','grp','z'}, dimensions={0} | all-to-all | bytes 262144 | tf_op jit(solution)/shard_map/all_to_all | solution.py:450
  41.5 1.4 %shard_map.111 = (bf16[8,4,2048]{2,1,0:T(4,128)(2,1)}, bf16[8,4,2048]{2,1,0:T(4,128)(2,1)}, bf16[8,4,2048]{2,1,0:T(4,128)(2,1)}) custom-call(bf16[256,256]{1,0:T(8,128)(2,1)S(1)} %get-tuple-element.26.spread_ref, bf16[32,8,256]{2,1,0:T(8,128)(2,1)S(1)} %all_to_all.11.back_ref, bf16[32,2048]{1,0:T(8,128)(2,1)S(1)} %get-tuple-element.44.cot_ref, ...), custom_call_target="tpu_custom_call" | custom-call | tf_op jit(solution)/shard_map/pallas_call | solution.py:340
  (2 shorter events, 0.1 us)
Async XLA Ops:
  1.5 7.9 %collective-permute-start = (bf16[8,2048]{1,0:T(8,128)(2,1)S(1)}, bf16[8,2048]{1,0:T(8,128)(2,1)S(1)}, u32[]{:S(2)}, u32[]{:S(2)}) collective-permute-start(bf16[8,2048]{1,0:T(8,128)(2,1)S(1)} %get-tuple-element.31), channel_id=1, source_target_pairs={{0,5},{1,4},{2,7},{3,6},{4,1},{5,0},{6,3},{7,2},{8,13},{9,12},{10,... | collective-permute-start | bytes 98312 | tf_op jit(solution)/shard_map/ppermute | solution.py:373
  5.1 5.2 %collective-permute-start.1 = (bf16[8,2048]{1,0:T(8,128)(2,1)S(1)}, bf16[8,2048]{1,0:T(8,128)(2,1)S(1)}, u32[]{:S(2)}, u32[]{:S(2)}) collective-permute-start(bf16[8,2048]{1,0:T(8,128)(2,1)S(1)} %get-tuple-element.32), channel_id=1, source_target_pairs={{0,7},{1,6},{2,5},{3,4},{4,3},{5,2},{6,1},{7,0},{8,15},{9,14},{10,... | collective-permute-start | bytes 98312 | tf_op jit(solution)/shard_map/ppermute | solution.py:373
  6.7 3.8 %collective-permute-start.2 = (bf16[8,2048]{1,0:T(8,128)(2,1)S(1)}, bf16[8,2048]{1,0:T(8,128)(2,1)S(1)}, u32[]{:S(2)}, u32[]{:S(2)}) collective-permute-start(bf16[8,2048]{1,0:T(8,128)(2,1)S(1)} %get-tuple-element.33), channel_id=1, source_target_pairs={{0,3},{1,2},{2,1},{3,0},{4,7},{5,6},{6,5},{7,4},{8,11},{9,10},{10,... | collective-permute-start | bytes 98312 | tf_op jit(solution)/shard_map/ppermute | solution.py:373
  10.7 1.7 %collective-permute-start.3 = (bf16[20,2048]{1,0:T(8,128)(2,1)S(1)}, bf16[20,2048]{1,0:T(8,128)(2,1)S(1)}, u32[]{:S(2)}, u32[]{:S(2)}) collective-permute-start(bf16[20,2048]{1,0:T(8,128)(2,1)S(1)} %get-tuple-element.35), channel_id=1, source_target_pairs={{0,1},{1,0},{2,3},{3,2},{4,5},{5,4},{6,7},{7,6},{8,9},{9,8},{10,11... | collective-permute-start | bytes 245768 | tf_op jit(solution)/shard_map/ppermute | solution.py:369
  27.8 1.5 %collective-permute-start.4 = (bf16[32,2,2048]{2,1,0:T(2,128)(2,1)S(1)}, bf16[32,2,2048]{2,1,0:T(2,128)(2,1)S(1)}, u32[]{:S(2)}, u32[]{:S(2)}) collective-permute-start(bf16[32,2,2048]{2,1,0:T(2,128)(2,1)S(1)} %all_to_all.10.near_ref), channel_id=1, source_target_pairs={{0,1},{1,0},{2,3},{3,2},{4,5},{5,4},{6,7},{7,6},{8,9},{9,8},{10,11... | collective-permute-start | bytes 786440 | tf_op jit(solution)/shard_map/ppermute | solution.py:369
  30.3 1.4 %collective-permute-start.5 = (bf16[64,1024]{1,0:T(8,128)(2,1)S(1)}, bf16[64,1024]{1,0:T(8,128)(2,1)S(1)}, u32[]{:S(2)}, u32[]{:S(2)}) collective-permute-start(bf16[64,1024]{1,0:T(8,128)(2,1)S(1)} %get-tuple-element.43), channel_id=1, source_target_pairs={{0,1},{1,0},{2,3},{3,2},{4,5},{5,4},{6,7},{7,6},{8,9},{9,8},{10,11... | collective-permute-start | bytes 393224 | tf_op jit(solution)/shard_map/ppermute | solution.py:369
